TPU v7x, 32 devices: a whole 2x2x4 slice. The times are simulated.
32 devices in a mesh: tm: 8 (over z, x), stream: 2 (over core), head: 2 (over y).
Axes of the slice: x: 2, y: 2, z: 4, core: 2. Of those that a mesh axis runs over, the one named last changes fastest.
Arguments:
- residual_signal: bfloat16 [2, 8192, 1024], P('stream', 'tm', 'head'), may hold values from -12 to 12
- prescale_amplifier: float32 [2, 1024], P('stream'), may hold values from 0.1 to 1.9
- triple_projector: bfloat16 [2, 1024, 8, 384], P('stream', None, 'head'), may hold values from -0.1875 to 0.1875
- score_scaler: float32 [2, 8], P('stream', 'head'), may hold values from 2 to 5
- recall_retained_logshare: float32 [2, 8, 8192], P('stream', 'head', 'tm'), may hold values from -1.9 to 0
- tile_retain_grid: int32 [16, 2], P('tm'), may hold values 0 or 1
- recall_store_flags: int32 [16], P('tm'), may hold values 0 or 1
- emission_projector: bfloat16 [2, 8, 128, 1024], P('stream', 'head'), may hold values from -0.25 to 0.25
- sideways_coupling_coef: bfloat16 [2, 8, 128, 1024], P('stream', 'head'), may hold values from -0.25 to 0.25
Outputs:
- update: bfloat16 [2, 8192, 1024], P('stream', 'tm', 'head')
All inputs are finite; a program needn't handle non-finite values. No bound on the sum of `tile_retain_grid` or of `recall_store_flags` on one device may be relied on, other than what follows from the above.
Results may differ from a plain program's by a relative error of at most 0.028.
Values may be sent and summed in bfloat16 or wider, within the bound.
No kernel may reach another device: no remote copies, remote signals or barrier semaphores. Data moves between devices by JAX's collectives and lax.ppermute only.
A program may use at most 64 MiB of HBM per device.

v0:
```python
import math

import jax
import jax.numpy as jnp
from jax import lax
from jax.sharding import PartitionSpec as P

BLOCK = 512


epsilon = 1e-06


def entering(value, axis, combine, identity):
    size, mine = (lax.axis_size(axis), lax.axis_index(axis))
    everything = jax.tree.map(
        lambda part, kind: lax.all_gather(part.astype(kind), axis),
        value,
        (jnp.bfloat16, jnp.bfloat16),
    )
    start = jax.tree.map(
        lambda part, zero: jnp.broadcast_to(jnp.asarray(zero, part.dtype), part.shape),
        value,
        identity,
    )

    def turn(k, before):
        reached = k < mine
        new = combine(
            before, jax.tree.map(lambda part, own: part[k].astype(own.dtype), everything, value)
        )
        return jax.tree.map(lambda a, b: jnp.where(reached, a, b), new, before)

    return lax.fori_loop(0, size, turn, start)


def unit_rms(values):
    return values * lax.rsqrt(jnp.mean(values * values, axis=-1, keepdims=True) + epsilon)


def block_attention(
    asker_lines, probe_array_facets, content_array_facets, temper, keep_table, facet_extent
):
    results = []
    for block_index in range(asker_lines.shape[0] // BLOCK):
        key_span = (block_index + 1) * BLOCK
        scores = jnp.einsum(
            "qhd,khd->hqk",
            asker_lines[block_index * BLOCK : key_span],
            probe_array_facets[:key_span],
            preferred_element_type=jnp.float32,
        )
        scores = scores * (temper / math.sqrt(facet_extent))[:, None, None]
        key_place = jnp.arange(key_span, dtype=jnp.int32)
        query_place = block_index * BLOCK + jnp.arange(BLOCK, dtype=jnp.int32)
        key_block = key_place // BLOCK
        earlier = (key_block < block_index) & (
            jnp.repeat(keep_table[block_index, : block_index + 1], BLOCK) == 1
        )
        diagonal = (key_block[None, :] == block_index) & (
            key_place[None, :] <= query_place[:, None]
        )
        allowed = earlier[None, :] | diagonal
        powers = jnp.where(allowed[None], jnp.exp(scores), 0.0)
        totals = jnp.sum(powers, axis=-1)
        weights = powers.astype(jnp.bfloat16)
        weighted = jnp.einsum(
            "hqk,khd->qhd",
            weights,
            content_array_facets[:key_span],
            preferred_element_type=jnp.float32,
        )
        results.append(weighted / jnp.transpose(totals)[:, :, None])
    return jnp.concatenate(results, axis=0)


def per_device(
    residual_signal,
    prescale_amplifier,
    triple_projector,
    score_scaler,
    recall_retained_logshare,
    tile_retain_grid,
    recall_store_flags,
    emission_projector,
    sideways_coupling_coef,
):
    gathered = lax.all_gather(residual_signal, "head", axis=2, tiled=True)[0]
    stretch_len = gathered.shape[0]
    full_width = gathered.shape[1]
    head_count = triple_projector.shape[2]
    facet_extent = emission_projector.shape[2]
    inputs = gathered.astype(jnp.float32)
    normed = (unit_rms(inputs) * prescale_amplifier[0]).astype(jnp.bfloat16)
    matrix = triple_projector[0].reshape(full_width, head_count * 3 * facet_extent)
    projected = jnp.dot(normed, matrix, preferred_element_type=jnp.float32).reshape(
        stretch_len, head_count, 3, facet_extent
    )
    asker_lines = unit_rms(projected[:, :, 0]).astype(jnp.bfloat16)
    probe_array_facets = unit_rms(projected[:, :, 1]).astype(jnp.bfloat16)
    content_array_facets = projected[:, :, 2].astype(jnp.bfloat16)
    local_portion = block_attention(
        asker_lines,
        probe_array_facets,
        content_array_facets,
        score_scaler[0],
        tile_retain_grid,
        facet_extent,
    )
    running = jnp.cumsum(recall_retained_logshare[0], axis=1)
    chosen = jnp.repeat(recall_store_flags, BLOCK).astype(jnp.float32)
    fading = jnp.exp(running[:, -1:] - running) * chosen[None, :]
    weighted_keys = (
        jnp.transpose(probe_array_facets.astype(jnp.float32), (1, 0, 2)) * fading[:, :, None]
    )
    summary = jnp.einsum(
        "htd,the->hde",
        weighted_keys,
        content_array_facets.astype(jnp.float32),
        precision=lax.Precision.HIGHEST,
    )
    stretch_decay = jnp.exp(running[:, -1])

    def combine(earlier, latter):
        return (earlier[0] * latter[0], latter[0][:, None, None] * earlier[1] + latter[1])

    carried = entering(
        (stretch_decay, summary),
        "tm",
        combine,
        (jnp.ones_like(stretch_decay), jnp.zeros_like(summary)),
    )
    memory_state = carried[1]
    total_tokens = stretch_len * lax.axis_size("tm")
    reading = jnp.einsum(
        "thd,hde->the",
        asker_lines.astype(jnp.float32),
        memory_state,
        precision=lax.Precision.HIGHEST,
    )
    recalled = (
        jnp.transpose(jnp.exp(running))[:, :, None]
        * reading
        * (1.0 / math.sqrt(facet_extent * total_tokens))
    )
    head_out = (
        (local_portion + recalled)
        .astype(jnp.bfloat16)
        .reshape(stretch_len, head_count * facet_extent)
    )
    own_matrix = emission_projector[0].reshape(head_count * facet_extent, full_width)
    side_matrix = sideways_coupling_coef[0].reshape(head_count * facet_extent, full_width)
    groups = lax.axis_size("head")
    slice_width = full_width // groups
    stream_here = lax.axis_index("stream")
    stacked = jnp.stack([own_matrix, side_matrix])

    def one_slot(slot_index):
        pick_index = (slot_index // groups != stream_here).astype(jnp.int32)
        source = lax.dynamic_index_in_dim(stacked, pick_index, 0, keepdims=False)
        columns = lax.dynamic_slice_in_dim(
            source, slot_index % groups * slice_width, slice_width, 1
        )
        return jnp.dot(head_out, columns, preferred_element_type=jnp.float32)

    slot_list = jnp.arange(
        stretch_len * lax.axis_size(("stream", "head")) // stretch_len, dtype=jnp.int32
    )
    update = lax.psum_scatter(
        lax.map(one_slot, slot_list)
        .reshape(stretch_len * lax.axis_size(("stream", "head")), slice_width)
        .astype(jnp.bfloat16),
        ("stream", "head"),
        scatter_dimension=0,
        tiled=True,
    )
    return update[None]


def solution(mesh):
    placed = (
        P("stream", "tm", "head"),
        P("stream", None),
        P("stream", None, "head", None),
        P("stream", "head"),
        P("stream", "head", "tm"),
        P("tm", None),
        P("tm"),
        P("stream", "head", None, None),
        P("stream", "head", None, None),
    )
    return jax.shard_map(
        per_device, mesh=mesh, in_specs=placed, out_specs=P("stream", "tm", "head"), check_vma=False
    )
```

profile of v0, /device:TPU:0, one launch (start us, length us, event | category | flops | bytes accessed | tf_op | source)
XLA Modules:
  0.0 188.4 jit_solution(15265977438590684571)
XLA Ops:
  6.5 0.7 all-gather.5.cloned.1.call-update
  7.3 0.7 copy.67
  8.0 1.1 reduce-window.6
  9.3 0.2 reduce-window.9
  9.8 1.2 dynamic-slice.6
  11.7 0.2 dynamic-update-slice
  11.9 23.1 %all-reduce = bf16[32]{0:T(256)(128)(2,1)S(1)} all-reduce(bf16[32]{0:T(256)(128)(2,1)S(1)} %dynamic-update-slice), channel_id=2, replica_groups=mesh['tm'=8,'stream'=2,'head'=2] {'tm'}, use_global_device_ids=true, to_apply=%add | all-reduce | flops 32 | bytes 128
  35.0 2.4 %copy.56 = bf16[128,8,4,384]{3,1,2,0:T(8,128)(2,1)S(1)} copy(bf16[128,8,4,384]{3,2,1,0:T(4,128)(2,1)} %bitcast.125) | data formatting | bytes 6291456
  37.5 2.9 %copy.34 = bf16[1536,1024]{1,0:T(8,128)(2,1)} copy(bf16[1536,1024]{0,1:T(8,128)(2,1)S(1)} %bitcast.123) | data formatting | bytes 6291456 | tf_op jit(solution)/shard_map/dot_general | solution.py:96
  40.4 0.5 slice.46
  41.9 1.7 pad_maximum_fusion
  43.7 0.9 fusion.41
  44.7 1.3 fusion.30
  45.9 2.1 %fusion.6 = f32[1024]{0:T(1024)S(1)} fusion(bf16[1,1024,1024]{2,1,0:T(8,128)(2,1)} %all-gather.5.cloned.1.call-done), kind=kLoop, calls=%fused_computation.12 | loop fusion | flops 3144704 | bytes 2101248 | tf_op jit(solution)/shard_map/reduce_sum | solution.py:38
  48.0 6.1 %fusion.67 = (bf16[1024,4,3,128]{0,3,2,1:T(8,128)(2,1)S(1)}, f32[1024,4,3,128]{0,3,2,1:T(8,128)S(1)}) fusion(bf16[4,3,128,1024]{3,2,1,0:T(8,128)(2,1)} %bitcast.126, bf16[1,1024,1024]{2,1,0:T(8,128)(2,1)} %all-gather.5.cloned.1.call-done, f32[1024]{0:T(1024)S(1)} %bitcast.136, f32[1024]{0:T(1024)S(1)} %add_rsqrt_fusion.2), kind=kOutput, calls=%fused_computation.99 | convolution fusion | flops 3226992640 | bytes 14688256 | tf_op jit(solution)/shard_map/dot_general | solution.py:96
  54.1 0.6 multiply_reduce_fusion.1
  54.7 0.6 multiply_convert_fusion.1
  55.3 0.6 copy-done.8
  55.9 0.4 copy-done
  56.3 2.0 %fusion.38 = bf16[4,128,128]{2,1,0:T(8,128)(2,1)} fusion(bf16[1024,4,128]{0,2,1:T(8,128)(2,1)S(1)} %get-tuple-element.269, f32[4,1024]{1,0:T(4,128)S(1)} %get-tuple-element.271, bf16[1024,4,3,128]{0,3,2,1:T(8,128)(2,1)S(1)} %get-tuple-element.272), kind=kOutput, calls=%fused_computation.49 | convolution fusion | flops 806420480 | bytes 2244608 | tf_op jit(solution)/shard_map/htd,the->hde/dot_general | solution.py:116
  58.3 0.2 reduce-scatter.2.cloned.1.call-start
  58.5 2.6 %fusion.14 = (f32[4,512]{1,0:T(4,128)S(1)}, f32[4,512,512]{1,2,0:T(8,128)S(1)}) fusion(f32[4]{0:T(128)S(1)} %multiply_bitcast_fusion, pred[512,512]{0,1:T(8,128)(4,1)} %fusion.41, bf16[1024,4,128]{0,2,1:T(8,128)(2,1)} %copy-done, bf16[1024,4,128]{0,2,1:T(8,128)(2,1)S(1)} %get-tuple-element.268), kind=kOutput, calls=%fused_computation.20 | convolution fusion | flops 271579136 | bytes 5513728 | tf_op jit(solution)/shard_map/qhd,khd->hqk/dot_general | solution.py:47
  61.2 2.0 %fusion.42 = f32[512,4,128]{0,2,1:T(8,128)} fusion(f32[4,512,512]{1,2,0:T(8,128)S(1)} %get-tuple-element.277, f32[4]{0:T(128)S(1)} %multiply_bitcast_fusion, pred[512,512]{0,1:T(8,128)(4,1)S(1)} %copy-done.3, bf16[1024,4,3,128]{0,3,2,1:T(8,128)(2,1)S(1)} %copy-done.9, f32[512,4]{0,1:T(4,128)S(1)} %bitcast.138), kind=kOutput, calls=%fused_computation.55 | convolution fusion | flops 271843328 | bytes 6038016 | tf_op jit(solution)/shard_map/hqk,khd->qhd/dot_general | solution.py:67
  63.2 2.6 %fusion.4 = (f32[4,512]{1,0:T(4,128)S(1)}, f32[4,512,1024]{2,1,0:T(8,128)S(1)}) fusion(f32[4]{0:T(128)S(1)} %multiply_bitcast_fusion, pred[512,1024]{1,0:T(8,128)(4,1)S(1)} %copy-done.2, bf16[1024,4,128]{0,2,1:T(8,128)(2,1)S(1)} %copy-done.1, bf16[1024,4,128]{0,2,1:T(8,128)(2,1)S(1)} %get-tuple-element.268), kind=kOutput, calls=%fused_computation.8 | convolution fusion | flops 543160320 | bytes 10494464 | tf_op jit(solution)/shard_map/qhd,khd->hqk/dot_general | solution.py:47
  65.8 2.8 %fusion.45 = f32[512,4,128]{0,2,1:T(8,128)} fusion(f32[4,512,1024]{2,1,0:T(8,128)S(1)} %get-tuple-element.275, f32[4]{0:T(128)S(1)} %multiply_bitcast_fusion, pred[512,1024]{1,0:T(8,128)(4,1)S(1)} %copy-done.2, bf16[1024,4,3,128]{0,3,2,1:T(8,128)(2,1)S(1)} %copy-done.9, f32[512,4]{0,1:T(4,128)S(1)} %bitcast.137), kind=kOutput, calls=%fused_computation.56 | convolution fusion | flops 543424512 | bytes 11018752 | tf_op jit(solution)/shard_map/hqk,khd->qhd/dot_general | solution.py:67
  68.7 28.8 %all-gather.7.cloned.1.call-done = bf16[32,128,128]{2,1,0:T(8,128)(2,1)} async-done(((bf16[4,128,128]{2,1,0:T(8,128)(2,1)}), bf16[32,128,128]{2,1,0:T(8,128)(2,1)}) %all-gather.7.cloned.1.call-update) | async-done | bytes 1048592 | tf_op jit(solution)/shard_map/all_gather | solution.py:17
  97.5 8.4 %while.28 = (s32[]{:T(128)}, f32[4,128,128]{2,1,0:T(8,128)S(1)}, s32[]{:T(128)}, bf16[8,4]{1,0:T(8,128)(2,1)S(1)}, bf16[8,4,128,128]{3,2,1,0:T(8,128)(2,1)}, /*index=5*/s32[]{:T(128)}, s32[]{:T(128)}) while((s32[]{:T(128)}, f32[4,128,128]{2,1,0:T(8,128)S(1)}, s32[]{:T(128)}, bf16[8,4]{1,0:T(8,128)(2,1)S(1)}, ...), condition=%wide.region_8.9_spmd.clone, body=%wide.region_7.8_spmd.clone.sunk | while | flops 327688 | bytes 655505 | solution.py:34
  97.5 1.0 fusion.78
  98.6 1.0 fusion.78
  99.6 1.0 fusion.78
  100.7 1.0 fusion.78
  101.7 1.0 fusion.78
  102.8 1.0 fusion.78
  103.8 1.0 fusion.78
  104.9 1.0 fusion.78
  105.9 3.7 %fusion.21 = bf16[1024,4,128]{0,2,1:T(8,128)(2,1)} fusion(f32[512,4,128]{0,2,1:T(8,128)} %fusion.45, f32[512,4,128]{0,2,1:T(8,128)} %fusion.42, f32[4,128,128]{2,1,0:T(8,128)S(1)} %get-tuple-element.206, bf16[1024,4,128]{0,2,1:T(8,128)(2,1)S(1)} %get-tuple-element.268, f32[1024,4]{0,1:T(4,128)S(1)} %get-tuple-element.270), kind=kOutput, calls=%fused_computation.29 | convolution fusion | flops 807927808 | bytes 4472832 | tf_op jit(solution)/shard_map/thd,hde->the/dot_general | solution.py:135
  109.6 1.5 copy.44
  111.1 21.1 %while.27 = (s32[]{:T(128)}, bf16[4,1024,512]{1,2,0:T(8,128)(2,1)}, s32[4]{0:T(128)S(1)}, s32[]{:T(128)}, bf16[2,512,1024]{2,1,0:T(8,128)(2,1)S(1)}, /*index=5*/...) while((s32[]{:T(128)}, bf16[4,1024,512]{1,2,0:T(8,128)(2,1)}, ...), condition=%wide.region_10.11_spmd, body=%wide.region_9.10_spmd.sunk | while | flops 536870912 | bytes 3670978 | solution.py:170
  111.1 0.6 dynamic_slice.42
  114.3 2.1 %bitcast_dynamic-update-slice_fusion.2 = bf16[4,1024,512]{1,2,0:T(8,128)(2,1)} fusion(bf16[4,1024,512]{1,2,0:T(8,128)(2,1)} %get-tuple-element.386, s32[]{:T(128)} %get-tuple-element.385, bf16[1024,512]{1,0:T(8,128)(2,1)S(1)} %get-tuple-element.402, bf16[2,512,1024]{2,1,0:T(8,128)(2,1)S(1)} %get-tuple-element.401, s32[]{:T(128)S(6)} %select_n.150, ...), kind=kOutput, calls=%fused_computation.clone.1 | convolution fusion | flops 536870912 | bytes 3670536 | tf_op jit(solution)/shard_map/while/body/eval_jaxpr/dot_general | solution.py:164
  116.4 0.6 dynamic_slice.42
  119.6 2.1 %bitcast_dynamic-update-slice_fusion.2 = bf16[4,1024,512]{1,2,0:T(8,128)(2,1)} fusion(bf16[4,1024,512]{1,2,0:T(8,128)(2,1)} %get-tuple-element.386, s32[]{:T(128)} %get-tuple-element.385, bf16[1024,512]{1,0:T(8,128)(2,1)S(1)} %get-tuple-element.402, bf16[2,512,1024]{2,1,0:T(8,128)(2,1)S(1)} %get-tuple-element.401, s32[]{:T(128)S(6)} %select_n.150, ...), kind=kOutput, calls=%fused_computation.clone.1 | convolution fusion | flops 536870912 | bytes 3670536 | tf_op jit(solution)/shard_map/while/body/eval_jaxpr/dot_general | solution.py:164
  121.7 0.6 dynamic_slice.42
  124.9 2.1 %bitcast_dynamic-update-slice_fusion.2 = bf16[4,1024,512]{1,2,0:T(8,128)(2,1)} fusion(bf16[4,1024,512]{1,2,0:T(8,128)(2,1)} %get-tuple-element.386, s32[]{:T(128)} %get-tuple-element.385, bf16[1024,512]{1,0:T(8,128)(2,1)S(1)} %get-tuple-element.402, bf16[2,512,1024]{2,1,0:T(8,128)(2,1)S(1)} %get-tuple-element.401, s32[]{:T(128)S(6)} %select_n.150, ...), kind=kOutput, calls=%fused_computation.clone.1 | convolution fusion | flops 536870912 | bytes 3670536 | tf_op jit(solution)/shard_map/while/body/eval_jaxpr/dot_general | solution.py:164
  126.9 0.6 dynamic_slice.42
  130.2 2.1 %bitcast_dynamic-update-slice_fusion.2 = bf16[4,1024,512]{1,2,0:T(8,128)(2,1)} fusion(bf16[4,1024,512]{1,2,0:T(8,128)(2,1)} %get-tuple-element.386, s32[]{:T(128)} %get-tuple-element.385, bf16[1024,512]{1,0:T(8,128)(2,1)S(1)} %get-tuple-element.402, bf16[2,512,1024]{2,1,0:T(8,128)(2,1)S(1)} %get-tuple-element.401, s32[]{:T(128)S(6)} %select_n.150, ...), kind=kOutput, calls=%fused_computation.clone.1 | convolution fusion | flops 536870912 | bytes 3670536 | tf_op jit(solution)/shard_map/while/body/eval_jaxpr/dot_general | solution.py:164
  132.2 6.2 %copy.45 = bf16[4,1024,512]{2,1,0:T(8,128)(2,1)} copy(bf16[4,1024,512]{1,2,0:T(8,128)(2,1)} %get-tuple-element.207) | data formatting | bytes 8388608 | tf_op jit(solution)/shard_map/convert_element_type | solution.py:172
  138.4 43.4 %reduce-scatter.2.cloned.1.call-done = bf16[1024,512]{1,0:T(8,128)(2,1)} async-done(((bf16[4096,512]{1,0:T(8,128)(2,1)}), bf16[1024,512]{1,0:T(8,128)(2,1)}) %reduce-scatter.2.cloned.1.call-update) | async-done | bytes 1048592 | tf_op jit(solution)/shard_map/reduce_scatter | solution.py:169
  (55 shorter events, 1.0 us)
Async XLA Ops:
  6.5 39.4 %all-gather.5.cloned.1.call-start = ((), (), s32[]{:S(2)}) async-start(), calls=%async_computation.1 | async-start | bytes 3145728 | tf_op jit(solution)/shard_map/all_gather | solution.py:88
  7.3 90.3 %all-gather.7.cloned.1.call-start = ((), (), s32[]{:S(2)}) async-start(), calls=%async_computation.3 | async-start | bytes 1179648 | tf_op jit(solution)/shard_map/all_gather | solution.py:17
  37.5 2.9 %copy-start.5 = (s32[2,2]{1,0:T(2,128)S(1)}, s32[2,2]{1,0:T(2,128)}, u32[]{:S(2)}) copy-start(s32[2,2]{1,0:T(2,128)} %param.18) | copy-start | bytes 52
  37.5 3.5 %copy-start.6 = (s32[2]{0:T(128)S(1)}, s32[2]{0:T(128)}, u32[]{:S(2)}) copy-start(s32[2]{0:T(128)} %param.19) | copy-start | bytes 28
  40.4 3.2 %copy-start.7 = (f32[1,4]{1,0:T(1,128)S(1)}, f32[1,4]{1,0:T(1,128)}, u32[]{:S(2)}) copy-start(f32[1,4]{1,0:T(1,128)} %param.16) | copy-start | bytes 52
  41.9 6.2 %copy-start.4 = (f32[1,1024]{1,0:T(1,128)S(1)}, f32[1,1024]{1,0:T(1,128)}, u32[]{:S(2)}) copy-start(f32[1,1024]{1,0:T(1,128)} %param.14) | copy-start | bytes 12292
  54.1 1.8 copy-start.8
  55.3 1.0 copy-start
  58.3 123.6 %reduce-scatter.2.cloned.1.call-start = ((), (), s32[]{:S(2)}) async-start(), calls=%async_computation.2 | async-start | bytes 5242880 | tf_op jit(solution)/shard_map/reduce_scatter | solution.py:169
  58.5 2.7 %copy-start.3 = (pred[512,512]{0,1:T(8,128)(4,1)S(1)}, pred[512,512]{0,1:T(8,128)(4,1)}, u32[]{:S(2)}) copy-start(pred[512,512]{0,1:T(8,128)(4,1)} %fusion.41) | copy-start | bytes 786436
  58.5 2.7 %copy-start.9 = (bf16[1024,4,3,128]{0,3,2,1:T(8,128)(2,1)S(1)}, bf16[1024,4,3,128]{0,3,2,1:T(8,128)(2,1)}, u32[]{:S(2)}) copy-start(bf16[1024,4,3,128]{0,3,2,1:T(8,128)(2,1)} %copy-done.8) | copy-start | bytes 9437188
  61.2 2.0 %copy-start.1 = (bf16[1024,4,128]{0,2,1:T(8,128)(2,1)S(1)}, bf16[1024,4,128]{0,2,1:T(8,128)(2,1)}, u32[]{:S(2)}) copy-start(bf16[1024,4,128]{0,2,1:T(8,128)(2,1)} %copy-done) | copy-start | bytes 3145732
  61.2 2.0 %copy-start.2 = (pred[512,1024]{1,0:T(8,128)(4,1)S(1)}, pred[512,1024]{1,0:T(8,128)(4,1)}, u32[]{:S(2)}) copy-start(pred[512,1024]{1,0:T(8,128)(4,1)} %fusion.30) | copy-start | bytes 1572868
Sparse Core Ops, SparseCore 0:
  8.9 35.8 all-gather.4
  58.4 39.0 all-gather.6
  138.6 43.2 reduce-scatter.1
where the time goes:
time: 189 us; the launch traced here: 188 us
  waiting for transfers between devices  73 us (39%)
  matrix products  30.1 us (16%)
  blocking collectives  23.1 us (12%)
  local copies, waits for them, and re-layouts  19.7 us (10%)
  other arithmetic  16.8 us (9%)
  between operations  14.7 us (8%)
  loops' own time  10.7 us (6%)
    reduce_scatter x1, waiting for transfers between devices, per_device(): lax.psum_scatter(lax.map(one_slot, slot_list).reshape(stretch_len * lax.a...  43.4 us
    all_gather x1, waiting for transfers between devices, entering(): lax.all_gather(part.astype(kind), axis)  28.8 us
    unnamed x1, blocking collectives  23.1 us
    another operation x1, loops' own time, per_device(): lax.map(one_slot, slot_list)  10.5 us
    dot_general x4, matrix products, one_slot(): return jnp.dot(head_out, columns, preferred_element_type=jnp.float32)  8.28 us
    select_n x8, other arithmetic, turn(): return jax.tree.map(lambda a, b: jnp.where(reached, a, b), new, before)  8.09 us
    convert_element_type x1, local copies, waits for them, and re-layouts, per_device(): update = lax.psum_scatter(lax.map(one_slot, slot_list).reshape(stretch_le...  6.2 us
    dot_general x1, matrix products, per_device(): jnp.dot(normed, matrix, preferred_element_type=jnp.float32)  6.09 us
  transfers between devices with their start and end apart: 3, of which 2 were waited for; matrix products, arithmetic and copies ran while one was open for 13% of the time, Pallas kernels for 0%

commit v1 on v0

v1 whole, which is shorter than its diff:
```python
import functools
import math

import jax
import jax.numpy as jnp
from jax import lax
from jax.experimental import pallas as pl
from jax.experimental.pallas import tpu as pltpu
from jax.sharding import PartitionSpec as P

BLOCK = 512
TILE = 256
TAIL = 16
IN_CHUNKS = 2
OUT_CHUNKS = 4
EPSILON = 1e-06
F32 = jnp.float32
BF16 = jnp.bfloat16
SMEM = pl.BlockSpec(memory_space=pltpu.SMEM)


def params(mib):
    return pltpu.CompilerParams(vmem_limit_bytes=mib * 1024 * 1024)


def dot(a, b):
    return lax.dot_general(a, b, (((1,), (0,)), ((), ())), preferred_element_type=F32)


def dot_nt(a, b):
    return lax.dot_general(a, b, (((1,), (1,)), ((), ())), preferred_element_type=F32)


def dot_tn(a, b):
    return lax.dot_general(a, b, (((0,), (0,)), ((), ())), preferred_element_type=F32)


def unit(values):
    return values * lax.rsqrt(jnp.mean(values * values, axis=-1, keepdims=True) + EPSILON)


def whole(shape):
    return pl.BlockSpec(shape, lambda i: (0,) * len(shape))


def qkv_kernel(shards, heads, dim, first, last, *refs):
    me_ref, gain_ref, w_ref, fade_ref, tail_ref, prev_ref = refs[:6]
    x_refs = refs[6 : 6 + shards]
    q_ref, k_ref, v_ref, sum_ref = refs[6 + shards : 10 + shards]
    width = x_refs[0].shape[1]
    step = pl.program_id(0)

    @pl.when(step == 0)
    def _():
        if first:
            sum_ref[...] = jnp.zeros_like(sum_ref)
        else:
            sum_ref[...] = prev_ref[...]

    me = me_ref[0]
    parts = [x[...].astype(F32) for x in x_refs]
    squares = sum(jnp.sum(p * p, axis=-1, keepdims=True) for p in parts)
    scale = lax.rsqrt(squares * (1.0 / (width * shards)) + EPSILON)
    total = None
    for k in range(shards):
        owner = lax.rem(me + k, shards)
        rows = pl.ds(pl.multiple_of(owner * width, width), width)
        normed = (parts[k] * scale * gain_ref[:, rows]).astype(BF16)
        term = dot(normed, w_ref[rows, :])
        total = term if total is None else total + term
    for h in range(heads):
        base = h * 3 * dim
        cols = slice(h * dim, (h + 1) * dim)
        q_ref[:, cols] = unit(total[:, base : base + dim]).astype(BF16)
        key = unit(total[:, base + dim : base + 2 * dim]).astype(BF16)
        value = total[:, base + 2 * dim : base + 3 * dim].astype(BF16)
        k_ref[:, cols] = key
        v_ref[:, cols] = value
        faded = (key.astype(F32) * fade_ref[:, h : h + 1]).astype(BF16)
        sum_ref[h] += dot_tn(faded, value)
    if last:
        load_ref = refs[10 + shards]

        @pl.when(step == pl.num_programs(0) - 1)
        def _():
            for h in range(heads):
                load_ref[h, :dim, :] = sum_ref[h].astype(BF16)
                load_ref[h, dim:, :] = tail_ref[h]


def qkv(me, gain, w, fade, tail, prev, xs, heads, dim, first, last):
    shards = len(xs)
    rows, width = xs[0].shape
    tile = min(TILE, rows)
    by_rows = lambda cols: pl.BlockSpec((tile, cols), lambda i: (i, 0))
    out_shape = [jax.ShapeDtypeStruct((rows, heads * dim), BF16)] * 3
    out_shape.append(jax.ShapeDtypeStruct((heads, dim, dim), F32))
    out_specs = [by_rows(heads * dim)] * 3 + [whole((heads, dim, dim))]
    if last:
        out_shape.append(jax.ShapeDtypeStruct((heads, dim + TAIL, dim), BF16))
        out_specs.append(whole((heads, dim + TAIL, dim)))
    return pl.pallas_call(
        functools.partial(qkv_kernel, shards, heads, dim, first, last),
        grid=(rows // tile,),
        in_specs=[
            SMEM,
            whole(gain.shape),
            whole(w.shape),
            by_rows(heads),
            whole(tail.shape),
            whole(prev.shape),
        ]
        + [by_rows(width)] * shards,
        out_specs=out_specs,
        out_shape=out_shape,
        compiler_params=params(40),
        cost_estimate=pl.CostEstimate(
            flops=2 * rows * w.shape[0] * w.shape[1], bytes_accessed=w.size * 2, transcendentals=0
        ),
        name="qkv",
    )(me, gain, w, fade, tail, prev, *xs)


def attention_kernel(pieces, head0, keep_ref, scale_ref, *refs):
    q_refs, k_refs, v_refs = refs[:pieces], refs[pieces : 2 * pieces], refs[2 * pieces : 3 * pieces]
    out_ref = refs[3 * pieces]
    scale = scale_ref[0, head0 + pl.program_id(0)]
    dim = out_ref.shape[1]
    joined = lambda rs: jnp.concatenate([r[...] for r in rs], axis=0)
    q, k, v = joined(q_refs), joined(k_refs), joined(v_refs)
    v = jnp.concatenate([v, jnp.ones_like(v)], axis=1)
    length = q.shape[0]
    per = BLOCK // TILE
    row = lax.broadcasted_iota(jnp.int32, (TILE, TILE), 0)
    col = lax.broadcasted_iota(jnp.int32, (TILE, TILE), 1)
    causal = col <= row
    for t in range(length // TILE):
        block = t // per
        mine = q[t * TILE : (t + 1) * TILE]
        span = slice(t * TILE, (t + 1) * TILE)
        powers = jnp.where(causal, jnp.exp(dot_nt(mine, k[span]) * scale), 0.0)
        total = dot(powers.astype(BF16), v[span])
        if t > block * per:
            span = slice(block * BLOCK, t * TILE)
            powers = jnp.exp(dot_nt(mine, k[span]) * scale)
            total += dot(powers.astype(BF16), v[span])
        for j in range(block):
            span = slice(j * BLOCK, (j + 1) * BLOCK)
            powers = jnp.exp(dot_nt(mine, k[span]) * scale)
            part = dot(powers.astype(BF16), v[span])
            total += jnp.where(keep_ref[block, j] == 1, part, 0.0)
        out_ref[t * TILE : (t + 1) * TILE, :] = (total[:, :dim] / total[:, dim:]).astype(BF16)


def attention(keep, scale, qs, ks, vs, head0, heads, dim):
    pieces = len(qs)
    length = sum(q.shape[0] for q in qs)
    spec = lambda rows: pl.BlockSpec((rows, dim), lambda h: (0, head0 + h))
    return pl.pallas_call(
        functools.partial(attention_kernel, pieces, head0),
        grid=(heads,),
        in_specs=[SMEM, SMEM] + [spec(a.shape[0]) for a in (*qs, *ks, *vs)],
        out_specs=pl.BlockSpec((length, dim), lambda h: (0, h)),
        out_shape=jax.ShapeDtypeStruct((length, heads * dim), BF16),
        compiler_params=params(40),
        cost_estimate=pl.CostEstimate(
            flops=heads * 3 * length * length * dim,
            bytes_accessed=heads * length * dim * 8,
            transcendentals=heads * length * length,
        ),
        name="attention",
    )(keep, scale, *qs, *ks, *vs)


def opened(ref, h, dim):
    body = ref[h, :dim, :].astype(F32)
    decay = ref[h, dim : dim + 1, :].astype(F32) + ref[h, dim + TAIL // 2 : dim + TAIL // 2 + 1, :].astype(F32)
    return body, decay


def pair_kernel(heads, dim, odd_ref, mine_ref, other_ref, out_ref):
    odd = odd_ref[0] == 1
    for h in range(heads):
        own, own_decay = opened(mine_ref, h, dim)
        far, far_decay = opened(other_ref, h, dim)
        early, late = jnp.where(odd, far, own), jnp.where(odd, own, far)
        late_decay = jnp.where(odd, own_decay, far_decay)
        both = own_decay * far_decay
        out_ref[h, :dim, :] = (late_decay * early + late).astype(BF16)
        high = both.astype(BF16)
        low = (both - high.astype(F32)).astype(BF16)
        out_ref[h, dim : dim + TAIL // 2, :] = jnp.broadcast_to(high, (TAIL // 2, dim))
        out_ref[h, dim + TAIL // 2 :, :] = jnp.broadcast_to(low, (TAIL // 2, dim))


def pair(odd, mine, other):
    heads, _, dim = mine.shape
    return pl.pallas_call(
        functools.partial(pair_kernel, heads, dim),
        in_specs=[SMEM] + [pl.BlockSpec(memory_space=pltpu.VMEM)] * 2,
        out_specs=pl.BlockSpec(memory_space=pltpu.VMEM),
        out_shape=jax.ShapeDtypeStruct(mine.shape, BF16),
        cost_estimate=pl.CostEstimate(flops=mine.size, bytes_accessed=mine.size * 6, transcendentals=0),
        name="pair",
    )(odd, mine, other)


def recall_kernel(count, groups, heads, dim, paired, odd_ref, gain_ref, q_ref, *refs):
    local_refs, refs = refs[:groups], refs[groups:]
    other_ref, far_refs = refs[0], refs[1 : 1 + count]
    out_ref = refs[1 + count]
    per = heads // groups
    for h in range(heads):
        state = None
        for ref in reversed(far_refs):
            body, decay = opened(ref, h, dim)
            state = body if state is None else body + decay * state
        if paired:
            body, decay = opened(other_ref, h, dim)
            later = body if state is None else decay * state + body
            first = jnp.zeros_like(body) if state is None else state
            state = jnp.where(odd_ref[0] == 1, later, first)
        if state is None:
            state = jnp.zeros((dim, dim), F32)
        cols = slice(h * dim, (h + 1) * dim)
        recalled = dot(q_ref[:, cols], state.astype(BF16)) * gain_ref[:, h : h + 1]
        local = local_refs[h // per][:, h % per * dim : (h % per + 1) * dim]
        out_ref[:, cols] = (local.astype(F32) + recalled).astype(BF16)


def recall(odd, gain, q, locals_, other, fars, index, chunk, q_index, paired):
    heads, _, dim = other.shape
    groups = len(locals_)
    rows = lambda cols, at: pl.BlockSpec((chunk, cols), lambda i: (at, 0))
    load = whole(other.shape)
    return pl.pallas_call(
        functools.partial(recall_kernel, len(fars), groups, heads, dim, paired),
        grid=(1,),
        in_specs=[SMEM, rows(heads, index), rows(heads * dim, q_index)]
        + [rows(heads // groups * dim, index)] * groups
        + [load] * (1 + len(fars)),
        out_specs=pl.BlockSpec((chunk, heads * dim), lambda i: (0, 0)),
        out_shape=jax.ShapeDtypeStruct((chunk, heads * dim), BF16),
        compiler_params=params(40),
        cost_estimate=pl.CostEstimate(
            flops=2 * chunk * heads * dim * dim, bytes_accessed=chunk * heads * dim * 6, transcendentals=0
        ),
        name="recall",
    )(odd, gain, q, *locals_, other, *fars)


def project_kernel(shards, me_ref, own_ref, side_ref, own_w_ref, side_w_ref, *out_refs):
    width = out_refs[0].shape[1]
    own, side = own_ref[...], side_ref[...]
    for k in reversed(range(shards)):
        owner = lax.rem(me_ref[0] + k, shards)
        cols = pl.ds(pl.multiple_of(owner * width, width), width)
        out = dot(own, own_w_ref[:, cols]) + dot(side, side_w_ref[:, cols])
        out_refs[k][...] = out.astype(out_refs[k].dtype)


def project(me, own, side, own_w, side_w, shards):
    rows = own.shape[0]
    width = own_w.shape[1] // shards
    vmem = pl.BlockSpec(memory_space=pltpu.VMEM)
    return pl.pallas_call(
        functools.partial(project_kernel, shards),
        in_specs=[SMEM] + [vmem] * 4,
        out_specs=[vmem] * shards,
        out_shape=[jax.ShapeDtypeStruct((rows, width), BF16)] * shards,
        compiler_params=params(40),
        cost_estimate=pl.CostEstimate(
            flops=4 * rows * own_w.size, bytes_accessed=own_w.size * 4, transcendentals=0
        ),
        name="project",
    )(me, own, side, own_w, side_w)


def per_device(
    residual_signal,
    prescale_amplifier,
    triple_projector,
    score_scaler,
    recall_retained_logshare,
    tile_retain_grid,
    recall_store_flags,
    emission_projector,
    sideways_coupling_coef,
):
    x = residual_signal[0]
    length = x.shape[0]
    shards = lax.axis_size("head")
    blocks = lax.axis_size("tm")
    heads = triple_projector.shape[2]
    dim = emission_projector.shape[2]
    me = lax.axis_index("head").astype(jnp.int32).reshape(1)
    place = lax.axis_index("tm")
    paired = blocks % 2 == 0
    odd = (place % 2 if paired else place * 0).astype(jnp.int32).reshape(1)
    swap_streams = [(0, 1), (1, 0)]

    in_rows = length // IN_CHUNKS
    received = []
    for c in range(IN_CHUNKS):
        piece = x[c * in_rows : (c + 1) * in_rows]
        xs = [piece]
        for k in range(1, shards):
            xs.append(lax.ppermute(piece, "head", [((d + k) % shards, d) for d in range(shards)]))
        received.append(xs)

    own_w = emission_projector[0].reshape(heads * dim, -1)
    side_mine = sideways_coupling_coef[0].reshape(heads * dim, -1)
    side_w = lax.ppermute(side_mine, "stream", swap_streams)

    running = jnp.cumsum(recall_retained_logshare[0], axis=1)
    flags = jnp.repeat(recall_store_flags, BLOCK).astype(F32)
    fade = jnp.transpose(jnp.exp(running[:, -1:] - running) * flags[None, :])
    reading = jnp.transpose(jnp.exp(running)) * (1.0 / math.sqrt(dim * length * blocks))
    decay = jnp.exp(running[:, -1])
    high = decay.astype(BF16)
    low = (decay - high.astype(F32)).astype(BF16)
    tail = jnp.concatenate(
        [jnp.broadcast_to(part[:, None, None], (heads, TAIL // 2, dim)) for part in (high, low)], axis=1
    )
    scale = score_scaler * (1.0 / math.sqrt(dim))
    gain = prescale_amplifier
    w = triple_projector[0].reshape(triple_projector.shape[1], -1)

    qs, ks, vs = [], [], []
    summary = jnp.zeros((heads, dim, dim), F32)
    for c in range(IN_CHUNKS):
        last = c == IN_CHUNKS - 1
        results = qkv(
            me,
            gain,
            w,
            fade[c * in_rows : (c + 1) * in_rows],
            tail,
            summary,
            received[c],
            heads,
            dim,
            c == 0,
            last,
        )
        qs.append(results[0])
        ks.append(results[1])
        vs.append(results[2])
        summary = results[3]
    mine = results[4]

    other, joint, step = mine, mine, 1
    if paired:
        step = 2
        other = lax.ppermute(mine, "tm", [(d, d ^ 1) for d in range(blocks)])
        joint = pair(odd, mine, other)
    fars = [
        lax.ppermute(joint, "tm", [(d, d + k) for d in range(blocks - k)])
        for k in range(step, blocks, step)
    ]

    groups = 2 if heads % 2 == 0 else 1
    per = heads // groups
    locals_ = [
        attention(tile_retain_grid, scale, qs, ks, vs, g * per, per, dim) for g in range(groups)
    ]

    chunk = length // OUT_CHUNKS
    per_piece = in_rows // chunk
    done = []
    for c in range(OUT_CHUNKS):
        head_out = recall(
            odd, reading, qs[c // per_piece], locals_, other, fars, c, chunk, c % per_piece, paired
        )
        side = lax.ppermute(head_out, "stream", swap_streams)
        outs = project(me, head_out, side, own_w, side_w, shards)
        total = outs[0].astype(F32)
        for k in range(1, shards):
            total += lax.ppermute(
                outs[k], "head", [(d, (d + k) % shards) for d in range(shards)]
            ).astype(F32)
        done.append(total.astype(BF16))
    return jnp.concatenate(done, axis=0)[None]


def solution(mesh):
    placed = (
        P("stream", "tm", "head"),
        P("stream", None),
        P("stream", None, "head", None),
        P("stream", "head"),
        P("stream", "head", "tm"),
        P("tm", None),
        P("tm"),
        P("stream", "head", None, None),
        P("stream", "head", None, None),
    )
    return jax.shard_map(
        per_device, mesh=mesh, in_specs=placed, out_specs=P("stream", "tm", "head"), check_vma=False
    )
```

time: 189 us -> 93.1 us (0.49)
  waiting for transfers between devices: 73 us -> 26.1 us
  matrix products: 30.1 us -> 0 us
  blocking collectives: 23.1 us -> 0 us
  Pallas kernels: 0 us -> 19.8 us
  starting transfers between devices: 0.26 us -> 19.9 us
  between operations: 14.7 us -> 0.3 us
  other arithmetic: 16.8 us -> 5.45 us
  loops' own time: 10.7 us -> 0 us
    reduce_scatter x1 -> x0, waiting for transfers between devices: 43.4 us -> none  [per_device(): lax.psum_scatter(lax.map(one_slot, slot_list).reshape(stretch_len * lax.a...]
    dot_general x11 -> x0, matrix products: 30.1 us -> none  [the longest x4 8.28 us: one_slot(): return jnp.dot(head_out, columns, preferred_element_type=jnp.float32)]
    all_gather x2 -> x0, waiting for transfers between devices: 28.8 us -> none  [the longest x1 28.8 us: entering(): lax.all_gather(part.astype(kind), axis)]
    ppermute x0 -> x15, waiting for transfers between devices: none -> 26.1 us  [the longest x4 18.5 us: per_device(): lax.ppermute(outs[k], 'head', [(d, (d + k) % shards) for d in range(shard...]
    unnamed x1 -> x0, blocking collectives: 23.1 us -> none
    ppermute x0 -> x15, starting transfers between devices: none -> 19.9 us  [the longest x3 9.49 us: per_device(): lax.ppermute(joint, 'tm', [(d, d + k) for d in range(blocks - k)])]
    pallas_call x0 -> x13, Pallas kernels: none -> 19.8 us  [the longest x2 7.54 us: qkv(): pl.pallas_call(functools.partial(qkv_kernel, shards, heads, dim, first, l...]
    unnamed x29 -> x50, local copies, waits for them, and re-layouts: 5.84 us -> 18 us
  transfers between devices with their start and end apart: 3 -> 15, of which waited for: 2 -> 7; matrix products, arithmetic and copies ran while one was open for 13% -> 11% of each run, Pallas kernels for 0% -> 21%
where the time goes in v1:
time: 93.1 us; the launch traced here: 92.4 us
  waiting for transfers between devices  26.1 us (28%)
  local copies, waits for them, and re-layouts  20.9 us (22%)
  starting transfers between devices  19.9 us (21%)
  Pallas kernels  19.8 us (21%)
  other arithmetic  5.45 us (6%)
    ppermute x4, waiting for transfers between devices, per_device(): lax.ppermute(outs[k], 'head', [(d, (d + k) % shards) for d in range(shard...  18.5 us
    unnamed x50, local copies, waits for them, and re-layouts  18 us
    ppermute x3, starting transfers between devices, per_device(): lax.ppermute(joint, 'tm', [(d, d + k) for d in range(blocks - k)])  9.49 us
    pallas_call x2, Pallas kernels, qkv(): pl.pallas_call(functools.partial(qkv_kernel, shards, heads, dim, first, l...  7.54 us
    pallas_call x2, Pallas kernels, attention(): pl.pallas_call(functools.partial(attention_kernel, pieces, head0), grid=(...  6.54 us
    ppermute x4, starting transfers between devices, per_device(): lax.ppermute(outs[k], 'head', [(d, (d + k) % shards) for d in range(shard...  4.31 us
    ppermute x2, waiting for transfers between devices, per_device(): lax.ppermute(piece, 'head', [((d + k) % shards, d) for d in range(shards)])  4.18 us
    ppermute x1, waiting for transfers between devices, per_device(): other = lax.ppermute(mine, 'tm', [(d, d ^ 1) for d in range(blocks)])  3.43 us
  transfers between devices with their start and end apart: 15, of which 7 were waited for; matrix products, arithmetic and copies ran while one was open for 11% of the time, Pallas kernels for 21%

profile of v1, /device:TPU:0, one launch (start us, length us, event | category | flops | bytes accessed | tf_op | source)
XLA Modules:
  0.0 92.4 jit_solution(1365452681177837765)
XLA Ops:
  0.0 1.3 %slice_bitcast_fusion = (bf16[512,512]{1,0:T(8,128)(2,1)S(1)}, bf16[512,512]{1,0:T(8,128)(2,1)S(1)}) fusion(bf16[1,1024,512]{2,1,0:T(8,128)(2,1)} %param.9), kind=kLoop, calls=%fused_computation.5 | loop fusion | bytes 2097152 | tf_op jit(solution)/shard_map/slice | solution.py:305
  1.3 3.0 %collective-permute-start = (bf16[512,512]{1,0:T(8,128)(2,1)S(1)}, bf16[512,512]{1,0:T(8,128)(2,1)S(1)}, u32[]{:S(2)}, u32[]{:S(2)}) collective-permute-start(bf16[512,512]{1,0:T(8,128)(2,1)S(1)} %get-tuple-element.38.refs_6_), channel_id=1, source_target_pairs={{1,0},{0,1},{3,2},{2,3},{5,4},{4,5},{7,6},{6,7},{9,8},{8,9},{11,10... | collective-permute-start | bytes 1572872 | tf_op jit(solution)/shard_map/ppermute | solution.py:308
  4.5 1.1 %reduce-window.6 = f32[4,8,128]{2,1,0:T(8,128)S(1)} reduce-window(f32[4,8,128]{2,1,0:T(8,128)S(1)} %bitcast.44, f32[]{:T(128)} %constant.29.clone.1), window={size=1x1x128 pad=0_0x0_0x127_0}, to_apply=%region_0.1 | reduce-window | flops 520192 | bytes 32772 | tf_op jit(solution)/shard_map/reduce-window
  6.3 0.8 copy-done.19
  7.1 2.0 %multiply_bitcast_fusion = (f32[1024,4]{1,0:T(8,128)}, f32[1024,4]{1,0:T(8,128)S(1)}) fusion(f32[1024]{0:T(1024)S(1)} %bitcast.45, f32[4]{0:T(128)S(1)} %slice_bitcast_fusion.2, f32[4,8,128]{0,2,1:T(8,128)} %copy-done.19), kind=kLoop, calls=%fused_computation.7 | loop fusion | flops 12288 | bytes 53264 | tf_op jit(solution)/shard_map/transpose | solution.py:317
  9.1 0.7 exponential_convert_fusion
  9.8 4.1 %copy.13 = bf16[128,8,4,384]{3,1,2,0:T(8,128)(2,1)} copy(bf16[128,8,4,384]{3,2,1,0:T(4,128)(2,1)} %bitcast.41) | data formatting | bytes 6291456
  13.9 1.1 %fusion = (f32[512,4]{1,0:T(8,128)S(1)}, f32[512,4]{1,0:T(8,128)S(1)}) fusion(f32[1024,4]{1,0:T(8,128)} %get-tuple-element.43), kind=kLoop, calls=%fused_computation.18 | loop fusion | bytes 32768 | tf_op jit(solution)/shard_map/slice | solution.py:337
  15.1 1.9 %collective-permute-done.refs_7_ = bf16[512,512]{1,0:T(8,128)(2,1)S(1)} collective-permute-done((bf16[512,512]{1,0:T(8,128)(2,1)S(1)}, bf16[512,512]{1,0:T(8,128)(2,1)S(1)}, u32[]{:S(2)}, u32[]{:S(2)}) %collective-permute-start) | collective-permute-done | bytes 524320 | tf_op jit(solution)/shard_map/ppermute | solution.py:308
  17.1 0.8 copy-done.5
  17.9 1.9 %copy-done.3 = bf16[128,8,4,384]{3,1,2,0:T(8,128)(2,1)S(1)} copy-done((bf16[128,8,4,384]{3,1,2,0:T(8,128)(2,1)S(1)}, bf16[128,8,4,384]{3,1,2,0:T(8,128)(2,1)}, u32[]{:S(2)}) %copy-start.3) | copy-done | bytes 3145752
  19.8 1.0 %copy-done.6 = bf16[512,512]{1,0:T(8,128)(2,1)S(1)} copy-done((bf16[512,512]{1,0:T(8,128)(2,1)S(1)}, bf16[512,512]{1,0:T(8,128)(2,1)}, u32[]{:S(2)}) %copy-start.6) | copy-done | bytes 524312
  20.8 2.9 %qkv.2 = (bf16[512,512]{1,0:T(8,128)(2,1)S(1)}, bf16[512,512]{1,0:T(8,128)(2,1)S(1)}, bf16[512,512]{1,0:T(8,128)(2,1)S(1)}, f32[4,128,128]{2,1,0:T(8,128)S(1)}) custom-call(s32[1]{0:T(128)} %bitcast.refs_0_.me_ref, f32[1,1024]{1,0:T(1,128)S(1)} %copy-done.7, bf16[1024,1536]{1,0:T(8,128)(2,1)S(1)} %bitcast.39, f32[512,4]{1,0:T(8,128)S(1)} %get-tuple-element.39.refs_3_, ...), custom_call_target="tpu_custom_call" | custom-call | flops 1610612736 | bytes 3145728 | tf_op jit(solution)/shard_map/qkv/pallas_call | solution.py:102
  23.8 0.8 copy-done.9
  24.6 0.8 copy-done.11
  25.4 2.2 %collective-permute-done.1.refs_7_ = bf16[512,512]{1,0:T(8,128)(2,1)} collective-permute-done((bf16[512,512]{1,0:T(8,128)(2,1)S(1)}, bf16[512,512]{1,0:T(8,128)(2,1)}, u32[]{:S(2)}, u32[]{:S(2)}) %collective-permute-start.1) | collective-permute-done | bytes 524320 | tf_op jit(solution)/shard_map/ppermute | solution.py:308
  27.6 4.6 %qkv.3 = (bf16[512,512]{1,0:T(8,128)(2,1)S(1)}, bf16[512,512]{1,0:T(8,128)(2,1)S(1)}, bf16[512,512]{1,0:T(8,128)(2,1)S(1)}, f32[4,128,128]{2,1,0:T(8,128)}, bf16[4,144,128]{2,1,0:T(8,128)(2,1)S(1)}) custom-call(s32[1]{0:T(128)} %bitcast.refs_0_.me_ref, f32[1,1024]{1,0:T(1,128)S(1)} %copy-done.7, bf16[1024,1536]{1,0:T(8,128)(2,1)S(1)} %bitcast.40, ...), custom_call_target="tpu_custom_call" | custom-call | flops 1610612736 | bytes 3145728 | tf_op jit(solution)/shard_map/qkv/pallas_call | solution.py:102
  32.2 0.8 copy-done.14
  33.0 0.8 copy-done.16
  33.8 1.7 %collective-permute-start.2 = (bf16[4,144,128]{2,1,0:T(8,128)(2,1)S(1)}, bf16[4,144,128]{2,1,0:T(8,128)(2,1)S(1)}, u32[]{:S(2)}, u32[]{:S(2)}) collective-permute-start(bf16[4,144,128]{2,1,0:T(8,128)(2,1)S(1)} %get-tuple-element.28.mine_ref), channel_id=1, source_target_pairs={{0,4},{4,0},{8,12},{12,8},{16,20},{20,16},{24,28},{28,24},{1,5},{5... | collective-permute-start | bytes 442376 | tf_op jit(solution)/shard_map/ppermute | solution.py:355
  35.5 3.4 %collective-permute-done.2.other_ref.refs_2_ = bf16[4,144,128]{2,1,0:T(8,128)(2,1)S(1)} collective-permute-done((bf16[4,144,128]{2,1,0:T(8,128)(2,1)S(1)}, bf16[4,144,128]{2,1,0:T(8,128)(2,1)S(1)}, u32[]{:S(2)}, u32[]{:S(2)}) %collective-permute-start.2) | collective-permute-done | bytes 147488 | tf_op jit(solution)/shard_map/ppermute | solution.py:355
  39.0 0.7 copy-done.1
  39.6 1.7 %pair.1 = bf16[4,144,128]{2,1,0:T(8,128)(2,1)} custom-call(s32[1]{0:T(128)} %bitcast.1.odd_ref, bf16[4,144,128]{2,1,0:T(8,128)(2,1)} %copy-done.4, bf16[4,144,128]{2,1,0:T(8,128)(2,1)} %copy-done.1), custom_call_target="tpu_custom_call" | custom-call | flops 73728 | bytes 442368 | tf_op jit(solution)/shard_map/pair/pallas_call | solution.py:198
  41.3 3.7 %collective-permute-start.3 = (bf16[4,144,128]{2,1,0:T(8,128)(2,1)}, bf16[4,144,128]{2,1,0:T(8,128)(2,1)S(1)}, u32[]{:S(2)}, u32[]{:S(2)}) collective-permute-start(bf16[4,144,128]{2,1,0:T(8,128)(2,1)} %pair.1), channel_id=1, source_target_pairs={{0,8},{4,12},{8,16},{12,20},{16,24},{20,28},{1,9},{5,13},{9,17},{1... | collective-permute-start | bytes 442376 | tf_op jit(solution)/shard_map/ppermute | solution.py:358
  45.0 4.5 %collective-permute-start.4 = (bf16[4,144,128]{2,1,0:T(8,128)(2,1)}, bf16[4,144,128]{2,1,0:T(8,128)(2,1)S(1)}, u32[]{:S(2)}, u32[]{:S(2)}) collective-permute-start(bf16[4,144,128]{2,1,0:T(8,128)(2,1)} %pair.1), channel_id=1, source_target_pairs={{0,16},{4,20},{8,24},{12,28},{1,17},{5,21},{9,25},{13,29},{2,18},{... | collective-permute-start | bytes 442376 | tf_op jit(solution)/shard_map/ppermute | solution.py:358
  49.6 1.3 %collective-permute-start.5 = (bf16[4,144,128]{2,1,0:T(8,128)(2,1)}, bf16[4,144,128]{2,1,0:T(8,128)(2,1)S(1)}, u32[]{:S(2)}, u32[]{:S(2)}) collective-permute-start(bf16[4,144,128]{2,1,0:T(8,128)(2,1)} %pair.1), channel_id=1, source_target_pairs={{0,24},{4,28},{1,25},{5,29},{2,26},{6,30},{3,27},{7,31}} | collective-permute-start | bytes 442376 | tf_op jit(solution)/shard_map/ppermute | solution.py:358
  50.9 1.0 %copy-done.10 = bf16[512,512]{1,0:T(8,128)(2,1)S(1)} copy-done((bf16[512,512]{1,0:T(8,128)(2,1)S(1)}, bf16[512,512]{1,0:T(8,128)(2,1)}, u32[]{:S(2)}) %copy-start.10) | copy-done | bytes 524312
  51.9 1.0 %copy-done.12 = bf16[512,512]{1,0:T(8,128)(2,1)S(1)} copy-done((bf16[512,512]{1,0:T(8,128)(2,1)S(1)}, bf16[512,512]{1,0:T(8,128)(2,1)}, u32[]{:S(2)}) %copy-start.12) | copy-done | bytes 524312
  53.0 1.0 %copy-done.15 = bf16[512,512]{1,0:T(8,128)(2,1)S(1)} copy-done((bf16[512,512]{1,0:T(8,128)(2,1)S(1)}, bf16[512,512]{1,0:T(8,128)(2,1)}, u32[]{:S(2)}) %copy-start.15) | copy-done | bytes 524312
  54.0 1.0 %copy-done.17 = bf16[512,512]{1,0:T(8,128)(2,1)S(1)} copy-done((bf16[512,512]{1,0:T(8,128)(2,1)S(1)}, bf16[512,512]{1,0:T(8,128)(2,1)}, u32[]{:S(2)}) %copy-start.17) | copy-done | bytes 524312
  55.0 3.3 %attention.2.refs_0_ = bf16[1024,256]{1,0:T(8,128)(2,1)S(1)} custom-call(s32[2,2]{1,0:T(2,128)S(1)} %copy-done.8, f32[1,4]{1,0:T(1,128)S(1)} %broadcast_multiply_fusion.scale_ref, bf16[512,512]{1,0:T(8,128)(2,1)S(1)} %get-tuple-element.21.refs_0_.q_ref, bf16[512,512]{1,0:T(8,128)(2,1)S(1)} %get-tuple-element.23.refs_1_.q_ref, ...), custom_call_target="tpu_custom_call" | custom-call | flops 805306368 | bytes 2097152 | tf_op jit(solution)/shard_map/attention/pallas_call | solution.py:159
  58.3 1.0 %copy-done.13 = bf16[512,512]{1,0:T(8,128)(2,1)S(1)} copy-done((bf16[512,512]{1,0:T(8,128)(2,1)S(1)}, bf16[512,512]{1,0:T(8,128)(2,1)}, u32[]{:S(2)}) %copy-start.13) | copy-done | bytes 524312
  59.4 3.3 %attention.3.refs_1_ = bf16[1024,256]{1,0:T(8,128)(2,1)S(1)} custom-call(s32[2,2]{1,0:T(2,128)S(1)} %copy-done.8, f32[1,4]{1,0:T(1,128)S(1)} %broadcast_multiply_fusion.scale_ref, bf16[512,512]{1,0:T(8,128)(2,1)S(1)} %get-tuple-element.21.refs_0_.q_ref, bf16[512,512]{1,0:T(8,128)(2,1)S(1)} %get-tuple-element.23.refs_1_.q_ref, ...), custom_call_target="tpu_custom_call" | custom-call | flops 805306368 | bytes 2097152 | tf_op jit(solution)/shard_map/attention/pallas_call | solution.py:159
  63.4 0.6 collective-permute-start.11
  64.6 0.6 collective-permute-start.6
  65.5 0.7 project.7
  66.2 1.6 %collective-permute-start.14 = (bf16[256,512]{1,0:T(8,128)(2,1)S(1)}, bf16[256,512]{1,0:T(8,128)(2,1)S(1)}, u32[]{:S(2)}, u32[]{:S(2)}) collective-permute-start(bf16[256,512]{1,0:T(8,128)(2,1)S(1)} %get-tuple-element.36), channel_id=1, source_target_pairs={{0,1},{1,0},{2,3},{3,2},{4,5},{5,4},{6,7},{7,6},{8,9},{9,8},{10,11... | collective-permute-start | bytes 786440 | tf_op jit(solution)/shard_map/ppermute | solution.py:379
  67.8 0.7 project.6
  68.5 0.6 collective-permute-start.12
  69.1 0.7 project.5
  69.8 1.6 %collective-permute-start.10 = (bf16[256,512]{1,0:T(8,128)(2,1)S(1)}, bf16[256,512]{1,0:T(8,128)(2,1)S(1)}, u32[]{:S(2)}, u32[]{:S(2)}) collective-permute-start(bf16[256,512]{1,0:T(8,128)(2,1)S(1)} %get-tuple-element.32), channel_id=1, source_target_pairs={{0,1},{1,0},{2,3},{3,2},{4,5},{5,4},{6,7},{7,6},{8,9},{9,8},{10,11... | collective-permute-start | bytes 786440 | tf_op jit(solution)/shard_map/ppermute | solution.py:379
  71.4 0.7 project.4
  72.1 0.6 collective-permute-start.8
  72.6 2.8 %collective-permute-done.14 = bf16[256,512]{1,0:T(8,128)(2,1)S(1)} collective-permute-done((bf16[256,512]{1,0:T(8,128)(2,1)S(1)}, bf16[256,512]{1,0:T(8,128)(2,1)S(1)}, u32[]{:S(2)}, u32[]{:S(2)}) %collective-permute-start.14) | collective-permute-done | bytes 262176 | tf_op jit(solution)/shard_map/ppermute | solution.py:379
  75.5 5.5 %collective-permute-done.12 = bf16[256,512]{1,0:T(8,128)(2,1)S(1)} collective-permute-done((bf16[256,512]{1,0:T(8,128)(2,1)S(1)}, bf16[256,512]{1,0:T(8,128)(2,1)S(1)}, u32[]{:S(2)}, u32[]{:S(2)}) %collective-permute-start.12) | collective-permute-done | bytes 262176 | tf_op jit(solution)/shard_map/ppermute | solution.py:379
  81.1 5.5 %collective-permute-done.10 = bf16[256,512]{1,0:T(8,128)(2,1)S(1)} collective-permute-done((bf16[256,512]{1,0:T(8,128)(2,1)S(1)}, bf16[256,512]{1,0:T(8,128)(2,1)S(1)}, u32[]{:S(2)}, u32[]{:S(2)}) %collective-permute-start.10) | collective-permute-done | bytes 262176 | tf_op jit(solution)/shard_map/ppermute | solution.py:379
  86.7 4.6 %collective-permute-done.8 = bf16[256,512]{1,0:T(8,128)(2,1)S(1)} collective-permute-done((bf16[256,512]{1,0:T(8,128)(2,1)S(1)}, bf16[256,512]{1,0:T(8,128)(2,1)S(1)}, u32[]{:S(2)}, u32[]{:S(2)}) %collective-permute-start.8) | collective-permute-done | bytes 262176 | tf_op jit(solution)/shard_map/ppermute | solution.py:379
  91.4 1.0 %maximum_bitcast_fusion = bf16[1,1024,512]{2,1,0:T(8,128)(2,1)} fusion(bf16[256,512]{1,0:T(8,128)(2,1)S(1)} %add_convert_fusion, bf16[256,512]{1,0:T(8,128)(2,1)S(1)} %add_convert_fusion.1, bf16[256,512]{1,0:T(8,128)(2,1)S(1)} %add_convert_fusion.2, bf16[256,512]{1,0:T(8,128)(2,1)S(1)} %add_convert_fusion.3), kind=kLoop, calls=%fused_computation | loop fusion | flops 4194304 | bytes 2097152 | tf_op jit(solution)/shard_map/broadcast_in_dim | solution.py:383
  (66 shorter events, 2.9 us)
Async XLA Ops:
  0.0 4.4 %copy-start.21 = (s32[2]{0:T(128)S(1)}, s32[2]{0:T(128)}, u32[]{:S(2)}) copy-start(s32[2]{0:T(128)} %param.15) | copy-start | bytes 28
  0.0 4.5 %copy-start.20 = (f32[1,4,1024]{2,1,0:T(4,128)S(1)}, f32[1,4,1024]{2,1,0:T(4,128)}, u32[]{:S(2)}) copy-start(f32[1,4,1024]{2,1,0:T(4,128)} %param.13) | copy-start | bytes 49156
  1.3 15.8 %collective-permute-start = (bf16[512,512]{1,0:T(8,128)(2,1)S(1)}, bf16[512,512]{1,0:T(8,128)(2,1)S(1)}, u32[]{:S(2)}, u32[]{:S(2)}) collective-permute-start(bf16[512,512]{1,0:T(8,128)(2,1)S(1)} %get-tuple-element.38.refs_6_), channel_id=1, source_target_pairs={{1,0},{0,1},{3,2},{2,3},{5,4},{4,5},{7,6},{6,7},{9,8},{8,9},{11,10... | collective-permute-start | bytes 1572872 | tf_op jit(solution)/shard_map/ppermute | solution.py:308
  4.3 23.3 %collective-permute-start.1 = (bf16[512,512]{1,0:T(8,128)(2,1)S(1)}, bf16[512,512]{1,0:T(8,128)(2,1)}, u32[]{:S(2)}, u32[]{:S(2)}) collective-permute-start(bf16[512,512]{1,0:T(8,128)(2,1)S(1)} %get-tuple-element.37.refs_6_), channel_id=1, source_target_pairs={{1,0},{0,1},{3,2},{2,3},{5,4},{4,5},{7,6},{6,7},{9,8},{8,9},{11,10... | collective-permute-start | bytes 1572872 | tf_op jit(solution)/shard_map/ppermute | solution.py:308
  4.4 60.8 %collective-permute-start.7 = (bf16[512,1024]{1,0:T(8,128)(2,1)}, bf16[512,1024]{1,0:T(8,128)(2,1)S(1)}, u32[]{:S(2)}, u32[]{:S(2)}) collective-permute-start(bf16[512,1024]{1,0:T(8,128)(2,1)} %bitcast.9), channel_id=1, source_target_pairs={{0,2},{2,0},{1,3},{3,1},{4,6},{6,4},{5,7},{7,5},{8,10},{10,8},{9,1... | collective-permute-start | bytes 3145736 | tf_op jit(solution)/shard_map/ppermute | solution.py:313
  6.3 0.8 copy-start.19
  9.8 8.1 %copy-start.7 = (f32[1,1024]{1,0:T(1,128)S(1)}, f32[1,1024]{1,0:T(1,128)}, u32[]{:S(2)}) copy-start(f32[1,1024]{1,0:T(1,128)} %refs_1_.3) | copy-start | bytes 12292
  17.1 0.8 copy-start.5
  17.9 1.9 %copy-start.3 = (bf16[128,8,4,384]{3,1,2,0:T(8,128)(2,1)S(1)}, bf16[128,8,4,384]{3,1,2,0:T(8,128)(2,1)}, u32[]{:S(2)}) copy-start(bf16[128,8,4,384]{3,1,2,0:T(8,128)(2,1)} %copy.13) | copy-start | bytes 9437188
  19.8 1.0 %copy-start.6 = (bf16[512,512]{1,0:T(8,128)(2,1)S(1)}, bf16[512,512]{1,0:T(8,128)(2,1)}, u32[]{:S(2)}) copy-start(bf16[512,512]{1,0:T(8,128)(2,1)} %copy-done.5) | copy-start | bytes 1572868
  23.8 0.8 copy-start.9
  24.6 0.8 copy-start.11
  27.6 8.0 %copy-start.22 = (f32[1,4]{1,0:T(1,128)S(1)}, f32[1,4]{1,0:T(1,128)}, u32[]{:S(2)}) copy-start(f32[1,4]{1,0:T(1,128)} %param.12) | copy-start | bytes 52
  27.6 23.3 %copy-start.8 = (s32[2,2]{1,0:T(2,128)S(1)}, s32[2,2]{1,0:T(2,128)}, u32[]{:S(2)}) copy-start(s32[2,2]{1,0:T(2,128)} %keep_ref.3) | copy-start | bytes 52
  32.2 0.8 copy-start.14
  33.0 0.8 copy-start.16
  33.8 5.2 %copy-start.4 = (bf16[4,144,128]{2,1,0:T(8,128)(2,1)}, bf16[4,144,128]{2,1,0:T(8,128)(2,1)S(1)}, u32[]{:S(2)}) copy-start(bf16[4,144,128]{2,1,0:T(8,128)(2,1)S(1)} %get-tuple-element.28.mine_ref) | copy-start | bytes 442372
  33.8 5.1 %collective-permute-start.2 = (bf16[4,144,128]{2,1,0:T(8,128)(2,1)S(1)}, bf16[4,144,128]{2,1,0:T(8,128)(2,1)S(1)}, u32[]{:S(2)}, u32[]{:S(2)}) collective-permute-start(bf16[4,144,128]{2,1,0:T(8,128)(2,1)S(1)} %get-tuple-element.28.mine_ref), channel_id=1, source_target_pairs={{0,4},{4,0},{8,12},{12,8},{16,20},{20,16},{24,28},{28,24},{1,5},{5... | collective-permute-start | bytes 442376 | tf_op jit(solution)/shard_map/ppermute | solution.py:355
  39.0 0.7 copy-start.1
  41.3 21.3 %collective-permute-start.3 = (bf16[4,144,128]{2,1,0:T(8,128)(2,1)}, bf16[4,144,128]{2,1,0:T(8,128)(2,1)S(1)}, u32[]{:S(2)}, u32[]{:S(2)}) collective-permute-start(bf16[4,144,128]{2,1,0:T(8,128)(2,1)} %pair.1), channel_id=1, source_target_pairs={{0,8},{4,12},{8,16},{12,20},{16,24},{20,28},{1,9},{5,13},{9,17},{1... | collective-permute-start | bytes 442376 | tf_op jit(solution)/shard_map/ppermute | solution.py:358
  45.0 17.6 %collective-permute-start.4 = (bf16[4,144,128]{2,1,0:T(8,128)(2,1)}, bf16[4,144,128]{2,1,0:T(8,128)(2,1)S(1)}, u32[]{:S(2)}, u32[]{:S(2)}) collective-permute-start(bf16[4,144,128]{2,1,0:T(8,128)(2,1)} %pair.1), channel_id=1, source_target_pairs={{0,16},{4,20},{8,24},{12,28},{1,17},{5,21},{9,25},{13,29},{2,18},{... | collective-permute-start | bytes 442376 | tf_op jit(solution)/shard_map/ppermute | solution.py:358
  49.6 13.1 %collective-permute-start.5 = (bf16[4,144,128]{2,1,0:T(8,128)(2,1)}, bf16[4,144,128]{2,1,0:T(8,128)(2,1)S(1)}, u32[]{:S(2)}, u32[]{:S(2)}) collective-permute-start(bf16[4,144,128]{2,1,0:T(8,128)(2,1)} %pair.1), channel_id=1, source_target_pairs={{0,24},{4,28},{1,25},{5,29},{2,26},{6,30},{3,27},{7,31}} | collective-permute-start | bytes 442376 | tf_op jit(solution)/shard_map/ppermute | solution.py:358
  50.9 1.0 %copy-start.10 = (bf16[512,512]{1,0:T(8,128)(2,1)S(1)}, bf16[512,512]{1,0:T(8,128)(2,1)}, u32[]{:S(2)}) copy-start(bf16[512,512]{1,0:T(8,128)(2,1)} %copy-done.9) | copy-start | bytes 1572868
  51.9 1.0 %copy-start.12 = (bf16[512,512]{1,0:T(8,128)(2,1)S(1)}, bf16[512,512]{1,0:T(8,128)(2,1)}, u32[]{:S(2)}) copy-start(bf16[512,512]{1,0:T(8,128)(2,1)} %copy-done.11) | copy-start | bytes 1572868
  53.0 1.0 %copy-start.15 = (bf16[512,512]{1,0:T(8,128)(2,1)S(1)}, bf16[512,512]{1,0:T(8,128)(2,1)}, u32[]{:S(2)}) copy-start(bf16[512,512]{1,0:T(8,128)(2,1)} %copy-done.14) | copy-start | bytes 1572868
  54.0 1.0 %copy-start.17 = (bf16[512,512]{1,0:T(8,128)(2,1)S(1)}, bf16[512,512]{1,0:T(8,128)(2,1)}, u32[]{:S(2)}) copy-start(bf16[512,512]{1,0:T(8,128)(2,1)} %copy-done.16) | copy-start | bytes 1572868
  55.0 3.3 %copy-start.18 = (bf16[512,512]{1,0:T(8,128)(2,1)S(1)}, bf16[512,512]{1,0:T(8,128)(2,1)}, u32[]{:S(2)}) copy-start(bf16[512,512]{1,0:T(8,128)(2,1)} %copy-done.16) | copy-start | bytes 1572868
  58.3 1.0 %copy-start.13 = (bf16[512,512]{1,0:T(8,128)(2,1)S(1)}, bf16[512,512]{1,0:T(8,128)(2,1)}, u32[]{:S(2)}) copy-start(bf16[512,512]{1,0:T(8,128)(2,1)} %copy-done.11) | copy-start | bytes 1572868
  59.4 3.3 %copy-start.2 = (bf16[4,144,128]{2,1,0:T(8,128)(2,1)S(1)}, bf16[4,144,128]{2,1,0:T(8,128)(2,1)}, u32[]{:S(2)}) copy-start(bf16[4,144,128]{2,1,0:T(8,128)(2,1)} %copy-done.1) | copy-start | bytes 442372
  63.0 2.2 %collective-permute-start.13 = (bf16[256,512]{1,0:T(8,128)(2,1)S(1)}, bf16[256,512]{1,0:T(8,128)(2,1)S(1)}, u32[]{:S(2)}, u32[]{:S(2)}) collective-permute-start(bf16[256,512]{1,0:T(8,128)(2,1)S(1)} %recall.7.own_ref), channel_id=1, source_target_pairs={{0,2},{2,0},{1,3},{3,1},{4,6},{6,4},{5,7},{7,5},{8,10},{10,8},{9,1... | collective-permute-start | bytes 786440 | tf_op jit(solution)/shard_map/ppermute | solution.py:375
  63.4 4.4 %collective-permute-start.11 = (bf16[256,512]{1,0:T(8,128)(2,1)S(1)}, bf16[256,512]{1,0:T(8,128)(2,1)S(1)}, u32[]{:S(2)}, u32[]{:S(2)}) collective-permute-start(bf16[256,512]{1,0:T(8,128)(2,1)S(1)} %recall.6.own_ref), channel_id=1, source_target_pairs={{0,2},{2,0},{1,3},{3,1},{4,6},{6,4},{5,7},{7,5},{8,10},{10,8},{9,1... | collective-permute-start | bytes 786440 | tf_op jit(solution)/shard_map/ppermute | solution.py:375
  64.2 1.2 %copy-start = (bf16[1,4,128,1024]{3,2,1,0:T(8,128)(2,1)S(1)}, bf16[1,4,128,1024]{3,2,1,0:T(8,128)(2,1)}, u32[]{:S(2)}) copy-start(bf16[1,4,128,1024]{3,2,1,0:T(8,128)(2,1)} %param.16) | copy-start | bytes 3145732
  64.3 4.8 %collective-permute-start.9 = (bf16[256,512]{1,0:T(8,128)(2,1)S(1)}, bf16[256,512]{1,0:T(8,128)(2,1)S(1)}, u32[]{:S(2)}, u32[]{:S(2)}) collective-permute-start(bf16[256,512]{1,0:T(8,128)(2,1)S(1)} %recall.5.own_ref), channel_id=1, source_target_pairs={{0,2},{2,0},{1,3},{3,1},{4,6},{6,4},{5,7},{7,5},{8,10},{10,8},{9,1... | collective-permute-start | bytes 786440 | tf_op jit(solution)/shard_map/ppermute | solution.py:375
  64.6 6.7 %collective-permute-start.6 = (bf16[256,512]{1,0:T(8,128)(2,1)S(1)}, bf16[256,512]{1,0:T(8,128)(2,1)S(1)}, u32[]{:S(2)}, u32[]{:S(2)}) collective-permute-start(bf16[256,512]{1,0:T(8,128)(2,1)S(1)} %recall.4.own_ref), channel_id=1, source_target_pairs={{0,2},{2,0},{1,3},{3,1},{4,6},{6,4},{5,7},{7,5},{8,10},{10,8},{9,1... | collective-permute-start | bytes 786440 | tf_op jit(solution)/shard_map/ppermute | solution.py:375
  66.2 9.2 %collective-permute-start.14 = (bf16[256,512]{1,0:T(8,128)(2,1)S(1)}, bf16[256,512]{1,0:T(8,128)(2,1)S(1)}, u32[]{:S(2)}, u32[]{:S(2)}) collective-permute-start(bf16[256,512]{1,0:T(8,128)(2,1)S(1)} %get-tuple-element.36), channel_id=1, source_target_pairs={{0,1},{1,0},{2,3},{3,2},{4,5},{5,4},{6,7},{7,6},{8,9},{9,8},{10,11... | collective-permute-start | bytes 786440 | tf_op jit(solution)/shard_map/ppermute | solution.py:379
  68.5 12.5 %collective-permute-start.12 = (bf16[256,512]{1,0:T(8,128)(2,1)S(1)}, bf16[256,512]{1,0:T(8,128)(2,1)S(1)}, u32[]{:S(2)}, u32[]{:S(2)}) collective-permute-start(bf16[256,512]{1,0:T(8,128)(2,1)S(1)} %get-tuple-element.34), channel_id=1, source_target_pairs={{0,1},{1,0},{2,3},{3,2},{4,5},{5,4},{6,7},{7,6},{8,9},{9,8},{10,11... | collective-permute-start | bytes 786440 | tf_op jit(solution)/shard_map/ppermute | solution.py:379
  69.8 16.9 %collective-permute-start.10 = (bf16[256,512]{1,0:T(8,128)(2,1)S(1)}, bf16[256,512]{1,0:T(8,128)(2,1)S(1)}, u32[]{:S(2)}, u32[]{:S(2)}) collective-permute-start(bf16[256,512]{1,0:T(8,128)(2,1)S(1)} %get-tuple-element.32), channel_id=1, source_target_pairs={{0,1},{1,0},{2,3},{3,2},{4,5},{5,4},{6,7},{7,6},{8,9},{9,8},{10,11... | collective-permute-start | bytes 786440 | tf_op jit(solution)/shard_map/ppermute | solution.py:379
  72.1 19.3 %collective-permute-start.8 = (bf16[256,512]{1,0:T(8,128)(2,1)S(1)}, bf16[256,512]{1,0:T(8,128)(2,1)S(1)}, u32[]{:S(2)}, u32[]{:S(2)}) collective-permute-start(bf16[256,512]{1,0:T(8,128)(2,1)S(1)} %get-tuple-element.30), channel_id=1, source_target_pairs={{0,1},{1,0},{2,3},{3,2},{4,5},{5,4},{6,7},{7,6},{8,9},{9,8},{10,11... | collective-permute-start | bytes 786440 | tf_op jit(solution)/shard_map/ppermute | solution.py:379

commit v2 on v0

v2 whole, which is shorter than its diff:
```python
import functools
import math

import jax
import jax.numpy as jnp
from jax import lax
from jax.experimental import pallas as pl
from jax.experimental.pallas import tpu as pltpu
from jax.sharding import PartitionSpec as P

BLOCK = 512
CHUNK = 256
TAIL = 16
EPSILON = 1e-06
F32 = jnp.float32
BF16 = jnp.bfloat16
SMEM = pl.BlockSpec(memory_space=pltpu.SMEM)
VMEM = pl.BlockSpec(memory_space=pltpu.VMEM)


def params():
    return pltpu.CompilerParams(vmem_limit_bytes=16 * 1024 * 1024)


def cost(flops, bytes_accessed, transcendentals=0):
    return pl.CostEstimate(
        flops=int(flops), bytes_accessed=int(bytes_accessed), transcendentals=int(transcendentals)
    )


def struct(shape, dtype=BF16):
    return jax.ShapeDtypeStruct(shape, dtype)


def dot(a, b):
    return lax.dot_general(a, b, (((1,), (0,)), ((), ())), preferred_element_type=F32)


def dot_nt(a, b):
    return lax.dot_general(a, b, (((1,), (1,)), ((), ())), preferred_element_type=F32)


def dot_tn(a, b):
    return lax.dot_general(a, b, (((0,), (0,)), ((), ())), preferred_element_type=F32)


def unit(values):
    return values * lax.rsqrt(jnp.mean(values * values, axis=-1, keepdims=True) + EPSILON)


def normed_parts(me, gain_ref, x_refs):
    shards, width = len(x_refs), x_refs[0].shape[1]
    parts = [x[...].astype(F32) for x in x_refs]
    squares = sum(jnp.sum(p * p, axis=-1, keepdims=True) for p in parts)
    scale = lax.rsqrt(squares * (1.0 / (width * shards)) + EPSILON)
    out = []
    for k, part in enumerate(parts):
        owner = lax.rem(me + k, shards)
        rows = pl.ds(pl.multiple_of(owner * width, width), width)
        out.append(((part * scale * gain_ref[:, rows]).astype(BF16), rows))
    return out


def projected(parts, w_ref, cols):
    total = None
    for part, rows in parts:
        term = dot(part, w_ref[rows, cols])
        total = term if total is None else total + term
    return total


def write_queries(parts, w_ref, q_ref, heads, dim):
    total = projected(parts, w_ref, slice(0, heads * dim))
    for h in range(heads):
        cols = slice(h * dim, (h + 1) * dim)
        q_ref[:, cols] = unit(total[:, cols]).astype(BF16)


def write_keys_values(parts, w_ref, fade_ref, k_ref, v_ref, sum_ref, heads, dim):
    keys = projected(parts, w_ref, slice(heads * dim, 2 * heads * dim))
    values = projected(parts, w_ref, slice(2 * heads * dim, 3 * heads * dim))
    for h in range(heads):
        cols = slice(h * dim, (h + 1) * dim)
        key = unit(keys[:, cols]).astype(BF16)
        value = values[:, cols].astype(BF16)
        k_ref[:, cols] = key
        v_ref[:, cols] = value
        faded = (key.astype(F32) * fade_ref[:, h : h + 1]).astype(BF16)
        sum_ref[h] += dot_tn(faded, value)


def qkv_kernel(heads, dim, me_ref, gain_ref, w_ref, fade_ref, prev_ref, *refs):
    x_refs, (q_ref, k_ref, v_ref, sum_ref) = refs[:-4], refs[-4:]
    sum_ref[...] = prev_ref[...]
    parts = normed_parts(me_ref[0], gain_ref, x_refs)
    write_keys_values(parts, w_ref, fade_ref, k_ref, v_ref, sum_ref, heads, dim)
    write_queries(parts, w_ref, q_ref, heads, dim)


def qkv(me, gain, w, fade, prev, xs, heads, dim):
    rows = xs[0].shape[0]
    return pl.pallas_call(
        functools.partial(qkv_kernel, heads, dim),
        in_specs=[SMEM] + [VMEM] * (4 + len(xs)),
        out_specs=[VMEM] * 4,
        out_shape=[struct((rows, heads * dim))] * 3 + [struct((heads, dim, dim), F32)],
        compiler_params=params(),
        cost_estimate=cost(4 * rows * w.size, 0),
        name="qkv",
    )(me, gain, w, fade, prev, *xs)


def last_kernel(heads, dim, me_ref, odd_ref, gain_ref, w_ref, fade_ref, prev_ref, tail_ref, *refs):
    x_refs, (k_ref, v_ref, keep_ref, send_ref, sum_ref) = refs[:-5], refs[-5:]
    half = dim // 2
    sum_ref[...] = prev_ref[...]
    parts = normed_parts(me_ref[0], gain_ref, x_refs)
    write_keys_values(parts, w_ref, fade_ref, k_ref, v_ref, sum_ref, heads, dim)
    odd = odd_ref[0]
    kept = pl.ds(pl.multiple_of(odd * half, half), half)
    sent = pl.ds(pl.multiple_of((1 - odd) * half, half), half)
    for h in range(heads):
        rows = slice(h * half, (h + 1) * half)
        keep_ref[rows, :] = sum_ref[h, kept, :]
        send_ref[rows, :] = sum_ref[h, sent, :].astype(BF16)
    send_ref[heads * half :, :] = tail_ref[...]


def last_keys_values(me, odd, gain, w, fade, prev, tail, xs, heads, dim):
    rows = xs[0].shape[0]
    size = heads * dim // 2
    return pl.pallas_call(
        functools.partial(last_kernel, heads, dim),
        in_specs=[SMEM, SMEM] + [VMEM] * (5 + len(xs)),
        out_specs=[VMEM] * 4,
        out_shape=[struct((rows, heads * dim))] * 2 + [struct((size, dim), F32), struct((size + TAIL, dim))],
        scratch_shapes=[pltpu.VMEM((heads, dim, dim), F32)],
        compiler_params=params(),
        cost_estimate=cost(3 * rows * w.size, 0),
        name="last_keys_values",
    )(me, odd, gain, w, fade, prev, tail, *xs)


def queries_kernel(heads, dim, me_ref, gain_ref, w_ref, *refs):
    parts = normed_parts(me_ref[0], gain_ref, refs[:-1])
    write_queries(parts, w_ref, refs[-1], heads, dim)


def last_queries(me, gain, w, xs, heads, dim):
    rows = xs[0].shape[0]
    return pl.pallas_call(
        functools.partial(queries_kernel, heads, dim),
        in_specs=[SMEM] + [VMEM] * (2 + len(xs)),
        out_specs=VMEM,
        out_shape=struct((rows, heads * dim)),
        compiler_params=params(),
        cost_estimate=cost(2 * rows * w.size, 0),
        name="last_queries",
    )(me, gain, w, *xs)


def attention_kernel(chunk, heads, dim, keep_ref, scale_ref, q_ref, *refs):
    k_refs, v_refs, out_ref = refs[: chunk + 1], refs[chunk + 1 : -1], refs[-1]
    rows = q_ref.shape[0]
    per = BLOCK // rows
    block = chunk // per
    causal = lax.broadcasted_iota(jnp.int32, (rows, rows), 1) <= lax.broadcasted_iota(
        jnp.int32, (rows, rows), 0
    )
    ones = jnp.ones((rows, dim), BF16)
    for h in range(heads):
        cols = slice(h * dim, (h + 1) * dim)
        query = q_ref[:, cols]
        total = None
        for j in range(chunk + 1):
            powers = jnp.exp(dot_nt(query, k_refs[j][:, cols]) * scale_ref[0, h])
            if j == chunk:
                powers = jnp.where(causal, powers, 0.0)
            part = dot(powers.astype(BF16), jnp.concatenate([v_refs[j][:, cols], ones], axis=1))
            if j // per < block:
                part = jnp.where(keep_ref[block, j // per] == 1, part, 0.0)
            total = part if total is None else total + part
        out_ref[:, cols] = (total[:, :dim] / total[:, dim:]).astype(BF16)


def attention(chunk, keep, scale, q, ks, vs, heads, dim):
    rows = q.shape[0]
    return pl.pallas_call(
        functools.partial(attention_kernel, chunk, heads, dim),
        in_specs=[SMEM, SMEM] + [VMEM] * (1 + len(ks) + len(vs)),
        out_specs=VMEM,
        out_shape=struct(q.shape),
        compiler_params=params(),
        cost_estimate=cost(
            (chunk + 1) * heads * 8 * rows * rows * dim, 0, (chunk + 1) * heads * rows * rows
        ),
        name="attention",
    )(keep, scale, q, *ks, *vs)


def decays_of(ref, size, h):
    high = ref[size + h : size + h + 1, :].astype(F32)
    low = ref[size + TAIL // 2 + h : size + TAIL // 2 + h + 1, :].astype(F32)
    return high + low


def pair_kernel(heads, odd_ref, tail_ref, keep_ref, came_ref, out_ref):
    size = keep_ref.shape[0]
    half = size // heads
    odd = odd_ref[0] == 1
    out_ref[size:, :] = jnp.zeros_like(tail_ref)
    for h in range(heads):
        rows = slice(h * half, (h + 1) * half)
        own, far = keep_ref[rows, :], came_ref[rows, :].astype(F32)
        own_decay, far_decay = decays_of(tail_ref, 0, h), decays_of(came_ref, size, h)
        late_decay = jnp.where(odd, own_decay, far_decay)
        early, late = jnp.where(odd, far, own), jnp.where(odd, own, far)
        out_ref[rows, :] = (late_decay * early + late).astype(BF16)
        both = own_decay * far_decay
        high = both.astype(BF16)
        out_ref[size + h : size + h + 1, :] = high
        out_ref[size + TAIL // 2 + h : size + TAIL // 2 + h + 1, :] = (both - high.astype(F32)).astype(BF16)


def pair(odd, tail, keep, came, heads):
    return pl.pallas_call(
        functools.partial(pair_kernel, heads),
        in_specs=[SMEM] + [VMEM] * 3,
        out_specs=VMEM,
        out_shape=struct(came.shape),
        compiler_params=params(),
        cost_estimate=cost(came.size * 8, 0),
        name="pair",
    )(odd, tail, keep, came)


def entering_kernel(heads, odd_ref, tail_ref, keep_ref, came_ref, *refs):
    far_refs, (stay_ref, send_ref) = refs[:-2], refs[-2:]
    size = keep_ref.shape[0]
    half = size // heads
    odd = odd_ref[0] == 1
    for h in range(heads):
        rows = slice(h * half, (h + 1) * half)
        state = jnp.zeros((half, keep_ref.shape[1]), F32)
        for ref in reversed(far_refs):
            state = ref[rows, :].astype(F32) + decays_of(ref, size, h) * state
        own, far = keep_ref[rows, :], came_ref[rows, :].astype(F32)
        decay = jnp.where(odd, decays_of(came_ref, size, h), decays_of(tail_ref, 0, h))
        later = decay * state + jnp.where(odd, far, own)
        stay_ref[rows, :] = jnp.where(odd, later, state).astype(BF16)
        send_ref[rows, :] = jnp.where(odd, state, later).astype(BF16)


def entering(odd, tail, keep, came, fars, heads):
    return pl.pallas_call(
        functools.partial(entering_kernel, heads),
        in_specs=[SMEM] + [VMEM] * (3 + len(fars)),
        out_specs=[VMEM] * 2,
        out_shape=[struct(keep.shape)] * 2,
        compiler_params=params(),
        cost_estimate=cost(came.size * 16, 0),
        name="entering",
    )(odd, tail, keep, came, *fars)


def recall_kernel(heads, dim, odd_ref, reading_ref, q_ref, local_ref, stay_ref, came_ref, out_ref):
    half = dim // 2
    odd = odd_ref[0] == 1
    for h in range(heads):
        rows = slice(h * half, (h + 1) * half)
        cols = slice(h * dim, (h + 1) * dim)
        stay, came = stay_ref[rows, :].astype(F32), came_ref[rows, :].astype(F32)
        state = jnp.concatenate([jnp.where(odd, came, stay), jnp.where(odd, stay, came)], axis=0)
        recalled = dot(q_ref[:, cols], state.astype(BF16)) * reading_ref[:, h : h + 1]
        out_ref[:, cols] = (local_ref[:, cols].astype(F32) + recalled).astype(BF16)


def recall(odd, reading, q, local, stay, came, heads, dim):
    return pl.pallas_call(
        functools.partial(recall_kernel, heads, dim),
        in_specs=[SMEM] + [VMEM] * 5,
        out_specs=VMEM,
        out_shape=struct(q.shape),
        compiler_params=params(),
        cost_estimate=cost(4 * q.size * dim, 0),
        name="recall",
    )(odd, reading, q, local, stay, came)


def project_kernel(shards, me_ref, own_ref, side_ref, own_w_ref, side_w_ref, *out_refs):
    width = out_refs[0].shape[1]
    own, side = own_ref[...], side_ref[...]
    for k in reversed(range(shards)):
        owner = lax.rem(me_ref[0] + k, shards)
        cols = pl.ds(pl.multiple_of(owner * width, width), width)
        out = dot(own, own_w_ref[:, cols]) + dot(side, side_w_ref[:, cols])
        out_refs[k][...] = out.astype(out_refs[k].dtype)


def project(me, own, side, own_w, side_w, shards):
    rows = own.shape[0]
    width = own_w.shape[1] // shards
    return pl.pallas_call(
        functools.partial(project_kernel, shards),
        in_specs=[SMEM] + [VMEM] * 4,
        out_specs=[VMEM] * shards,
        out_shape=[struct((rows, width))] * shards,
        compiler_params=params(),
        cost_estimate=cost(4 * rows * own_w.size, 0),
        name="project",
    )(me, own, side, own_w, side_w)


def finish_kernel(count, *refs):
    total = refs[0][...].astype(F32)
    for ref in refs[1:count]:
        total += ref[...].astype(F32)
    refs[-1][...] = total.astype(BF16)


def finish(parts, result, chunk, length):
    rows, width = parts[0].shape
    whole = pl.BlockSpec((rows, width), lambda i: (0, 0))
    more = [] if result is None else [result]
    return pl.pallas_call(
        functools.partial(finish_kernel, len(parts)),
        grid=(1,),
        in_specs=[whole] * len(parts) + [pl.BlockSpec(memory_space=pl.ANY)] * len(more),
        out_specs=pl.BlockSpec((rows, width), lambda i: (chunk, 0)),
        out_shape=struct((length, width)),
        input_output_aliases={len(parts): 0} if more else {},
        compiler_params=params(),
        cost_estimate=cost(rows * width * 2, rows * width * 6),
        name="finish",
    )(*parts, *more)


def per_device(
    residual_signal,
    prescale_amplifier,
    triple_projector,
    score_scaler,
    recall_retained_logshare,
    tile_retain_grid,
    recall_store_flags,
    emission_projector,
    sideways_coupling_coef,
):
    x = residual_signal[0]
    length = x.shape[0]
    chunks = length // CHUNK
    shards = lax.axis_size("head")
    blocks = lax.axis_size("tm")
    heads = triple_projector.shape[2]
    dim = emission_projector.shape[2]
    me = lax.axis_index("head").astype(jnp.int32).reshape(1)
    odd = lax.rem(lax.axis_index("tm"), 2).astype(jnp.int32).reshape(1)
    swap_streams = [(0, 1), (1, 0)]
    swap_pairs = [(d, d ^ 1) for d in range(blocks)]

    received = []
    for c in range(chunks):
        piece = x[c * CHUNK : (c + 1) * CHUNK]
        piece, x = lax.optimization_barrier((piece, x))
        xs = [piece]
        for k in range(1, shards):
            xs.append(lax.ppermute(piece, "head", [((d + k) % shards, d) for d in range(shards)]))
        received.append(xs)

    own_w = emission_projector[0].reshape(heads * dim, -1)
    side_w = lax.ppermute(
        sideways_coupling_coef[0].reshape(heads * dim, -1), "stream", swap_streams
    )

    running = jnp.cumsum(recall_retained_logshare[0], axis=1)
    flags = jnp.repeat(recall_store_flags, BLOCK).astype(F32)
    fade = jnp.transpose(jnp.exp(running[:, -1:] - running) * flags[None, :])
    reading = jnp.transpose(jnp.exp(running)) * (1.0 / math.sqrt(dim * length * blocks))
    decay = jnp.exp(running[:, -1])
    high = decay.astype(BF16)
    low = (decay - high.astype(F32)).astype(BF16)
    tail = jnp.concatenate(
        [
            jnp.broadcast_to(jnp.pad(part, (0, TAIL // 2 - heads))[:, None], (TAIL // 2, dim))
            for part in (high, low)
        ],
        axis=0,
    )
    scale = score_scaler * (1.0 / math.sqrt(dim))
    gain = prescale_amplifier
    w = triple_projector[0].reshape(-1, heads, 3, dim)
    w = jnp.transpose(w, (0, 2, 1, 3)).reshape(-1, 3 * heads * dim)
    rows_of = lambda array, c: array[c * CHUNK : (c + 1) * CHUNK]

    qs, ks, vs, locals_ = [], [], [], []
    summary = jnp.zeros((heads, dim, dim), F32)
    for c in range(chunks - 1):
        q, k, v, summary = qkv(me, gain, w, rows_of(fade, c), summary, received[c], heads, dim)
        qs.append(q)
        ks.append(k)
        vs.append(v)
        locals_.append(attention(c, tile_retain_grid, scale, q, ks, vs, heads, dim))
    k, v, keep, sent = last_keys_values(
        me, odd, gain, w, rows_of(fade, chunks - 1), summary, tail, received[-1], heads, dim
    )
    ks.append(k)
    vs.append(v)

    came = lax.ppermute(sent, "tm", swap_pairs)
    joint = pair(odd, tail, keep, came, heads)
    fars = [
        lax.ppermute(joint, "tm", [(d, d + 2 * k) for d in range(blocks - 2 * k)])
        for k in range(1, blocks // 2)
    ]
    stay, sent = entering(odd, tail, keep, came, fars, heads)
    state = lax.ppermute(sent, "tm", swap_pairs)

    qs.append(last_queries(me, gain, w, received[-1], heads, dim))
    locals_.append(attention(chunks - 1, tile_retain_grid, scale, qs[-1], ks, vs, heads, dim))

    result = None
    for c in range(chunks):
        head_out = recall(odd, rows_of(reading, c), qs[c], locals_[c], stay, state, heads, dim)
        side = lax.ppermute(head_out, "stream", swap_streams)
        outs = project(me, head_out, side, own_w, side_w, shards)
        parts = [outs[0]]
        for k in range(1, shards):
            parts.append(
                lax.ppermute(outs[k], "head", [(d, (d + k) % shards) for d in range(shards)])
            )
        result = finish(parts, result, c, length)
    return result[None]


def solution(mesh):
    placed = (
        P("stream", "tm", "head"),
        P("stream", None),
        P("stream", None, "head", None),
        P("stream", "head"),
        P("stream", "head", "tm"),
        P("tm", None),
        P("tm"),
        P("stream", "head", None, None),
        P("stream", "head", None, None),
    )
    return jax.shard_map(
        per_device, mesh=mesh, in_specs=placed, out_specs=P("stream", "tm", "head"), check_vma=False
    )
```

time: 189 us -> 99.3 us (0.53)
  waiting for transfers between devices: 73 us -> 21.4 us
  matrix products: 30.1 us -> 0 us
  starting transfers between devices: 0.26 us -> 24 us
  blocking collectives: 23.1 us -> 0 us
  Pallas kernels: 0 us -> 20.1 us
  between operations: 14.7 us -> 0.29 us
  other arithmetic: 16.8 us -> 4.88 us
  loops' own time: 10.7 us -> 0 us
  local copies, waits for them, and re-layouts: 19.7 us -> 27.8 us
    reduce_scatter x1 -> x0, waiting for transfers between devices: 43.4 us -> none  [per_device(): lax.psum_scatter(lax.map(one_slot, slot_list).reshape(stretch_len * lax.a...]
    dot_general x11 -> x0, matrix products: 30.1 us -> none  [the longest x4 8.28 us: one_slot(): return jnp.dot(head_out, columns, preferred_element_type=jnp.float32)]
    all_gather x2 -> x0, waiting for transfers between devices: 28.8 us -> none  [the longest x1 28.8 us: entering(): lax.all_gather(part.astype(kind), axis)]
    ppermute x0 -> x18, starting transfers between devices: none -> 24 us  [the longest x3 9.7 us: per_device(): lax.ppermute(joint, 'tm', [(d, d + 2 * k) for d in range(blocks - 2 * k)])]
    unnamed x1 -> x0, blocking collectives: 23.1 us -> none
    ppermute x0 -> x18, waiting for transfers between devices: none -> 21.4 us  [the longest x4 16.4 us: per_device(): lax.ppermute(outs[k], 'head', [(d, (d + k) % shards) for d in range(shard...]
    pallas_call x0 -> x23, Pallas kernels: none -> 20.1 us  [the longest x4 6.13 us: attention(): pl.pallas_call(functools.partial(attention_kernel, chunk, heads, dim), in...]
    another operation x2 -> x0, loops' own time: 10.7 us -> none  [the longest x1 10.5 us: per_device(): lax.map(one_slot, slot_list)]
  transfers between devices with their start and end apart: 3 -> 18, of which waited for: 2 -> 5; matrix products, arithmetic and copies ran while one was open for 13% -> 27% of each run, Pallas kernels for 0% -> 20%
where the time goes in v2:
time: 99.3 us; the launch traced here: 98.4 us
  local copies, waits for them, and re-layouts  27.8 us (28%)
  starting transfers between devices  24 us (24%)
  waiting for transfers between devices  21.4 us (22%)
  Pallas kernels  20.1 us (20%)
  other arithmetic  4.88 us (5%)
    ppermute x4, waiting for transfers between devices, per_device(): lax.ppermute(outs[k], 'head', [(d, (d + k) % shards) for d in range(shard...  16.4 us
    ppermute x3, starting transfers between devices, per_device(): lax.ppermute(joint, 'tm', [(d, d + 2 * k) for d in range(blocks - 2 * k)])  9.7 us
    unnamed x16, local copies, waits for them, and re-layouts  8.65 us
    pallas_call x4, Pallas kernels, attention(): pl.pallas_call(functools.partial(attention_kernel, chunk, heads, dim), in...  6.13 us
    reshape x1, local copies, waits for them, and re-layouts, per_device(): w = jnp.transpose(w, (0, 2, 1, 3)).reshape(-1, 3 * heads * dim)  6.1 us
    transpose x1, local copies, waits for them, and re-layouts, per_device(): w = jnp.transpose(w, (0, 2, 1, 3)).reshape(-1, 3 * heads * dim)  5.99 us
    pallas_call x3, Pallas kernels, qkv(): pl.pallas_call(functools.partial(qkv_kernel, heads, dim), in_specs=[SMEM]...  5.27 us
    ppermute x4, starting transfers between devices, per_device(): lax.ppermute(piece, 'head', [((d + k) % shards, d) for d in range(shards)])  5.14 us
  transfers between devices with their start and end apart: 18, of which 5 were waited for; matrix products, arithmetic and copies ran while one was open for 27% of the time, Pallas kernels for 20%

profile of v2, /device:TPU:0, one launch (start us, length us, event | category | flops | bytes accessed | tf_op | source)
XLA Modules:
  0.0 98.4 jit_solution(5168947400962646398)
XLA Ops:
  0.0 1.0 slice_bitcast_fusion.refs_0_
  1.0 1.0 slice.54.refs_0_
  1.9 1.0 slice.55.refs_0_
  2.9 1.0 slice.56.refs_0_
  3.9 3.0 %collective-permute-start = (bf16[256,512]{1,0:T(8,128)(2,1)S(1)}, bf16[256,512]{1,0:T(8,128)(2,1)S(1)}, u32[]{:S(2)}, u32[]{:S(2)}) collective-permute-start(bf16[256,512]{1,0:T(8,128)(2,1)S(1)} %slice.56.refs_0_), channel_id=1, source_target_pairs={{1,0},{0,1},{3,2},{2,3},{5,4},{4,5},{7,6},{6,7},{9,8},{8,9},{11,10... | collective-permute-start | bytes 786440 | tf_op jit(solution)/shard_map/ppermute | solution.py:367
  7.0 1.9 %collective-permute-start.2 = (bf16[256,512]{1,0:T(8,128)(2,1)S(1)}, bf16[256,512]{1,0:T(8,128)(2,1)S(1)}, u32[]{:S(2)}, u32[]{:S(2)}) collective-permute-start(bf16[256,512]{1,0:T(8,128)(2,1)S(1)} %slice.54.refs_0_), channel_id=1, source_target_pairs={{1,0},{0,1},{3,2},{2,3},{5,4},{4,5},{7,6},{6,7},{9,8},{8,9},{11,10... | collective-permute-start | bytes 786440 | tf_op jit(solution)/shard_map/ppermute | solution.py:367
  9.0 0.7 convert_element_type.23
  9.8 0.7 copy.21
  10.5 1.1 %reduce-window.6 = f32[4,8,128]{2,1,0:T(8,128)S(1)} reduce-window(f32[4,8,128]{2,1,0:T(8,128)S(1)} %bitcast.43, f32[]{:T(128)} %constant.23.clone.1), window={size=1x1x128 pad=0_0x0_0x127_0}, to_apply=%region_0.0 | reduce-window | flops 520192 | bytes 32772 | tf_op jit(solution)/shard_map/reduce-window
  12.0 1.0 %copy.15 = f32[4,8,128]{0,2,1:T(8,128)} copy(f32[4,8,128]{2,1,0:T(8,128)S(1)} %broadcast_add_fusion) | data formatting | bytes 32768 | tf_op jit(solution)/shard_map/reduce_window_sum
  13.1 0.7 slice_bitcast_fusion.1
  13.8 2.1 %multiply_bitcast_fusion = (f32[1024,4]{1,0:T(8,128)}, f32[1024,4]{1,0:T(8,128)S(1)}) fusion(f32[1024]{0:T(1024)S(1)} %bitcast.44, f32[4]{0:T(128)S(1)} %slice_bitcast_fusion.1, f32[4,8,128]{0,2,1:T(8,128)} %copy.15), kind=kLoop, calls=%fused_computation | loop fusion | flops 12288 | bytes 53264 | tf_op jit(solution)/shard_map/transpose | solution.py:377
  15.9 5.9 %copy.16 = bf16[1,1024,4,384]{1,3,2,0:T(8,128)(2,1)} copy(bf16[1,1024,4,384]{3,2,1,0:T(4,128)(2,1)} %param.11) | data formatting | bytes 6291456 | tf_op args[2]
  21.8 6.0 %copy.17 = bf16[1024,3,4,128]{3,2,1,0:T(4,128)(2,1)} copy(bf16[1024,3,4,128]{0,3,1,2:T(8,128)(2,1)} %bitcast.37) | data formatting | bytes 6291456 | tf_op jit(solution)/shard_map/transpose | solution.py:392
  27.8 6.1 %reshape.34.w_ref = bf16[1024,1536]{1,0:T(8,128)(2,1)} reshape(bf16[1024,3,4,128]{3,2,1,0:T(4,128)(2,1)} %copy.17) | data formatting | bytes 6291456 | tf_op jit(solution)/shard_map/reshape | solution.py:392
  33.9 1.1 %fusion.2 = (f32[256,4]{1,0:T(8,128)S(1)}, f32[256,4]{1,0:T(8,128)S(1)}, f32[256,4]{1,0:T(8,128)S(1)}, f32[256,4]{1,0:T(8,128)S(1)}) fusion(f32[1024,4]{1,0:T(8,128)} %get-tuple-element.81), kind=kLoop, calls=%fused_computation.15 | loop fusion | bytes 32768 | tf_op jit(solution)/shard_map/slice | solution.py:393
  35.0 0.7 exponential_convert_fusion
  35.9 1.9 %copy-done.1 = bf16[1024,1536]{1,0:T(8,128)(2,1)S(1)} copy-done((bf16[1024,1536]{1,0:T(8,128)(2,1)S(1)}, bf16[1024,1536]{1,0:T(8,128)(2,1)}, u32[]{:S(2)}) %copy-start.1) | copy-done | bytes 3145752
  37.7 2.4 %qkv.3 = (bf16[256,512]{1,0:T(8,128)(2,1)S(1)}, bf16[256,512]{1,0:T(8,128)(2,1)S(1)}, bf16[256,512]{1,0:T(8,128)(2,1)S(1)}, f32[4,128,128]{2,1,0:T(8,128)S(1)}) custom-call(s32[1]{0:T(128)} %bitcast.me_ref, f32[1,1024]{1,0:T(1,128)S(1)} %copy-done.3, bf16[1024,1536]{1,0:T(8,128)(2,1)S(1)} %copy-done.1, f32[256,4]{1,0:T(8,128)S(1)} %get-tuple-element.80.fade_ref, ...), custom_call_target="tpu_custom_call" | custom-call | flops 1610612736 | tf_op jit(solution)/shard_map/qkv/pallas_call | solution.py:102
  40.1 1.4 %qkv.4 = (bf16[256,512]{1,0:T(8,128)(2,1)S(1)}, bf16[256,512]{1,0:T(8,128)(2,1)S(1)}, bf16[256,512]{1,0:T(8,128)(2,1)S(1)}, f32[4,128,128]{2,1,0:T(8,128)S(1)}) custom-call(s32[1]{0:T(128)} %bitcast.me_ref, f32[1,1024]{1,0:T(1,128)S(1)} %copy-done.3, bf16[1024,1536]{1,0:T(8,128)(2,1)S(1)} %copy-done.1, f32[256,4]{1,0:T(8,128)S(1)} %get-tuple-element.79.fade_ref, ...), custom_call_target="tpu_custom_call" | custom-call | flops 1610612736 | tf_op jit(solution)/shard_map/qkv/pallas_call | solution.py:102
  41.6 1.4 %qkv.5 = (bf16[256,512]{1,0:T(8,128)(2,1)S(1)}, bf16[256,512]{1,0:T(8,128)(2,1)S(1)}, bf16[256,512]{1,0:T(8,128)(2,1)S(1)}, f32[4,128,128]{2,1,0:T(8,128)S(1)}) custom-call(s32[1]{0:T(128)} %bitcast.me_ref, f32[1,1024]{1,0:T(1,128)S(1)} %copy-done.3, bf16[1024,1536]{1,0:T(8,128)(2,1)S(1)} %copy-done.1, f32[256,4]{1,0:T(8,128)S(1)} %get-tuple-element.78.fade_ref, ...), custom_call_target="tpu_custom_call" | custom-call | flops 1610612736 | tf_op jit(solution)/shard_map/qkv/pallas_call | solution.py:102
  43.2 1.0 %last_keys_values.1 = (bf16[256,512]{1,0:T(8,128)(2,1)S(1)}, bf16[256,512]{1,0:T(8,128)(2,1)S(1)}, f32[256,128]{1,0:T(8,128)S(1)}, bf16[272,128]{1,0:T(8,128)(2,1)S(1)}) custom-call(s32[1]{0:T(128)} %bitcast.me_ref, s32[1]{0:T(128)} %bitcast.1.odd_ref, f32[1,1024]{1,0:T(1,128)S(1)} %copy-done.3, bf16[1024,1536]{1,0:T(8,128)(2,1)S(1)} %copy-done.1, ...), custom_call_target="tpu_custom_call" | custom-call | flops 1207959552 | tf_op jit(solution)/shard_map/last_keys_values/pallas_call | solution.py:132
  44.2 2.0 %collective-permute-start.4 = (bf16[272,128]{1,0:T(8,128)(2,1)S(1)}, bf16[272,128]{1,0:T(8,128)(2,1)S(1)}, u32[]{:S(2)}, u32[]{:S(2)}) collective-permute-start(bf16[272,128]{1,0:T(8,128)(2,1)S(1)} %get-tuple-element.57), channel_id=1, source_target_pairs={{0,4},{4,0},{8,12},{12,8},{16,20},{20,16},{24,28},{28,24},{1,5},{5... | collective-permute-start | bytes 208904 | tf_op jit(solution)/shard_map/ppermute | solution.py:409
  46.2 2.8 %collective-permute-done.4.came_ref = bf16[272,128]{1,0:T(8,128)(2,1)S(1)} collective-permute-done((bf16[272,128]{1,0:T(8,128)(2,1)S(1)}, bf16[272,128]{1,0:T(8,128)(2,1)S(1)}, u32[]{:S(2)}, u32[]{:S(2)}) %collective-permute-start.4) | collective-permute-done | bytes 69664 | tf_op jit(solution)/shard_map/ppermute | solution.py:409
  49.1 3.7 %collective-permute-start.5 = (bf16[272,128]{1,0:T(8,128)(2,1)S(1)}, bf16[272,128]{1,0:T(8,128)(2,1)S(1)}, u32[]{:S(2)}, u32[]{:S(2)}) collective-permute-start(bf16[272,128]{1,0:T(8,128)(2,1)S(1)} %pair.1), channel_id=1, source_target_pairs={{0,8},{4,12},{8,16},{12,20},{16,24},{20,28},{1,9},{5,13},{9,17},{1... | collective-permute-start | bytes 208904 | tf_op jit(solution)/shard_map/ppermute | solution.py:412
  52.8 4.5 %collective-permute-start.6 = (bf16[272,128]{1,0:T(8,128)(2,1)S(1)}, bf16[272,128]{1,0:T(8,128)(2,1)S(1)}, u32[]{:S(2)}, u32[]{:S(2)}) collective-permute-start(bf16[272,128]{1,0:T(8,128)(2,1)S(1)} %pair.1), channel_id=1, source_target_pairs={{0,16},{4,20},{8,24},{12,28},{1,17},{5,21},{9,25},{13,29},{2,18},{... | collective-permute-start | bytes 208904 | tf_op jit(solution)/shard_map/ppermute | solution.py:412
  57.3 1.5 %collective-permute-start.7 = (bf16[272,128]{1,0:T(8,128)(2,1)S(1)}, bf16[272,128]{1,0:T(8,128)(2,1)S(1)}, u32[]{:S(2)}, u32[]{:S(2)}) collective-permute-start(bf16[272,128]{1,0:T(8,128)(2,1)S(1)} %pair.1), channel_id=1, source_target_pairs={{0,24},{4,28},{1,25},{5,29},{2,26},{6,30},{3,27},{7,31}} | collective-permute-start | bytes 208904 | tf_op jit(solution)/shard_map/ppermute | solution.py:412
  58.8 1.7 %attention.5.local_ref = bf16[256,512]{1,0:T(8,128)(2,1)S(1)} custom-call(s32[2,2]{1,0:T(2,128)S(1)} %copy-done.4, f32[1,4]{1,0:T(1,128)S(1)} %broadcast_multiply_fusion.scale_ref, bf16[256,512]{1,0:T(8,128)(2,1)S(1)} %get-tuple-element.62.q_ref, bf16[256,512]{1,0:T(8,128)(2,1)S(1)} %get-tuple-element.43.refs_0_, ...), custom_call_target="tpu_custom_call" | custom-call | flops 805306368 | tf_op jit(solution)/shard_map/attention/pallas_call | solution.py:188
  60.6 1.5 %collective-permute-start.8 = (bf16[256,128]{1,0:T(8,128)(2,1)S(1)}, bf16[256,128]{1,0:T(8,128)(2,1)S(1)}, u32[]{:S(2)}, u32[]{:S(2)}) collective-permute-start(bf16[256,128]{1,0:T(8,128)(2,1)S(1)} %get-tuple-element.59), channel_id=1, source_target_pairs={{0,4},{4,0},{8,12},{12,8},{16,20},{20,16},{24,28},{28,24},{1,5},{5... | collective-permute-start | bytes 196616 | tf_op jit(solution)/shard_map/ppermute | solution.py:416
  62.2 0.7 last_queries.1.q_ref
  62.9 2.1 %collective-permute-done.8.came_ref = bf16[256,128]{1,0:T(8,128)(2,1)S(1)} collective-permute-done((bf16[256,128]{1,0:T(8,128)(2,1)S(1)}, bf16[256,128]{1,0:T(8,128)(2,1)S(1)}, u32[]{:S(2)}, u32[]{:S(2)}) %collective-permute-start.8) | collective-permute-done | bytes 65568 | tf_op jit(solution)/shard_map/ppermute | solution.py:416
  65.3 1.4 %attention.6.local_ref = bf16[256,512]{1,0:T(8,128)(2,1)S(1)} custom-call(s32[2,2]{1,0:T(2,128)S(1)} %copy-done.4, f32[1,4]{1,0:T(1,128)S(1)} %broadcast_multiply_fusion.scale_ref, bf16[256,512]{1,0:T(8,128)(2,1)S(1)} %get-tuple-element.65.q_ref, bf16[256,512]{1,0:T(8,128)(2,1)S(1)} %get-tuple-element.43.refs_0_, ...), custom_call_target="tpu_custom_call" | custom-call | flops 536870912 | tf_op jit(solution)/shard_map/attention/pallas_call | solution.py:188
  66.7 1.1 %attention.7.local_ref = bf16[256,512]{1,0:T(8,128)(2,1)S(1)} custom-call(s32[2,2]{1,0:T(2,128)S(1)} %copy-done.4, f32[1,4]{1,0:T(1,128)S(1)} %broadcast_multiply_fusion.scale_ref, bf16[256,512]{1,0:T(8,128)(2,1)S(1)} %get-tuple-element.68.q_ref, bf16[256,512]{1,0:T(8,128)(2,1)S(1)} %get-tuple-element.43.refs_0_, ...), custom_call_target="tpu_custom_call" | custom-call | flops 268435456 | tf_op jit(solution)/shard_map/attention/pallas_call | solution.py:188
  69.0 1.9 %attention.4.local_ref = bf16[256,512]{1,0:T(8,128)(2,1)S(1)} custom-call(s32[2,2]{1,0:T(2,128)S(1)} %copy-done.4, f32[1,4]{1,0:T(1,128)S(1)} %broadcast_multiply_fusion.scale_ref, bf16[256,512]{1,0:T(8,128)(2,1)S(1)} %last_queries.1.q_ref, bf16[256,512]{1,0:T(8,128)(2,1)S(1)} %get-tuple-element.43.refs_0_, bf16[256,512]{1,0:T(8,128)(2,1)S(1)} %get-tuple-element.46.refs_1_, ...), custom_call_target="tpu_custom_call" | custom-call | flops 1073741824 | tf_op jit(solution)/shard_map/attention/pallas_call | solution.py:188
  71.7 0.7 project.5
  72.4 1.6 %collective-permute-start.13 = (bf16[256,512]{1,0:T(8,128)(2,1)S(1)}, bf16[256,512]{1,0:T(8,128)(2,1)S(1)}, u32[]{:S(2)}, u32[]{:S(2)}) collective-permute-start(bf16[256,512]{1,0:T(8,128)(2,1)S(1)} %get-tuple-element.64), channel_id=1, source_target_pairs={{0,1},{1,0},{2,3},{3,2},{4,5},{5,4},{6,7},{7,6},{8,9},{9,8},{10,11... | collective-permute-start | bytes 786440 | tf_op jit(solution)/shard_map/ppermute | solution.py:429
  74.0 0.7 project.6
  74.7 0.6 collective-permute-start.15
  75.3 0.7 project.7
  76.0 1.6 %collective-permute-start.17 = (bf16[256,512]{1,0:T(8,128)(2,1)S(1)}, bf16[256,512]{1,0:T(8,128)(2,1)S(1)}, u32[]{:S(2)}, u32[]{:S(2)}) collective-permute-start(bf16[256,512]{1,0:T(8,128)(2,1)S(1)} %get-tuple-element.70), channel_id=1, source_target_pairs={{0,1},{1,0},{2,3},{3,2},{4,5},{5,4},{6,7},{7,6},{8,9},{9,8},{10,11... | collective-permute-start | bytes 786440 | tf_op jit(solution)/shard_map/ppermute | solution.py:429
  77.6 0.7 project.4
  78.3 0.6 collective-permute-start.11
  78.9 14.0 %collective-permute-done.17.refs_1_ = bf16[256,512]{1,0:T(8,128)(2,1)S(1)} collective-permute-done((bf16[256,512]{1,0:T(8,128)(2,1)S(1)}, bf16[256,512]{1,0:T(8,128)(2,1)S(1)}, u32[]{:S(2)}, u32[]{:S(2)}) %collective-permute-start.17) | collective-permute-done | bytes 262176 | tf_op jit(solution)/shard_map/ppermute | solution.py:429
  92.9 0.8 finish.4.refs_2_
  93.7 0.8 finish.5.refs_2_
  94.4 0.8 finish.6.refs_2_
  95.2 2.4 %collective-permute-done.11.refs_1_ = bf16[256,512]{1,0:T(8,128)(2,1)S(1)} collective-permute-done((bf16[256,512]{1,0:T(8,128)(2,1)S(1)}, bf16[256,512]{1,0:T(8,128)(2,1)S(1)}, u32[]{:S(2)}, u32[]{:S(2)}) %collective-permute-start.11) | collective-permute-done | bytes 262176 | tf_op jit(solution)/shard_map/ppermute | solution.py:429
  97.6 0.8 finish.7
  (48 shorter events, 3.3 us)
Async XLA Ops:
  3.9 39.2 %collective-permute-start = (bf16[256,512]{1,0:T(8,128)(2,1)S(1)}, bf16[256,512]{1,0:T(8,128)(2,1)S(1)}, u32[]{:S(2)}, u32[]{:S(2)}) collective-permute-start(bf16[256,512]{1,0:T(8,128)(2,1)S(1)} %slice.56.refs_0_), channel_id=1, source_target_pairs={{1,0},{0,1},{3,2},{2,3},{5,4},{4,5},{7,6},{6,7},{9,8},{8,9},{11,10... | collective-permute-start | bytes 786440 | tf_op jit(solution)/shard_map/ppermute | solution.py:367
  6.9 28.9 %collective-permute-start.1 = (bf16[256,512]{1,0:T(8,128)(2,1)S(1)}, bf16[256,512]{1,0:T(8,128)(2,1)}, u32[]{:S(2)}, u32[]{:S(2)}) collective-permute-start(bf16[256,512]{1,0:T(8,128)(2,1)S(1)} %slice_bitcast_fusion.refs_0_), channel_id=1, source_target_pairs={{1,0},{0,1},{3,2},{2,3},{5,4},{4,5},{7,6},{6,7},{9,8},{8,9},{11,10... | collective-permute-start | bytes 786440 | tf_op jit(solution)/shard_map/ppermute | solution.py:367
  7.0 33.1 %collective-permute-start.2 = (bf16[256,512]{1,0:T(8,128)(2,1)S(1)}, bf16[256,512]{1,0:T(8,128)(2,1)S(1)}, u32[]{:S(2)}, u32[]{:S(2)}) collective-permute-start(bf16[256,512]{1,0:T(8,128)(2,1)S(1)} %slice.54.refs_0_), channel_id=1, source_target_pairs={{1,0},{0,1},{3,2},{2,3},{5,4},{4,5},{7,6},{6,7},{9,8},{8,9},{11,10... | collective-permute-start | bytes 786440 | tf_op jit(solution)/shard_map/ppermute | solution.py:367
  9.0 32.6 %collective-permute-start.3 = (bf16[256,512]{1,0:T(8,128)(2,1)S(1)}, bf16[256,512]{1,0:T(8,128)(2,1)S(1)}, u32[]{:S(2)}, u32[]{:S(2)}) collective-permute-start(bf16[256,512]{1,0:T(8,128)(2,1)S(1)} %slice.55.refs_0_), channel_id=1, source_target_pairs={{1,0},{0,1},{3,2},{2,3},{5,4},{4,5},{7,6},{6,7},{9,8},{8,9},{11,10... | collective-permute-start | bytes 786440 | tf_op jit(solution)/shard_map/ppermute | solution.py:367
  9.0 62.7 %collective-permute-start.10 = (bf16[512,1024]{1,0:T(8,128)(2,1)}, bf16[512,1024]{1,0:T(8,128)(2,1)S(1)}, u32[]{:S(2)}, u32[]{:S(2)}) collective-permute-start(bf16[512,1024]{1,0:T(8,128)(2,1)} %bitcast.47), channel_id=1, source_target_pairs={{0,2},{2,0},{1,3},{3,1},{4,6},{6,4},{5,7},{7,5},{8,10},{10,8},{9,1... | collective-permute-start | bytes 3145736 | tf_op jit(solution)/shard_map/ppermute | solution.py:371
  27.8 8.0 %copy-start.3 = (f32[1,1024]{1,0:T(1,128)S(1)}, f32[1,1024]{1,0:T(1,128)}, u32[]{:S(2)}) copy-start(f32[1,1024]{1,0:T(1,128)} %gain_ref.9) | copy-start | bytes 12292
  35.9 1.9 %copy-start.1 = (bf16[1024,1536]{1,0:T(8,128)(2,1)S(1)}, bf16[1024,1536]{1,0:T(8,128)(2,1)}, u32[]{:S(2)}) copy-start(bf16[1024,1536]{1,0:T(8,128)(2,1)} %reshape.34.w_ref) | copy-start | bytes 9437188
  43.1 3.1 %copy-start.5 = (f32[1,4]{1,0:T(1,128)S(1)}, f32[1,4]{1,0:T(1,128)}, u32[]{:S(2)}) copy-start(f32[1,4]{1,0:T(1,128)} %param.12) | copy-start | bytes 52
  43.1 15.7 %copy-start.4 = (s32[2,2]{1,0:T(2,128)S(1)}, s32[2,2]{1,0:T(2,128)}, u32[]{:S(2)}) copy-start(s32[2,2]{1,0:T(2,128)} %keep_ref.7) | copy-start | bytes 52
  43.2 19.0 %copy-start.2 = (bf16[1024,1536]{1,0:T(8,128)(2,1)S(1)}, bf16[1024,1536]{1,0:T(8,128)(2,1)}, u32[]{:S(2)}) copy-start(bf16[1024,1536]{1,0:T(8,128)(2,1)} %reshape.34.w_ref) | copy-start | bytes 9437188
  44.2 4.8 %collective-permute-start.4 = (bf16[272,128]{1,0:T(8,128)(2,1)S(1)}, bf16[272,128]{1,0:T(8,128)(2,1)S(1)}, u32[]{:S(2)}, u32[]{:S(2)}) collective-permute-start(bf16[272,128]{1,0:T(8,128)(2,1)S(1)} %get-tuple-element.57), channel_id=1, source_target_pairs={{0,4},{4,0},{8,12},{12,8},{16,20},{20,16},{24,28},{28,24},{1,5},{5... | collective-permute-start | bytes 208904 | tf_op jit(solution)/shard_map/ppermute | solution.py:409
  49.1 11.4 %collective-permute-start.5 = (bf16[272,128]{1,0:T(8,128)(2,1)S(1)}, bf16[272,128]{1,0:T(8,128)(2,1)S(1)}, u32[]{:S(2)}, u32[]{:S(2)}) collective-permute-start(bf16[272,128]{1,0:T(8,128)(2,1)S(1)} %pair.1), channel_id=1, source_target_pairs={{0,8},{4,12},{8,16},{12,20},{16,24},{20,28},{1,9},{5,13},{9,17},{1... | collective-permute-start | bytes 208904 | tf_op jit(solution)/shard_map/ppermute | solution.py:412
  52.8 7.7 %collective-permute-start.6 = (bf16[272,128]{1,0:T(8,128)(2,1)S(1)}, bf16[272,128]{1,0:T(8,128)(2,1)S(1)}, u32[]{:S(2)}, u32[]{:S(2)}) collective-permute-start(bf16[272,128]{1,0:T(8,128)(2,1)S(1)} %pair.1), channel_id=1, source_target_pairs={{0,16},{4,20},{8,24},{12,28},{1,17},{5,21},{9,25},{13,29},{2,18},{... | collective-permute-start | bytes 208904 | tf_op jit(solution)/shard_map/ppermute | solution.py:412
  57.3 3.2 %collective-permute-start.7 = (bf16[272,128]{1,0:T(8,128)(2,1)S(1)}, bf16[272,128]{1,0:T(8,128)(2,1)S(1)}, u32[]{:S(2)}, u32[]{:S(2)}) collective-permute-start(bf16[272,128]{1,0:T(8,128)(2,1)S(1)} %pair.1), channel_id=1, source_target_pairs={{0,24},{4,28},{1,25},{5,29},{2,26},{6,30},{3,27},{7,31}} | collective-permute-start | bytes 208904 | tf_op jit(solution)/shard_map/ppermute | solution.py:412
  60.6 4.3 %collective-permute-start.8 = (bf16[256,128]{1,0:T(8,128)(2,1)S(1)}, bf16[256,128]{1,0:T(8,128)(2,1)S(1)}, u32[]{:S(2)}, u32[]{:S(2)}) collective-permute-start(bf16[256,128]{1,0:T(8,128)(2,1)S(1)} %get-tuple-element.59), channel_id=1, source_target_pairs={{0,4},{4,0},{8,12},{12,8},{16,20},{20,16},{24,28},{28,24},{1,5},{5... | collective-permute-start | bytes 196616 | tf_op jit(solution)/shard_map/ppermute | solution.py:416
  65.2 6.5 %collective-permute-start.12 = (bf16[256,512]{1,0:T(8,128)(2,1)S(1)}, bf16[256,512]{1,0:T(8,128)(2,1)S(1)}, u32[]{:S(2)}, u32[]{:S(2)}) collective-permute-start(bf16[256,512]{1,0:T(8,128)(2,1)S(1)} %recall.5.own_ref), channel_id=1, source_target_pairs={{0,2},{2,0},{1,3},{3,1},{4,6},{6,4},{5,7},{7,5},{8,10},{10,8},{9,1... | collective-permute-start | bytes 786440 | tf_op jit(solution)/shard_map/ppermute | solution.py:424
  68.1 3.6 %copy-start = (bf16[1,4,128,1024]{3,2,1,0:T(8,128)(2,1)S(1)}, bf16[1,4,128,1024]{3,2,1,0:T(8,128)(2,1)}, u32[]{:S(2)}) copy-start(bf16[1,4,128,1024]{3,2,1,0:T(8,128)(2,1)} %param.16) | copy-start | bytes 3145732
  68.1 5.9 %collective-permute-start.14 = (bf16[256,512]{1,0:T(8,128)(2,1)S(1)}, bf16[256,512]{1,0:T(8,128)(2,1)S(1)}, u32[]{:S(2)}, u32[]{:S(2)}) collective-permute-start(bf16[256,512]{1,0:T(8,128)(2,1)S(1)} %recall.6.own_ref), channel_id=1, source_target_pairs={{0,2},{2,0},{1,3},{3,1},{4,6},{6,4},{5,7},{7,5},{8,10},{10,8},{9,1... | collective-permute-start | bytes 786440 | tf_op jit(solution)/shard_map/ppermute | solution.py:424
  68.9 6.4 %collective-permute-start.16 = (bf16[256,512]{1,0:T(8,128)(2,1)S(1)}, bf16[256,512]{1,0:T(8,128)(2,1)S(1)}, u32[]{:S(2)}, u32[]{:S(2)}) collective-permute-start(bf16[256,512]{1,0:T(8,128)(2,1)S(1)} %recall.7.own_ref), channel_id=1, source_target_pairs={{0,2},{2,0},{1,3},{3,1},{4,6},{6,4},{5,7},{7,5},{8,10},{10,8},{9,1... | collective-permute-start | bytes 786440 | tf_op jit(solution)/shard_map/ppermute | solution.py:424
  71.1 6.5 %collective-permute-start.9 = (bf16[256,512]{1,0:T(8,128)(2,1)S(1)}, bf16[256,512]{1,0:T(8,128)(2,1)S(1)}, u32[]{:S(2)}, u32[]{:S(2)}) collective-permute-start(bf16[256,512]{1,0:T(8,128)(2,1)S(1)} %recall.4.own_ref), channel_id=1, source_target_pairs={{0,2},{2,0},{1,3},{3,1},{4,6},{6,4},{5,7},{7,5},{8,10},{10,8},{9,1... | collective-permute-start | bytes 786440 | tf_op jit(solution)/shard_map/ppermute | solution.py:424
  72.4 22.0 %collective-permute-start.13 = (bf16[256,512]{1,0:T(8,128)(2,1)S(1)}, bf16[256,512]{1,0:T(8,128)(2,1)S(1)}, u32[]{:S(2)}, u32[]{:S(2)}) collective-permute-start(bf16[256,512]{1,0:T(8,128)(2,1)S(1)} %get-tuple-element.64), channel_id=1, source_target_pairs={{0,1},{1,0},{2,3},{3,2},{4,5},{5,4},{6,7},{7,6},{8,9},{9,8},{10,11... | collective-permute-start | bytes 786440 | tf_op jit(solution)/shard_map/ppermute | solution.py:429
  74.7 18.9 %collective-permute-start.15 = (bf16[256,512]{1,0:T(8,128)(2,1)S(1)}, bf16[256,512]{1,0:T(8,128)(2,1)S(1)}, u32[]{:S(2)}, u32[]{:S(2)}) collective-permute-start(bf16[256,512]{1,0:T(8,128)(2,1)S(1)} %get-tuple-element.67), channel_id=1, source_target_pairs={{0,1},{1,0},{2,3},{3,2},{4,5},{5,4},{6,7},{7,6},{8,9},{9,8},{10,11... | collective-permute-start | bytes 786440 | tf_op jit(solution)/shard_map/ppermute | solution.py:429
  76.0 16.9 %collective-permute-start.17 = (bf16[256,512]{1,0:T(8,128)(2,1)S(1)}, bf16[256,512]{1,0:T(8,128)(2,1)S(1)}, u32[]{:S(2)}, u32[]{:S(2)}) collective-permute-start(bf16[256,512]{1,0:T(8,128)(2,1)S(1)} %get-tuple-element.70), channel_id=1, source_target_pairs={{0,1},{1,0},{2,3},{3,2},{4,5},{5,4},{6,7},{7,6},{8,9},{9,8},{10,11... | collective-permute-start | bytes 786440 | tf_op jit(solution)/shard_map/ppermute | solution.py:429
  78.3 19.3 %collective-permute-start.11 = (bf16[256,512]{1,0:T(8,128)(2,1)S(1)}, bf16[256,512]{1,0:T(8,128)(2,1)S(1)}, u32[]{:S(2)}, u32[]{:S(2)}) collective-permute-start(bf16[256,512]{1,0:T(8,128)(2,1)S(1)} %get-tuple-element.61), channel_id=1, source_target_pairs={{0,1},{1,0},{2,3},{3,2},{4,5},{5,4},{6,7},{7,6},{8,9},{9,8},{10,11... | collective-permute-start | bytes 786440 | tf_op jit(solution)/shard_map/ppermute | solution.py:429

commit v3 on v2

v3 whole, which is shorter than its diff:
```python
import functools
import math

import jax
import jax.numpy as jnp
from jax import lax
from jax.experimental import pallas as pl
from jax.experimental.pallas import tpu as pltpu
from jax.sharding import PartitionSpec as P

BLOCK = 512
CHUNK = 256
TAIL = 16
EPSILON = 1e-06
F32 = jnp.float32
BF16 = jnp.bfloat16
SMEM = pl.BlockSpec(memory_space=pltpu.SMEM)
VMEM = pl.BlockSpec(memory_space=pltpu.VMEM)


def params():
    return pltpu.CompilerParams(vmem_limit_bytes=16 * 1024 * 1024)


def cost(flops, bytes_accessed, transcendentals=0):
    return pl.CostEstimate(
        flops=int(flops), bytes_accessed=int(bytes_accessed), transcendentals=int(transcendentals)
    )


def struct(shape, dtype=BF16):
    return jax.ShapeDtypeStruct(shape, dtype)


def dot(a, b):
    return lax.dot_general(a, b, (((1,), (0,)), ((), ())), preferred_element_type=F32)


def dot_nt(a, b):
    return lax.dot_general(a, b, (((1,), (1,)), ((), ())), preferred_element_type=F32)


def dot_tn(a, b):
    return lax.dot_general(a, b, (((0,), (0,)), ((), ())), preferred_element_type=F32)


def unit(values):
    return values * lax.rsqrt(jnp.mean(values * values, axis=-1, keepdims=True) + EPSILON)


def prepare_kernel(heads, factor, logs_ref, flags_ref, fade_ref, reading_ref, tail_ref, rows_ref):
    length = logs_ref.shape[1]
    rows_ref[...] = jnp.zeros_like(rows_ref)
    rows_ref[:heads, :] = logs_ref[...]
    running = rows_ref[...]
    place = lax.broadcasted_iota(jnp.int32, running.shape, 1)
    step = 1
    while step < length:
        running += jnp.where(place >= step, pltpu.roll(running, step, 1), 0.0)
        step *= 2
    last = running[:, length - 1 :]
    chosen = jnp.zeros_like(running)
    for block in range(length // BLOCK):
        inside = (place >= block * BLOCK) & (place < (block + 1) * BLOCK)
        chosen = jnp.where(inside, flags_ref[block].astype(F32), chosen)
    fade_ref[...] = jnp.transpose(jnp.exp(last - running) * chosen)
    reading_ref[...] = jnp.transpose(jnp.exp(running) * factor)
    decay = jnp.exp(last)
    high = decay.astype(BF16).astype(F32)
    both = jnp.concatenate([high, decay - high], axis=0)
    tail_ref[...] = jnp.broadcast_to(both, tail_ref.shape).astype(BF16)


def prepare(logs, flags, dim, factor):
    heads, length = logs.shape
    lines = TAIL // 2
    return pl.pallas_call(
        functools.partial(prepare_kernel, heads, factor),
        in_specs=[VMEM, SMEM],
        out_specs=[VMEM] * 3,
        out_shape=[struct((length, lines), F32)] * 2 + [struct((TAIL, dim))],
        scratch_shapes=[pltpu.VMEM((lines, length), F32)],
        compiler_params=params(),
        cost_estimate=cost(40 * lines * length, 0),
        name="prepare",
    )(logs, flags)


def normed_parts(me, gain_ref, x_refs):
    shards, width = len(x_refs), x_refs[0].shape[1]
    parts = [x[...].astype(F32) for x in x_refs]
    squares = sum(jnp.sum(p * p, axis=-1, keepdims=True) for p in parts)
    scale = lax.rsqrt(squares * (1.0 / (width * shards)) + EPSILON)
    out = []
    for k, part in enumerate(parts):
        owner = lax.rem(me + k, shards)
        rows = pl.ds(pl.multiple_of(owner * width, width), width)
        out.append(((part * scale * gain_ref[:, rows]).astype(BF16), rows))
    return out


def projected(parts, w_ref, cols):
    total = None
    for part, rows in parts:
        term = dot(part, w_ref[rows, cols])
        total = term if total is None else total + term
    return total


def add_summary(sum_ref, h, key, value, fade_ref, first):
    fade = fade_ref[first : first + key.shape[0], h : h + 1]
    sum_ref[h] += dot_tn((key.astype(F32) * fade).astype(BF16), value)


def qkv_kernel(heads, dim, first, me_ref, gain_ref, w_ref, fade_ref, *refs):
    refs, (q_ref, k_ref, v_ref, sum_ref) = refs[:-4], refs[-4:]
    if first == 0:
        sum_ref[...] = jnp.zeros_like(sum_ref)
        x_refs = refs
    else:
        sum_ref[...] = refs[0][...]
        x_refs = refs[1:]
    parts = normed_parts(me_ref[0], gain_ref, x_refs)
    total = projected(parts, w_ref, slice(None))
    for h in range(heads):
        base = 3 * h * dim
        cols = slice(h * dim, (h + 1) * dim)
        q_ref[:, cols] = unit(total[:, base : base + dim]).astype(BF16)
        key = unit(total[:, base + dim : base + 2 * dim]).astype(BF16)
        value = total[:, base + 2 * dim : base + 3 * dim].astype(BF16)
        k_ref[:, cols] = key
        v_ref[:, cols] = value
        add_summary(sum_ref, h, key, value, fade_ref, first)


def qkv(me, gain, w, fade, prev, xs, heads, dim, first):
    rows = xs[0].shape[0]
    before = [prev] if first else []
    return pl.pallas_call(
        functools.partial(qkv_kernel, heads, dim, first),
        in_specs=[SMEM] + [VMEM] * (3 + len(before) + len(xs)),
        out_specs=[VMEM] * 4,
        out_shape=[struct((rows, heads * dim))] * 3 + [struct((heads, dim, dim), F32)],
        compiler_params=params(),
        cost_estimate=cost(4 * rows * w.size, 0),
        name="qkv",
    )(me, gain, w, fade, *before, *xs)


def last_kernel(heads, dim, first, me_ref, gain_ref, w_ref, fade_ref, prev_ref, tail_ref, *refs):
    x_refs, (k_ref, v_ref, send_ref, sum_ref) = refs[:-4], refs[-4:]
    sum_ref[...] = prev_ref[...]
    parts = normed_parts(me_ref[0], gain_ref, x_refs)
    for h in range(heads):
        base = 3 * h * dim
        cols = slice(h * dim, (h + 1) * dim)
        both = projected(parts, w_ref, slice(base + dim, base + 3 * dim))
        key = unit(both[:, :dim]).astype(BF16)
        value = both[:, dim:].astype(BF16)
        k_ref[:, cols] = key
        v_ref[:, cols] = value
        add_summary(sum_ref, h, key, value, fade_ref, first)
        send_ref[cols, :] = sum_ref[h].astype(BF16)
    send_ref[heads * dim :, :] = tail_ref[...]


def last_keys_values(me, gain, w, fade, prev, tail, xs, heads, dim, first):
    rows = xs[0].shape[0]
    return pl.pallas_call(
        functools.partial(last_kernel, heads, dim, first),
        in_specs=[SMEM] + [VMEM] * (5 + len(xs)),
        out_specs=[VMEM] * 3,
        out_shape=[struct((rows, heads * dim))] * 2 + [struct((heads * dim + TAIL, dim))],
        scratch_shapes=[pltpu.VMEM((heads, dim, dim), F32)],
        compiler_params=params(),
        cost_estimate=cost(3 * rows * w.size, 0),
        name="last_keys_values",
    )(me, gain, w, fade, prev, tail, *xs)


def queries_kernel(heads, dim, me_ref, gain_ref, w_ref, *refs):
    q_ref = refs[-1]
    parts = normed_parts(me_ref[0], gain_ref, refs[:-1])
    for h in range(heads):
        base = 3 * h * dim
        cols = slice(h * dim, (h + 1) * dim)
        q_ref[:, cols] = unit(projected(parts, w_ref, slice(base, base + dim))).astype(BF16)


def last_queries(me, gain, w, xs, heads, dim):
    rows = xs[0].shape[0]
    return pl.pallas_call(
        functools.partial(queries_kernel, heads, dim),
        in_specs=[SMEM] + [VMEM] * (2 + len(xs)),
        out_specs=VMEM,
        out_shape=struct((rows, heads * dim)),
        compiler_params=params(),
        cost_estimate=cost(2 * rows * w.size, 0),
        name="last_queries",
    )(me, gain, w, *xs)


def attention_kernel(chunk, heads, dim, keep_ref, scale_ref, q_ref, *refs):
    k_refs, v_refs, out_ref = refs[: chunk + 1], refs[chunk + 1 : -1], refs[-1]
    rows = q_ref.shape[0]
    per = BLOCK // rows
    block = chunk // per
    causal = lax.broadcasted_iota(jnp.int32, (rows, rows), 1) <= lax.broadcasted_iota(
        jnp.int32, (rows, rows), 0
    )
    ones = jnp.ones((rows, dim), BF16)
    for h in range(heads):
        cols = slice(h * dim, (h + 1) * dim)
        query = q_ref[:, cols]
        total = None
        for j in range(chunk + 1):
            powers = jnp.exp(dot_nt(query, k_refs[j][:, cols]) * scale_ref[0, h])
            if j == chunk:
                powers = jnp.where(causal, powers, 0.0)
            part = dot(powers.astype(BF16), jnp.concatenate([v_refs[j][:, cols], ones], axis=1))
            if j // per < block:
                part = jnp.where(keep_ref[block, j // per] == 1, part, 0.0)
            total = part if total is None else total + part
        out_ref[:, cols] = (total[:, :dim] / total[:, dim:]).astype(BF16)


def attention(chunk, keep, scale, q, ks, vs, heads, dim):
    rows = q.shape[0]
    return pl.pallas_call(
        functools.partial(attention_kernel, chunk, heads, dim),
        in_specs=[SMEM, SMEM] + [VMEM] * (1 + len(ks) + len(vs)),
        out_specs=VMEM,
        out_shape=struct(q.shape),
        compiler_params=params(),
        cost_estimate=cost(
            (chunk + 1) * heads * 8 * rows * rows * dim, 0, (chunk + 1) * heads * rows * rows
        ),
        name="attention",
    )(keep, scale, q, *ks, *vs)


def body_and_decay(ref, h, dim):
    size = ref.shape[0] - TAIL
    high = ref[size + h : size + h + 1, :].astype(F32)
    low = ref[size + TAIL // 2 + h : size + TAIL // 2 + h + 1, :].astype(F32)
    return ref[h * dim : (h + 1) * dim, :].astype(F32), high + low


def scanned(place, refs, h, dim):
    count = len(refs)
    loaded = [body_and_decay(ref, h, dim) for ref in refs]
    state, since = jnp.zeros((dim, refs[0].shape[1]), F32), jnp.ones((1, refs[0].shape[1]), F32)
    before, before_decay = state, since
    for j in range(count):
        before = jnp.where(place == j, state, before)
        before_decay = jnp.where(place == j, since, before_decay)
        body, decay = loaded[0]
        for k in range(1, count):
            here = place == (j ^ k)
            body = jnp.where(here, loaded[k][0], body)
            decay = jnp.where(here, loaded[k][1], decay)
        state = decay * state + body
        since = since * decay
    return before, before_decay, state, since


def quad_kernel(heads, dim, place_ref, *refs):
    refs, (before_ref, decay_ref, total_ref) = refs[:-3], refs[-3:]
    size = heads * dim
    total_ref[size:, :] = jnp.zeros((TAIL, total_ref.shape[1]), BF16)
    for h in range(heads):
        rows = slice(h * dim, (h + 1) * dim)
        before, before_decay, state, since = scanned(place_ref[0], refs, h, dim)
        before_ref[rows, :] = before
        decay_ref[h : h + 1, :] = before_decay
        total_ref[rows, :] = state.astype(BF16)
        high = since.astype(BF16)
        total_ref[size + h : size + h + 1, :] = high
        low = (since - high.astype(F32)).astype(BF16)
        total_ref[size + TAIL // 2 + h : size + TAIL // 2 + h + 1, :] = low


def quad(place, loads, heads, dim):
    shape = loads[0].shape
    return pl.pallas_call(
        functools.partial(quad_kernel, heads, dim),
        in_specs=[SMEM] + [VMEM] * len(loads),
        out_specs=[VMEM] * 3,
        out_shape=[
            struct((heads * dim, shape[1]), F32),
            struct((TAIL // 2, shape[1]), F32),
            struct(shape),
        ],
        compiler_params=params(),
        cost_estimate=cost(loads[0].size * 40, 0),
        name="quad",
    )(place, *loads)


def entering_kernel(heads, dim, place_ref, before_ref, decay_ref, *refs):
    refs, out_ref = refs[:-1], refs[-1]
    for h in range(heads):
        rows = slice(h * dim, (h + 1) * dim)
        earlier = scanned(place_ref[0], refs, h, dim)[0]
        out_ref[rows, :] = (before_ref[rows, :] + decay_ref[h : h + 1, :] * earlier).astype(BF16)


def entering(place, before, decay, totals, heads, dim):
    return pl.pallas_call(
        functools.partial(entering_kernel, heads, dim),
        in_specs=[SMEM] + [VMEM] * (2 + len(totals)),
        out_specs=VMEM,
        out_shape=struct(before.shape),
        compiler_params=params(),
        cost_estimate=cost(before.size * 20, 0),
        name="entering",
    )(place, before, decay, *totals)


def recall_kernel(heads, dim, first, reading_ref, q_ref, local_ref, state_ref, out_ref):
    for h in range(heads):
        cols = slice(h * dim, (h + 1) * dim)
        reading = reading_ref[first : first + q_ref.shape[0], h : h + 1]
        recalled = dot(q_ref[:, cols], state_ref[cols, :]) * reading
        out_ref[:, cols] = (local_ref[:, cols].astype(F32) + recalled).astype(BF16)


def recall(reading, q, local, state, heads, dim, first):
    return pl.pallas_call(
        functools.partial(recall_kernel, heads, dim, first),
        in_specs=[VMEM] * 4,
        out_specs=VMEM,
        out_shape=struct(q.shape),
        compiler_params=params(),
        cost_estimate=cost(4 * q.size * dim, 0),
        name="recall",
    )(reading, q, local, state)


def project_kernel(shards, me_ref, own_ref, side_ref, own_w_ref, side_w_ref, *out_refs):
    width = out_refs[0].shape[1]
    own, side = own_ref[...], side_ref[...]
    for k in reversed(range(shards)):
        owner = lax.rem(me_ref[0] + k, shards)
        cols = pl.ds(pl.multiple_of(owner * width, width), width)
        out = dot(own, own_w_ref[:, cols]) + dot(side, side_w_ref[:, cols])
        out_refs[k][...] = out.astype(out_refs[k].dtype)


def project(me, own, side, own_w, side_w, shards):
    rows = own.shape[0]
    width = own_w.shape[1] // shards
    return pl.pallas_call(
        functools.partial(project_kernel, shards),
        in_specs=[SMEM] + [VMEM] * 4,
        out_specs=[VMEM] * shards,
        out_shape=[struct((rows, width))] * shards,
        compiler_params=params(),
        cost_estimate=cost(4 * rows * own_w.size, 0),
        name="project",
    )(me, own, side, own_w, side_w)


def finish_kernel(count, *refs):
    total = refs[0][...].astype(F32)
    for ref in refs[1:count]:
        total += ref[...].astype(F32)
    refs[-1][...] = total.astype(BF16)


def finish(parts, result, chunk, length):
    rows, width = parts[0].shape
    whole = pl.BlockSpec((rows, width), lambda i: (0, 0))
    more = [] if result is None else [result]
    return pl.pallas_call(
        functools.partial(finish_kernel, len(parts)),
        grid=(1,),
        in_specs=[whole] * len(parts) + [pl.BlockSpec(memory_space=pl.ANY)] * len(more),
        out_specs=pl.BlockSpec((rows, width), lambda i: (chunk, 0)),
        out_shape=struct((length, width)),
        input_output_aliases={len(parts): 0} if more else {},
        compiler_params=params(),
        cost_estimate=cost(rows * width * 2, rows * width * 6),
        name="finish",
    )(*parts, *more)


def per_device(
    residual_signal,
    prescale_amplifier,
    triple_projector,
    score_scaler,
    recall_retained_logshare,
    tile_retain_grid,
    recall_store_flags,
    emission_projector,
    sideways_coupling_coef,
):
    x = residual_signal[0]
    length = x.shape[0]
    chunks = length // CHUNK
    shards = lax.axis_size("head")
    blocks = lax.axis_size("tm")
    heads = triple_projector.shape[2]
    dim = emission_projector.shape[2]
    me = lax.axis_index("head").astype(jnp.int32).reshape(1)
    place = lax.axis_index("tm").astype(jnp.int32).reshape(1)
    swap_streams = [(0, 1), (1, 0)]
    tied = lambda *arrays: lax.optimization_barrier(arrays)

    received = []
    for c in range(chunks):
        piece = x[c * CHUNK : (c + 1) * CHUNK]
        xs = [piece]
        for k in range(1, shards):
            xs.append(lax.ppermute(piece, "head", [((d + k) % shards, d) for d in range(shards)]))
        received.append(xs)

    own_w = emission_projector[0].reshape(heads * dim, -1)
    side_w = lax.ppermute(
        sideways_coupling_coef[0].reshape(heads * dim, -1), "stream", swap_streams
    )
    fade, reading, tail = prepare(
        recall_retained_logshare[0],
        recall_store_flags,
        dim,
        1.0 / math.sqrt(dim * length * blocks),
    )
    scale = score_scaler * (1.0 / math.sqrt(dim))
    gain = prescale_amplifier
    w = triple_projector[0].reshape(-1, 3 * heads * dim)

    qs, ks, vs, locals_ = [], [], [], []
    summary = None
    for c in range(chunks - 1):
        q, k, v, summary = qkv(
            me, gain, w, fade, summary, received[c], heads, dim, c * CHUNK
        )
        qs.append(q)
        ks.append(k)
        vs.append(v)
        locals_.append(attention(c, tile_retain_grid, scale, q, ks, vs, heads, dim))
    summary, *locals_ = tied(summary, *locals_)
    k, v, sent = last_keys_values(
        me, gain, w, fade, summary, tail, received[-1], heads, dim, (chunks - 1) * CHUNK
    )
    ks.append(k)
    vs.append(v)

    quad_size = min(4, blocks)
    loads = [sent] + [
        lax.ppermute(sent, "tm", [(d, d ^ k) for d in range(blocks)]) for k in range(1, quad_size)
    ]
    qs.append(last_queries(me, gain, w, received[-1], heads, dim))
    locals_.append(attention(chunks - 1, tile_retain_grid, scale, qs[-1], ks, vs, heads, dim))
    *loads, locals_[-1] = tied(*loads, locals_[-1])
    before, decay, total = quad(lax.rem(place, quad_size), loads, heads, dim)
    totals = [total] + [
        lax.ppermute(total, "tm", [(d, d ^ (quad_size * k)) for d in range(blocks)])
        for k in range(1, blocks // quad_size)
    ]
    state = entering(lax.div(place, quad_size), before, decay, totals, heads, dim)

    result = None
    for c in range(chunks):
        head_out = recall(reading, qs[c], locals_[c], state, heads, dim, c * CHUNK)
        side = lax.ppermute(head_out, "stream", swap_streams)
        outs = project(me, head_out, side, own_w, side_w, shards)
        parts = [outs[0]]
        for k in range(1, shards):
            parts.append(
                lax.ppermute(outs[k], "head", [(d, (d + k) % shards) for d in range(shards)])
            )
        result = finish(parts, result, c, length)
    return result[None]


def solution(mesh):
    placed = (
        P("stream", "tm", "head"),
        P("stream", None),
        P("stream", None, "head", None),
        P("stream", "head"),
        P("stream", "head", "tm"),
        P("tm", None),
        P("tm"),
        P("stream", "head", None, None),
        P("stream", "head", None, None),
    )
    return jax.shard_map(
        per_device, mesh=mesh, in_specs=placed, out_specs=P("stream", "tm", "head"), check_vma=False
    )
```

time: 99.3 us -> 79 us (0.80)
  local copies, waits for them, and re-layouts: 27.8 us -> 8.62 us
  starting transfers between devices: 24 us -> 17.1 us
  Pallas kernels: 20.1 us -> 25.5 us
  waiting for transfers between devices: 21.4 us -> 26.5 us
  other arithmetic: 4.88 us -> 0.66 us
    ppermute x5 -> x4, starting transfers between devices: 13.2 us -> 6.37 us  [the longest x3 3.55 us: per_device(): lax.ppermute(sent, 'tm', [(d, d ^ k) for d in range(blocks)])]
    reshape x1 -> x0, local copies, waits for them, and re-layouts: 6.1 us -> none  [per_device(): w = jnp.transpose(w, (0, 2, 1, 3)).reshape(-1, 3 * heads * dim)]
    transpose x1 -> x0, local copies, waits for them, and re-layouts: 5.99 us -> none  [per_device(): w = jnp.transpose(w, (0, 2, 1, 3)).reshape(-1, 3 * heads * dim)]
    pallas_call x10 -> x11, Pallas kernels: 7.35 us -> 12.5 us  [the longest x3 7.45 us: qkv(): pl.pallas_call(functools.partial(qkv_kernel, heads, dim, first), in_specs...]
    ppermute x5 -> x4, waiting for transfers between devices: 4.99 us -> 10.1 us  [the longest x1 6.15 us: per_device(): lax.ppermute(total, 'tm', [(d, d ^ quad_size * k) for d in range(blocks)])]
    slice x4 -> x1, local copies, waits for them, and re-layouts: 3.88 us -> 1.25 us  [per_device(): piece = x[c * CHUNK:(c + 1) * CHUNK]]
    transpose x1 -> x0, other arithmetic: 2.06 us -> none  [per_device(): fade = jnp.transpose(jnp.exp(running[:, -1:] - running) * flags[None, :])]
    another operation x3 -> x0, other arithmetic: 1.39 us -> none
  transfers between devices with their start and end apart: 18 -> 17, of which waited for: 5 -> 7; matrix products, arithmetic and copies ran while one was open for 27% -> 6% of each run, Pallas kernels for 20% -> 31%
where the time goes in v3:
time: 79 us; the launch traced here: 78.6 us
  waiting for transfers between devices  26.5 us (34%)
  Pallas kernels  25.5 us (32%)
  starting transfers between devices  17.1 us (22%)
  local copies, waits for them, and re-layouts  8.62 us (11%)
    ppermute x4, waiting for transfers between devices, per_device(): lax.ppermute(outs[k], 'head', [(d, (d + k) % shards) for d in range(shard...  16.4 us
    pallas_call x3, Pallas kernels, qkv(): pl.pallas_call(functools.partial(qkv_kernel, heads, dim, first), in_specs...  7.45 us
    unnamed x15, local copies, waits for them, and re-layouts  7.37 us
    ppermute x1, waiting for transfers between devices, per_device(): lax.ppermute(total, 'tm', [(d, d ^ quad_size * k) for d in range(blocks)])  6.15 us
    pallas_call x4, Pallas kernels, attention(): pl.pallas_call(functools.partial(attention_kernel, chunk, heads, dim), in...  6.15 us
    ppermute x4, starting transfers between devices, per_device(): lax.ppermute(piece, 'head', [((d + k) % shards, d) for d in range(shards)])  5.14 us
    ppermute x4, starting transfers between devices, per_device(): lax.ppermute(outs[k], 'head', [(d, (d + k) % shards) for d in range(shard...  4.31 us
    ppermute x3, waiting for transfers between devices, per_device(): lax.ppermute(sent, 'tm', [(d, d ^ k) for d in range(blocks)])  3.96 us
  transfers between devices with their start and end apart: 17, of which 7 were waited for; matrix products, arithmetic and copies ran while one was open for 6% of the time, Pallas kernels for 31%

profile of v3, /device:TPU:0, one launch (start us, length us, event | category | flops | bytes accessed | tf_op | source)
XLA Modules:
  0.0 78.6 jit_solution(11116794836930275086)
XLA Ops:
  0.0 1.3 %slice_bitcast_fusion = (bf16[256,512]{1,0:T(8,128)(2,1)S(1)}, bf16[256,512]{1,0:T(8,128)(2,1)S(1)}, bf16[256,512]{1,0:T(8,128)(2,1)S(1)}, bf16[256,512]{1,0:T(8,128)(2,1)S(1)}) fusion(bf16[1,1024,512]{2,1,0:T(8,128)(2,1)} %param.9), kind=kLoop, calls=%fused_computation | loop fusion | bytes 2097152 | tf_op jit(solution)/shard_map/slice | solution.py:413
  1.3 3.0 %collective-permute-start.1 = (bf16[256,512]{1,0:T(8,128)(2,1)S(1)}, bf16[256,512]{1,0:T(8,128)(2,1)}, u32[]{:S(2)}, u32[]{:S(2)}) collective-permute-start(bf16[256,512]{1,0:T(8,128)(2,1)S(1)} %get-tuple-element.82.refs_0_), channel_id=1, source_target_pairs={{1,0},{0,1},{3,2},{2,3},{5,4},{4,5},{7,6},{6,7},{9,8},{8,9},{11,10... | collective-permute-start | bytes 786440 | tf_op jit(solution)/shard_map/ppermute | solution.py:416
  4.4 1.9 %collective-permute-start.3 = (bf16[256,512]{1,0:T(8,128)(2,1)S(1)}, bf16[256,512]{1,0:T(8,128)(2,1)}, u32[]{:S(2)}, u32[]{:S(2)}) collective-permute-start(bf16[256,512]{1,0:T(8,128)(2,1)S(1)} %get-tuple-element.81.refs_1_), channel_id=1, source_target_pairs={{1,0},{0,1},{3,2},{2,3},{5,4},{4,5},{7,6},{6,7},{9,8},{8,9},{11,10... | collective-permute-start | bytes 786440 | tf_op jit(solution)/shard_map/ppermute | solution.py:416
  6.4 0.7 broadcast_multiply_fusion.scale_ref
  7.1 0.7 copy-done.3
  7.8 0.7 copy-done.6
  8.4 1.4 %prepare.1 = (f32[1024,8]{1,0:T(8,128)S(1)}, f32[1024,8]{1,0:T(8,128)S(1)}, bf16[16,128]{1,0:T(8,128)(2,1)S(1)}) custom-call(f32[4,1024]{1,0:T(4,128)S(1)} %bitcast.26, s32[2]{0:T(128)S(1)} %copy-done.6), custom_call_target="tpu_custom_call" | custom-call | flops 327680 | tf_op jit(solution)/shard_map/prepare/pallas_call | solution.py:77
  9.9 4.1 %copy.13 = bf16[128,8,4,384]{3,1,2,0:T(8,128)(2,1)} copy(bf16[128,8,4,384]{3,2,1,0:T(4,128)(2,1)} %bitcast.27) | data formatting | bytes 6291456
  14.0 1.9 %copy-done.1 = bf16[128,8,4,384]{3,1,2,0:T(8,128)(2,1)S(1)} copy-done((bf16[128,8,4,384]{3,1,2,0:T(8,128)(2,1)S(1)}, bf16[128,8,4,384]{3,1,2,0:T(8,128)(2,1)}, u32[]{:S(2)}) %copy-start.1) | copy-done | bytes 3145752
  15.8 2.4 %qkv.3 = (bf16[256,512]{1,0:T(8,128)(2,1)S(1)}, bf16[256,512]{1,0:T(8,128)(2,1)S(1)}, bf16[256,512]{1,0:T(8,128)(2,1)S(1)}, f32[4,128,128]{2,1,0:T(8,128)S(1)}) custom-call(s32[1]{0:T(128)} %bitcast.me_ref, f32[1,1024]{1,0:T(1,128)S(1)} %copy-done.4, bf16[1024,1536]{1,0:T(8,128)(2,1)S(1)} %bitcast.21, f32[1024,8]{1,0:T(8,128)S(1)} %get-tuple-element.44.fade_ref, ...), custom_call_target="tpu_custom_call" | custom-call | flops 1610612736 | tf_op jit(solution)/shard_map/qkv/pallas_call | solution.py:139
  18.3 2.6 %qkv.4 = (bf16[256,512]{1,0:T(8,128)(2,1)S(1)}, bf16[256,512]{1,0:T(8,128)(2,1)S(1)}, bf16[256,512]{1,0:T(8,128)(2,1)S(1)}, f32[4,128,128]{2,1,0:T(8,128)S(1)}) custom-call(s32[1]{0:T(128)} %bitcast.me_ref, f32[1,1024]{1,0:T(1,128)S(1)} %copy-done.4, bf16[1024,1536]{1,0:T(8,128)(2,1)S(1)} %bitcast.22, f32[1024,8]{1,0:T(8,128)S(1)} %get-tuple-element.44.fade_ref, ...), custom_call_target="tpu_custom_call" | custom-call | flops 1610612736 | tf_op jit(solution)/shard_map/qkv/pallas_call | solution.py:139
  20.9 1.4 %attention.5.local_ref = bf16[256,512]{1,0:T(8,128)(2,1)S(1)} custom-call(s32[2,2]{1,0:T(2,128)S(1)} %copy-done.5, f32[1,4]{1,0:T(1,128)S(1)} %broadcast_multiply_fusion.scale_ref, bf16[256,512]{1,0:T(8,128)(2,1)S(1)} %get-tuple-element.51.q_ref, bf16[256,512]{1,0:T(8,128)(2,1)S(1)} %get-tuple-element.49.refs_0_, ...), custom_call_target="tpu_custom_call" | custom-call | flops 536870912 | tf_op jit(solution)/shard_map/attention/pallas_call | solution.py:229
  22.4 1.1 %attention.4.local_ref = bf16[256,512]{1,0:T(8,128)(2,1)S(1)} custom-call(s32[2,2]{1,0:T(2,128)S(1)} %copy-done.5, f32[1,4]{1,0:T(1,128)S(1)} %broadcast_multiply_fusion.scale_ref, bf16[256,512]{1,0:T(8,128)(2,1)S(1)} %get-tuple-element.48.q_ref, bf16[256,512]{1,0:T(8,128)(2,1)S(1)} %get-tuple-element.49.refs_0_, ...), custom_call_target="tpu_custom_call" | custom-call | flops 268435456 | tf_op jit(solution)/shard_map/attention/pallas_call | solution.py:229
  23.5 2.4 %qkv.5 = (bf16[256,512]{1,0:T(8,128)(2,1)S(1)}, bf16[256,512]{1,0:T(8,128)(2,1)S(1)}, bf16[256,512]{1,0:T(8,128)(2,1)S(1)}, f32[4,128,128]{2,1,0:T(8,128)S(1)}) custom-call(s32[1]{0:T(128)} %bitcast.me_ref, f32[1,1024]{1,0:T(1,128)S(1)} %copy-done.4, bf16[1024,1536]{1,0:T(8,128)(2,1)S(1)} %bitcast.23, f32[1024,8]{1,0:T(8,128)S(1)} %get-tuple-element.44.fade_ref, ...), custom_call_target="tpu_custom_call" | custom-call | flops 1610612736 | tf_op jit(solution)/shard_map/qkv/pallas_call | solution.py:139
  26.0 1.7 %attention.6.local_ref = bf16[256,512]{1,0:T(8,128)(2,1)S(1)} custom-call(s32[2,2]{1,0:T(2,128)S(1)} %copy-done.5, f32[1,4]{1,0:T(1,128)S(1)} %broadcast_multiply_fusion.scale_ref, bf16[256,512]{1,0:T(8,128)(2,1)S(1)} %get-tuple-element.54.q_ref, bf16[256,512]{1,0:T(8,128)(2,1)S(1)} %get-tuple-element.49.refs_0_, ...), custom_call_target="tpu_custom_call" | custom-call | flops 805306368 | tf_op jit(solution)/shard_map/attention/pallas_call | solution.py:229
  27.6 2.2 %last_keys_values.1 = (bf16[256,512]{1,0:T(8,128)(2,1)S(1)}, bf16[256,512]{1,0:T(8,128)(2,1)S(1)}, bf16[528,128]{1,0:T(8,128)(2,1)S(1)}) custom-call(s32[1]{0:T(128)} %bitcast.me_ref, f32[1,1024]{1,0:T(1,128)S(1)} %copy-done.4, bf16[1024,1536]{1,0:T(8,128)(2,1)S(1)} %bitcast.24, f32[1024,8]{1,0:T(8,128)S(1)} %get-tuple-element.44.fade_ref, ...), custom_call_target="tpu_custom_call" | custom-call | flops 1207959552 | tf_op jit(solution)/shard_map/last_keys_values/pallas_call | solution.py:169
  29.8 2.0 %collective-permute-start.4 = (bf16[528,128]{1,0:T(8,128)(2,1)S(1)}, bf16[528,128]{1,0:T(8,128)(2,1)S(1)}, u32[]{:S(2)}, u32[]{:S(2)}) collective-permute-start(bf16[528,128]{1,0:T(8,128)(2,1)S(1)} %get-tuple-element.63.refs_0_), channel_id=1, source_target_pairs={{0,4},{4,0},{8,12},{12,8},{16,20},{20,16},{24,28},{28,24},{1,5},{5... | collective-permute-start | bytes 405512 | tf_op jit(solution)/shard_map/ppermute | solution.py:452
  31.8 1.6 %collective-permute-start.5 = (bf16[528,128]{1,0:T(8,128)(2,1)S(1)}, bf16[528,128]{1,0:T(8,128)(2,1)S(1)}, u32[]{:S(2)}, u32[]{:S(2)}) collective-permute-start(bf16[528,128]{1,0:T(8,128)(2,1)S(1)} %get-tuple-element.63.refs_0_), channel_id=1, source_target_pairs={{0,8},{4,12},{8,0},{12,4},{16,24},{20,28},{24,16},{28,20},{1,9},{5... | collective-permute-start | bytes 405512 | tf_op jit(solution)/shard_map/ppermute | solution.py:452
  33.4 0.9 %last_queries.1.q_ref = bf16[256,512]{1,0:T(8,128)(2,1)S(1)} custom-call(s32[1]{0:T(128)} %bitcast.me_ref, f32[1,1024]{1,0:T(1,128)S(1)} %copy-done.4, bf16[1024,1536]{1,0:T(8,128)(2,1)S(1)} %bitcast.25, bf16[256,512]{1,0:T(8,128)(2,1)S(1)} %get-tuple-element.83.refs_0_, bf16[256,512]{1,0:T(8,128)(2,1)S(1)} %collective-permute-done.refs_1_), custom_call_target="tpu_custom_call" | custom-call | flops 805306368 | tf_op jit(solution)/shard_map/last_queries/pallas_call | solution.py:192
  34.3 1.9 %attention.7.local_ref = bf16[256,512]{1,0:T(8,128)(2,1)S(1)} custom-call(s32[2,2]{1,0:T(2,128)S(1)} %copy-done.5, f32[1,4]{1,0:T(1,128)S(1)} %broadcast_multiply_fusion.scale_ref, bf16[256,512]{1,0:T(8,128)(2,1)S(1)} %last_queries.1.q_ref, bf16[256,512]{1,0:T(8,128)(2,1)S(1)} %get-tuple-element.49.refs_0_, bf16[256,512]{1,0:T(8,128)(2,1)S(1)} %get-tuple-element.52.refs_1_, ...), custom_call_target="tpu_custom_call" | custom-call | flops 1073741824 | tf_op jit(solution)/shard_map/attention/pallas_call | solution.py:229
  36.2 2.0 %collective-permute-done.5.refs_2_ = bf16[528,128]{1,0:T(8,128)(2,1)S(1)} collective-permute-done((bf16[528,128]{1,0:T(8,128)(2,1)S(1)}, bf16[528,128]{1,0:T(8,128)(2,1)S(1)}, u32[]{:S(2)}, u32[]{:S(2)}) %collective-permute-start.5) | collective-permute-done | bytes 135200 | tf_op jit(solution)/shard_map/ppermute | solution.py:452
  38.2 2.0 %collective-permute-done.6.refs_3_ = bf16[528,128]{1,0:T(8,128)(2,1)S(1)} collective-permute-done((bf16[528,128]{1,0:T(8,128)(2,1)S(1)}, bf16[528,128]{1,0:T(8,128)(2,1)S(1)}, u32[]{:S(2)}, u32[]{:S(2)}) %collective-permute-start.6) | collective-permute-done | bytes 135200 | tf_op jit(solution)/shard_map/ppermute | solution.py:452
  40.2 0.3 quad.1
  40.5 2.8 %collective-permute-start.7 = (bf16[528,128]{1,0:T(8,128)(2,1)S(1)}, bf16[528,128]{1,0:T(8,128)(2,1)S(1)}, u32[]{:S(2)}, u32[]{:S(2)}) collective-permute-start(bf16[528,128]{1,0:T(8,128)(2,1)S(1)} %get-tuple-element.69.refs_0_), channel_id=1, source_target_pairs={{0,16},{4,20},{8,24},{12,28},{16,0},{20,4},{24,8},{28,12},{1,17},{... | collective-permute-start | bytes 405512 | tf_op jit(solution)/shard_map/ppermute | solution.py:459
  43.3 6.2 %collective-permute-done.7.refs_1_ = bf16[528,128]{1,0:T(8,128)(2,1)S(1)} collective-permute-done((bf16[528,128]{1,0:T(8,128)(2,1)S(1)}, bf16[528,128]{1,0:T(8,128)(2,1)S(1)}, u32[]{:S(2)}, u32[]{:S(2)}) %collective-permute-start.7) | collective-permute-done | bytes 135200 | tf_op jit(solution)/shard_map/ppermute | solution.py:459
  49.6 0.4 recall.7.own_ref
  50.1 0.2 recall.6.own_ref
  50.3 0.6 collective-permute-start.13
  50.9 0.2 recall.5.own_ref
  51.1 0.1 collective-permute-start.11
  51.2 0.2 recall.4.own_ref
  51.4 0.6 collective-permute-start.8
  52.0 0.7 project.7
  52.7 1.6 %collective-permute-start.16 = (bf16[256,512]{1,0:T(8,128)(2,1)S(1)}, bf16[256,512]{1,0:T(8,128)(2,1)S(1)}, u32[]{:S(2)}, u32[]{:S(2)}) collective-permute-start(bf16[256,512]{1,0:T(8,128)(2,1)S(1)} %get-tuple-element.80), channel_id=1, source_target_pairs={{0,1},{1,0},{2,3},{3,2},{4,5},{5,4},{6,7},{7,6},{8,9},{9,8},{10,11... | collective-permute-start | bytes 786440 | tf_op jit(solution)/shard_map/ppermute | solution.py:472
  54.4 0.7 project.6
  55.1 0.5 collective-permute-start.14
  55.6 0.7 project.5
  56.3 1.6 %collective-permute-start.12 = (bf16[256,512]{1,0:T(8,128)(2,1)S(1)}, bf16[256,512]{1,0:T(8,128)(2,1)S(1)}, u32[]{:S(2)}, u32[]{:S(2)}) collective-permute-start(bf16[256,512]{1,0:T(8,128)(2,1)S(1)} %get-tuple-element.74), channel_id=1, source_target_pairs={{0,1},{1,0},{2,3},{3,2},{4,5},{5,4},{6,7},{7,6},{8,9},{9,8},{10,11... | collective-permute-start | bytes 786440 | tf_op jit(solution)/shard_map/ppermute | solution.py:472
  58.0 0.7 project.4
  58.7 0.5 collective-permute-start.10
  59.2 2.8 %collective-permute-done.16.refs_1_ = bf16[256,512]{1,0:T(8,128)(2,1)S(1)} collective-permute-done((bf16[256,512]{1,0:T(8,128)(2,1)S(1)}, bf16[256,512]{1,0:T(8,128)(2,1)S(1)}, u32[]{:S(2)}, u32[]{:S(2)}) %collective-permute-start.16) | collective-permute-done | bytes 262176 | tf_op jit(solution)/shard_map/ppermute | solution.py:472
  62.0 0.8 finish.4.refs_2_
  62.7 4.9 %collective-permute-done.14.refs_1_ = bf16[256,512]{1,0:T(8,128)(2,1)S(1)} collective-permute-done((bf16[256,512]{1,0:T(8,128)(2,1)S(1)}, bf16[256,512]{1,0:T(8,128)(2,1)S(1)}, u32[]{:S(2)}, u32[]{:S(2)}) %collective-permute-start.14) | collective-permute-done | bytes 262176 | tf_op jit(solution)/shard_map/ppermute | solution.py:472
  67.6 0.8 finish.5.refs_2_
  68.3 4.9 %collective-permute-done.12.refs_1_ = bf16[256,512]{1,0:T(8,128)(2,1)S(1)} collective-permute-done((bf16[256,512]{1,0:T(8,128)(2,1)S(1)}, bf16[256,512]{1,0:T(8,128)(2,1)S(1)}, u32[]{:S(2)}, u32[]{:S(2)}) %collective-permute-start.12) | collective-permute-done | bytes 262176 | tf_op jit(solution)/shard_map/ppermute | solution.py:472
  73.2 0.8 finish.6.refs_2_
  74.0 3.9 %collective-permute-done.10.refs_1_ = bf16[256,512]{1,0:T(8,128)(2,1)S(1)} collective-permute-done((bf16[256,512]{1,0:T(8,128)(2,1)S(1)}, bf16[256,512]{1,0:T(8,128)(2,1)S(1)}, u32[]{:S(2)}, u32[]{:S(2)}) %collective-permute-start.10) | collective-permute-done | bytes 262176 | tf_op jit(solution)/shard_map/ppermute | solution.py:472
  77.9 0.8 finish.7
  (27 shorter events, 0.4 us)
Async XLA Ops:
  1.3 12.7 %collective-permute-start.1 = (bf16[256,512]{1,0:T(8,128)(2,1)S(1)}, bf16[256,512]{1,0:T(8,128)(2,1)}, u32[]{:S(2)}, u32[]{:S(2)}) collective-permute-start(bf16[256,512]{1,0:T(8,128)(2,1)S(1)} %get-tuple-element.82.refs_0_), channel_id=1, source_target_pairs={{1,0},{0,1},{3,2},{2,3},{5,4},{4,5},{7,6},{6,7},{9,8},{8,9},{11,10... | collective-permute-start | bytes 786440 | tf_op jit(solution)/shard_map/ppermute | solution.py:416
  4.3 14.0 %collective-permute-start.2 = (bf16[256,512]{1,0:T(8,128)(2,1)S(1)}, bf16[256,512]{1,0:T(8,128)(2,1)}, u32[]{:S(2)}, u32[]{:S(2)}) collective-permute-start(bf16[256,512]{1,0:T(8,128)(2,1)S(1)} %get-tuple-element.84.refs_1_), channel_id=1, source_target_pairs={{1,0},{0,1},{3,2},{2,3},{5,4},{4,5},{7,6},{6,7},{9,8},{8,9},{11,10... | collective-permute-start | bytes 786440 | tf_op jit(solution)/shard_map/ppermute | solution.py:416
  4.4 19.1 %collective-permute-start.3 = (bf16[256,512]{1,0:T(8,128)(2,1)S(1)}, bf16[256,512]{1,0:T(8,128)(2,1)}, u32[]{:S(2)}, u32[]{:S(2)}) collective-permute-start(bf16[256,512]{1,0:T(8,128)(2,1)S(1)} %get-tuple-element.81.refs_1_), channel_id=1, source_target_pairs={{1,0},{0,1},{3,2},{2,3},{5,4},{4,5},{7,6},{6,7},{9,8},{8,9},{11,10... | collective-permute-start | bytes 786440 | tf_op jit(solution)/shard_map/ppermute | solution.py:416
  6.3 21.3 %collective-permute-start = (bf16[256,512]{1,0:T(8,128)(2,1)S(1)}, bf16[256,512]{1,0:T(8,128)(2,1)S(1)}, u32[]{:S(2)}, u32[]{:S(2)}) collective-permute-start(bf16[256,512]{1,0:T(8,128)(2,1)S(1)} %get-tuple-element.83.refs_0_), channel_id=1, source_target_pairs={{1,0},{0,1},{3,2},{2,3},{5,4},{4,5},{7,6},{6,7},{9,8},{8,9},{11,10... | collective-permute-start | bytes 786440 | tf_op jit(solution)/shard_map/ppermute | solution.py:416
  6.4 45.6 %collective-permute-start.9 = (bf16[512,1024]{1,0:T(8,128)(2,1)}, bf16[512,1024]{1,0:T(8,128)(2,1)S(1)}, u32[]{:S(2)}, u32[]{:S(2)}) collective-permute-start(bf16[512,1024]{1,0:T(8,128)(2,1)} %bitcast.28), channel_id=1, source_target_pairs={{0,2},{2,0},{1,3},{3,1},{4,6},{6,4},{5,7},{7,5},{8,10},{10,8},{9,1... | collective-permute-start | bytes 3145736 | tf_op jit(solution)/shard_map/ppermute | solution.py:420
  7.1 0.7 copy-start.3
  7.8 0.7 copy-start.6
  9.9 4.1 %copy-start.4 = (f32[1,1024]{1,0:T(1,128)S(1)}, f32[1,1024]{1,0:T(1,128)}, u32[]{:S(2)}) copy-start(f32[1,1024]{1,0:T(1,128)} %gain_ref.9) | copy-start | bytes 12292
  14.0 1.9 %copy-start.1 = (bf16[128,8,4,384]{3,1,2,0:T(8,128)(2,1)S(1)}, bf16[128,8,4,384]{3,1,2,0:T(8,128)(2,1)}, u32[]{:S(2)}) copy-start(bf16[128,8,4,384]{3,1,2,0:T(8,128)(2,1)} %copy.13) | copy-start | bytes 9437188
  18.3 2.6 %copy-start.5 = (s32[2,2]{1,0:T(2,128)S(1)}, s32[2,2]{1,0:T(2,128)}, u32[]{:S(2)}) copy-start(s32[2,2]{1,0:T(2,128)} %keep_ref.7) | copy-start | bytes 52
  18.3 5.2 %copy-start.2 = (bf16[128,8,4,384]{3,1,2,0:T(8,128)(2,1)S(1)}, bf16[128,8,4,384]{3,1,2,0:T(8,128)(2,1)}, u32[]{:S(2)}) copy-start(bf16[128,8,4,384]{3,1,2,0:T(8,128)(2,1)} %copy.13) | copy-start | bytes 9437188
  29.8 6.4 %collective-permute-start.4 = (bf16[528,128]{1,0:T(8,128)(2,1)S(1)}, bf16[528,128]{1,0:T(8,128)(2,1)S(1)}, u32[]{:S(2)}, u32[]{:S(2)}) collective-permute-start(bf16[528,128]{1,0:T(8,128)(2,1)S(1)} %get-tuple-element.63.refs_0_), channel_id=1, source_target_pairs={{0,4},{4,0},{8,12},{12,8},{16,20},{20,16},{24,28},{28,24},{1,5},{5... | collective-permute-start | bytes 405512 | tf_op jit(solution)/shard_map/ppermute | solution.py:452
  31.8 6.4 %collective-permute-start.5 = (bf16[528,128]{1,0:T(8,128)(2,1)S(1)}, bf16[528,128]{1,0:T(8,128)(2,1)S(1)}, u32[]{:S(2)}, u32[]{:S(2)}) collective-permute-start(bf16[528,128]{1,0:T(8,128)(2,1)S(1)} %get-tuple-element.63.refs_0_), channel_id=1, source_target_pairs={{0,8},{4,12},{8,0},{12,4},{16,24},{20,28},{24,16},{28,20},{1,9},{5... | collective-permute-start | bytes 405512 | tf_op jit(solution)/shard_map/ppermute | solution.py:452
  33.4 6.8 %collective-permute-start.6 = (bf16[528,128]{1,0:T(8,128)(2,1)S(1)}, bf16[528,128]{1,0:T(8,128)(2,1)S(1)}, u32[]{:S(2)}, u32[]{:S(2)}) collective-permute-start(bf16[528,128]{1,0:T(8,128)(2,1)S(1)} %get-tuple-element.63.refs_0_), channel_id=1, source_target_pairs={{0,12},{4,8},{8,4},{12,0},{16,28},{20,24},{24,20},{28,16},{1,13},{... | collective-permute-start | bytes 405512 | tf_op jit(solution)/shard_map/ppermute | solution.py:452
  40.5 9.0 %collective-permute-start.7 = (bf16[528,128]{1,0:T(8,128)(2,1)S(1)}, bf16[528,128]{1,0:T(8,128)(2,1)S(1)}, u32[]{:S(2)}, u32[]{:S(2)}) collective-permute-start(bf16[528,128]{1,0:T(8,128)(2,1)S(1)} %get-tuple-element.69.refs_0_), channel_id=1, source_target_pairs={{0,16},{4,20},{8,24},{12,28},{16,0},{20,4},{24,8},{28,12},{1,17},{... | collective-permute-start | bytes 405512 | tf_op jit(solution)/shard_map/ppermute | solution.py:459
  49.5 2.5 %copy-start = (bf16[1,4,128,1024]{3,2,1,0:T(8,128)(2,1)S(1)}, bf16[1,4,128,1024]{3,2,1,0:T(8,128)(2,1)}, u32[]{:S(2)}) copy-start(bf16[1,4,128,1024]{3,2,1,0:T(8,128)(2,1)} %param.16) | copy-start | bytes 3145732
  50.0 2.0 %collective-permute-start.15 = (bf16[256,512]{1,0:T(8,128)(2,1)S(1)}, bf16[256,512]{1,0:T(8,128)(2,1)S(1)}, u32[]{:S(2)}, u32[]{:S(2)}) collective-permute-start(bf16[256,512]{1,0:T(8,128)(2,1)S(1)} %recall.7.own_ref), channel_id=1, source_target_pairs={{0,2},{2,0},{1,3},{3,1},{4,6},{6,4},{5,7},{7,5},{8,10},{10,8},{9,1... | collective-permute-start | bytes 786440 | tf_op jit(solution)/shard_map/ppermute | solution.py:467
  50.3 4.1 %collective-permute-start.13 = (bf16[256,512]{1,0:T(8,128)(2,1)S(1)}, bf16[256,512]{1,0:T(8,128)(2,1)S(1)}, u32[]{:S(2)}, u32[]{:S(2)}) collective-permute-start(bf16[256,512]{1,0:T(8,128)(2,1)S(1)} %recall.6.own_ref), channel_id=1, source_target_pairs={{0,2},{2,0},{1,3},{3,1},{4,6},{6,4},{5,7},{7,5},{8,10},{10,8},{9,1... | collective-permute-start | bytes 786440 | tf_op jit(solution)/shard_map/ppermute | solution.py:467
  51.1 4.5 %collective-permute-start.11 = (bf16[256,512]{1,0:T(8,128)(2,1)S(1)}, bf16[256,512]{1,0:T(8,128)(2,1)S(1)}, u32[]{:S(2)}, u32[]{:S(2)}) collective-permute-start(bf16[256,512]{1,0:T(8,128)(2,1)S(1)} %recall.5.own_ref), channel_id=1, source_target_pairs={{0,2},{2,0},{1,3},{3,1},{4,6},{6,4},{5,7},{7,5},{8,10},{10,8},{9,1... | collective-permute-start | bytes 786440 | tf_op jit(solution)/shard_map/ppermute | solution.py:467
  51.4 6.5 %collective-permute-start.8 = (bf16[256,512]{1,0:T(8,128)(2,1)S(1)}, bf16[256,512]{1,0:T(8,128)(2,1)S(1)}, u32[]{:S(2)}, u32[]{:S(2)}) collective-permute-start(bf16[256,512]{1,0:T(8,128)(2,1)S(1)} %recall.4.own_ref), channel_id=1, source_target_pairs={{0,2},{2,0},{1,3},{3,1},{4,6},{6,4},{5,7},{7,5},{8,10},{10,8},{9,1... | collective-permute-start | bytes 786440 | tf_op jit(solution)/shard_map/ppermute | solution.py:467
  52.7 9.2 %collective-permute-start.16 = (bf16[256,512]{1,0:T(8,128)(2,1)S(1)}, bf16[256,512]{1,0:T(8,128)(2,1)S(1)}, u32[]{:S(2)}, u32[]{:S(2)}) collective-permute-start(bf16[256,512]{1,0:T(8,128)(2,1)S(1)} %get-tuple-element.80), channel_id=1, source_target_pairs={{0,1},{1,0},{2,3},{3,2},{4,5},{5,4},{6,7},{7,6},{8,9},{9,8},{10,11... | collective-permute-start | bytes 786440 | tf_op jit(solution)/shard_map/ppermute | solution.py:472
  55.1 12.5 %collective-permute-start.14 = (bf16[256,512]{1,0:T(8,128)(2,1)S(1)}, bf16[256,512]{1,0:T(8,128)(2,1)S(1)}, u32[]{:S(2)}, u32[]{:S(2)}) collective-permute-start(bf16[256,512]{1,0:T(8,128)(2,1)S(1)} %get-tuple-element.77), channel_id=1, source_target_pairs={{0,1},{1,0},{2,3},{3,2},{4,5},{5,4},{6,7},{7,6},{8,9},{9,8},{10,11... | collective-permute-start | bytes 786440 | tf_op jit(solution)/shard_map/ppermute | solution.py:472
  56.3 16.9 %collective-permute-start.12 = (bf16[256,512]{1,0:T(8,128)(2,1)S(1)}, bf16[256,512]{1,0:T(8,128)(2,1)S(1)}, u32[]{:S(2)}, u32[]{:S(2)}) collective-permute-start(bf16[256,512]{1,0:T(8,128)(2,1)S(1)} %get-tuple-element.74), channel_id=1, source_target_pairs={{0,1},{1,0},{2,3},{3,2},{4,5},{5,4},{6,7},{7,6},{8,9},{9,8},{10,11... | collective-permute-start | bytes 786440 | tf_op jit(solution)/shard_map/ppermute | solution.py:472
  58.7 19.2 %collective-permute-start.10 = (bf16[256,512]{1,0:T(8,128)(2,1)S(1)}, bf16[256,512]{1,0:T(8,128)(2,1)S(1)}, u32[]{:S(2)}, u32[]{:S(2)}) collective-permute-start(bf16[256,512]{1,0:T(8,128)(2,1)S(1)} %get-tuple-element.71), channel_id=1, source_target_pairs={{0,1},{1,0},{2,3},{3,2},{4,5},{5,4},{6,7},{7,6},{8,9},{9,8},{10,11... | collective-permute-start | bytes 786440 | tf_op jit(solution)/shard_map/ppermute | solution.py:472

commit v4 on v3

--- a/solution.py
+++ b/solution.py
@@ -121,13 +121,14 @@
         sum_ref[...] = refs[0][...]
         x_refs = refs[1:]
     parts = normed_parts(me_ref[0], gain_ref, x_refs)
-    total = projected(parts, w_ref, slice(None))
-    for h in range(heads):
-        base = 3 * h * dim
+    wide = heads * dim
+    thirds = [projected(parts, w_ref, slice(i * wide, (i + 1) * wide)) for i in range(3)]
+    taken = lambda at: thirds[at * dim // wide][:, at * dim % wide : at * dim % wide + dim]
+    for h in range(heads):
         cols = slice(h * dim, (h + 1) * dim)
-        q_ref[:, cols] = unit(total[:, base : base + dim]).astype(BF16)
-        key = unit(total[:, base + dim : base + 2 * dim]).astype(BF16)
-        value = total[:, base + 2 * dim : base + 3 * dim].astype(BF16)
+        q_ref[:, cols] = unit(taken(3 * h)).astype(BF16)
+        key = unit(taken(3 * h + 1)).astype(BF16)
+        value = taken(3 * h + 2).astype(BF16)
         k_ref[:, cols] = key
         v_ref[:, cols] = value
         add_summary(sum_ref, h, key, value, fade_ref, first)
@@ -151,12 +152,13 @@
     x_refs, (k_ref, v_ref, send_ref, sum_ref) = refs[:-4], refs[-4:]
     sum_ref[...] = prev_ref[...]
     parts = normed_parts(me_ref[0], gain_ref, x_refs)
-    for h in range(heads):
-        base = 3 * h * dim
+    pairs = [
+        projected(parts, w_ref, slice((3 * h + 1) * dim, (3 * h + 3) * dim)) for h in range(heads)
+    ]
+    for h in range(heads):
         cols = slice(h * dim, (h + 1) * dim)
-        both = projected(parts, w_ref, slice(base + dim, base + 3 * dim))
-        key = unit(both[:, :dim]).astype(BF16)
-        value = both[:, dim:].astype(BF16)
+        key = unit(pairs[h][:, :dim]).astype(BF16)
+        value = pairs[h][:, dim:].astype(BF16)
         k_ref[:, cols] = key
         v_ref[:, cols] = value
         add_summary(sum_ref, h, key, value, fade_ref, first)
@@ -212,9 +214,10 @@
     for h in range(heads):
         cols = slice(h * dim, (h + 1) * dim)
         query = q_ref[:, cols]
+        scale = scale_ref[0, h] * (1.0 / math.sqrt(dim))
         total = None
         for j in range(chunk + 1):
-            powers = jnp.exp(dot_nt(query, k_refs[j][:, cols]) * scale_ref[0, h])
+            powers = jnp.exp(dot_nt(query, k_refs[j][:, cols]) * scale)
             if j == chunk:
                 powers = jnp.where(causal, powers, 0.0)
             part = dot(powers.astype(BF16), jnp.concatenate([v_refs[j][:, cols], ones], axis=1))
@@ -426,7 +429,6 @@
         dim,
         1.0 / math.sqrt(dim * length * blocks),
     )
-    scale = score_scaler * (1.0 / math.sqrt(dim))
     gain = prescale_amplifier
     w = triple_projector[0].reshape(-1, 3 * heads * dim)
 
@@ -439,7 +441,7 @@
         qs.append(q)
         ks.append(k)
         vs.append(v)
-        locals_.append(attention(c, tile_retain_grid, scale, q, ks, vs, heads, dim))
+        locals_.append(attention(c, tile_retain_grid, score_scaler, q, ks, vs, heads, dim))
     summary, *locals_ = tied(summary, *locals_)
     k, v, sent = last_keys_values(
         me, gain, w, fade, summary, tail, received[-1], heads, dim, (chunks - 1) * CHUNK
@@ -452,7 +454,7 @@
         lax.ppermute(sent, "tm", [(d, d ^ k) for d in range(blocks)]) for k in range(1, quad_size)
     ]
     qs.append(last_queries(me, gain, w, received[-1], heads, dim))
-    locals_.append(attention(chunks - 1, tile_retain_grid, scale, qs[-1], ks, vs, heads, dim))
+    locals_.append(attention(chunks - 1, tile_retain_grid, score_scaler, qs[-1], ks, vs, heads, dim))
     *loads, locals_[-1] = tied(*loads, locals_[-1])
     before, decay, total = quad(lax.rem(place, quad_size), loads, heads, dim)
     totals = [total] + [

time: 79 us -> 76.5 us (0.968)
  Pallas kernels: 25.5 us -> 24 us
    pallas_call x1, Pallas kernels: 2.17 us -> 1.11 us  [last_keys_values(): pl.pallas_call(functools.partial(last_kernel, heads, dim, first), in_spec...]
    ppermute x4, waiting for transfers between devices: 0.01 us -> 0.86 us  [per_device(): lax.ppermute(piece, 'head', [((d + k) % shards, d) for d in range(shards)])]
    unnamed x15 -> x17, local copies, waits for them, and re-layouts: 7.37 us -> 7.37 us
  transfers between devices with their start and end apart: 17 -> 17, of which waited for: 7 -> 9; matrix products, arithmetic and copies ran while one was open for 6% -> 5% of each run, Pallas kernels for 31% -> 31%
where the time goes in v4:
time: 76.5 us; the launch traced here: 76.2 us
  waiting for transfers between devices  26.2 us (34%)
  Pallas kernels  24 us (31%)
  starting transfers between devices  17.1 us (22%)
  local copies, waits for them, and re-layouts  8.64 us (11%)
    ppermute x4, waiting for transfers between devices, per_device(): lax.ppermute(outs[k], 'head', [(d, (d + k) % shards) for d in range(shard...  16.4 us
    unnamed x17, local copies, waits for them, and re-layouts  7.37 us
    pallas_call x3, Pallas kernels, qkv(): pl.pallas_call(functools.partial(qkv_kernel, heads, dim, first), in_specs...  7.1 us
    pallas_call x4, Pallas kernels, attention(): pl.pallas_call(functools.partial(attention_kernel, chunk, heads, dim), in...  6.14 us
    ppermute x1, waiting for transfers between devices, per_device(): lax.ppermute(total, 'tm', [(d, d ^ quad_size * k) for d in range(blocks)])  5.74 us
    ppermute x4, starting transfers between devices, per_device(): lax.ppermute(piece, 'head', [((d + k) % shards, d) for d in range(shards)])  5.14 us
    ppermute x4, starting transfers between devices, per_device(): lax.ppermute(outs[k], 'head', [(d, (d + k) % shards) for d in range(shard...  4.31 us
    ppermute x3, starting transfers between devices, per_device(): lax.ppermute(sent, 'tm', [(d, d ^ k) for d in range(blocks)])  3.55 us
  transfers between devices with their start and end apart: 17, of which 9 were waited for; matrix products, arithmetic and copies ran while one was open for 5% of the time, Pallas kernels for 31%

profile of v4, /device:TPU:0, one launch (start us, length us, event | category | flops | bytes accessed | tf_op | source)
XLA Modules:
  0.0 76.2 jit_solution(852709646320401092)
XLA Ops:
  0.0 1.3 %slice_bitcast_fusion = (bf16[256,512]{1,0:T(8,128)(2,1)S(1)}, bf16[256,512]{1,0:T(8,128)(2,1)S(1)}, bf16[256,512]{1,0:T(8,128)(2,1)S(1)}, bf16[256,512]{1,0:T(8,128)(2,1)S(1)}) fusion(bf16[1,1024,512]{2,1,0:T(8,128)(2,1)} %param.9), kind=kLoop, calls=%fused_computation | loop fusion | bytes 2097152 | tf_op jit(solution)/shard_map/slice | solution.py:416
  1.3 3.0 %collective-permute-start.1 = (bf16[256,512]{1,0:T(8,128)(2,1)S(1)}, bf16[256,512]{1,0:T(8,128)(2,1)}, u32[]{:S(2)}, u32[]{:S(2)}) collective-permute-start(bf16[256,512]{1,0:T(8,128)(2,1)S(1)} %get-tuple-element.82.refs_0_), channel_id=1, source_target_pairs={{1,0},{0,1},{3,2},{2,3},{5,4},{4,5},{7,6},{6,7},{9,8},{8,9},{11,10... | collective-permute-start | bytes 786440 | tf_op jit(solution)/shard_map/ppermute | solution.py:419
  4.4 1.9 %collective-permute-start.3 = (bf16[256,512]{1,0:T(8,128)(2,1)S(1)}, bf16[256,512]{1,0:T(8,128)(2,1)}, u32[]{:S(2)}, u32[]{:S(2)}) collective-permute-start(bf16[256,512]{1,0:T(8,128)(2,1)S(1)} %get-tuple-element.81.refs_1_), channel_id=1, source_target_pairs={{1,0},{0,1},{3,2},{2,3},{5,4},{4,5},{7,6},{6,7},{9,8},{8,9},{11,10... | collective-permute-start | bytes 786440 | tf_op jit(solution)/shard_map/ppermute | solution.py:419
  6.4 0.7 copy-done.3
  7.1 0.7 copy-done.7
  7.8 1.4 %prepare.1 = (f32[1024,8]{1,0:T(8,128)S(1)}, f32[1024,8]{1,0:T(8,128)S(1)}, bf16[16,128]{1,0:T(8,128)(2,1)S(1)}) custom-call(f32[4,1024]{1,0:T(4,128)S(1)} %bitcast.26, s32[2]{0:T(128)S(1)} %copy-done.7), custom_call_target="tpu_custom_call" | custom-call | flops 327680 | tf_op jit(solution)/shard_map/prepare/pallas_call | solution.py:77
  9.2 4.1 %copy.13 = bf16[128,8,4,384]{3,1,2,0:T(8,128)(2,1)} copy(bf16[128,8,4,384]{3,2,1,0:T(4,128)(2,1)} %bitcast.27) | data formatting | bytes 6291456
  13.3 1.9 %copy-done.1 = bf16[128,8,4,384]{3,1,2,0:T(8,128)(2,1)S(1)} copy-done((bf16[128,8,4,384]{3,1,2,0:T(8,128)(2,1)S(1)}, bf16[128,8,4,384]{3,1,2,0:T(8,128)(2,1)}, u32[]{:S(2)}) %copy-start.1) | copy-done | bytes 3145752
  15.2 2.3 %qkv.3 = (bf16[256,512]{1,0:T(8,128)(2,1)S(1)}, bf16[256,512]{1,0:T(8,128)(2,1)S(1)}, bf16[256,512]{1,0:T(8,128)(2,1)S(1)}, f32[4,128,128]{2,1,0:T(8,128)S(1)}) custom-call(s32[1]{0:T(128)} %bitcast.me_ref, f32[1,1024]{1,0:T(1,128)S(1)} %copy-done.4, bf16[1024,1536]{1,0:T(8,128)(2,1)S(1)} %bitcast.21, f32[1024,8]{1,0:T(8,128)S(1)} %get-tuple-element.44.fade_ref, ...), custom_call_target="tpu_custom_call" | custom-call | flops 1610612736 | tf_op jit(solution)/shard_map/qkv/pallas_call | solution.py:140
  17.6 2.5 %qkv.4 = (bf16[256,512]{1,0:T(8,128)(2,1)S(1)}, bf16[256,512]{1,0:T(8,128)(2,1)S(1)}, bf16[256,512]{1,0:T(8,128)(2,1)S(1)}, f32[4,128,128]{2,1,0:T(8,128)S(1)}) custom-call(s32[1]{0:T(128)} %bitcast.me_ref, f32[1,1024]{1,0:T(1,128)S(1)} %copy-done.4, bf16[1024,1536]{1,0:T(8,128)(2,1)S(1)} %bitcast.22, f32[1024,8]{1,0:T(8,128)S(1)} %get-tuple-element.44.fade_ref, ...), custom_call_target="tpu_custom_call" | custom-call | flops 1610612736 | tf_op jit(solution)/shard_map/qkv/pallas_call | solution.py:140
  20.1 1.4 %attention.5.local_ref = bf16[256,512]{1,0:T(8,128)(2,1)S(1)} custom-call(s32[2,2]{1,0:T(2,128)S(1)} %copy-done.5, f32[1,4]{1,0:T(1,128)S(1)} %copy-done.6, bf16[256,512]{1,0:T(8,128)(2,1)S(1)} %get-tuple-element.51.q_ref, bf16[256,512]{1,0:T(8,128)(2,1)S(1)} %get-tuple-element.49.refs_0_, bf16[256,512]{1,0:T(8,128)(2,1)S(1)} %get-tuple-element.52.refs_1_, ...), custom_call_target="tpu_custom_call" | custom-call | flops 536870912 | tf_op jit(solution)/shard_map/attention/pallas_call | solution.py:232
  21.5 1.1 %attention.4.local_ref = bf16[256,512]{1,0:T(8,128)(2,1)S(1)} custom-call(s32[2,2]{1,0:T(2,128)S(1)} %copy-done.5, f32[1,4]{1,0:T(1,128)S(1)} %copy-done.6, bf16[256,512]{1,0:T(8,128)(2,1)S(1)} %get-tuple-element.48.q_ref, bf16[256,512]{1,0:T(8,128)(2,1)S(1)} %get-tuple-element.49.refs_0_, bf16[256,512]{1,0:T(8,128)(2,1)S(1)} %get-tuple-element.50.refs_1_.refs_2_.refs_3_.refs_4_), custom_call_target="tpu_custom_call" | custom-call | flops 268435456 | tf_op jit(solution)/shard_map/attention/pallas_call | solution.py:232
  22.8 2.3 %qkv.5 = (bf16[256,512]{1,0:T(8,128)(2,1)S(1)}, bf16[256,512]{1,0:T(8,128)(2,1)S(1)}, bf16[256,512]{1,0:T(8,128)(2,1)S(1)}, f32[4,128,128]{2,1,0:T(8,128)S(1)}) custom-call(s32[1]{0:T(128)} %bitcast.me_ref, f32[1,1024]{1,0:T(1,128)S(1)} %copy-done.4, bf16[1024,1536]{1,0:T(8,128)(2,1)S(1)} %bitcast.23, f32[1024,8]{1,0:T(8,128)S(1)} %get-tuple-element.44.fade_ref, ...), custom_call_target="tpu_custom_call" | custom-call | flops 1610612736 | tf_op jit(solution)/shard_map/qkv/pallas_call | solution.py:140
  25.1 1.7 %attention.6.local_ref = bf16[256,512]{1,0:T(8,128)(2,1)S(1)} custom-call(s32[2,2]{1,0:T(2,128)S(1)} %copy-done.5, f32[1,4]{1,0:T(1,128)S(1)} %copy-done.6, bf16[256,512]{1,0:T(8,128)(2,1)S(1)} %get-tuple-element.54.q_ref, bf16[256,512]{1,0:T(8,128)(2,1)S(1)} %get-tuple-element.49.refs_0_, bf16[256,512]{1,0:T(8,128)(2,1)S(1)} %get-tuple-element.52.refs_1_, ...), custom_call_target="tpu_custom_call" | custom-call | flops 805306368 | tf_op jit(solution)/shard_map/attention/pallas_call | solution.py:232
  26.8 0.7 collective-permute-done.refs_1_
  27.5 1.1 %last_keys_values.1 = (bf16[256,512]{1,0:T(8,128)(2,1)S(1)}, bf16[256,512]{1,0:T(8,128)(2,1)S(1)}, bf16[528,128]{1,0:T(8,128)(2,1)S(1)}) custom-call(s32[1]{0:T(128)} %bitcast.me_ref, f32[1,1024]{1,0:T(1,128)S(1)} %copy-done.4, bf16[1024,1536]{1,0:T(8,128)(2,1)S(1)} %bitcast.24, f32[1024,8]{1,0:T(8,128)S(1)} %get-tuple-element.44.fade_ref, ...), custom_call_target="tpu_custom_call" | custom-call | flops 1207959552 | tf_op jit(solution)/shard_map/last_keys_values/pallas_call | solution.py:171
  28.6 1.8 %collective-permute-start.4 = (bf16[528,128]{1,0:T(8,128)(2,1)S(1)}, bf16[528,128]{1,0:T(8,128)(2,1)S(1)}, u32[]{:S(2)}, u32[]{:S(2)}) collective-permute-start(bf16[528,128]{1,0:T(8,128)(2,1)S(1)} %get-tuple-element.63.refs_0_), channel_id=1, source_target_pairs={{0,4},{4,0},{8,12},{12,8},{16,20},{20,16},{24,28},{28,24},{1,5},{5... | collective-permute-start | bytes 405512 | tf_op jit(solution)/shard_map/ppermute | solution.py:454
  30.4 1.6 %collective-permute-start.5 = (bf16[528,128]{1,0:T(8,128)(2,1)S(1)}, bf16[528,128]{1,0:T(8,128)(2,1)S(1)}, u32[]{:S(2)}, u32[]{:S(2)}) collective-permute-start(bf16[528,128]{1,0:T(8,128)(2,1)S(1)} %get-tuple-element.63.refs_0_), channel_id=1, source_target_pairs={{0,8},{4,12},{8,0},{12,4},{16,24},{20,28},{24,16},{28,20},{1,9},{5... | collective-permute-start | bytes 405512 | tf_op jit(solution)/shard_map/ppermute | solution.py:454
  31.9 0.2 collective-permute-start.6
  32.1 0.9 %last_queries.1.q_ref = bf16[256,512]{1,0:T(8,128)(2,1)S(1)} custom-call(s32[1]{0:T(128)} %bitcast.me_ref, f32[1,1024]{1,0:T(1,128)S(1)} %copy-done.4, bf16[1024,1536]{1,0:T(8,128)(2,1)S(1)} %bitcast.25, bf16[256,512]{1,0:T(8,128)(2,1)S(1)} %get-tuple-element.83.refs_0_, bf16[256,512]{1,0:T(8,128)(2,1)S(1)} %collective-permute-done.refs_1_), custom_call_target="tpu_custom_call" | custom-call | flops 805306368 | tf_op jit(solution)/shard_map/last_queries/pallas_call | solution.py:194
  33.1 1.9 %attention.7.local_ref = bf16[256,512]{1,0:T(8,128)(2,1)S(1)} custom-call(s32[2,2]{1,0:T(2,128)S(1)} %copy-done.5, f32[1,4]{1,0:T(1,128)S(1)} %copy-done.6, bf16[256,512]{1,0:T(8,128)(2,1)S(1)} %last_queries.1.q_ref, bf16[256,512]{1,0:T(8,128)(2,1)S(1)} %get-tuple-element.49.refs_0_, bf16[256,512]{1,0:T(8,128)(2,1)S(1)} %get-tuple-element.52.refs_1_, ...), custom_call_target="tpu_custom_call" | custom-call | flops 1073741824 | tf_op jit(solution)/shard_map/attention/pallas_call | solution.py:232
  35.0 1.9 %collective-permute-done.5.refs_2_ = bf16[528,128]{1,0:T(8,128)(2,1)S(1)} collective-permute-done((bf16[528,128]{1,0:T(8,128)(2,1)S(1)}, bf16[528,128]{1,0:T(8,128)(2,1)S(1)}, u32[]{:S(2)}, u32[]{:S(2)}) %collective-permute-start.5) | collective-permute-done | bytes 135200 | tf_op jit(solution)/shard_map/ppermute | solution.py:454
  36.9 1.3 %collective-permute-done.6.refs_3_ = bf16[528,128]{1,0:T(8,128)(2,1)S(1)} collective-permute-done((bf16[528,128]{1,0:T(8,128)(2,1)S(1)}, bf16[528,128]{1,0:T(8,128)(2,1)S(1)}, u32[]{:S(2)}, u32[]{:S(2)}) %collective-permute-start.6) | collective-permute-done | bytes 135200 | tf_op jit(solution)/shard_map/ppermute | solution.py:454
  38.2 0.3 quad.1
  38.5 2.8 %collective-permute-start.7 = (bf16[528,128]{1,0:T(8,128)(2,1)S(1)}, bf16[528,128]{1,0:T(8,128)(2,1)S(1)}, u32[]{:S(2)}, u32[]{:S(2)}) collective-permute-start(bf16[528,128]{1,0:T(8,128)(2,1)S(1)} %get-tuple-element.69.refs_0_), channel_id=1, source_target_pairs={{0,16},{4,20},{8,24},{12,28},{16,0},{20,4},{24,8},{28,12},{1,17},{... | collective-permute-start | bytes 405512 | tf_op jit(solution)/shard_map/ppermute | solution.py:461
  41.3 5.7 %collective-permute-done.7.refs_1_ = bf16[528,128]{1,0:T(8,128)(2,1)S(1)} collective-permute-done((bf16[528,128]{1,0:T(8,128)(2,1)S(1)}, bf16[528,128]{1,0:T(8,128)(2,1)S(1)}, u32[]{:S(2)}, u32[]{:S(2)}) %collective-permute-start.7) | collective-permute-done | bytes 135200 | tf_op jit(solution)/shard_map/ppermute | solution.py:461
  47.1 0.2 recall.7.own_ref
  47.5 0.2 recall.6.own_ref
  47.7 0.6 collective-permute-start.13
  48.3 0.4 recall.5.own_ref
  48.7 0.2 recall.4.own_ref
  49.0 0.6 collective-permute-start.8
  49.6 0.7 project.7
  50.3 1.6 %collective-permute-start.16 = (bf16[256,512]{1,0:T(8,128)(2,1)S(1)}, bf16[256,512]{1,0:T(8,128)(2,1)S(1)}, u32[]{:S(2)}, u32[]{:S(2)}) collective-permute-start(bf16[256,512]{1,0:T(8,128)(2,1)S(1)} %get-tuple-element.80), channel_id=1, source_target_pairs={{0,1},{1,0},{2,3},{3,2},{4,5},{5,4},{6,7},{7,6},{8,9},{9,8},{10,11... | collective-permute-start | bytes 786440 | tf_op jit(solution)/shard_map/ppermute | solution.py:474
  51.9 0.7 project.6
  52.6 0.5 collective-permute-start.14
  53.2 0.7 project.5
  53.9 1.6 %collective-permute-start.12 = (bf16[256,512]{1,0:T(8,128)(2,1)S(1)}, bf16[256,512]{1,0:T(8,128)(2,1)S(1)}, u32[]{:S(2)}, u32[]{:S(2)}) collective-permute-start(bf16[256,512]{1,0:T(8,128)(2,1)S(1)} %get-tuple-element.74), channel_id=1, source_target_pairs={{0,1},{1,0},{2,3},{3,2},{4,5},{5,4},{6,7},{7,6},{8,9},{9,8},{10,11... | collective-permute-start | bytes 786440 | tf_op jit(solution)/shard_map/ppermute | solution.py:474
  55.5 0.7 project.4
  56.2 0.5 collective-permute-start.10
  56.7 2.8 %collective-permute-done.16.refs_1_ = bf16[256,512]{1,0:T(8,128)(2,1)S(1)} collective-permute-done((bf16[256,512]{1,0:T(8,128)(2,1)S(1)}, bf16[256,512]{1,0:T(8,128)(2,1)S(1)}, u32[]{:S(2)}, u32[]{:S(2)}) %collective-permute-start.16) | collective-permute-done | bytes 262176 | tf_op jit(solution)/shard_map/ppermute | solution.py:474
  59.5 0.8 %finish.4.refs_2_ = bf16[1024,512]{1,0:T(8,128)(2,1)} custom-call(bf16[256,512]{1,0:T(8,128)(2,1)S(1)} %get-tuple-element.79.refs_0_, bf16[256,512]{1,0:T(8,128)(2,1)S(1)} %collective-permute-done.16.refs_1_), custom_call_target="tpu_custom_call" | custom-call | flops 262144 | bytes 786432 | tf_op jit(solution)/shard_map/finish/pallas_call | solution.py:378
  60.3 4.9 %collective-permute-done.14.refs_1_ = bf16[256,512]{1,0:T(8,128)(2,1)S(1)} collective-permute-done((bf16[256,512]{1,0:T(8,128)(2,1)S(1)}, bf16[256,512]{1,0:T(8,128)(2,1)S(1)}, u32[]{:S(2)}, u32[]{:S(2)}) %collective-permute-start.14) | collective-permute-done | bytes 262176 | tf_op jit(solution)/shard_map/ppermute | solution.py:474
  65.1 0.8 %finish.5.refs_2_ = bf16[1024,512]{1,0:T(8,128)(2,1)} custom-call(bf16[256,512]{1,0:T(8,128)(2,1)S(1)} %get-tuple-element.76.refs_0_, bf16[256,512]{1,0:T(8,128)(2,1)S(1)} %collective-permute-done.14.refs_1_, bf16[1024,512]{1,0:T(8,128)(2,1)} %finish.4.refs_2_), custom_call_target="tpu_custom_call", output_to_operand_aliasing={{}: (2, {})} | custom-call | flops 262144 | bytes 786432 | tf_op jit(solution)/shard_map/finish/pallas_call | solution.py:378
  65.9 4.9 %collective-permute-done.12.refs_1_ = bf16[256,512]{1,0:T(8,128)(2,1)S(1)} collective-permute-done((bf16[256,512]{1,0:T(8,128)(2,1)S(1)}, bf16[256,512]{1,0:T(8,128)(2,1)S(1)}, u32[]{:S(2)}, u32[]{:S(2)}) %collective-permute-start.12) | collective-permute-done | bytes 262176 | tf_op jit(solution)/shard_map/ppermute | solution.py:474
  70.7 0.8 %finish.6.refs_2_ = bf16[1024,512]{1,0:T(8,128)(2,1)} custom-call(bf16[256,512]{1,0:T(8,128)(2,1)S(1)} %get-tuple-element.73.refs_0_, bf16[256,512]{1,0:T(8,128)(2,1)S(1)} %collective-permute-done.12.refs_1_, bf16[1024,512]{1,0:T(8,128)(2,1)} %finish.5.refs_2_), custom_call_target="tpu_custom_call", output_to_operand_aliasing={{}: (2, {})} | custom-call | flops 262144 | bytes 786432 | tf_op jit(solution)/shard_map/finish/pallas_call | solution.py:378
  71.5 3.9 %collective-permute-done.10.refs_1_ = bf16[256,512]{1,0:T(8,128)(2,1)S(1)} collective-permute-done((bf16[256,512]{1,0:T(8,128)(2,1)S(1)}, bf16[256,512]{1,0:T(8,128)(2,1)S(1)}, u32[]{:S(2)}, u32[]{:S(2)}) %collective-permute-start.10) | collective-permute-done | bytes 262176 | tf_op jit(solution)/shard_map/ppermute | solution.py:474
  75.4 0.8 %finish.7 = bf16[1024,512]{1,0:T(8,128)(2,1)} custom-call(bf16[256,512]{1,0:T(8,128)(2,1)S(1)} %get-tuple-element.70.refs_0_, bf16[256,512]{1,0:T(8,128)(2,1)S(1)} %collective-permute-done.10.refs_1_, bf16[1024,512]{1,0:T(8,128)(2,1)} %finish.6.refs_2_), custom_call_target="tpu_custom_call", output_to_operand_aliasing={{}: (2, {})} | custom-call | flops 262144 | bytes 786432 | tf_op jit(solution)/shard_map/finish/pallas_call | solution.py:378
  (28 shorter events, 0.6 us)
Async XLA Ops:
  1.3 12.0 %collective-permute-start.1 = (bf16[256,512]{1,0:T(8,128)(2,1)S(1)}, bf16[256,512]{1,0:T(8,128)(2,1)}, u32[]{:S(2)}, u32[]{:S(2)}) collective-permute-start(bf16[256,512]{1,0:T(8,128)(2,1)S(1)} %get-tuple-element.82.refs_0_), channel_id=1, source_target_pairs={{1,0},{0,1},{3,2},{2,3},{5,4},{4,5},{7,6},{6,7},{9,8},{8,9},{11,10... | collective-permute-start | bytes 786440 | tf_op jit(solution)/shard_map/ppermute | solution.py:419
  4.3 13.2 %collective-permute-start.2 = (bf16[256,512]{1,0:T(8,128)(2,1)S(1)}, bf16[256,512]{1,0:T(8,128)(2,1)}, u32[]{:S(2)}, u32[]{:S(2)}) collective-permute-start(bf16[256,512]{1,0:T(8,128)(2,1)S(1)} %get-tuple-element.84.refs_1_), channel_id=1, source_target_pairs={{1,0},{0,1},{3,2},{2,3},{5,4},{4,5},{7,6},{6,7},{9,8},{8,9},{11,10... | collective-permute-start | bytes 786440 | tf_op jit(solution)/shard_map/ppermute | solution.py:419
  4.4 18.4 %collective-permute-start.3 = (bf16[256,512]{1,0:T(8,128)(2,1)S(1)}, bf16[256,512]{1,0:T(8,128)(2,1)}, u32[]{:S(2)}, u32[]{:S(2)}) collective-permute-start(bf16[256,512]{1,0:T(8,128)(2,1)S(1)} %get-tuple-element.81.refs_1_), channel_id=1, source_target_pairs={{1,0},{0,1},{3,2},{2,3},{5,4},{4,5},{7,6},{6,7},{9,8},{8,9},{11,10... | collective-permute-start | bytes 786440 | tf_op jit(solution)/shard_map/ppermute | solution.py:419
  6.3 21.1 %collective-permute-start = (bf16[256,512]{1,0:T(8,128)(2,1)S(1)}, bf16[256,512]{1,0:T(8,128)(2,1)S(1)}, u32[]{:S(2)}, u32[]{:S(2)}) collective-permute-start(bf16[256,512]{1,0:T(8,128)(2,1)S(1)} %get-tuple-element.83.refs_0_), channel_id=1, source_target_pairs={{1,0},{0,1},{3,2},{2,3},{5,4},{4,5},{7,6},{6,7},{9,8},{8,9},{11,10... | collective-permute-start | bytes 786440 | tf_op jit(solution)/shard_map/ppermute | solution.py:419
  6.4 43.1 %collective-permute-start.9 = (bf16[512,1024]{1,0:T(8,128)(2,1)}, bf16[512,1024]{1,0:T(8,128)(2,1)S(1)}, u32[]{:S(2)}, u32[]{:S(2)}) collective-permute-start(bf16[512,1024]{1,0:T(8,128)(2,1)} %bitcast.28), channel_id=1, source_target_pairs={{0,2},{2,0},{1,3},{3,1},{4,6},{6,4},{5,7},{7,5},{8,10},{10,8},{9,1... | collective-permute-start | bytes 3145736 | tf_op jit(solution)/shard_map/ppermute | solution.py:423
  6.4 0.7 copy-start.3
  7.1 0.7 copy-start.7
  9.2 4.1 %copy-start.4 = (f32[1,1024]{1,0:T(1,128)S(1)}, f32[1,1024]{1,0:T(1,128)}, u32[]{:S(2)}) copy-start(f32[1,1024]{1,0:T(1,128)} %gain_ref.9) | copy-start | bytes 12292
  13.3 1.9 %copy-start.1 = (bf16[128,8,4,384]{3,1,2,0:T(8,128)(2,1)S(1)}, bf16[128,8,4,384]{3,1,2,0:T(8,128)(2,1)}, u32[]{:S(2)}) copy-start(bf16[128,8,4,384]{3,1,2,0:T(8,128)(2,1)} %copy.13) | copy-start | bytes 9437188
  17.5 2.5 %copy-start.5 = (s32[2,2]{1,0:T(2,128)S(1)}, s32[2,2]{1,0:T(2,128)}, u32[]{:S(2)}) copy-start(s32[2,2]{1,0:T(2,128)} %keep_ref.7) | copy-start | bytes 52
  17.5 2.5 %copy-start.6 = (f32[1,4]{1,0:T(1,128)S(1)}, f32[1,4]{1,0:T(1,128)}, u32[]{:S(2)}) copy-start(f32[1,4]{1,0:T(1,128)} %scale_ref.7) | copy-start | bytes 52
  17.6 5.2 %copy-start.2 = (bf16[128,8,4,384]{3,1,2,0:T(8,128)(2,1)S(1)}, bf16[128,8,4,384]{3,1,2,0:T(8,128)(2,1)}, u32[]{:S(2)}) copy-start(bf16[128,8,4,384]{3,1,2,0:T(8,128)(2,1)} %copy.13) | copy-start | bytes 9437188
  28.6 6.4 %collective-permute-start.4 = (bf16[528,128]{1,0:T(8,128)(2,1)S(1)}, bf16[528,128]{1,0:T(8,128)(2,1)S(1)}, u32[]{:S(2)}, u32[]{:S(2)}) collective-permute-start(bf16[528,128]{1,0:T(8,128)(2,1)S(1)} %get-tuple-element.63.refs_0_), channel_id=1, source_target_pairs={{0,4},{4,0},{8,12},{12,8},{16,20},{20,16},{24,28},{28,24},{1,5},{5... | collective-permute-start | bytes 405512 | tf_op jit(solution)/shard_map/ppermute | solution.py:454
  30.4 6.5 %collective-permute-start.5 = (bf16[528,128]{1,0:T(8,128)(2,1)S(1)}, bf16[528,128]{1,0:T(8,128)(2,1)S(1)}, u32[]{:S(2)}, u32[]{:S(2)}) collective-permute-start(bf16[528,128]{1,0:T(8,128)(2,1)S(1)} %get-tuple-element.63.refs_0_), channel_id=1, source_target_pairs={{0,8},{4,12},{8,0},{12,4},{16,24},{20,28},{24,16},{28,20},{1,9},{5... | collective-permute-start | bytes 405512 | tf_op jit(solution)/shard_map/ppermute | solution.py:454
  31.9 6.2 %collective-permute-start.6 = (bf16[528,128]{1,0:T(8,128)(2,1)S(1)}, bf16[528,128]{1,0:T(8,128)(2,1)S(1)}, u32[]{:S(2)}, u32[]{:S(2)}) collective-permute-start(bf16[528,128]{1,0:T(8,128)(2,1)S(1)} %get-tuple-element.63.refs_0_), channel_id=1, source_target_pairs={{0,12},{4,8},{8,4},{12,0},{16,28},{20,24},{24,20},{28,16},{1,13},{... | collective-permute-start | bytes 405512 | tf_op jit(solution)/shard_map/ppermute | solution.py:454
  38.5 8.6 %collective-permute-start.7 = (bf16[528,128]{1,0:T(8,128)(2,1)S(1)}, bf16[528,128]{1,0:T(8,128)(2,1)S(1)}, u32[]{:S(2)}, u32[]{:S(2)}) collective-permute-start(bf16[528,128]{1,0:T(8,128)(2,1)S(1)} %get-tuple-element.69.refs_0_), channel_id=1, source_target_pairs={{0,16},{4,20},{8,24},{12,28},{16,0},{20,4},{24,8},{28,12},{1,17},{... | collective-permute-start | bytes 405512 | tf_op jit(solution)/shard_map/ppermute | solution.py:461
  47.1 2.5 %copy-start = (bf16[1,4,128,1024]{3,2,1,0:T(8,128)(2,1)S(1)}, bf16[1,4,128,1024]{3,2,1,0:T(8,128)(2,1)}, u32[]{:S(2)}) copy-start(bf16[1,4,128,1024]{3,2,1,0:T(8,128)(2,1)} %param.16) | copy-start | bytes 3145732
  47.4 2.2 %collective-permute-start.15 = (bf16[256,512]{1,0:T(8,128)(2,1)S(1)}, bf16[256,512]{1,0:T(8,128)(2,1)S(1)}, u32[]{:S(2)}, u32[]{:S(2)}) collective-permute-start(bf16[256,512]{1,0:T(8,128)(2,1)S(1)} %recall.7.own_ref), channel_id=1, source_target_pairs={{0,2},{2,0},{1,3},{3,1},{4,6},{6,4},{5,7},{7,5},{8,10},{10,8},{9,1... | collective-permute-start | bytes 786440 | tf_op jit(solution)/shard_map/ppermute | solution.py:469
  47.7 4.2 %collective-permute-start.13 = (bf16[256,512]{1,0:T(8,128)(2,1)S(1)}, bf16[256,512]{1,0:T(8,128)(2,1)S(1)}, u32[]{:S(2)}, u32[]{:S(2)}) collective-permute-start(bf16[256,512]{1,0:T(8,128)(2,1)S(1)} %recall.6.own_ref), channel_id=1, source_target_pairs={{0,2},{2,0},{1,3},{3,1},{4,6},{6,4},{5,7},{7,5},{8,10},{10,8},{9,1... | collective-permute-start | bytes 786440 | tf_op jit(solution)/shard_map/ppermute | solution.py:469
  48.7 4.5 %collective-permute-start.11 = (bf16[256,512]{1,0:T(8,128)(2,1)S(1)}, bf16[256,512]{1,0:T(8,128)(2,1)S(1)}, u32[]{:S(2)}, u32[]{:S(2)}) collective-permute-start(bf16[256,512]{1,0:T(8,128)(2,1)S(1)} %recall.5.own_ref), channel_id=1, source_target_pairs={{0,2},{2,0},{1,3},{3,1},{4,6},{6,4},{5,7},{7,5},{8,10},{10,8},{9,1... | collective-permute-start | bytes 786440 | tf_op jit(solution)/shard_map/ppermute | solution.py:469
  49.0 6.5 %collective-permute-start.8 = (bf16[256,512]{1,0:T(8,128)(2,1)S(1)}, bf16[256,512]{1,0:T(8,128)(2,1)S(1)}, u32[]{:S(2)}, u32[]{:S(2)}) collective-permute-start(bf16[256,512]{1,0:T(8,128)(2,1)S(1)} %recall.4.own_ref), channel_id=1, source_target_pairs={{0,2},{2,0},{1,3},{3,1},{4,6},{6,4},{5,7},{7,5},{8,10},{10,8},{9,1... | collective-permute-start | bytes 786440 | tf_op jit(solution)/shard_map/ppermute | solution.py:469
  50.3 9.2 %collective-permute-start.16 = (bf16[256,512]{1,0:T(8,128)(2,1)S(1)}, bf16[256,512]{1,0:T(8,128)(2,1)S(1)}, u32[]{:S(2)}, u32[]{:S(2)}) collective-permute-start(bf16[256,512]{1,0:T(8,128)(2,1)S(1)} %get-tuple-element.80), channel_id=1, source_target_pairs={{0,1},{1,0},{2,3},{3,2},{4,5},{5,4},{6,7},{7,6},{8,9},{9,8},{10,11... | collective-permute-start | bytes 786440 | tf_op jit(solution)/shard_map/ppermute | solution.py:474
  52.6 12.5 %collective-permute-start.14 = (bf16[256,512]{1,0:T(8,128)(2,1)S(1)}, bf16[256,512]{1,0:T(8,128)(2,1)S(1)}, u32[]{:S(2)}, u32[]{:S(2)}) collective-permute-start(bf16[256,512]{1,0:T(8,128)(2,1)S(1)} %get-tuple-element.77), channel_id=1, source_target_pairs={{0,1},{1,0},{2,3},{3,2},{4,5},{5,4},{6,7},{7,6},{8,9},{9,8},{10,11... | collective-permute-start | bytes 786440 | tf_op jit(solution)/shard_map/ppermute | solution.py:474
  53.9 16.9 %collective-permute-start.12 = (bf16[256,512]{1,0:T(8,128)(2,1)S(1)}, bf16[256,512]{1,0:T(8,128)(2,1)S(1)}, u32[]{:S(2)}, u32[]{:S(2)}) collective-permute-start(bf16[256,512]{1,0:T(8,128)(2,1)S(1)} %get-tuple-element.74), channel_id=1, source_target_pairs={{0,1},{1,0},{2,3},{3,2},{4,5},{5,4},{6,7},{7,6},{8,9},{9,8},{10,11... | collective-permute-start | bytes 786440 | tf_op jit(solution)/shard_map/ppermute | solution.py:474
  56.2 19.2 %collective-permute-start.10 = (bf16[256,512]{1,0:T(8,128)(2,1)S(1)}, bf16[256,512]{1,0:T(8,128)(2,1)S(1)}, u32[]{:S(2)}, u32[]{:S(2)}) collective-permute-start(bf16[256,512]{1,0:T(8,128)(2,1)S(1)} %get-tuple-element.71), channel_id=1, source_target_pairs={{0,1},{1,0},{2,3},{3,2},{4,5},{5,4},{6,7},{7,6},{8,9},{9,8},{10,11... | collective-permute-start | bytes 786440 | tf_op jit(solution)/shard_map/ppermute | solution.py:474

commit v5 on v4

--- a/solution.py
+++ b/solution.py
@@ -67,8 +67,11 @@
     reading_ref[...] = jnp.transpose(jnp.exp(running) * factor)
     decay = jnp.exp(last)
     high = decay.astype(BF16).astype(F32)
-    both = jnp.concatenate([high, decay - high], axis=0)
-    tail_ref[...] = jnp.broadcast_to(both, tail_ref.shape).astype(BF16)
+    low = decay - high
+    size = (TAIL // 2, tail_ref.shape[2])
+    for h in range(heads):
+        parts = [jnp.broadcast_to(part[h : h + 1, :], size) for part in (high, low)]
+        tail_ref[h] = jnp.concatenate(parts, axis=0).astype(BF16)
 
 
 def prepare(logs, flags, dim, factor):
@@ -78,7 +81,7 @@
         functools.partial(prepare_kernel, heads, factor),
         in_specs=[VMEM, SMEM],
         out_specs=[VMEM] * 3,
-        out_shape=[struct((length, lines), F32)] * 2 + [struct((TAIL, dim))],
+        out_shape=[struct((length, lines), F32)] * 2 + [struct((heads, TAIL, dim))],
         scratch_shapes=[pltpu.VMEM((lines, length), F32)],
         compiler_params=params(),
         cost_estimate=cost(40 * lines * length, 0),
@@ -162,17 +165,21 @@
         k_ref[:, cols] = key
         v_ref[:, cols] = value
         add_summary(sum_ref, h, key, value, fade_ref, first)
-        send_ref[cols, :] = sum_ref[h].astype(BF16)
-    send_ref[heads * dim :, :] = tail_ref[...]
-
-
-def last_keys_values(me, gain, w, fade, prev, tail, xs, heads, dim, first):
+    blocks, part = send_ref.shape[0], send_ref.shape[1] - TAIL
+    for j in range(blocks):
+        h, row = divmod(j * part, dim)
+        send_ref[j, :part, :] = sum_ref[h, row : row + part, :].astype(BF16)
+        send_ref[j, part:, :] = tail_ref[h]
+
+
+def last_keys_values(me, gain, w, fade, prev, tail, xs, heads, dim, first, blocks):
     rows = xs[0].shape[0]
     return pl.pallas_call(
         functools.partial(last_kernel, heads, dim, first),
         in_specs=[SMEM] + [VMEM] * (5 + len(xs)),
         out_specs=[VMEM] * 3,
-        out_shape=[struct((rows, heads * dim))] * 2 + [struct((heads * dim + TAIL, dim))],
+        out_shape=[struct((rows, heads * dim))] * 2
+        + [struct((blocks, heads * dim // blocks + TAIL, dim))],
         scratch_shapes=[pltpu.VMEM((heads, dim, dim), F32)],
         compiler_params=params(),
         cost_estimate=cost(3 * rows * w.size, 0),
@@ -242,82 +249,28 @@
     )(keep, scale, q, *ks, *vs)
 
 
-def body_and_decay(ref, h, dim):
-    size = ref.shape[0] - TAIL
-    high = ref[size + h : size + h + 1, :].astype(F32)
-    low = ref[size + TAIL // 2 + h : size + TAIL // 2 + h + 1, :].astype(F32)
-    return ref[h * dim : (h + 1) * dim, :].astype(F32), high + low
-
-
-def scanned(place, refs, h, dim):
-    count = len(refs)
-    loaded = [body_and_decay(ref, h, dim) for ref in refs]
-    state, since = jnp.zeros((dim, refs[0].shape[1]), F32), jnp.ones((1, refs[0].shape[1]), F32)
-    before, before_decay = state, since
-    for j in range(count):
-        before = jnp.where(place == j, state, before)
-        before_decay = jnp.where(place == j, since, before_decay)
-        body, decay = loaded[0]
-        for k in range(1, count):
-            here = place == (j ^ k)
-            body = jnp.where(here, loaded[k][0], body)
-            decay = jnp.where(here, loaded[k][1], decay)
-        state = decay * state + body
-        since = since * decay
-    return before, before_decay, state, since
-
-
-def quad_kernel(heads, dim, place_ref, *refs):
-    refs, (before_ref, decay_ref, total_ref) = refs[:-3], refs[-3:]
-    size = heads * dim
-    total_ref[size:, :] = jnp.zeros((TAIL, total_ref.shape[1]), BF16)
-    for h in range(heads):
-        rows = slice(h * dim, (h + 1) * dim)
-        before, before_decay, state, since = scanned(place_ref[0], refs, h, dim)
-        before_ref[rows, :] = before
-        decay_ref[h : h + 1, :] = before_decay
-        total_ref[rows, :] = state.astype(BF16)
-        high = since.astype(BF16)
-        total_ref[size + h : size + h + 1, :] = high
-        low = (since - high.astype(F32)).astype(BF16)
-        total_ref[size + TAIL // 2 + h : size + TAIL // 2 + h + 1, :] = low
-
-
-def quad(place, loads, heads, dim):
-    shape = loads[0].shape
-    return pl.pallas_call(
-        functools.partial(quad_kernel, heads, dim),
-        in_specs=[SMEM] + [VMEM] * len(loads),
-        out_specs=[VMEM] * 3,
-        out_shape=[
-            struct((heads * dim, shape[1]), F32),
-            struct((TAIL // 2, shape[1]), F32),
-            struct(shape),
-        ],
-        compiler_params=params(),
-        cost_estimate=cost(loads[0].size * 40, 0),
-        name="quad",
-    )(place, *loads)
-
-
-def entering_kernel(heads, dim, place_ref, before_ref, decay_ref, *refs):
-    refs, out_ref = refs[:-1], refs[-1]
-    for h in range(heads):
-        rows = slice(h * dim, (h + 1) * dim)
-        earlier = scanned(place_ref[0], refs, h, dim)[0]
-        out_ref[rows, :] = (before_ref[rows, :] + decay_ref[h : h + 1, :] * earlier).astype(BF16)
-
-
-def entering(place, before, decay, totals, heads, dim):
-    return pl.pallas_call(
-        functools.partial(entering_kernel, heads, dim),
-        in_specs=[SMEM] + [VMEM] * (2 + len(totals)),
+def scan_kernel(came_ref, out_ref):
+    blocks, part, dim = out_ref.shape
+    state = jnp.zeros((part, dim), F32)
+    for c in range(blocks):
+        out_ref[c] = state.astype(BF16)
+        if c < blocks - 1:
+            half = part + TAIL // 2
+            decay = came_ref[c, part : part + 1, :].astype(F32) + came_ref[c, half : half + 1, :].astype(F32)
+            state = decay * state + came_ref[c, :part, :].astype(F32)
+
+
+def scan(came):
+    blocks, rows, dim = came.shape
+    return pl.pallas_call(
+        scan_kernel,
+        in_specs=[VMEM],
         out_specs=VMEM,
-        out_shape=struct(before.shape),
-        compiler_params=params(),
-        cost_estimate=cost(before.size * 20, 0),
-        name="entering",
-    )(place, before, decay, *totals)
+        out_shape=struct((blocks, rows - TAIL, dim)),
+        compiler_params=params(),
+        cost_estimate=cost(came.size * 10, 0),
+        name="scan",
+    )(came)
 
 
 def recall_kernel(heads, dim, first, reading_ref, q_ref, local_ref, state_ref, out_ref):
@@ -407,7 +360,6 @@
     heads = triple_projector.shape[2]
     dim = emission_projector.shape[2]
     me = lax.axis_index("head").astype(jnp.int32).reshape(1)
-    place = lax.axis_index("tm").astype(jnp.int32).reshape(1)
     swap_streams = [(0, 1), (1, 0)]
     tied = lambda *arrays: lax.optimization_barrier(arrays)
 
@@ -444,27 +396,22 @@
         locals_.append(attention(c, tile_retain_grid, score_scaler, q, ks, vs, heads, dim))
     summary, *locals_ = tied(summary, *locals_)
     k, v, sent = last_keys_values(
-        me, gain, w, fade, summary, tail, received[-1], heads, dim, (chunks - 1) * CHUNK
+        me, gain, w, fade, summary, tail, received[-1], heads, dim, (chunks - 1) * CHUNK, blocks
     )
     ks.append(k)
     vs.append(v)
 
-    quad_size = min(4, blocks)
-    loads = [sent] + [
-        lax.ppermute(sent, "tm", [(d, d ^ k) for d in range(blocks)]) for k in range(1, quad_size)
-    ]
-    qs.append(last_queries(me, gain, w, received[-1], heads, dim))
-    locals_.append(attention(chunks - 1, tile_retain_grid, score_scaler, qs[-1], ks, vs, heads, dim))
-    *loads, locals_[-1] = tied(*loads, locals_[-1])
-    before, decay, total = quad(lax.rem(place, quad_size), loads, heads, dim)
-    totals = [total] + [
-        lax.ppermute(total, "tm", [(d, d ^ (quad_size * k)) for d in range(blocks)])
-        for k in range(1, blocks // quad_size)
-    ]
-    state = entering(lax.div(place, quad_size), before, decay, totals, heads, dim)
-
-    result = None
+    came = lax.all_to_all(sent, "tm", 0, 0)
+    state = lax.all_to_all(scan(came), "tm", 0, 0).reshape(heads * dim, dim)
+
+    result, finished = None, []
     for c in range(chunks):
+        if c == chunks - 1:
+            xs, finished[0] = tied(received[-1], finished[0])
+            qs.append(last_queries(me, gain, w, xs, heads, dim))
+            locals_.append(
+                attention(c, tile_retain_grid, score_scaler, qs[-1], ks, vs, heads, dim)
+            )
         head_out = recall(reading, qs[c], locals_[c], state, heads, dim, c * CHUNK)
         side = lax.ppermute(head_out, "stream", swap_streams)
         outs = project(me, head_out, side, own_w, side_w, shards)
@@ -473,7 +420,9 @@
             parts.append(
                 lax.ppermute(outs[k], "head", [(d, (d + k) % shards) for d in range(shards)])
             )
-        result = finish(parts, result, c, length)
+        finished.append(parts)
+    for c in range(chunks):
+        result = finish(finished[c], result, c, length)
     return result[None]
 
 

time: 76.5 us -> 94.4 us (1.23)
  blocking collectives: 0 us -> 23.1 us
  starting transfers between devices: 17.1 us -> 11.2 us
  waiting for transfers between devices: 26.2 us -> 30.9 us
  local copies, waits for them, and re-layouts: 8.64 us -> 5.09 us
    all_to_all x0 -> x2, blocking collectives: none -> 23.1 us  [the longest x1 13.4 us: per_device(): came = lax.all_to_all(sent, 'tm', 0, 0)]
    ppermute x4, waiting for transfers between devices: 0.86 us -> 11.1 us  [per_device(): lax.ppermute(piece, 'head', [((d + k) % shards, d) for d in range(shards)])]
    ppermute x4 -> x0, waiting for transfers between devices: 8.92 us -> none  [the longest x1 5.74 us: per_device(): lax.ppermute(total, 'tm', [(d, d ^ quad_size * k) for d in range(blocks)])]
    ppermute x4 -> x0, starting transfers between devices: 6.38 us -> none  [the longest x3 3.55 us: per_device(): lax.ppermute(sent, 'tm', [(d, d ^ k) for d in range(blocks)])]
    unnamed x17 -> x13, local copies, waits for them, and re-layouts: 7.37 us -> 3.84 us
    ppermute x4, waiting for transfers between devices: 16.4 us -> 18.2 us  [per_device(): lax.ppermute(outs[k], 'head', [(d, (d + k) % shards) for d in range(shard...]
    ppermute x4, waiting for transfers between devices: 0.01 us -> 1.53 us  [per_device(): side = lax.ppermute(head_out, 'stream', swap_streams)]
    ppermute x4, starting transfers between devices: 4.31 us -> 5.33 us  [per_device(): lax.ppermute(outs[k], 'head', [(d, (d + k) % shards) for d in range(shard...]
  transfers between devices with their start and end apart: 17 -> 13, of which waited for: 9 -> 6; matrix products, arithmetic and copies ran while one was open for 5% -> 3% of each run, Pallas kernels for 31% -> 23%
where the time goes in v5:
time: 94.4 us; the launch traced here: 94.1 us
  waiting for transfers between devices  30.9 us (33%)
  Pallas kernels  23.4 us (25%)
  blocking collectives  23.1 us (24%)
  starting transfers between devices  11.2 us (12%)
  local copies, waits for them, and re-layouts  5.09 us (5%)
    ppermute x4, waiting for transfers between devices, per_device(): lax.ppermute(outs[k], 'head', [(d, (d + k) % shards) for d in range(shard...  18.2 us
    all_to_all x1, blocking collectives, per_device(): came = lax.all_to_all(sent, 'tm', 0, 0)  13.4 us
    ppermute x4, waiting for transfers between devices, per_device(): lax.ppermute(piece, 'head', [((d + k) % shards, d) for d in range(shards)])  11.1 us
    all_to_all x1, blocking collectives, per_device(): state = lax.all_to_all(scan(came), 'tm', 0, 0).reshape(heads * dim, dim)  9.74 us
    pallas_call x3, Pallas kernels, qkv(): pl.pallas_call(functools.partial(qkv_kernel, heads, dim, first), in_specs...  6.95 us
    pallas_call x4, Pallas kernels, attention(): pl.pallas_call(functools.partial(attention_kernel, chunk, heads, dim), in...  6.14 us
    ppermute x4, starting transfers between devices, per_device(): lax.ppermute(outs[k], 'head', [(d, (d + k) % shards) for d in range(shard...  5.33 us
    ppermute x4, starting transfers between devices, per_device(): lax.ppermute(piece, 'head', [((d + k) % shards, d) for d in range(shards)])  5.14 us
  transfers between devices with their start and end apart: 13, of which 6 were waited for; matrix products, arithmetic and copies ran while one was open for 3% of the time, Pallas kernels for 23%

profile of v5, /device:TPU:0, one launch (start us, length us, event | category | flops | bytes accessed | tf_op | source)
XLA Modules:
  0.0 94.1 jit_solution(9264000023236412890)
XLA Ops:
  0.0 1.3 %slice_bitcast_fusion = (bf16[256,512]{1,0:T(8,128)(2,1)S(1)}, bf16[256,512]{1,0:T(8,128)(2,1)S(1)}, bf16[256,512]{1,0:T(8,128)(2,1)S(1)}, bf16[256,512]{1,0:T(8,128)(2,1)S(1)}) fusion(bf16[1,1024,512]{2,1,0:T(8,128)(2,1)} %param.9), kind=kLoop, calls=%fused_computation | loop fusion | bytes 2097152 | tf_op jit(solution)/shard_map/slice | solution.py:368
  1.3 3.0 %collective-permute-start.1 = (bf16[256,512]{1,0:T(8,128)(2,1)S(1)}, bf16[256,512]{1,0:T(8,128)(2,1)}, u32[]{:S(2)}, u32[]{:S(2)}) collective-permute-start(bf16[256,512]{1,0:T(8,128)(2,1)S(1)} %get-tuple-element.74.refs_0_), channel_id=1, source_target_pairs={{1,0},{0,1},{3,2},{2,3},{5,4},{4,5},{7,6},{6,7},{9,8},{8,9},{11,10... | collective-permute-start | bytes 786440 | tf_op jit(solution)/shard_map/ppermute | solution.py:371
  4.3 0.1 collective-permute-start.2
  4.4 1.9 %collective-permute-start = (bf16[256,512]{1,0:T(8,128)(2,1)S(1)}, bf16[256,512]{1,0:T(8,128)(2,1)S(1)}, u32[]{:S(2)}, u32[]{:S(2)}) collective-permute-start(bf16[256,512]{1,0:T(8,128)(2,1)S(1)} %get-tuple-element.59.refs_0_), channel_id=1, source_target_pairs={{1,0},{0,1},{3,2},{2,3},{5,4},{4,5},{7,6},{6,7},{9,8},{8,9},{11,10... | collective-permute-start | bytes 786440 | tf_op jit(solution)/shard_map/ppermute | solution.py:371
  6.3 0.1 collective-permute-start.3
  6.4 0.7 copy-done.1
  7.1 0.7 copy-done.5
  7.8 1.5 %prepare.1 = (f32[1024,8]{1,0:T(8,128)S(1)}, f32[1024,8]{1,0:T(8,128)S(1)}, bf16[4,16,128]{2,1,0:T(8,128)(2,1)S(1)}) custom-call(f32[4,1024]{1,0:T(4,128)S(1)} %bitcast.30, s32[2]{0:T(128)S(1)} %copy-done.5), custom_call_target="tpu_custom_call" | custom-call | flops 327680 | tf_op jit(solution)/shard_map/prepare/pallas_call | solution.py:80
  9.3 0.0 copy-start.2
  9.3 2.4 %copy.13 = bf16[128,8,4,384]{3,1,2,0:T(8,128)(2,1)S(1)} copy(bf16[128,8,4,384]{3,2,1,0:T(4,128)(2,1)} %bitcast.31) | data formatting | bytes 6291456
  11.7 2.3 %qkv.3 = (bf16[256,512]{1,0:T(8,128)(2,1)S(1)}, bf16[256,512]{1,0:T(8,128)(2,1)S(1)}, bf16[256,512]{1,0:T(8,128)(2,1)S(1)}, f32[4,128,128]{2,1,0:T(8,128)S(1)}) custom-call(s32[1]{0:T(128)} %bitcast.me_ref, f32[1,1024]{1,0:T(1,128)S(1)} %copy-done.2, bf16[1024,1536]{1,0:T(8,128)(2,1)S(1)} %bitcast.17, f32[1024,8]{1,0:T(8,128)S(1)} %get-tuple-element.40.fade_ref, ...), custom_call_target="tpu_custom_call" | custom-call | flops 1610612736 | tf_op jit(solution)/shard_map/qkv/pallas_call | solution.py:143
  14.1 3.1 %collective-permute-done.2.refs_2_ = bf16[256,512]{1,0:T(8,128)(2,1)} collective-permute-done((bf16[256,512]{1,0:T(8,128)(2,1)S(1)}, bf16[256,512]{1,0:T(8,128)(2,1)}, u32[]{:S(2)}, u32[]{:S(2)}) %collective-permute-start.2) | collective-permute-done | bytes 262176 | tf_op jit(solution)/shard_map/ppermute | solution.py:371
  17.1 2.3 %qkv.4 = (bf16[256,512]{1,0:T(8,128)(2,1)S(1)}, bf16[256,512]{1,0:T(8,128)(2,1)S(1)}, bf16[256,512]{1,0:T(8,128)(2,1)S(1)}, f32[4,128,128]{2,1,0:T(8,128)S(1)}) custom-call(s32[1]{0:T(128)} %bitcast.me_ref, f32[1,1024]{1,0:T(1,128)S(1)} %copy-done.2, bf16[1024,1536]{1,0:T(8,128)(2,1)S(1)} %bitcast.18, f32[1024,8]{1,0:T(8,128)S(1)} %get-tuple-element.40.fade_ref, ...), custom_call_target="tpu_custom_call" | custom-call | flops 1610612736 | tf_op jit(solution)/shard_map/qkv/pallas_call | solution.py:143
  19.5 0.0 copy-start.3
  19.5 8.1 %collective-permute-done.3.refs_2_ = bf16[256,512]{1,0:T(8,128)(2,1)} collective-permute-done((bf16[256,512]{1,0:T(8,128)(2,1)S(1)}, bf16[256,512]{1,0:T(8,128)(2,1)}, u32[]{:S(2)}, u32[]{:S(2)}) %collective-permute-start.3) | collective-permute-done | bytes 262176 | tf_op jit(solution)/shard_map/ppermute | solution.py:371
  27.6 2.3 %qkv.5 = (bf16[256,512]{1,0:T(8,128)(2,1)S(1)}, bf16[256,512]{1,0:T(8,128)(2,1)S(1)}, bf16[256,512]{1,0:T(8,128)(2,1)S(1)}, f32[4,128,128]{2,1,0:T(8,128)S(1)}) custom-call(s32[1]{0:T(128)} %bitcast.me_ref, f32[1,1024]{1,0:T(1,128)S(1)} %copy-done.2, bf16[1024,1536]{1,0:T(8,128)(2,1)S(1)} %bitcast.19, f32[1024,8]{1,0:T(8,128)S(1)} %get-tuple-element.40.fade_ref, ...), custom_call_target="tpu_custom_call" | custom-call | flops 1610612736 | tf_op jit(solution)/shard_map/qkv/pallas_call | solution.py:143
  29.9 1.1 %attention.4.local_ref = bf16[256,512]{1,0:T(8,128)(2,1)S(1)} custom-call(s32[2,2]{1,0:T(2,128)S(1)} %copy-done.3, f32[1,4]{1,0:T(1,128)S(1)} %copy-done.4, bf16[256,512]{1,0:T(8,128)(2,1)S(1)} %get-tuple-element.41.q_ref, bf16[256,512]{1,0:T(8,128)(2,1)S(1)} %get-tuple-element.45.refs_0_, bf16[256,512]{1,0:T(8,128)(2,1)S(1)} %get-tuple-element.46.refs_1_.refs_2_.refs_3_.refs_4_), custom_call_target="tpu_custom_call" | custom-call | flops 268435456 | tf_op jit(solution)/shard_map/attention/pallas_call | solution.py:239
  31.0 1.4 %attention.5.local_ref = bf16[256,512]{1,0:T(8,128)(2,1)S(1)} custom-call(s32[2,2]{1,0:T(2,128)S(1)} %copy-done.3, f32[1,4]{1,0:T(1,128)S(1)} %copy-done.4, bf16[256,512]{1,0:T(8,128)(2,1)S(1)} %get-tuple-element.47.q_ref, bf16[256,512]{1,0:T(8,128)(2,1)S(1)} %get-tuple-element.45.refs_0_, bf16[256,512]{1,0:T(8,128)(2,1)S(1)} %get-tuple-element.48.refs_1_, ...), custom_call_target="tpu_custom_call" | custom-call | flops 536870912 | tf_op jit(solution)/shard_map/attention/pallas_call | solution.py:239
  32.5 1.7 %attention.6.local_ref = bf16[256,512]{1,0:T(8,128)(2,1)S(1)} custom-call(s32[2,2]{1,0:T(2,128)S(1)} %copy-done.3, f32[1,4]{1,0:T(1,128)S(1)} %copy-done.4, bf16[256,512]{1,0:T(8,128)(2,1)S(1)} %get-tuple-element.50.q_ref, bf16[256,512]{1,0:T(8,128)(2,1)S(1)} %get-tuple-element.45.refs_0_, bf16[256,512]{1,0:T(8,128)(2,1)S(1)} %get-tuple-element.48.refs_1_, ...), custom_call_target="tpu_custom_call" | custom-call | flops 805306368 | tf_op jit(solution)/shard_map/attention/pallas_call | solution.py:239
  34.2 1.1 %last_keys_values.1 = (bf16[256,512]{1,0:T(8,128)(2,1)S(1)}, bf16[256,512]{1,0:T(8,128)(2,1)S(1)}, bf16[8,80,128]{2,1,0:T(8,128)(2,1)S(1)}) custom-call(s32[1]{0:T(128)} %bitcast.me_ref, f32[1,1024]{1,0:T(1,128)S(1)} %copy-done.2, bf16[1024,1536]{1,0:T(8,128)(2,1)S(1)} %bitcast.20, f32[1024,8]{1,0:T(8,128)S(1)} %get-tuple-element.40.fade_ref, ...), custom_call_target="tpu_custom_call" | custom-call | flops 1207959552 | tf_op jit(solution)/shard_map/last_keys_values/pallas_call | solution.py:177
  35.3 13.4 %all_to_all.10.came_ref = bf16[8,80,128]{2,1,0:T(8,128)(2,1)S(1)} all-to-all(bf16[8,80,128]{2,1,0:T(8,128)(2,1)S(1)} %get-tuple-element.56), channel_id=1, replica_groups=mesh['tm'=8,'stream'=2,'head'=2] {'tm'}, dimensions={0} | all-to-all | bytes 327680 | tf_op jit(solution)/shard_map/all_to_all | solution.py:404
  48.7 9.7 %all_to_all.11 = bf16[8,64,128]{2,1,0:T(8,128)(2,1)S(1)} all-to-all(bf16[8,64,128]{2,1,0:T(8,128)(2,1)S(1)} %scan.1), channel_id=1, replica_groups=mesh['tm'=8,'stream'=2,'head'=2] {'tm'}, dimensions={0} | all-to-all | bytes 262144 | tf_op jit(solution)/shard_map/all_to_all | solution.py:405
  58.4 0.2 recall.4.own_ref
  58.7 0.1 collective-permute-start.4
  58.8 1.5 %collective-permute-done.4.side_ref = bf16[256,512]{1,0:T(8,128)(2,1)S(1)} collective-permute-done((bf16[256,512]{1,0:T(8,128)(2,1)S(1)}, bf16[256,512]{1,0:T(8,128)(2,1)S(1)}, u32[]{:S(2)}, u32[]{:S(2)}) %collective-permute-start.4) | collective-permute-done | bytes 262176 | tf_op jit(solution)/shard_map/ppermute | solution.py:416
  60.3 0.7 project.4
  61.0 1.6 %collective-permute-start.6 = (bf16[256,512]{1,0:T(8,128)(2,1)S(1)}, bf16[256,512]{1,0:T(8,128)(2,1)S(1)}, u32[]{:S(2)}, u32[]{:S(2)}) collective-permute-start(bf16[256,512]{1,0:T(8,128)(2,1)S(1)} %get-tuple-element.58), channel_id=1, source_target_pairs={{0,1},{1,0},{2,3},{3,2},{4,5},{5,4},{6,7},{7,6},{8,9},{9,8},{10,11... | collective-permute-start | bytes 786440 | tf_op jit(solution)/shard_map/ppermute | solution.py:421
  62.6 0.2 recall.6.own_ref
  62.8 0.1 collective-permute-start.9
  62.9 0.2 recall.7.own_ref
  63.1 0.6 collective-permute-start.11
  63.7 5.7 %collective-permute-done.6.refs_1_ = bf16[256,512]{1,0:T(8,128)(2,1)S(1)} collective-permute-done((bf16[256,512]{1,0:T(8,128)(2,1)S(1)}, bf16[256,512]{1,0:T(8,128)(2,1)S(1)}, u32[]{:S(2)}, u32[]{:S(2)}) %collective-permute-start.6) | collective-permute-done | bytes 262176 | tf_op jit(solution)/shard_map/ppermute | solution.py:421
  69.4 0.9 last_queries.1.q_ref
  70.3 1.9 %attention.7.local_ref = bf16[256,512]{1,0:T(8,128)(2,1)S(1)} custom-call(s32[2,2]{1,0:T(2,128)S(1)} %copy-done.3, f32[1,4]{1,0:T(1,128)S(1)} %copy-done.4, bf16[256,512]{1,0:T(8,128)(2,1)S(1)} %last_queries.1.q_ref, bf16[256,512]{1,0:T(8,128)(2,1)S(1)} %get-tuple-element.45.refs_0_, bf16[256,512]{1,0:T(8,128)(2,1)S(1)} %get-tuple-element.48.refs_1_, ...), custom_call_target="tpu_custom_call" | custom-call | flops 1073741824 | tf_op jit(solution)/shard_map/attention/pallas_call | solution.py:239
  72.2 0.2 recall.5.own_ref
  72.5 0.1 collective-permute-start.7
  72.6 0.7 project.6
  73.3 1.6 %collective-permute-start.10 = (bf16[256,512]{1,0:T(8,128)(2,1)S(1)}, bf16[256,512]{1,0:T(8,128)(2,1)S(1)}, u32[]{:S(2)}, u32[]{:S(2)}) collective-permute-start(bf16[256,512]{1,0:T(8,128)(2,1)S(1)} %get-tuple-element.67), channel_id=1, source_target_pairs={{0,1},{1,0},{2,3},{3,2},{4,5},{5,4},{6,7},{7,6},{8,9},{9,8},{10,11... | collective-permute-start | bytes 786440 | tf_op jit(solution)/shard_map/ppermute | solution.py:421
  74.9 0.7 project.7
  75.6 0.6 collective-permute-start.12
  76.2 0.7 project.5
  76.9 1.6 %collective-permute-start.8 = (bf16[256,512]{1,0:T(8,128)(2,1)S(1)}, bf16[256,512]{1,0:T(8,128)(2,1)S(1)}, u32[]{:S(2)}, u32[]{:S(2)}) collective-permute-start(bf16[256,512]{1,0:T(8,128)(2,1)S(1)} %get-tuple-element.64), channel_id=1, source_target_pairs={{0,1},{1,0},{2,3},{3,2},{4,5},{5,4},{6,7},{7,6},{8,9},{9,8},{10,11... | collective-permute-start | bytes 786440 | tf_op jit(solution)/shard_map/ppermute | solution.py:421
  78.5 0.8 finish.4.refs_2_
  79.2 8.9 %collective-permute-done.12.refs_1_ = bf16[256,512]{1,0:T(8,128)(2,1)S(1)} collective-permute-done((bf16[256,512]{1,0:T(8,128)(2,1)S(1)}, bf16[256,512]{1,0:T(8,128)(2,1)S(1)}, u32[]{:S(2)}, u32[]{:S(2)}) %collective-permute-start.12) | collective-permute-done | bytes 262176 | tf_op jit(solution)/shard_map/ppermute | solution.py:421
  88.1 0.8 finish.5.refs_2_
  88.9 0.8 finish.6.refs_2_
  89.6 3.7 %collective-permute-done.8.refs_1_ = bf16[256,512]{1,0:T(8,128)(2,1)S(1)} collective-permute-done((bf16[256,512]{1,0:T(8,128)(2,1)S(1)}, bf16[256,512]{1,0:T(8,128)(2,1)S(1)}, u32[]{:S(2)}, u32[]{:S(2)}) %collective-permute-start.8) | collective-permute-done | bytes 262176 | tf_op jit(solution)/shard_map/ppermute | solution.py:421
  93.3 0.8 finish.7
  (17 shorter events, 0.1 us)
Async XLA Ops:
  1.3 10.5 %collective-permute-start.1 = (bf16[256,512]{1,0:T(8,128)(2,1)S(1)}, bf16[256,512]{1,0:T(8,128)(2,1)}, u32[]{:S(2)}, u32[]{:S(2)}) collective-permute-start(bf16[256,512]{1,0:T(8,128)(2,1)S(1)} %get-tuple-element.74.refs_0_), channel_id=1, source_target_pairs={{1,0},{0,1},{3,2},{2,3},{5,4},{4,5},{7,6},{6,7},{9,8},{8,9},{11,10... | collective-permute-start | bytes 786440 | tf_op jit(solution)/shard_map/ppermute | solution.py:371
  4.3 12.9 %collective-permute-start.2 = (bf16[256,512]{1,0:T(8,128)(2,1)S(1)}, bf16[256,512]{1,0:T(8,128)(2,1)}, u32[]{:S(2)}, u32[]{:S(2)}) collective-permute-start(bf16[256,512]{1,0:T(8,128)(2,1)S(1)} %get-tuple-element.76.refs_1_), channel_id=1, source_target_pairs={{1,0},{0,1},{3,2},{2,3},{5,4},{4,5},{7,6},{6,7},{9,8},{8,9},{11,10... | collective-permute-start | bytes 786440 | tf_op jit(solution)/shard_map/ppermute | solution.py:371
  4.4 29.8 %collective-permute-start = (bf16[256,512]{1,0:T(8,128)(2,1)S(1)}, bf16[256,512]{1,0:T(8,128)(2,1)S(1)}, u32[]{:S(2)}, u32[]{:S(2)}) collective-permute-start(bf16[256,512]{1,0:T(8,128)(2,1)S(1)} %get-tuple-element.59.refs_0_), channel_id=1, source_target_pairs={{1,0},{0,1},{3,2},{2,3},{5,4},{4,5},{7,6},{6,7},{9,8},{8,9},{11,10... | collective-permute-start | bytes 786440 | tf_op jit(solution)/shard_map/ppermute | solution.py:371
  6.3 21.2 %collective-permute-start.3 = (bf16[256,512]{1,0:T(8,128)(2,1)S(1)}, bf16[256,512]{1,0:T(8,128)(2,1)}, u32[]{:S(2)}, u32[]{:S(2)}) collective-permute-start(bf16[256,512]{1,0:T(8,128)(2,1)S(1)} %get-tuple-element.73.refs_1_), channel_id=1, source_target_pairs={{1,0},{0,1},{3,2},{2,3},{5,4},{4,5},{7,6},{6,7},{9,8},{8,9},{11,10... | collective-permute-start | bytes 786440 | tf_op jit(solution)/shard_map/ppermute | solution.py:371
  6.4 53.9 %collective-permute-start.5 = (bf16[512,1024]{1,0:T(8,128)(2,1)}, bf16[512,1024]{1,0:T(8,128)(2,1)S(1)}, u32[]{:S(2)}, u32[]{:S(2)}) collective-permute-start(bf16[512,1024]{1,0:T(8,128)(2,1)} %bitcast.32), channel_id=1, source_target_pairs={{0,2},{2,0},{1,3},{3,1},{4,6},{6,4},{5,7},{7,5},{8,10},{10,8},{9,1... | collective-permute-start | bytes 3145736 | tf_op jit(solution)/shard_map/ppermute | solution.py:375
  6.4 0.7 copy-start.1
  7.1 0.7 copy-start.5
  9.3 2.5 %copy-start.2 = (f32[1,1024]{1,0:T(1,128)S(1)}, f32[1,1024]{1,0:T(1,128)}, u32[]{:S(2)}) copy-start(f32[1,1024]{1,0:T(1,128)} %gain_ref.9) | copy-start | bytes 12292
  19.5 10.4 %copy-start.3 = (s32[2,2]{1,0:T(2,128)S(1)}, s32[2,2]{1,0:T(2,128)}, u32[]{:S(2)}) copy-start(s32[2,2]{1,0:T(2,128)} %keep_ref.7) | copy-start | bytes 52
  19.5 10.4 %copy-start.4 = (f32[1,4]{1,0:T(1,128)S(1)}, f32[1,4]{1,0:T(1,128)}, u32[]{:S(2)}) copy-start(f32[1,4]{1,0:T(1,128)} %scale_ref.7) | copy-start | bytes 52
  34.1 26.1 %copy-start = (bf16[1,4,128,1024]{3,2,1,0:T(8,128)(2,1)S(1)}, bf16[1,4,128,1024]{3,2,1,0:T(8,128)(2,1)}, u32[]{:S(2)}) copy-start(bf16[1,4,128,1024]{3,2,1,0:T(8,128)(2,1)} %param.16) | copy-start | bytes 3145732
  58.7 1.6 %collective-permute-start.4 = (bf16[256,512]{1,0:T(8,128)(2,1)S(1)}, bf16[256,512]{1,0:T(8,128)(2,1)S(1)}, u32[]{:S(2)}, u32[]{:S(2)}) collective-permute-start(bf16[256,512]{1,0:T(8,128)(2,1)S(1)} %recall.4.own_ref), channel_id=1, source_target_pairs={{0,2},{2,0},{1,3},{3,1},{4,6},{6,4},{5,7},{7,5},{8,10},{10,8},{9,1... | collective-permute-start | bytes 786440 | tf_op jit(solution)/shard_map/ppermute | solution.py:416
  61.0 8.4 %collective-permute-start.6 = (bf16[256,512]{1,0:T(8,128)(2,1)S(1)}, bf16[256,512]{1,0:T(8,128)(2,1)S(1)}, u32[]{:S(2)}, u32[]{:S(2)}) collective-permute-start(bf16[256,512]{1,0:T(8,128)(2,1)S(1)} %get-tuple-element.58), channel_id=1, source_target_pairs={{0,1},{1,0},{2,3},{3,2},{4,5},{5,4},{6,7},{7,6},{8,9},{9,8},{10,11... | collective-permute-start | bytes 786440 | tf_op jit(solution)/shard_map/ppermute | solution.py:421
  62.8 9.7 %collective-permute-start.9 = (bf16[256,512]{1,0:T(8,128)(2,1)S(1)}, bf16[256,512]{1,0:T(8,128)(2,1)S(1)}, u32[]{:S(2)}, u32[]{:S(2)}) collective-permute-start(bf16[256,512]{1,0:T(8,128)(2,1)S(1)} %recall.6.own_ref), channel_id=1, source_target_pairs={{0,2},{2,0},{1,3},{3,1},{4,6},{6,4},{5,7},{7,5},{8,10},{10,8},{9,1... | collective-permute-start | bytes 786440 | tf_op jit(solution)/shard_map/ppermute | solution.py:416
  63.1 11.7 %collective-permute-start.11 = (bf16[256,512]{1,0:T(8,128)(2,1)S(1)}, bf16[256,512]{1,0:T(8,128)(2,1)S(1)}, u32[]{:S(2)}, u32[]{:S(2)}) collective-permute-start(bf16[256,512]{1,0:T(8,128)(2,1)S(1)} %recall.7.own_ref), channel_id=1, source_target_pairs={{0,2},{2,0},{1,3},{3,1},{4,6},{6,4},{5,7},{7,5},{8,10},{10,8},{9,1... | collective-permute-start | bytes 786440 | tf_op jit(solution)/shard_map/ppermute | solution.py:416
  72.5 3.7 %collective-permute-start.7 = (bf16[256,512]{1,0:T(8,128)(2,1)S(1)}, bf16[256,512]{1,0:T(8,128)(2,1)S(1)}, u32[]{:S(2)}, u32[]{:S(2)}) collective-permute-start(bf16[256,512]{1,0:T(8,128)(2,1)S(1)} %recall.5.own_ref), channel_id=1, source_target_pairs={{0,2},{2,0},{1,3},{3,1},{4,6},{6,4},{5,7},{7,5},{8,10},{10,8},{9,1... | collective-permute-start | bytes 786440 | tf_op jit(solution)/shard_map/ppermute | solution.py:416
  73.3 15.6 %collective-permute-start.10 = (bf16[256,512]{1,0:T(8,128)(2,1)S(1)}, bf16[256,512]{1,0:T(8,128)(2,1)S(1)}, u32[]{:S(2)}, u32[]{:S(2)}) collective-permute-start(bf16[256,512]{1,0:T(8,128)(2,1)S(1)} %get-tuple-element.67), channel_id=1, source_target_pairs={{0,1},{1,0},{2,3},{3,2},{4,5},{5,4},{6,7},{7,6},{8,9},{9,8},{10,11... | collective-permute-start | bytes 786440 | tf_op jit(solution)/shard_map/ppermute | solution.py:421
  75.6 12.5 %collective-permute-start.12 = (bf16[256,512]{1,0:T(8,128)(2,1)S(1)}, bf16[256,512]{1,0:T(8,128)(2,1)S(1)}, u32[]{:S(2)}, u32[]{:S(2)}) collective-permute-start(bf16[256,512]{1,0:T(8,128)(2,1)S(1)} %get-tuple-element.70), channel_id=1, source_target_pairs={{0,1},{1,0},{2,3},{3,2},{4,5},{5,4},{6,7},{7,6},{8,9},{9,8},{10,11... | collective-permute-start | bytes 786440 | tf_op jit(solution)/shard_map/ppermute | solution.py:421
  76.9 16.4 %collective-permute-start.8 = (bf16[256,512]{1,0:T(8,128)(2,1)S(1)}, bf16[256,512]{1,0:T(8,128)(2,1)S(1)}, u32[]{:S(2)}, u32[]{:S(2)}) collective-permute-start(bf16[256,512]{1,0:T(8,128)(2,1)S(1)} %get-tuple-element.64), channel_id=1, source_target_pairs={{0,1},{1,0},{2,3},{3,2},{4,5},{5,4},{6,7},{7,6},{8,9},{9,8},{10,11... | collective-permute-start | bytes 786440 | tf_op jit(solution)/shard_map/ppermute | solution.py:421

commit v6 on v4

--- a/solution.py
+++ b/solution.py
@@ -48,7 +48,8 @@
     return values * lax.rsqrt(jnp.mean(values * values, axis=-1, keepdims=True) + EPSILON)
 
 
-def prepare_kernel(heads, factor, logs_ref, flags_ref, fade_ref, reading_ref, tail_ref, rows_ref):
+def prepare_kernel(heads, factor, logs_ref, flags_ref, fade_ref, tail_ref, *refs):
+    reading_refs, rows_ref = refs[:-1], refs[-1]
     length = logs_ref.shape[1]
     rows_ref[...] = jnp.zeros_like(rows_ref)
     rows_ref[:heads, :] = logs_ref[...]
@@ -64,21 +65,28 @@
         inside = (place >= block * BLOCK) & (place < (block + 1) * BLOCK)
         chosen = jnp.where(inside, flags_ref[block].astype(F32), chosen)
     fade_ref[...] = jnp.transpose(jnp.exp(last - running) * chosen)
-    reading_ref[...] = jnp.transpose(jnp.exp(running) * factor)
+    reading = jnp.transpose(jnp.exp(running) * factor)
+    for c, ref in enumerate(reading_refs):
+        ref[...] = reading[c * CHUNK : (c + 1) * CHUNK]
     decay = jnp.exp(last)
     high = decay.astype(BF16).astype(F32)
-    both = jnp.concatenate([high, decay - high], axis=0)
-    tail_ref[...] = jnp.broadcast_to(both, tail_ref.shape).astype(BF16)
-
-
-def prepare(logs, flags, dim, factor):
+    lines, groups = running.shape[0], tail_ref.shape[0]
+    for g in range(groups):
+        both = [jnp.broadcast_to(part, (lines, tail_ref.shape[2])) for part in (high, decay - high)]
+        if g > 0:
+            both = [pltpu.roll(part, lines - g * (heads // groups), 0) for part in both]
+        tail_ref[g] = jnp.concatenate(both, axis=0).astype(BF16)
+
+
+def prepare(logs, flags, dim, factor, groups):
     heads, length = logs.shape
     lines = TAIL // 2
     return pl.pallas_call(
         functools.partial(prepare_kernel, heads, factor),
         in_specs=[VMEM, SMEM],
-        out_specs=[VMEM] * 3,
-        out_shape=[struct((length, lines), F32)] * 2 + [struct((TAIL, dim))],
+        out_specs=[VMEM] * (2 + length // CHUNK),
+        out_shape=[struct((length, lines), F32), struct((groups, TAIL, dim))]
+        + [struct((CHUNK, lines), F32)] * (length // CHUNK),
         scratch_shapes=[pltpu.VMEM((lines, length), F32)],
         compiler_params=params(),
         cost_estimate=cost(40 * lines * length, 0),
@@ -148,8 +156,9 @@
     )(me, gain, w, fade, *before, *xs)
 
 
-def last_kernel(heads, dim, first, me_ref, gain_ref, w_ref, fade_ref, prev_ref, tail_ref, *refs):
-    x_refs, (k_ref, v_ref, send_ref, sum_ref) = refs[:-4], refs[-4:]
+def last_kernel(shards, heads, dim, first, me_ref, gain_ref, w_ref, fade_ref, prev_ref, tail_ref, *refs):
+    x_refs, (k_ref, v_ref, *send_refs, sum_ref) = refs[:shards], refs[shards:]
+    per = heads // len(send_refs)
     sum_ref[...] = prev_ref[...]
     parts = normed_parts(me_ref[0], gain_ref, x_refs)
     pairs = [
@@ -162,17 +171,21 @@
         k_ref[:, cols] = key
         v_ref[:, cols] = value
         add_summary(sum_ref, h, key, value, fade_ref, first)
-        send_ref[cols, :] = sum_ref[h].astype(BF16)
-    send_ref[heads * dim :, :] = tail_ref[...]
+        g, at = divmod(h, per)
+        send_refs[g][at * dim : (at + 1) * dim, :] = sum_ref[h].astype(BF16)
+    for g, send_ref in enumerate(send_refs):
+        send_ref[per * dim :, :] = tail_ref[g]
 
 
 def last_keys_values(me, gain, w, fade, prev, tail, xs, heads, dim, first):
     rows = xs[0].shape[0]
-    return pl.pallas_call(
-        functools.partial(last_kernel, heads, dim, first),
+    groups = tail.shape[0]
+    return pl.pallas_call(
+        functools.partial(last_kernel, len(xs), heads, dim, first),
         in_specs=[SMEM] + [VMEM] * (5 + len(xs)),
-        out_specs=[VMEM] * 3,
-        out_shape=[struct((rows, heads * dim))] * 2 + [struct((heads * dim + TAIL, dim))],
+        out_specs=[VMEM] * (2 + groups),
+        out_shape=[struct((rows, heads * dim))] * 2
+        + [struct((heads // groups * dim + TAIL, dim))] * groups,
         scratch_shapes=[pltpu.VMEM((heads, dim, dim), F32)],
         compiler_params=params(),
         cost_estimate=cost(3 * rows * w.size, 0),
@@ -320,24 +333,27 @@
     )(place, before, decay, *totals)
 
 
-def recall_kernel(heads, dim, first, reading_ref, q_ref, local_ref, state_ref, out_ref):
+def recall_kernel(heads, dim, reading_ref, q_ref, local_ref, *refs):
+    state_refs, out_ref = refs[:-1], refs[-1]
+    per = heads // len(state_refs)
     for h in range(heads):
         cols = slice(h * dim, (h + 1) * dim)
-        reading = reading_ref[first : first + q_ref.shape[0], h : h + 1]
-        recalled = dot(q_ref[:, cols], state_ref[cols, :]) * reading
+        g, at = divmod(h, per)
+        state = state_refs[g][at * dim : (at + 1) * dim, :]
+        recalled = dot(q_ref[:, cols], state) * reading_ref[:, h : h + 1]
         out_ref[:, cols] = (local_ref[:, cols].astype(F32) + recalled).astype(BF16)
 
 
-def recall(reading, q, local, state, heads, dim, first):
-    return pl.pallas_call(
-        functools.partial(recall_kernel, heads, dim, first),
-        in_specs=[VMEM] * 4,
+def recall(reading, q, local, states, heads, dim):
+    return pl.pallas_call(
+        functools.partial(recall_kernel, heads, dim),
+        in_specs=[VMEM] * (3 + len(states)),
         out_specs=VMEM,
         out_shape=struct(q.shape),
         compiler_params=params(),
         cost_estimate=cost(4 * q.size * dim, 0),
         name="recall",
-    )(reading, q, local, state)
+    )(reading, q, local, *states)
 
 
 def project_kernel(shards, me_ref, own_ref, side_ref, own_w_ref, side_w_ref, *out_refs):
@@ -414,6 +430,8 @@
     received = []
     for c in range(chunks):
         piece = x[c * CHUNK : (c + 1) * CHUNK]
+        if c > 2:
+            piece, received[c - 3] = tied(piece, received[c - 3])
         xs = [piece]
         for k in range(1, shards):
             xs.append(lax.ppermute(piece, "head", [((d + k) % shards, d) for d in range(shards)]))
@@ -423,11 +441,13 @@
     side_w = lax.ppermute(
         sideways_coupling_coef[0].reshape(heads * dim, -1), "stream", swap_streams
     )
-    fade, reading, tail = prepare(
+    groups = 2 if heads % 2 == 0 else 1
+    fade, tail, *readings = prepare(
         recall_retained_logshare[0],
         recall_store_flags,
         dim,
         1.0 / math.sqrt(dim * length * blocks),
+        groups,
     )
     gain = prescale_amplifier
     w = triple_projector[0].reshape(-1, 3 * heads * dim)
@@ -442,30 +462,47 @@
         ks.append(k)
         vs.append(v)
         locals_.append(attention(c, tile_retain_grid, score_scaler, q, ks, vs, heads, dim))
-    summary, *locals_ = tied(summary, *locals_)
-    k, v, sent = last_keys_values(
+    summary, side_w, *locals_ = tied(summary, side_w, *locals_)
+    k, v, *sents = last_keys_values(
         me, gain, w, fade, summary, tail, received[-1], heads, dim, (chunks - 1) * CHUNK
     )
     ks.append(k)
     vs.append(v)
 
-    quad_size = min(4, blocks)
-    loads = [sent] + [
-        lax.ppermute(sent, "tm", [(d, d ^ k) for d in range(blocks)]) for k in range(1, quad_size)
-    ]
+    quad_size, per = min(4, blocks), heads // groups
+    loads, befores, decays, totals, far, states = [], [], [], [], [], []
+    for sent in sents:
+        loads.append(
+            [sent]
+            + [
+                lax.ppermute(sent, "tm", [(d, d ^ k) for d in range(blocks)])
+                for k in range(1, quad_size)
+            ]
+        )
+    for g in range(groups):
+        before, decay, total = quad(lax.rem(place, quad_size), loads[g], per, dim)
+        befores.append(before)
+        decays.append(decay)
+        totals.append(total)
+        far.append(
+            [
+                lax.ppermute(total, "tm", [(d, d ^ (quad_size * k)) for d in range(blocks)])
+                for k in range(1, blocks // quad_size)
+            ]
+        )
     qs.append(last_queries(me, gain, w, received[-1], heads, dim))
     locals_.append(attention(chunks - 1, tile_retain_grid, score_scaler, qs[-1], ks, vs, heads, dim))
-    *loads, locals_[-1] = tied(*loads, locals_[-1])
-    before, decay, total = quad(lax.rem(place, quad_size), loads, heads, dim)
-    totals = [total] + [
-        lax.ppermute(total, "tm", [(d, d ^ (quad_size * k)) for d in range(blocks)])
-        for k in range(1, blocks // quad_size)
-    ]
-    state = entering(lax.div(place, quad_size), before, decay, totals, heads, dim)
-
-    result = None
+    far, locals_[-1] = tied(far, locals_[-1])
+    for g in range(groups):
+        states.append(
+            entering(
+                lax.div(place, quad_size), befores[g], decays[g], [totals[g], *far[g]], per, dim
+            )
+        )
+
+    result, finished = None, []
     for c in range(chunks):
-        head_out = recall(reading, qs[c], locals_[c], state, heads, dim, c * CHUNK)
+        head_out = recall(readings[c], qs[c], locals_[c], states, heads, dim)
         side = lax.ppermute(head_out, "stream", swap_streams)
         outs = project(me, head_out, side, own_w, side_w, shards)
         parts = [outs[0]]
@@ -473,7 +510,9 @@
             parts.append(
                 lax.ppermute(outs[k], "head", [(d, (d + k) % shards) for d in range(shards)])
             )
-        result = finish(parts, result, c, length)
+        finished.append(parts)
+    for c in range(chunks):
+        result = finish(finished[c], result, c, length)
     return result[None]
 
 

time: 76.5 us -> 81.9 us (1.071)
  starting transfers between devices: 17.1 us -> 21.8 us
  waiting for transfers between devices: 26.2 us -> 22.3 us
  local copies, waits for them, and re-layouts: 8.64 us -> 12.4 us
    ppermute x3 -> x6, starting transfers between devices: 3.55 us -> 7.58 us  [per_device(): lax.ppermute(sent, 'tm', [(d, d ^ k) for d in range(blocks)])]
    unnamed x17 -> x77, local copies, waits for them, and re-layouts: 7.37 us -> 11.2 us
    ppermute x3 -> x6, waiting for transfers between devices: 3.18 us -> 0.02 us  [per_device(): lax.ppermute(sent, 'tm', [(d, d ^ k) for d in range(blocks)])]
    ppermute x1 -> x2, waiting for transfers between devices: 5.74 us -> 3.44 us  [per_device(): lax.ppermute(total, 'tm', [(d, d ^ quad_size * k) for d in range(blocks)])]
    ppermute x4, waiting for transfers between devices: 0.86 us -> 2.42 us  [per_device(): lax.ppermute(piece, 'head', [((d + k) % shards, d) for d in range(shards)])]
    pallas_call x3, Pallas kernels: 7.1 us -> 6.06 us  [qkv(): pl.pallas_call(functools.partial(qkv_kernel, heads, dim, first), in_specs...]
    pallas_call x1 -> x2, Pallas kernels: 0.32 us -> 1.29 us  [quad(): pl.pallas_call(functools.partial(quad_kernel, heads, dim), in_specs=[SMEM...]
    ppermute x1 -> x2, starting transfers between devices: 2.82 us -> 3.24 us  [per_device(): lax.ppermute(total, 'tm', [(d, d ^ quad_size * k) for d in range(blocks)])]
  transfers between devices with their start and end apart: 17 -> 21, of which waited for: 9 -> 9; matrix products, arithmetic and copies ran while one was open for 5% -> 5% of each run, Pallas kernels for 31% -> 26%
where the time goes in v6:
time: 81.9 us; the launch traced here: 81.6 us
  Pallas kernels  24.6 us (30%)
  waiting for transfers between devices  22.3 us (27%)
  starting transfers between devices  21.8 us (27%)
  local copies, waits for them, and re-layouts  12.4 us (15%)
    ppermute x4, waiting for transfers between devices, per_device(): lax.ppermute(outs[k], 'head', [(d, (d + k) % shards) for d in range(shard...  16.4 us
    unnamed x77, local copies, waits for them, and re-layouts  11.2 us
    ppermute x6, starting transfers between devices, per_device(): lax.ppermute(sent, 'tm', [(d, d ^ k) for d in range(blocks)])  7.58 us
    pallas_call x4, Pallas kernels, attention(): pl.pallas_call(functools.partial(attention_kernel, chunk, heads, dim), in...  6.13 us
    pallas_call x3, Pallas kernels, qkv(): pl.pallas_call(functools.partial(qkv_kernel, heads, dim, first), in_specs...  6.06 us
    ppermute x4, starting transfers between devices, per_device(): lax.ppermute(piece, 'head', [((d + k) % shards, d) for d in range(shards)])  4.93 us
    ppermute x4, starting transfers between devices, per_device(): lax.ppermute(outs[k], 'head', [(d, (d + k) % shards) for d in range(shard...  4.31 us
    ppermute x2, waiting for transfers between devices, per_device(): lax.ppermute(total, 'tm', [(d, d ^ quad_size * k) for d in range(blocks)])  3.44 us
  transfers between devices with their start and end apart: 21, of which 9 were waited for; matrix products, arithmetic and copies ran while one was open for 5% of the time, Pallas kernels for 26%

profile of v6, /device:TPU:0, one launch (start us, length us, event | category | flops | bytes accessed | tf_op | source)
XLA Modules:
  0.0 81.6 jit_solution(10524360796570495615)
XLA Ops:
  0.5 1.3 %slice_bitcast_fusion = (bf16[256,512]{1,0:T(8,128)(2,1)S(1)}, bf16[256,512]{1,0:T(8,128)(2,1)S(1)}, bf16[256,512]{1,0:T(8,128)(2,1)S(1)}, bf16[256,512]{1,0:T(8,128)(2,1)S(1)}) fusion(bf16[1,1024,512]{2,1,0:T(8,128)(2,1)} %param.9), kind=kLoop, calls=%fused_computation | loop fusion | bytes 2097152 | tf_op jit(solution)/shard_map/slice | solution.py:432
  1.7 2.6 %collective-permute-start = (bf16[256,512]{1,0:T(8,128)(2,1)S(1)}, bf16[256,512]{1,0:T(8,128)(2,1)S(1)}, u32[]{:S(2)}, u32[]{:S(2)}) collective-permute-start(bf16[256,512]{1,0:T(8,128)(2,1)S(1)} %get-tuple-element.55.refs_0_), channel_id=1, source_target_pairs={{1,0},{0,1},{3,2},{2,3},{5,4},{4,5},{7,6},{6,7},{9,8},{8,9},{11,10... | collective-permute-start | bytes 786440 | tf_op jit(solution)/shard_map/ppermute | solution.py:437
  4.4 1.9 %collective-permute-start.3 = (bf16[256,512]{1,0:T(8,128)(2,1)S(1)}, bf16[256,512]{1,0:T(8,128)(2,1)}, u32[]{:S(2)}, u32[]{:S(2)}) collective-permute-start(bf16[256,512]{1,0:T(8,128)(2,1)S(1)} %get-tuple-element.99.refs_1_), channel_id=1, source_target_pairs={{1,0},{0,1},{3,2},{2,3},{5,4},{4,5},{7,6},{6,7},{9,8},{8,9},{11,10... | collective-permute-start | bytes 786440 | tf_op jit(solution)/shard_map/ppermute | solution.py:437
  6.3 0.7 copy-done.15
  7.1 0.7 copy-done.19
  7.7 1.4 %prepare.1 = (f32[1024,8]{1,0:T(8,128)S(1)}, bf16[2,16,128]{2,1,0:T(8,128)(2,1)S(1)}, f32[256,8]{1,0:T(8,128)S(1)}, f32[256,8]{1,0:T(8,128)S(1)}, f32[256,8]{1,0:T(8,128)S(1)}, /*index=5*/f32[256,8]{1,0:T(8,128)S(1)}) custom-call(f32[4,1024]{1,0:T(4,128)S(1)} %bitcast.26, s32[2]{0:T(128)S(1)} %copy-done.19), custom_call_target="tpu_custom_call" | custom-call | flops 327680 | tf_op jit(solution)/shard_map/prepare/pallas_call | solution.py:84
  9.1 0.8 copy-done.20
  10.5 2.6 %copy.13 = bf16[128,8,4,384]{3,1,2,0:T(8,128)(2,1)S(1)} copy(bf16[128,8,4,384]{3,2,1,0:T(4,128)(2,1)} %bitcast.27) | data formatting | bytes 6291456
  13.2 0.7 copy-done.22
  14.3 1.0 %copy-done.23 = bf16[256,512]{1,0:T(8,128)(2,1)S(1)} copy-done((bf16[256,512]{1,0:T(8,128)(2,1)S(1)}, bf16[256,512]{1,0:T(8,128)(2,1)}, u32[]{:S(2)}) %copy-start.23) | copy-done | bytes 262168
  15.3 1.4 %qkv.3 = (bf16[256,512]{1,0:T(8,128)(2,1)S(1)}, bf16[256,512]{1,0:T(8,128)(2,1)S(1)}, bf16[256,512]{1,0:T(8,128)(2,1)S(1)}, f32[4,128,128]{2,1,0:T(8,128)S(1)}) custom-call(s32[1]{0:T(128)} %bitcast.me_ref, f32[1,1024]{1,0:T(1,128)S(1)} %copy-done.16, bf16[1024,1536]{1,0:T(8,128)(2,1)S(1)} %bitcast.21, f32[1024,8]{1,0:T(8,128)S(1)} %copy-done.21, ...), custom_call_target="tpu_custom_call" | custom-call | flops 1610612736 | tf_op jit(solution)/shard_map/qkv/pallas_call | solution.py:148
  17.2 2.4 %qkv.4 = (bf16[256,512]{1,0:T(8,128)(2,1)S(1)}, bf16[256,512]{1,0:T(8,128)(2,1)S(1)}, bf16[256,512]{1,0:T(8,128)(2,1)S(1)}, f32[4,128,128]{2,1,0:T(8,128)S(1)}) custom-call(s32[1]{0:T(128)} %bitcast.me_ref, f32[1,1024]{1,0:T(1,128)S(1)} %copy-done.16, bf16[1024,1536]{1,0:T(8,128)(2,1)S(1)} %bitcast.22, f32[1024,8]{1,0:T(8,128)S(1)} %copy-done.21, ...), custom_call_target="tpu_custom_call" | custom-call | flops 1610612736 | tf_op jit(solution)/shard_map/qkv/pallas_call | solution.py:148
  19.6 1.4 %attention.5.local_ref = bf16[256,512]{1,0:T(8,128)(2,1)S(1)} custom-call(s32[2,2]{1,0:T(2,128)S(1)} %copy-done.17, f32[1,4]{1,0:T(1,128)S(1)} %copy-done.18, bf16[256,512]{1,0:T(8,128)(2,1)S(1)} %get-tuple-element.63.q_ref, bf16[256,512]{1,0:T(8,128)(2,1)S(1)} %get-tuple-element.61.refs_0_, bf16[256,512]{1,0:T(8,128)(2,1)S(1)} %get-tuple-element.64.refs_1_, ...), custom_call_target="tpu_custom_call" | custom-call | flops 536870912 | tf_op jit(solution)/shard_map/attention/pallas_call | solution.py:245
  21.1 1.1 %attention.4.local_ref = bf16[256,512]{1,0:T(8,128)(2,1)S(1)} custom-call(s32[2,2]{1,0:T(2,128)S(1)} %copy-done.17, f32[1,4]{1,0:T(1,128)S(1)} %copy-done.18, bf16[256,512]{1,0:T(8,128)(2,1)S(1)} %get-tuple-element.60.q_ref, bf16[256,512]{1,0:T(8,128)(2,1)S(1)} %get-tuple-element.61.refs_0_, ...), custom_call_target="tpu_custom_call" | custom-call | flops 268435456 | tf_op jit(solution)/shard_map/attention/pallas_call | solution.py:245
  22.2 0.6 collective-permute-done.3.refs_2_
  22.8 2.3 %qkv.5 = (bf16[256,512]{1,0:T(8,128)(2,1)S(1)}, bf16[256,512]{1,0:T(8,128)(2,1)S(1)}, bf16[256,512]{1,0:T(8,128)(2,1)S(1)}, f32[4,128,128]{2,1,0:T(8,128)S(1)}) custom-call(s32[1]{0:T(128)} %bitcast.me_ref, f32[1,1024]{1,0:T(1,128)S(1)} %copy-done.16, bf16[1024,1536]{1,0:T(8,128)(2,1)S(1)} %bitcast.23, f32[1024,8]{1,0:T(8,128)S(1)} %copy-done.21, ...), custom_call_target="tpu_custom_call" | custom-call | flops 1610612736 | tf_op jit(solution)/shard_map/qkv/pallas_call | solution.py:148
  25.2 1.7 %attention.6.local_ref = bf16[256,512]{1,0:T(8,128)(2,1)S(1)} custom-call(s32[2,2]{1,0:T(2,128)S(1)} %copy-done.17, f32[1,4]{1,0:T(1,128)S(1)} %copy-done.18, bf16[256,512]{1,0:T(8,128)(2,1)S(1)} %get-tuple-element.66.q_ref, bf16[256,512]{1,0:T(8,128)(2,1)S(1)} %get-tuple-element.61.refs_0_, bf16[256,512]{1,0:T(8,128)(2,1)S(1)} %get-tuple-element.64.refs_1_, ...), custom_call_target="tpu_custom_call" | custom-call | flops 805306368 | tf_op jit(solution)/shard_map/attention/pallas_call | solution.py:245
  26.9 1.3 %collective-permute-done.1.refs_1_ = bf16[256,512]{1,0:T(8,128)(2,1)S(1)} collective-permute-done((bf16[256,512]{1,0:T(8,128)(2,1)S(1)}, bf16[256,512]{1,0:T(8,128)(2,1)S(1)}, u32[]{:S(2)}, u32[]{:S(2)}) %collective-permute-start.1) | collective-permute-done | bytes 262176 | tf_op jit(solution)/shard_map/ppermute | solution.py:437
  28.1 1.8 %last_keys_values.1 = (bf16[256,512]{1,0:T(8,128)(2,1)S(1)}, bf16[256,512]{1,0:T(8,128)(2,1)S(1)}, bf16[272,128]{1,0:T(8,128)(2,1)S(1)}, bf16[272,128]{1,0:T(8,128)(2,1)}) custom-call(s32[1]{0:T(128)} %bitcast.me_ref, f32[1,1024]{1,0:T(1,128)S(1)} %copy-done.16, bf16[1024,1536]{1,0:T(8,128)(2,1)S(1)} %bitcast.24, f32[1024,8]{1,0:T(8,128)S(1)} %copy-done.21, ...), custom_call_target="tpu_custom_call" | custom-call | flops 1207959552 | tf_op jit(solution)/shard_map/last_keys_values/pallas_call | solution.py:183
  29.9 0.6 copy-done.13
  30.5 0.7 copy-done.26
  31.3 0.7 copy-done.28
  32.0 1.8 %collective-permute-start.10 = (bf16[272,128]{1,0:T(8,128)(2,1)}, bf16[272,128]{1,0:T(8,128)(2,1)}, u32[]{:S(2)}, u32[]{:S(2)}) collective-permute-start(bf16[272,128]{1,0:T(8,128)(2,1)} %get-tuple-element.73.refs_0_), channel_id=1, source_target_pairs={{0,8},{4,12},{8,0},{12,4},{16,24},{20,28},{24,16},{28,20},{1,9},{5... | collective-permute-start | bytes 208904 | tf_op jit(solution)/shard_map/ppermute | solution.py:478
  33.8 1.4 %collective-permute-start.11 = (bf16[272,128]{1,0:T(8,128)(2,1)}, bf16[272,128]{1,0:T(8,128)(2,1)S(1)}, u32[]{:S(2)}, u32[]{:S(2)}) collective-permute-start(bf16[272,128]{1,0:T(8,128)(2,1)} %get-tuple-element.73.refs_0_), channel_id=1, source_target_pairs={{0,12},{4,8},{8,4},{12,0},{16,28},{20,24},{24,20},{28,16},{1,13},{... | collective-permute-start | bytes 208904 | tf_op jit(solution)/shard_map/ppermute | solution.py:478
  35.5 1.7 %collective-permute-start.5 = (bf16[272,128]{1,0:T(8,128)(2,1)}, bf16[272,128]{1,0:T(8,128)(2,1)S(1)}, u32[]{:S(2)}, u32[]{:S(2)}) collective-permute-start(bf16[272,128]{1,0:T(8,128)(2,1)} %copy-done.13), channel_id=1, source_target_pairs={{0,4},{4,0},{8,12},{12,8},{16,20},{20,16},{24,28},{28,24},{1,5},{5... | collective-permute-start | bytes 208904 | tf_op jit(solution)/shard_map/ppermute | solution.py:478
  37.2 1.6 %collective-permute-start.6 = (bf16[272,128]{1,0:T(8,128)(2,1)}, bf16[272,128]{1,0:T(8,128)(2,1)S(1)}, u32[]{:S(2)}, u32[]{:S(2)}) collective-permute-start(bf16[272,128]{1,0:T(8,128)(2,1)} %copy-done.13), channel_id=1, source_target_pairs={{0,8},{4,12},{8,0},{12,4},{16,24},{20,28},{24,16},{28,20},{1,9},{5... | collective-permute-start | bytes 208904 | tf_op jit(solution)/shard_map/ppermute | solution.py:478
  38.7 0.8 collective-permute-start.7
  39.6 1.9 %copy-done.2 = bf16[128,8,4,384]{3,1,2,0:T(8,128)(2,1)S(1)} copy-done((bf16[128,8,4,384]{3,1,2,0:T(8,128)(2,1)S(1)}, bf16[128,8,4,384]{3,1,2,0:T(8,128)(2,1)}, u32[]{:S(2)}) %copy-start.2) | copy-done | bytes 3145752
  41.5 0.9 %last_queries.1.q_ref = bf16[256,512]{1,0:T(8,128)(2,1)S(1)} custom-call(s32[1]{0:T(128)} %bitcast.me_ref, f32[1,1024]{1,0:T(1,128)S(1)} %copy-done.16, bf16[1024,1536]{1,0:T(8,128)(2,1)S(1)} %bitcast.25, bf16[256,512]{1,0:T(8,128)(2,1)S(1)} %get-tuple-element.53.refs_0_, bf16[256,512]{1,0:T(8,128)(2,1)S(1)} %collective-permute-done.1.refs_1_), custom_call_target="tpu_custom_call" | custom-call | flops 805306368 | tf_op jit(solution)/shard_map/last_queries/pallas_call | solution.py:207
  42.4 1.1 %quad.3 = (f32[256,128]{1,0:T(8,128)S(1)}, f32[8,128]{1,0:T(8,128)S(1)}, bf16[272,128]{1,0:T(8,128)(2,1)S(1)}) custom-call(s32[1]{0:T(128)S(6)} %rem.19.place_ref, bf16[272,128]{1,0:T(8,128)(2,1)} %get-tuple-element.73.refs_0_, bf16[272,128]{1,0:T(8,128)(2,1)S(1)} %collective-permute-done.9.refs_1_, bf16[272,128]{1,0:T(8,128)(2,1)} %collective-permute-done.10.refs_2_, ...), custom_call_target="tpu_custom_call" | custom-call | flops 1392640 | tf_op jit(solution)/shard_map/quad/pallas_call | solution.py:301
  43.6 2.7 %collective-permute-start.12 = (bf16[272,128]{1,0:T(8,128)(2,1)S(1)}, bf16[272,128]{1,0:T(8,128)(2,1)S(1)}, u32[]{:S(2)}, u32[]{:S(2)}) collective-permute-start(bf16[272,128]{1,0:T(8,128)(2,1)S(1)} %get-tuple-element.74.refs_0_), channel_id=1, source_target_pairs={{0,16},{4,20},{8,24},{12,28},{16,0},{20,4},{24,8},{28,12},{1,17},{... | collective-permute-start | bytes 208904 | tf_op jit(solution)/shard_map/ppermute | solution.py:489
  47.0 1.9 %attention.7.local_ref = bf16[256,512]{1,0:T(8,128)(2,1)S(1)} custom-call(s32[2,2]{1,0:T(2,128)S(1)} %copy-done.17, f32[1,4]{1,0:T(1,128)S(1)} %copy-done.18, bf16[256,512]{1,0:T(8,128)(2,1)S(1)} %last_queries.1.q_ref, bf16[256,512]{1,0:T(8,128)(2,1)S(1)} %get-tuple-element.61.refs_0_, bf16[256,512]{1,0:T(8,128)(2,1)S(1)} %copy-done.31, ...), custom_call_target="tpu_custom_call" | custom-call | flops 1073741824 | tf_op jit(solution)/shard_map/attention/pallas_call | solution.py:245
  49.0 1.7 %collective-permute-done.12.refs_1_ = bf16[272,128]{1,0:T(8,128)(2,1)S(1)} collective-permute-done((bf16[272,128]{1,0:T(8,128)(2,1)S(1)}, bf16[272,128]{1,0:T(8,128)(2,1)S(1)}, u32[]{:S(2)}, u32[]{:S(2)}) %collective-permute-start.12) | collective-permute-done | bytes 69664 | tf_op jit(solution)/shard_map/ppermute | solution.py:489
  50.7 1.7 %collective-permute-done.8.refs_1_ = bf16[272,128]{1,0:T(8,128)(2,1)S(1)} collective-permute-done((bf16[272,128]{1,0:T(8,128)(2,1)S(1)}, bf16[272,128]{1,0:T(8,128)(2,1)S(1)}, u32[]{:S(2)}, u32[]{:S(2)}) %collective-permute-start.8) | collective-permute-done | bytes 69664 | tf_op jit(solution)/shard_map/ppermute | solution.py:489
  55.0 0.7 project.7
  55.7 1.6 %collective-permute-start.20 = (bf16[256,512]{1,0:T(8,128)(2,1)S(1)}, bf16[256,512]{1,0:T(8,128)(2,1)S(1)}, u32[]{:S(2)}, u32[]{:S(2)}) collective-permute-start(bf16[256,512]{1,0:T(8,128)(2,1)S(1)} %get-tuple-element.98), channel_id=1, source_target_pairs={{0,1},{1,0},{2,3},{3,2},{4,5},{5,4},{6,7},{7,6},{8,9},{9,8},{10,11... | collective-permute-start | bytes 786440 | tf_op jit(solution)/shard_map/ppermute | solution.py:511
  57.3 0.7 project.6
  58.6 0.7 project.5
  59.3 1.6 %collective-permute-start.16 = (bf16[256,512]{1,0:T(8,128)(2,1)S(1)}, bf16[256,512]{1,0:T(8,128)(2,1)S(1)}, u32[]{:S(2)}, u32[]{:S(2)}) collective-permute-start(bf16[256,512]{1,0:T(8,128)(2,1)S(1)} %get-tuple-element.90), channel_id=1, source_target_pairs={{0,1},{1,0},{2,3},{3,2},{4,5},{5,4},{6,7},{7,6},{8,9},{9,8},{10,11... | collective-permute-start | bytes 786440 | tf_op jit(solution)/shard_map/ppermute | solution.py:511
  60.9 0.7 project.4
  62.1 2.8 %collective-permute-done.20.refs_1_ = bf16[256,512]{1,0:T(8,128)(2,1)S(1)} collective-permute-done((bf16[256,512]{1,0:T(8,128)(2,1)S(1)}, bf16[256,512]{1,0:T(8,128)(2,1)S(1)}, u32[]{:S(2)}, u32[]{:S(2)}) %collective-permute-start.20) | collective-permute-done | bytes 262176 | tf_op jit(solution)/shard_map/ppermute | solution.py:511
  64.9 0.8 finish.4.refs_2_
  65.7 4.9 %collective-permute-done.18.refs_1_ = bf16[256,512]{1,0:T(8,128)(2,1)S(1)} collective-permute-done((bf16[256,512]{1,0:T(8,128)(2,1)S(1)}, bf16[256,512]{1,0:T(8,128)(2,1)S(1)}, u32[]{:S(2)}, u32[]{:S(2)}) %collective-permute-start.18) | collective-permute-done | bytes 262176 | tf_op jit(solution)/shard_map/ppermute | solution.py:511
  70.5 0.8 finish.5.refs_2_
  71.3 4.9 %collective-permute-done.16.refs_1_ = bf16[256,512]{1,0:T(8,128)(2,1)S(1)} collective-permute-done((bf16[256,512]{1,0:T(8,128)(2,1)S(1)}, bf16[256,512]{1,0:T(8,128)(2,1)S(1)}, u32[]{:S(2)}, u32[]{:S(2)}) %collective-permute-start.16) | collective-permute-done | bytes 262176 | tf_op jit(solution)/shard_map/ppermute | solution.py:511
  76.2 0.8 finish.6.refs_2_
  76.9 3.9 %collective-permute-done.14.refs_1_ = bf16[256,512]{1,0:T(8,128)(2,1)S(1)} collective-permute-done((bf16[256,512]{1,0:T(8,128)(2,1)S(1)}, bf16[256,512]{1,0:T(8,128)(2,1)S(1)}, u32[]{:S(2)}, u32[]{:S(2)}) %collective-permute-start.14) | collective-permute-done | bytes 262176 | tf_op jit(solution)/shard_map/ppermute | solution.py:511
  80.8 0.8 finish.7
  (98 shorter events, 6.8 us)
Async XLA Ops:
  0.0 26.9 %collective-permute-start.4 = (bf16[512,1024]{1,0:T(8,128)(2,1)}, bf16[512,1024]{1,0:T(8,128)(2,1)S(1)}, u32[]{:S(2)}, u32[]{:S(2)}) collective-permute-start(bf16[512,1024]{1,0:T(8,128)(2,1)} %bitcast.28), channel_id=1, source_target_pairs={{0,2},{2,0},{1,3},{3,1},{4,6},{6,4},{5,7},{7,5},{8,10},{10,8},{9,1... | collective-permute-start | bytes 3145736 | tf_op jit(solution)/shard_map/ppermute | solution.py:441
  1.7 11.4 %copy-start.5 = (bf16[256,512]{1,0:T(8,128)(2,1)}, bf16[256,512]{1,0:T(8,128)(2,1)S(1)}, u32[]{:S(2)}) copy-start(bf16[256,512]{1,0:T(8,128)(2,1)S(1)} %get-tuple-element.99.refs_1_) | copy-start | bytes 786436
  1.7 11.5 %collective-permute-start = (bf16[256,512]{1,0:T(8,128)(2,1)S(1)}, bf16[256,512]{1,0:T(8,128)(2,1)S(1)}, u32[]{:S(2)}, u32[]{:S(2)}) collective-permute-start(bf16[256,512]{1,0:T(8,128)(2,1)S(1)} %get-tuple-element.55.refs_0_), channel_id=1, source_target_pairs={{1,0},{0,1},{3,2},{2,3},{5,4},{4,5},{7,6},{6,7},{9,8},{8,9},{11,10... | collective-permute-start | bytes 786440 | tf_op jit(solution)/shard_map/ppermute | solution.py:437
  4.3 12.9 %collective-permute-start.2 = (bf16[256,512]{1,0:T(8,128)(2,1)S(1)}, bf16[256,512]{1,0:T(8,128)(2,1)}, u32[]{:S(2)}, u32[]{:S(2)}) collective-permute-start(bf16[256,512]{1,0:T(8,128)(2,1)S(1)} %get-tuple-element.102.refs_1_), channel_id=1, source_target_pairs={{1,0},{0,1},{3,2},{2,3},{5,4},{4,5},{7,6},{6,7},{9,8},{8,9},{11,10... | collective-permute-start | bytes 786440 | tf_op jit(solution)/shard_map/ppermute | solution.py:437
  4.4 18.4 %collective-permute-start.3 = (bf16[256,512]{1,0:T(8,128)(2,1)S(1)}, bf16[256,512]{1,0:T(8,128)(2,1)}, u32[]{:S(2)}, u32[]{:S(2)}) collective-permute-start(bf16[256,512]{1,0:T(8,128)(2,1)S(1)} %get-tuple-element.99.refs_1_), channel_id=1, source_target_pairs={{1,0},{0,1},{3,2},{2,3},{5,4},{4,5},{7,6},{6,7},{9,8},{8,9},{11,10... | collective-permute-start | bytes 786440 | tf_op jit(solution)/shard_map/ppermute | solution.py:437
  10.5 2.6 %copy-start.9 = (f32[256,8]{1,0:T(8,128)}, f32[256,8]{1,0:T(8,128)S(1)}, u32[]{:S(2)}) copy-start(f32[256,8]{1,0:T(8,128)S(1)} %get-tuple-element.91.reading_ref) | copy-start | bytes 24580
  10.5 2.7 %copy-start.11 = (f32[256,8]{1,0:T(8,128)}, f32[256,8]{1,0:T(8,128)S(1)}, u32[]{:S(2)}) copy-start(f32[256,8]{1,0:T(8,128)S(1)} %get-tuple-element.95.reading_ref) | copy-start | bytes 24580
  10.5 3.7 %copy-start.16 = (f32[1,1024]{1,0:T(1,128)S(1)}, f32[1,1024]{1,0:T(1,128)}, u32[]{:S(2)}) copy-start(f32[1,1024]{1,0:T(1,128)} %gain_ref.9) | copy-start | bytes 12292
  10.5 3.7 %copy-start.21 = (f32[1024,8]{1,0:T(8,128)S(1)}, f32[1024,8]{1,0:T(8,128)}, u32[]{:S(2)}) copy-start(f32[1024,8]{1,0:T(8,128)} %copy-done.20) | copy-start | bytes 98308
  13.2 15.0 %copy-start.1 = (bf16[128,8,4,384]{3,1,2,0:T(8,128)(2,1)}, bf16[128,8,4,384]{3,1,2,0:T(8,128)(2,1)S(1)}, u32[]{:S(2)}) copy-start(bf16[128,8,4,384]{3,1,2,0:T(8,128)(2,1)S(1)} %copy.13) | copy-start | bytes 9437188
  13.9 14.2 %collective-permute-start.1 = (bf16[256,512]{1,0:T(8,128)(2,1)S(1)}, bf16[256,512]{1,0:T(8,128)(2,1)S(1)}, u32[]{:S(2)}, u32[]{:S(2)}) collective-permute-start(bf16[256,512]{1,0:T(8,128)(2,1)S(1)} %get-tuple-element.53.refs_0_), channel_id=1, source_target_pairs={{1,0},{0,1},{3,2},{2,3},{5,4},{4,5},{7,6},{6,7},{9,8},{8,9},{11,10... | collective-permute-start | bytes 786440 | tf_op jit(solution)/shard_map/ppermute | solution.py:437
  16.7 2.9 %copy-start.17 = (s32[2,2]{1,0:T(2,128)S(1)}, s32[2,2]{1,0:T(2,128)}, u32[]{:S(2)}) copy-start(s32[2,2]{1,0:T(2,128)} %keep_ref.7) | copy-start | bytes 52
  16.7 2.9 %copy-start.18 = (f32[1,4]{1,0:T(1,128)S(1)}, f32[1,4]{1,0:T(1,128)}, u32[]{:S(2)}) copy-start(f32[1,4]{1,0:T(1,128)} %scale_ref.7) | copy-start | bytes 52
  17.2 5.6 %copy-start.6 = (bf16[256,512]{1,0:T(8,128)(2,1)S(1)}, bf16[256,512]{1,0:T(8,128)(2,1)}, u32[]{:S(2)}) copy-start(bf16[256,512]{1,0:T(8,128)(2,1)} %copy-done.5) | copy-start | bytes 786436
  19.6 5.6 %copy-start.30 = (bf16[256,512]{1,0:T(8,128)(2,1)}, bf16[256,512]{1,0:T(8,128)(2,1)S(1)}, u32[]{:S(2)}) copy-start(bf16[256,512]{1,0:T(8,128)(2,1)S(1)} %get-tuple-element.64.refs_1_) | copy-start | bytes 786436
  19.6 5.6 %copy-start.32 = (bf16[256,512]{1,0:T(8,128)(2,1)}, bf16[256,512]{1,0:T(8,128)(2,1)S(1)}, u32[]{:S(2)}) copy-start(bf16[256,512]{1,0:T(8,128)(2,1)S(1)} %get-tuple-element.65.refs_3_.refs_4_.refs_5_) | copy-start | bytes 786436
  22.8 5.3 %copy-start.25 = (bf16[2,16,128]{2,1,0:T(8,128)(2,1)S(1)}, bf16[2,16,128]{2,1,0:T(8,128)(2,1)}, u32[]{:S(2)}) copy-start(bf16[2,16,128]{2,1,0:T(8,128)(2,1)} %copy-done.24) | copy-start | bytes 24580
  25.1 3.0 %copy-start.36 = (bf16[256,512]{1,0:T(8,128)(2,1)}, bf16[256,512]{1,0:T(8,128)(2,1)S(1)}, u32[]{:S(2)}) copy-start(bf16[256,512]{1,0:T(8,128)(2,1)S(1)} %get-tuple-element.68.refs_5_.refs_6_) | copy-start | bytes 786436
  25.2 4.8 %copy-start.34 = (bf16[256,512]{1,0:T(8,128)(2,1)}, bf16[256,512]{1,0:T(8,128)(2,1)S(1)}, u32[]{:S(2)}) copy-start(bf16[256,512]{1,0:T(8,128)(2,1)S(1)} %get-tuple-element.67.refs_2_) | copy-start | bytes 786436
  26.8 3.1 %copy-start.3 = (bf16[256,512]{1,0:T(8,128)(2,1)}, bf16[256,512]{1,0:T(8,128)(2,1)S(1)}, u32[]{:S(2)}) copy-start(bf16[256,512]{1,0:T(8,128)(2,1)S(1)} %attention.6.local_ref) | copy-start | bytes 786436
  32.0 6.8 %collective-permute-start.10 = (bf16[272,128]{1,0:T(8,128)(2,1)}, bf16[272,128]{1,0:T(8,128)(2,1)}, u32[]{:S(2)}, u32[]{:S(2)}) collective-permute-start(bf16[272,128]{1,0:T(8,128)(2,1)} %get-tuple-element.73.refs_0_), channel_id=1, source_target_pairs={{0,8},{4,12},{8,0},{12,4},{16,24},{20,28},{24,16},{28,20},{1,9},{5... | collective-permute-start | bytes 208904 | tf_op jit(solution)/shard_map/ppermute | solution.py:478
  33.8 8.7 %collective-permute-start.11 = (bf16[272,128]{1,0:T(8,128)(2,1)}, bf16[272,128]{1,0:T(8,128)(2,1)S(1)}, u32[]{:S(2)}, u32[]{:S(2)}) collective-permute-start(bf16[272,128]{1,0:T(8,128)(2,1)} %get-tuple-element.73.refs_0_), channel_id=1, source_target_pairs={{0,12},{4,8},{8,4},{12,0},{16,28},{20,24},{24,20},{28,16},{1,13},{... | collective-permute-start | bytes 208904 | tf_op jit(solution)/shard_map/ppermute | solution.py:478
  35.1 7.3 %collective-permute-start.9 = (bf16[272,128]{1,0:T(8,128)(2,1)}, bf16[272,128]{1,0:T(8,128)(2,1)S(1)}, u32[]{:S(2)}, u32[]{:S(2)}) collective-permute-start(bf16[272,128]{1,0:T(8,128)(2,1)} %get-tuple-element.73.refs_0_), channel_id=1, source_target_pairs={{0,4},{4,0},{8,12},{12,8},{16,20},{20,16},{24,28},{28,24},{1,5},{5... | collective-permute-start | bytes 208904 | tf_op jit(solution)/shard_map/ppermute | solution.py:478
  35.5 10.8 %collective-permute-start.5 = (bf16[272,128]{1,0:T(8,128)(2,1)}, bf16[272,128]{1,0:T(8,128)(2,1)S(1)}, u32[]{:S(2)}, u32[]{:S(2)}) collective-permute-start(bf16[272,128]{1,0:T(8,128)(2,1)} %copy-done.13), channel_id=1, source_target_pairs={{0,4},{4,0},{8,12},{12,8},{16,20},{20,16},{24,28},{28,24},{1,5},{5... | collective-permute-start | bytes 208904 | tf_op jit(solution)/shard_map/ppermute | solution.py:478
  37.2 9.1 %collective-permute-start.6 = (bf16[272,128]{1,0:T(8,128)(2,1)}, bf16[272,128]{1,0:T(8,128)(2,1)S(1)}, u32[]{:S(2)}, u32[]{:S(2)}) collective-permute-start(bf16[272,128]{1,0:T(8,128)(2,1)} %copy-done.13), channel_id=1, source_target_pairs={{0,8},{4,12},{8,0},{12,4},{16,24},{20,28},{24,16},{28,20},{1,9},{5... | collective-permute-start | bytes 208904 | tf_op jit(solution)/shard_map/ppermute | solution.py:478
  38.7 7.5 %collective-permute-start.7 = (bf16[272,128]{1,0:T(8,128)(2,1)}, bf16[272,128]{1,0:T(8,128)(2,1)S(1)}, u32[]{:S(2)}, u32[]{:S(2)}) collective-permute-start(bf16[272,128]{1,0:T(8,128)(2,1)} %copy-done.13), channel_id=1, source_target_pairs={{0,12},{4,8},{8,4},{12,0},{16,28},{20,24},{24,20},{28,16},{1,13},{... | collective-permute-start | bytes 208904 | tf_op jit(solution)/shard_map/ppermute | solution.py:478
  41.4 4.8 %copy-start.14 = (bf16[272,128]{1,0:T(8,128)(2,1)S(1)}, bf16[272,128]{1,0:T(8,128)(2,1)}, u32[]{:S(2)}) copy-start(bf16[272,128]{1,0:T(8,128)(2,1)} %copy-done.13) | copy-start | bytes 208900
  41.4 5.5 %copy-start.27 = (bf16[256,512]{1,0:T(8,128)(2,1)S(1)}, bf16[256,512]{1,0:T(8,128)(2,1)}, u32[]{:S(2)}) copy-start(bf16[256,512]{1,0:T(8,128)(2,1)} %copy-done.26) | copy-start | bytes 786436
  41.4 5.5 %copy-start.29 = (bf16[256,512]{1,0:T(8,128)(2,1)S(1)}, bf16[256,512]{1,0:T(8,128)(2,1)}, u32[]{:S(2)}) copy-start(bf16[256,512]{1,0:T(8,128)(2,1)} %copy-done.28) | copy-start | bytes 786436
  41.4 5.5 %copy-start.31 = (bf16[256,512]{1,0:T(8,128)(2,1)S(1)}, bf16[256,512]{1,0:T(8,128)(2,1)}, u32[]{:S(2)}) copy-start(bf16[256,512]{1,0:T(8,128)(2,1)} %copy-done.30) | copy-start | bytes 786436
  41.5 5.5 %copy-start.33 = (bf16[256,512]{1,0:T(8,128)(2,1)S(1)}, bf16[256,512]{1,0:T(8,128)(2,1)}, u32[]{:S(2)}) copy-start(bf16[256,512]{1,0:T(8,128)(2,1)} %copy-done.32) | copy-start | bytes 786436
  41.5 5.5 %copy-start.35 = (bf16[256,512]{1,0:T(8,128)(2,1)S(1)}, bf16[256,512]{1,0:T(8,128)(2,1)}, u32[]{:S(2)}) copy-start(bf16[256,512]{1,0:T(8,128)(2,1)} %copy-done.34) | copy-start | bytes 786436
  41.5 5.5 %copy-start.37 = (bf16[256,512]{1,0:T(8,128)(2,1)S(1)}, bf16[256,512]{1,0:T(8,128)(2,1)}, u32[]{:S(2)}) copy-start(bf16[256,512]{1,0:T(8,128)(2,1)} %copy-done.36) | copy-start | bytes 786436
  42.4 10.3 %copy-start.12 = (f32[256,8]{1,0:T(8,128)S(1)}, f32[256,8]{1,0:T(8,128)}, u32[]{:S(2)}) copy-start(f32[256,8]{1,0:T(8,128)} %copy-done.11) | copy-start | bytes 24580
  42.4 10.6 %copy-start.10 = (f32[256,8]{1,0:T(8,128)S(1)}, f32[256,8]{1,0:T(8,128)}, u32[]{:S(2)}) copy-start(f32[256,8]{1,0:T(8,128)} %copy-done.9) | copy-start | bytes 24580
  43.6 7.2 %collective-permute-start.12 = (bf16[272,128]{1,0:T(8,128)(2,1)S(1)}, bf16[272,128]{1,0:T(8,128)(2,1)S(1)}, u32[]{:S(2)}, u32[]{:S(2)}) collective-permute-start(bf16[272,128]{1,0:T(8,128)(2,1)S(1)} %get-tuple-element.74.refs_0_), channel_id=1, source_target_pairs={{0,16},{4,20},{8,24},{12,28},{16,0},{20,4},{24,8},{28,12},{1,17},{... | collective-permute-start | bytes 208904 | tf_op jit(solution)/shard_map/ppermute | solution.py:489
  46.4 6.0 %collective-permute-start.8 = (bf16[272,128]{1,0:T(8,128)(2,1)S(1)}, bf16[272,128]{1,0:T(8,128)(2,1)S(1)}, u32[]{:S(2)}, u32[]{:S(2)}) collective-permute-start(bf16[272,128]{1,0:T(8,128)(2,1)S(1)} %get-tuple-element.72.refs_0_), channel_id=1, source_target_pairs={{0,16},{4,20},{8,24},{12,28},{16,0},{20,4},{24,8},{28,12},{1,17},{... | collective-permute-start | bytes 208904 | tf_op jit(solution)/shard_map/ppermute | solution.py:489
  47.0 6.8 %copy-start.4 = (bf16[256,512]{1,0:T(8,128)(2,1)S(1)}, bf16[256,512]{1,0:T(8,128)(2,1)}, u32[]{:S(2)}) copy-start(bf16[256,512]{1,0:T(8,128)(2,1)} %copy-done.3) | copy-start | bytes 786436
  47.0 6.8 %copy-start.8 = (f32[256,8]{1,0:T(8,128)S(1)}, f32[256,8]{1,0:T(8,128)}, u32[]{:S(2)}) copy-start(f32[256,8]{1,0:T(8,128)} %copy-done.7) | copy-start | bytes 24580
  49.0 6.0 %copy-start = (bf16[1,4,128,1024]{3,2,1,0:T(8,128)(2,1)S(1)}, bf16[1,4,128,1024]{3,2,1,0:T(8,128)(2,1)}, u32[]{:S(2)}) copy-start(bf16[1,4,128,1024]{3,2,1,0:T(8,128)(2,1)} %param.16) | copy-start | bytes 3145732
  53.0 2.0 %collective-permute-start.19 = (bf16[256,512]{1,0:T(8,128)(2,1)S(1)}, bf16[256,512]{1,0:T(8,128)(2,1)S(1)}, u32[]{:S(2)}, u32[]{:S(2)}) collective-permute-start(bf16[256,512]{1,0:T(8,128)(2,1)S(1)} %recall.7.own_ref), channel_id=1, source_target_pairs={{0,2},{2,0},{1,3},{3,1},{4,6},{6,4},{5,7},{7,5},{8,10},{10,8},{9,1... | collective-permute-start | bytes 786440 | tf_op jit(solution)/shard_map/ppermute | solution.py:506
  53.3 4.0 %collective-permute-start.17 = (bf16[256,512]{1,0:T(8,128)(2,1)S(1)}, bf16[256,512]{1,0:T(8,128)(2,1)S(1)}, u32[]{:S(2)}, u32[]{:S(2)}) collective-permute-start(bf16[256,512]{1,0:T(8,128)(2,1)S(1)} %recall.6.own_ref), channel_id=1, source_target_pairs={{0,2},{2,0},{1,3},{3,1},{4,6},{6,4},{5,7},{7,5},{8,10},{10,8},{9,1... | collective-permute-start | bytes 786440 | tf_op jit(solution)/shard_map/ppermute | solution.py:506
  54.1 4.5 %collective-permute-start.15 = (bf16[256,512]{1,0:T(8,128)(2,1)S(1)}, bf16[256,512]{1,0:T(8,128)(2,1)S(1)}, u32[]{:S(2)}, u32[]{:S(2)}) collective-permute-start(bf16[256,512]{1,0:T(8,128)(2,1)S(1)} %recall.5.own_ref), channel_id=1, source_target_pairs={{0,2},{2,0},{1,3},{3,1},{4,6},{6,4},{5,7},{7,5},{8,10},{10,8},{9,1... | collective-permute-start | bytes 786440 | tf_op jit(solution)/shard_map/ppermute | solution.py:506
  54.4 6.4 %collective-permute-start.13 = (bf16[256,512]{1,0:T(8,128)(2,1)S(1)}, bf16[256,512]{1,0:T(8,128)(2,1)S(1)}, u32[]{:S(2)}, u32[]{:S(2)}) collective-permute-start(bf16[256,512]{1,0:T(8,128)(2,1)S(1)} %recall.4.own_ref), channel_id=1, source_target_pairs={{0,2},{2,0},{1,3},{3,1},{4,6},{6,4},{5,7},{7,5},{8,10},{10,8},{9,1... | collective-permute-start | bytes 786440 | tf_op jit(solution)/shard_map/ppermute | solution.py:506
  55.7 9.2 %collective-permute-start.20 = (bf16[256,512]{1,0:T(8,128)(2,1)S(1)}, bf16[256,512]{1,0:T(8,128)(2,1)S(1)}, u32[]{:S(2)}, u32[]{:S(2)}) collective-permute-start(bf16[256,512]{1,0:T(8,128)(2,1)S(1)} %get-tuple-element.98), channel_id=1, source_target_pairs={{0,1},{1,0},{2,3},{3,2},{4,5},{5,4},{6,7},{7,6},{8,9},{9,8},{10,11... | collective-permute-start | bytes 786440 | tf_op jit(solution)/shard_map/ppermute | solution.py:511
  58.0 12.6 %collective-permute-start.18 = (bf16[256,512]{1,0:T(8,128)(2,1)S(1)}, bf16[256,512]{1,0:T(8,128)(2,1)S(1)}, u32[]{:S(2)}, u32[]{:S(2)}) collective-permute-start(bf16[256,512]{1,0:T(8,128)(2,1)S(1)} %get-tuple-element.94), channel_id=1, source_target_pairs={{0,1},{1,0},{2,3},{3,2},{4,5},{5,4},{6,7},{7,6},{8,9},{9,8},{10,11... | collective-permute-start | bytes 786440 | tf_op jit(solution)/shard_map/ppermute | solution.py:511
  59.3 16.9 %collective-permute-start.16 = (bf16[256,512]{1,0:T(8,128)(2,1)S(1)}, bf16[256,512]{1,0:T(8,128)(2,1)S(1)}, u32[]{:S(2)}, u32[]{:S(2)}) collective-permute-start(bf16[256,512]{1,0:T(8,128)(2,1)S(1)} %get-tuple-element.90), channel_id=1, source_target_pairs={{0,1},{1,0},{2,3},{3,2},{4,5},{5,4},{6,7},{7,6},{8,9},{9,8},{10,11... | collective-permute-start | bytes 786440 | tf_op jit(solution)/shard_map/ppermute | solution.py:511
  61.6 19.3 %collective-permute-start.14 = (bf16[256,512]{1,0:T(8,128)(2,1)S(1)}, bf16[256,512]{1,0:T(8,128)(2,1)S(1)}, u32[]{:S(2)}, u32[]{:S(2)}) collective-permute-start(bf16[256,512]{1,0:T(8,128)(2,1)S(1)} %get-tuple-element.86), channel_id=1, source_target_pairs={{0,1},{1,0},{2,3},{3,2},{4,5},{5,4},{6,7},{7,6},{8,9},{9,8},{10,11... | collective-permute-start | bytes 786440 | tf_op jit(solution)/shard_map/ppermute | solution.py:511
  (11 other events, 11.1 us)

commit v7 on v4

--- a/solution.py
+++ b/solution.py
@@ -10,6 +10,7 @@
 
 BLOCK = 512
 CHUNK = 256
+LAST = 128
 TAIL = 16
 EPSILON = 1e-06
 F32 = jnp.float32
@@ -48,7 +49,8 @@
     return values * lax.rsqrt(jnp.mean(values * values, axis=-1, keepdims=True) + EPSILON)
 
 
-def prepare_kernel(heads, factor, logs_ref, flags_ref, fade_ref, reading_ref, tail_ref, rows_ref):
+def prepare_kernel(heads, factor, logs_ref, flags_ref, fade_ref, tail_ref, *refs):
+    reading_refs, rows_ref = refs[:-1], refs[-1]
     length = logs_ref.shape[1]
     rows_ref[...] = jnp.zeros_like(rows_ref)
     rows_ref[:heads, :] = logs_ref[...]
@@ -64,21 +66,26 @@
         inside = (place >= block * BLOCK) & (place < (block + 1) * BLOCK)
         chosen = jnp.where(inside, flags_ref[block].astype(F32), chosen)
     fade_ref[...] = jnp.transpose(jnp.exp(last - running) * chosen)
-    reading_ref[...] = jnp.transpose(jnp.exp(running) * factor)
+    reading = jnp.transpose(jnp.exp(running) * factor)
+    first = 0
+    for ref in reading_refs:
+        ref[...] = reading[first : first + ref.shape[0]]
+        first += ref.shape[0]
     decay = jnp.exp(last)
     high = decay.astype(BF16).astype(F32)
     both = jnp.concatenate([high, decay - high], axis=0)
     tail_ref[...] = jnp.broadcast_to(both, tail_ref.shape).astype(BF16)
 
 
-def prepare(logs, flags, dim, factor):
+def prepare(logs, flags, dim, factor, sizes):
     heads, length = logs.shape
     lines = TAIL // 2
     return pl.pallas_call(
         functools.partial(prepare_kernel, heads, factor),
         in_specs=[VMEM, SMEM],
-        out_specs=[VMEM] * 3,
-        out_shape=[struct((length, lines), F32)] * 2 + [struct((TAIL, dim))],
+        out_specs=[VMEM] * (2 + len(sizes)),
+        out_shape=[struct((length, lines), F32), struct((TAIL, dim))]
+        + [struct((size, lines), F32) for size in sizes],
         scratch_shapes=[pltpu.VMEM((lines, length), F32)],
         compiler_params=params(),
         cost_estimate=cost(40 * lines * length, 0),
@@ -202,41 +209,43 @@
     )(me, gain, w, *xs)
 
 
-def attention_kernel(chunk, heads, dim, keep_ref, scale_ref, q_ref, *refs):
-    k_refs, v_refs, out_ref = refs[: chunk + 1], refs[chunk + 1 : -1], refs[-1]
+def attention_kernel(first, heads, dim, keep_ref, scale_ref, q_ref, *refs):
+    count = len(refs) // 2
+    k_refs, v_refs, out_ref = refs[:count], refs[count:-1], refs[-1]
     rows = q_ref.shape[0]
-    per = BLOCK // rows
-    block = chunk // per
+    block = first // BLOCK
     causal = lax.broadcasted_iota(jnp.int32, (rows, rows), 1) <= lax.broadcasted_iota(
         jnp.int32, (rows, rows), 0
     )
-    ones = jnp.ones((rows, dim), BF16)
     for h in range(heads):
         cols = slice(h * dim, (h + 1) * dim)
         query = q_ref[:, cols]
         scale = scale_ref[0, h] * (1.0 / math.sqrt(dim))
-        total = None
-        for j in range(chunk + 1):
+        total, at = None, 0
+        for j in range(count):
+            keys = k_refs[j].shape[0]
             powers = jnp.exp(dot_nt(query, k_refs[j][:, cols]) * scale)
-            if j == chunk:
+            if at == first:
                 powers = jnp.where(causal, powers, 0.0)
+            ones = jnp.ones((keys, dim), BF16)
             part = dot(powers.astype(BF16), jnp.concatenate([v_refs[j][:, cols], ones], axis=1))
-            if j // per < block:
-                part = jnp.where(keep_ref[block, j // per] == 1, part, 0.0)
+            if at // BLOCK < block:
+                part = jnp.where(keep_ref[block, at // BLOCK] == 1, part, 0.0)
             total = part if total is None else total + part
+            at += keys
         out_ref[:, cols] = (total[:, :dim] / total[:, dim:]).astype(BF16)
 
 
-def attention(chunk, keep, scale, q, ks, vs, heads, dim):
+def attention(first, keep, scale, q, ks, vs, heads, dim):
     rows = q.shape[0]
     return pl.pallas_call(
-        functools.partial(attention_kernel, chunk, heads, dim),
+        functools.partial(attention_kernel, first, heads, dim),
         in_specs=[SMEM, SMEM] + [VMEM] * (1 + len(ks) + len(vs)),
         out_specs=VMEM,
         out_shape=struct(q.shape),
         compiler_params=params(),
         cost_estimate=cost(
-            (chunk + 1) * heads * 8 * rows * rows * dim, 0, (chunk + 1) * heads * rows * rows
+            heads * 8 * rows * (first + rows) * dim, 0, heads * rows * (first + rows)
         ),
         name="attention",
     )(keep, scale, q, *ks, *vs)
@@ -320,17 +329,16 @@
     )(place, before, decay, *totals)
 
 
-def recall_kernel(heads, dim, first, reading_ref, q_ref, local_ref, state_ref, out_ref):
+def recall_kernel(heads, dim, reading_ref, q_ref, local_ref, state_ref, out_ref):
     for h in range(heads):
         cols = slice(h * dim, (h + 1) * dim)
-        reading = reading_ref[first : first + q_ref.shape[0], h : h + 1]
-        recalled = dot(q_ref[:, cols], state_ref[cols, :]) * reading
+        recalled = dot(q_ref[:, cols], state_ref[cols, :]) * reading_ref[:, h : h + 1]
         out_ref[:, cols] = (local_ref[:, cols].astype(F32) + recalled).astype(BF16)
 
 
-def recall(reading, q, local, state, heads, dim, first):
-    return pl.pallas_call(
-        functools.partial(recall_kernel, heads, dim, first),
+def recall(reading, q, local, state, heads, dim):
+    return pl.pallas_call(
+        functools.partial(recall_kernel, heads, dim),
         in_specs=[VMEM] * 4,
         out_specs=VMEM,
         out_shape=struct(q.shape),
@@ -371,8 +379,9 @@
     refs[-1][...] = total.astype(BF16)
 
 
-def finish(parts, result, chunk, length):
+def finish(parts, result, first, length):
     rows, width = parts[0].shape
+    chunk = first // rows
     whole = pl.BlockSpec((rows, width), lambda i: (0, 0))
     more = [] if result is None else [result]
     return pl.pallas_call(
@@ -401,7 +410,9 @@
 ):
     x = residual_signal[0]
     length = x.shape[0]
-    chunks = length // CHUNK
+    sizes = [CHUNK] * (length // CHUNK - 1) + [LAST] * (CHUNK // LAST)
+    firsts = [sum(sizes[:c]) for c in range(len(sizes))]
+    chunks = len(sizes)
     shards = lax.axis_size("head")
     blocks = lax.axis_size("tm")
     heads = triple_projector.shape[2]
@@ -411,40 +422,40 @@
     swap_streams = [(0, 1), (1, 0)]
     tied = lambda *arrays: lax.optimization_barrier(arrays)
 
+    own_w = emission_projector[0].reshape(heads * dim, -1)
+    side_w = lax.ppermute(
+        sideways_coupling_coef[0].reshape(heads * dim, -1), "stream", swap_streams
+    )
+    fade, tail, *readings = prepare(
+        recall_retained_logshare[0],
+        recall_store_flags,
+        dim,
+        1.0 / math.sqrt(dim * length * blocks),
+        sizes,
+    )
     received = []
-    for c in range(chunks):
-        piece = x[c * CHUNK : (c + 1) * CHUNK]
+    for first, size in zip(firsts, sizes):
+        piece = x[first : first + size]
+        if size < CHUNK:
+            piece, fade = tied(piece, fade)
         xs = [piece]
         for k in range(1, shards):
             xs.append(lax.ppermute(piece, "head", [((d + k) % shards, d) for d in range(shards)]))
         received.append(xs)
-
-    own_w = emission_projector[0].reshape(heads * dim, -1)
-    side_w = lax.ppermute(
-        sideways_coupling_coef[0].reshape(heads * dim, -1), "stream", swap_streams
-    )
-    fade, reading, tail = prepare(
-        recall_retained_logshare[0],
-        recall_store_flags,
-        dim,
-        1.0 / math.sqrt(dim * length * blocks),
-    )
     gain = prescale_amplifier
     w = triple_projector[0].reshape(-1, 3 * heads * dim)
 
     qs, ks, vs, locals_ = [], [], [], []
     summary = None
-    for c in range(chunks - 1):
-        q, k, v, summary = qkv(
-            me, gain, w, fade, summary, received[c], heads, dim, c * CHUNK
-        )
+    for c, first in enumerate(firsts[:-1]):
+        q, k, v, summary = qkv(me, gain, w, fade, summary, received[c], heads, dim, first)
         qs.append(q)
         ks.append(k)
         vs.append(v)
-        locals_.append(attention(c, tile_retain_grid, score_scaler, q, ks, vs, heads, dim))
+        locals_.append(attention(first, tile_retain_grid, score_scaler, q, ks, vs, heads, dim))
     summary, *locals_ = tied(summary, *locals_)
     k, v, sent = last_keys_values(
-        me, gain, w, fade, summary, tail, received[-1], heads, dim, (chunks - 1) * CHUNK
+        me, gain, w, fade, summary, tail, received[-1], heads, dim, firsts[-1]
     )
     ks.append(k)
     vs.append(v)
@@ -454,7 +465,7 @@
         lax.ppermute(sent, "tm", [(d, d ^ k) for d in range(blocks)]) for k in range(1, quad_size)
     ]
     qs.append(last_queries(me, gain, w, received[-1], heads, dim))
-    locals_.append(attention(chunks - 1, tile_retain_grid, score_scaler, qs[-1], ks, vs, heads, dim))
+    locals_.append(attention(firsts[-1], tile_retain_grid, score_scaler, qs[-1], ks, vs, heads, dim))
     *loads, locals_[-1] = tied(*loads, locals_[-1])
     before, decay, total = quad(lax.rem(place, quad_size), loads, heads, dim)
     totals = [total] + [
@@ -464,8 +475,8 @@
     state = entering(lax.div(place, quad_size), before, decay, totals, heads, dim)
 
     result = None
-    for c in range(chunks):
-        head_out = recall(reading, qs[c], locals_[c], state, heads, dim, c * CHUNK)
+    for c in [chunks - 2, *range(chunks - 2), chunks - 1]:
+        head_out = recall(readings[c], qs[c], locals_[c], state, heads, dim)
         side = lax.ppermute(head_out, "stream", swap_streams)
         outs = project(me, head_out, side, own_w, side_w, shards)
         parts = [outs[0]]
@@ -473,7 +484,9 @@
             parts.append(
                 lax.ppermute(outs[k], "head", [(d, (d + k) % shards) for d in range(shards)])
             )
-        result = finish(parts, result, c, length)
+        if result is None:
+            state, parts[0] = tied(state, parts[0])
+        result = finish(parts, result, firsts[c], length)
     return result[None]
 
 

time: 76.5 us -> 97.8 us (1.28)
  Pallas kernels: 24 us -> 38 us
  local copies, waits for them, and re-layouts: 8.64 us -> 15.2 us
  waiting for transfers between devices: 26.2 us -> 23.8 us
  starting transfers between devices: 17.1 us -> 19.3 us
    pallas_call x4 -> x5, Pallas kernels: 2.83 us -> 9.22 us  [project(): pl.pallas_call(functools.partial(project_kernel, shards), in_specs=[SMEM]...]
    unnamed x17 -> x109, local copies, waits for them, and re-layouts: 7.37 us -> 11.6 us
    ppermute x4 -> x5, waiting for transfers between devices: 16.4 us -> 12.9 us  [per_device(): lax.ppermute(outs[k], 'head', [(d, (d + k) % shards) for d in range(shard...]
    pallas_call x3 -> x4, Pallas kernels: 7.1 us -> 9.71 us  [qkv(): pl.pallas_call(functools.partial(qkv_kernel, heads, dim, first), in_specs...]
    slice x1 -> x2, local copies, waits for them, and re-layouts: 1.27 us -> 3.59 us  [per_device(): piece = x[first:first + size]]
    ppermute x4 -> x5, starting transfers between devices: 5.14 us -> 7.02 us  [per_device(): lax.ppermute(piece, 'head', [((d + k) % shards, d) for d in range(shards)])]
    pallas_call x1, Pallas kernels: 1.11 us -> 2.46 us  [last_keys_values(): pl.pallas_call(functools.partial(last_kernel, heads, dim, first), in_spec...]
    ppermute x4 -> x5, waiting for transfers between devices: 0.01 us -> 1.35 us  [per_device(): side = lax.ppermute(head_out, 'stream', swap_streams)]
  transfers between devices with their start and end apart: 17 -> 20, of which waited for: 9 -> 5; matrix products, arithmetic and copies ran while one was open for 5% -> 4% of each run, Pallas kernels for 31% -> 36%
where the time goes in v7:
time: 97.8 us; the launch traced here: 97.2 us
  Pallas kernels  38 us (39%)
  waiting for transfers between devices  23.8 us (24%)
  starting transfers between devices  19.3 us (20%)
  local copies, waits for them, and re-layouts  15.2 us (16%)
    ppermute x5, waiting for transfers between devices, per_device(): lax.ppermute(outs[k], 'head', [(d, (d + k) % shards) for d in range(shard...  12.9 us
    unnamed x109, local copies, waits for them, and re-layouts  11.6 us
    pallas_call x4, Pallas kernels, qkv(): pl.pallas_call(functools.partial(qkv_kernel, heads, dim, first), in_specs...  9.71 us
    pallas_call x5, Pallas kernels, project(): pl.pallas_call(functools.partial(project_kernel, shards), in_specs=[SMEM]...  9.22 us
    pallas_call x5, Pallas kernels, attention(): pl.pallas_call(functools.partial(attention_kernel, first, heads, dim), in...  7.14 us
    ppermute x5, starting transfers between devices, per_device(): lax.ppermute(piece, 'head', [((d + k) % shards, d) for d in range(shards)])  7.02 us
    ppermute x1, waiting for transfers between devices, per_device(): lax.ppermute(total, 'tm', [(d, d ^ quad_size * k) for d in range(blocks)])  6.2 us
    ppermute x5, starting transfers between devices, per_device(): lax.ppermute(outs[k], 'head', [(d, (d + k) % shards) for d in range(shard...  4.76 us
  transfers between devices with their start and end apart: 20, of which 5 were waited for; matrix products, arithmetic and copies ran while one was open for 4% of the time, Pallas kernels for 36%

profile of v7, /device:TPU:0, one launch (start us, length us, event | category | flops | bytes accessed | tf_op | source)
XLA Modules:
  0.0 97.2 jit_solution(6731274144250557954)
XLA Ops:
  0.0 2.0 %slice_bitcast_fusion = (bf16[256,512]{1,0:T(8,128)(2,1)}, bf16[256,512]{1,0:T(8,128)(2,1)S(1)}, bf16[256,512]{1,0:T(8,128)(2,1)}) fusion(bf16[1,1024,512]{2,1,0:T(8,128)(2,1)} %param.9), kind=kLoop, calls=%fused_computation | loop fusion | bytes 1572864 | tf_op jit(solution)/shard_map/slice | solution.py:438
  2.0 3.0 %collective-permute-start.1 = (bf16[256,512]{1,0:T(8,128)(2,1)S(1)}, bf16[256,512]{1,0:T(8,128)(2,1)}, u32[]{:S(2)}, u32[]{:S(2)}) collective-permute-start(bf16[256,512]{1,0:T(8,128)(2,1)S(1)} %get-tuple-element.116.refs_0_), channel_id=1, source_target_pairs={{1,0},{0,1},{3,2},{2,3},{5,4},{4,5},{7,6},{6,7},{9,8},{8,9},{11,10... | collective-permute-start | bytes 786440 | tf_op jit(solution)/shard_map/ppermute | solution.py:443
  5.0 2.0 %collective-permute-start.3 = (bf16[256,512]{1,0:T(8,128)(2,1)}, bf16[256,512]{1,0:T(8,128)(2,1)}, u32[]{:S(2)}, u32[]{:S(2)}) collective-permute-start(bf16[256,512]{1,0:T(8,128)(2,1)} %get-tuple-element.115.refs_1_), channel_id=1, source_target_pairs={{1,0},{0,1},{3,2},{2,3},{5,4},{4,5},{7,6},{6,7},{9,8},{8,9},{11,10... | collective-permute-start | bytes 786440 | tf_op jit(solution)/shard_map/ppermute | solution.py:443
  7.0 1.6 %slice_bitcast_fusion.3 = (bf16[128,512]{1,0:T(8,128)(2,1)}, bf16[128,512]{1,0:T(8,128)(2,1)S(1)}) fusion(bf16[1,1024,512]{2,1,0:T(8,128)(2,1)} %param.9), kind=kLoop, calls=%fused_computation.3 | loop fusion | bytes 524288 | tf_op jit(solution)/shard_map/slice | solution.py:438
  8.6 0.7 copy-done.50
  9.3 0.7 copy-done.53
  10.0 1.4 %prepare.1 = (f32[1024,8]{1,0:T(8,128)S(1)}, bf16[16,128]{1,0:T(8,128)(2,1)S(1)}, f32[256,8]{1,0:T(8,128)S(1)}, f32[256,8]{1,0:T(8,128)S(1)}, f32[256,8]{1,0:T(8...) custom-call(f32[4,1024]{1,0:T(4,128)S(1)} %bitcast.30, s32[2]{0:T(128)S(1)} %copy-done.53), custom_call_target="tpu_custom_call" | custom-call | flops 327680 | tf_op jit(solution)/shard_map/prepare/pallas_call | solution.py:83
  11.4 0.8 copy-done.3
  12.8 0.7 copy-done.41
  13.5 0.7 copy-done.43
  15.4 2.0 %collective-permute-start = (bf16[128,512]{1,0:T(8,128)(2,1)S(1)}, bf16[128,512]{1,0:T(8,128)(2,1)}, u32[]{:S(2)}, u32[]{:S(2)}) collective-permute-start(bf16[128,512]{1,0:T(8,128)(2,1)S(1)} %get-tuple-element.63.refs_0_), channel_id=1, source_target_pairs={{1,0},{0,1},{3,2},{2,3},{5,4},{4,5},{7,6},{6,7},{9,8},{8,9},{11,10... | collective-permute-start | bytes 393224 | tf_op jit(solution)/shard_map/ppermute | solution.py:443
  17.4 2.5 %copy.14 = bf16[128,8,4,384]{3,1,2,0:T(8,128)(2,1)S(1)} copy(bf16[128,8,4,384]{3,2,1,0:T(4,128)(2,1)} %bitcast.31) | data formatting | bytes 6291456
  20.0 0.9 copy-done.34
  21.0 2.3 %qkv.4 = (bf16[256,512]{1,0:T(8,128)(2,1)S(1)}, bf16[256,512]{1,0:T(8,128)(2,1)S(1)}, bf16[256,512]{1,0:T(8,128)(2,1)S(1)}, f32[4,128,128]{2,1,0:T(8,128)S(1)}) custom-call(s32[1]{0:T(128)} %bitcast.me_ref, f32[1,1024]{1,0:T(1,128)S(1)} %copy-done.49, bf16[1024,1536]{1,0:T(8,128)(2,1)S(1)} %bitcast.19, f32[1024,8]{1,0:T(8,128)S(1)} %copy-done.4, ...), custom_call_target="tpu_custom_call" | custom-call | flops 1610612736 | tf_op jit(solution)/shard_map/qkv/pallas_call | solution.py:147
  23.3 2.6 %qkv.5 = (bf16[256,512]{1,0:T(8,128)(2,1)S(1)}, bf16[256,512]{1,0:T(8,128)(2,1)S(1)}, bf16[256,512]{1,0:T(8,128)(2,1)S(1)}, f32[4,128,128]{2,1,0:T(8,128)S(1)}) custom-call(s32[1]{0:T(128)} %bitcast.me_ref, f32[1,1024]{1,0:T(1,128)S(1)} %copy-done.49, bf16[1024,1536]{1,0:T(8,128)(2,1)S(1)} %bitcast.20, f32[1024,8]{1,0:T(8,128)S(1)} %copy-done.4, ...), custom_call_target="tpu_custom_call" | custom-call | flops 1610612736 | tf_op jit(solution)/shard_map/qkv/pallas_call | solution.py:147
  26.0 2.7 %qkv.6 = (bf16[256,512]{1,0:T(8,128)(2,1)S(1)}, bf16[256,512]{1,0:T(8,128)(2,1)S(1)}, bf16[256,512]{1,0:T(8,128)(2,1)S(1)}, f32[4,128,128]{2,1,0:T(8,128)S(1)}) custom-call(s32[1]{0:T(128)} %bitcast.me_ref, f32[1,1024]{1,0:T(1,128)S(1)} %copy-done.49, bf16[1024,1536]{1,0:T(8,128)(2,1)S(1)} %bitcast.21, f32[1024,8]{1,0:T(8,128)S(1)} %copy-done.4, ...), custom_call_target="tpu_custom_call" | custom-call | flops 1610612736 | tf_op jit(solution)/shard_map/qkv/pallas_call | solution.py:147
  28.7 2.2 %qkv.7 = (bf16[128,512]{1,0:T(8,128)(2,1)S(1)}, bf16[128,512]{1,0:T(8,128)(2,1)S(1)}, bf16[128,512]{1,0:T(8,128)(2,1)S(1)}, f32[4,128,128]{2,1,0:T(8,128)S(1)}) custom-call(s32[1]{0:T(128)} %bitcast.me_ref, f32[1,1024]{1,0:T(1,128)S(1)} %copy-done.49, bf16[1024,1536]{1,0:T(8,128)(2,1)S(1)} %bitcast.22, f32[1024,8]{1,0:T(8,128)S(1)} %copy-done.4, ...), custom_call_target="tpu_custom_call" | custom-call | flops 805306368 | tf_op jit(solution)/shard_map/qkv/pallas_call | solution.py:147
  30.9 1.4 %attention.8.local_ref = bf16[128,512]{1,0:T(8,128)(2,1)S(1)} custom-call(s32[2,2]{1,0:T(2,128)S(1)} %copy-done.51, f32[1,4]{1,0:T(1,128)S(1)} %copy-done.52, bf16[128,512]{1,0:T(8,128)(2,1)S(1)} %get-tuple-element.79.q_ref, bf16[256,512]{1,0:T(8,128)(2,1)S(1)} %get-tuple-element.71.refs_0_, bf16[256,512]{1,0:T(8,128)(2,1)S(1)} %get-tuple-element.74.refs_1_, ...), custom_call_target="tpu_custom_call" | custom-call | flops 469762048 | tf_op jit(solution)/shard_map/attention/pallas_call | solution.py:241
  32.3 1.1 %attention.5.local_ref = bf16[256,512]{1,0:T(8,128)(2,1)S(1)} custom-call(s32[2,2]{1,0:T(2,128)S(1)} %copy-done.51, f32[1,4]{1,0:T(1,128)S(1)} %copy-done.52, bf16[256,512]{1,0:T(8,128)(2,1)S(1)} %get-tuple-element.70.q_ref, bf16[256,512]{1,0:T(8,128)(2,1)S(1)} %get-tuple-element.71.refs_0_, ...), custom_call_target="tpu_custom_call" | custom-call | flops 268435456 | tf_op jit(solution)/shard_map/attention/pallas_call | solution.py:241
  33.5 0.7 copy-done.15
  34.1 1.4 %attention.6.local_ref = bf16[256,512]{1,0:T(8,128)(2,1)S(1)} custom-call(s32[2,2]{1,0:T(2,128)S(1)} %copy-done.51, f32[1,4]{1,0:T(1,128)S(1)} %copy-done.52, bf16[256,512]{1,0:T(8,128)(2,1)S(1)} %get-tuple-element.73.q_ref, bf16[256,512]{1,0:T(8,128)(2,1)S(1)} %get-tuple-element.71.refs_0_, bf16[256,512]{1,0:T(8,128)(2,1)S(1)} %get-tuple-element.74.refs_1_, ...), custom_call_target="tpu_custom_call" | custom-call | flops 536870912 | tf_op jit(solution)/shard_map/attention/pallas_call | solution.py:241
  35.6 0.7 copy-done.31
  36.3 1.7 %attention.7.local_ref = bf16[256,512]{1,0:T(8,128)(2,1)S(1)} custom-call(s32[2,2]{1,0:T(2,128)S(1)} %copy-done.51, f32[1,4]{1,0:T(1,128)S(1)} %copy-done.52, bf16[256,512]{1,0:T(8,128)(2,1)S(1)} %get-tuple-element.76.q_ref, bf16[256,512]{1,0:T(8,128)(2,1)S(1)} %get-tuple-element.71.refs_0_, bf16[256,512]{1,0:T(8,128)(2,1)S(1)} %get-tuple-element.74.refs_1_, ...), custom_call_target="tpu_custom_call" | custom-call | flops 805306368 | tf_op jit(solution)/shard_map/attention/pallas_call | solution.py:241
  38.0 2.5 %last_keys_values.1 = (bf16[128,512]{1,0:T(8,128)(2,1)S(1)}, bf16[128,512]{1,0:T(8,128)(2,1)S(1)}, bf16[528,128]{1,0:T(8,128)(2,1)}) custom-call(s32[1]{0:T(128)} %bitcast.me_ref, f32[1,1024]{1,0:T(1,128)S(1)} %copy-done.49, bf16[1024,1536]{1,0:T(8,128)(2,1)S(1)} %bitcast.23, f32[1024,8]{1,0:T(8,128)S(1)} %copy-done.4, ...), custom_call_target="tpu_custom_call" | custom-call | flops 603979776 | tf_op jit(solution)/shard_map/last_keys_values/pallas_call | solution.py:178
  41.1 0.7 copy-done.37
  41.8 1.5 %collective-permute-start.5 = (bf16[528,128]{1,0:T(8,128)(2,1)}, bf16[528,128]{1,0:T(8,128)(2,1)}, u32[]{:S(2)}, u32[]{:S(2)}) collective-permute-start(bf16[528,128]{1,0:T(8,128)(2,1)} %get-tuple-element.88.refs_0_), channel_id=1, source_target_pairs={{0,4},{4,0},{8,12},{12,8},{16,20},{20,16},{24,28},{28,24},{1,5},{5... | collective-permute-start | bytes 405512 | tf_op jit(solution)/shard_map/ppermute | solution.py:465
  43.3 1.6 %collective-permute-start.6 = (bf16[528,128]{1,0:T(8,128)(2,1)}, bf16[528,128]{1,0:T(8,128)(2,1)}, u32[]{:S(2)}, u32[]{:S(2)}) collective-permute-start(bf16[528,128]{1,0:T(8,128)(2,1)} %get-tuple-element.88.refs_0_), channel_id=1, source_target_pairs={{0,8},{4,12},{8,0},{12,4},{16,24},{20,28},{24,16},{28,20},{1,9},{5... | collective-permute-start | bytes 405512 | tf_op jit(solution)/shard_map/ppermute | solution.py:465
  45.4 1.7 %last_queries.1.q_ref = bf16[128,512]{1,0:T(8,128)(2,1)S(1)} custom-call(s32[1]{0:T(128)} %bitcast.me_ref, f32[1,1024]{1,0:T(1,128)S(1)} %copy-done.49, bf16[1024,1536]{1,0:T(8,128)(2,1)S(1)} %bitcast.24, bf16[128,512]{1,0:T(8,128)(2,1)S(1)} %get-tuple-element.63.refs_0_, bf16[128,512]{1,0:T(8,128)(2,1)} %collective-permute-done.refs_1_), custom_call_target="tpu_custom_call" | custom-call | flops 402653184 | tf_op jit(solution)/shard_map/last_queries/pallas_call | solution.py:201
  47.2 1.5 %attention.9.local_ref = bf16[128,512]{1,0:T(8,128)(2,1)S(1)} custom-call(s32[2,2]{1,0:T(2,128)S(1)} %copy-done.51, f32[1,4]{1,0:T(1,128)S(1)} %copy-done.52, bf16[128,512]{1,0:T(8,128)(2,1)S(1)} %last_queries.1.q_ref, bf16[256,512]{1,0:T(8,128)(2,1)S(1)} %get-tuple-element.71.refs_0_, bf16[256,512]{1,0:T(8,128)(2,1)S(1)} %copy-done.6, ...), custom_call_target="tpu_custom_call" | custom-call | flops 536870912 | tf_op jit(solution)/shard_map/attention/pallas_call | solution.py:241
  48.8 1.2 %collective-permute-done.6.refs_2_ = bf16[528,128]{1,0:T(8,128)(2,1)} collective-permute-done((bf16[528,128]{1,0:T(8,128)(2,1)}, bf16[528,128]{1,0:T(8,128)(2,1)}, u32[]{:S(2)}, u32[]{:S(2)}) %collective-permute-start.6) | collective-permute-done | bytes 135200 | tf_op jit(solution)/shard_map/ppermute | solution.py:465
  50.0 2.1 %collective-permute-done.7.refs_3_ = bf16[528,128]{1,0:T(8,128)(2,1)} collective-permute-done((bf16[528,128]{1,0:T(8,128)(2,1)}, bf16[528,128]{1,0:T(8,128)(2,1)}, u32[]{:S(2)}, u32[]{:S(2)}) %collective-permute-start.7) | collective-permute-done | bytes 135200 | tf_op jit(solution)/shard_map/ppermute | solution.py:465
  52.1 1.6 %quad.1 = (f32[512,128]{1,0:T(8,128)S(1)}, f32[8,128]{1,0:T(8,128)S(1)}, bf16[528,128]{1,0:T(8,128)(2,1)S(1)}) custom-call(s32[1]{0:T(128)S(6)} %rem.9.place_ref, bf16[528,128]{1,0:T(8,128)(2,1)} %get-tuple-element.88.refs_0_, bf16[528,128]{1,0:T(8,128)(2,1)} %collective-permute-done.5.refs_1_, bf16[528,128]{1,0:T(8,128)(2,1)} %collective-permute-done.6.refs_2_, ...), custom_call_target="tpu_custom_call" | custom-call | flops 2703360 | tf_op jit(solution)/shard_map/quad/pallas_call | solution.py:297
  53.7 2.6 %collective-permute-start.8 = (bf16[528,128]{1,0:T(8,128)(2,1)S(1)}, bf16[528,128]{1,0:T(8,128)(2,1)S(1)}, u32[]{:S(2)}, u32[]{:S(2)}) collective-permute-start(bf16[528,128]{1,0:T(8,128)(2,1)S(1)} %get-tuple-element.94.refs_0_), channel_id=1, source_target_pairs={{0,16},{4,20},{8,24},{12,28},{16,0},{20,4},{24,8},{28,12},{1,17},{... | collective-permute-start | bytes 405512 | tf_op jit(solution)/shard_map/ppermute | solution.py:472
  56.4 6.2 %collective-permute-done.8.refs_1_ = bf16[528,128]{1,0:T(8,128)(2,1)S(1)} collective-permute-done((bf16[528,128]{1,0:T(8,128)(2,1)S(1)}, bf16[528,128]{1,0:T(8,128)(2,1)S(1)}, u32[]{:S(2)}, u32[]{:S(2)}) %collective-permute-start.8) | collective-permute-done | bytes 135200 | tf_op jit(solution)/shard_map/ppermute | solution.py:472
  63.0 1.3 %collective-permute-done.9.side_ref = bf16[128,512]{1,0:T(8,128)(2,1)S(1)} collective-permute-done((bf16[128,512]{1,0:T(8,128)(2,1)S(1)}, bf16[128,512]{1,0:T(8,128)(2,1)S(1)}, u32[]{:S(2)}, u32[]{:S(2)}) %collective-permute-start.9) | collective-permute-done | bytes 131104 | tf_op jit(solution)/shard_map/ppermute | solution.py:480
  64.3 1.7 %project.5 = (bf16[128,512]{1,0:T(8,128)(2,1)S(1)}, bf16[128,512]{1,0:T(8,128)(2,1)S(1)}) custom-call(s32[1]{0:T(128)} %bitcast.me_ref, bf16[128,512]{1,0:T(8,128)(2,1)S(1)} %recall.5.own_ref, bf16[128,512]{1,0:T(8,128)(2,1)S(1)} %collective-permute-done.9.side_ref, bf16[512,1024]{1,0:T(8,128)(2,1)S(1)} %bitcast.25, ...), custom_call_target="tpu_custom_call" | custom-call | flops 268435456 | tf_op jit(solution)/shard_map/project/pallas_call | solution.py:364
  68.3 1.9 %project.9 = (bf16[256,512]{1,0:T(8,128)(2,1)S(1)}, bf16[256,512]{1,0:T(8,128)(2,1)S(1)}) custom-call(s32[1]{0:T(128)} %bitcast.me_ref, bf16[256,512]{1,0:T(8,128)(2,1)S(1)} %recall.9.own_ref, bf16[256,512]{1,0:T(8,128)(2,1)S(1)} %collective-permute-done.17.side_ref, bf16[512,1024]{1,0:T(8,128)(2,1)S(1)} %bitcast.26, ...), custom_call_target="tpu_custom_call" | custom-call | flops 536870912 | tf_op jit(solution)/shard_map/project/pallas_call | solution.py:364
  70.7 1.9 %project.8 = (bf16[256,512]{1,0:T(8,128)(2,1)S(1)}, bf16[256,512]{1,0:T(8,128)(2,1)S(1)}) custom-call(s32[1]{0:T(128)} %bitcast.me_ref, bf16[256,512]{1,0:T(8,128)(2,1)S(1)} %recall.8.own_ref, bf16[256,512]{1,0:T(8,128)(2,1)S(1)} %collective-permute-done.15.side_ref, bf16[512,1024]{1,0:T(8,128)(2,1)S(1)} %bitcast.27, ...), custom_call_target="tpu_custom_call" | custom-call | flops 536870912 | tf_op jit(solution)/shard_map/project/pallas_call | solution.py:364
  72.7 1.6 %collective-permute-start.16 = (bf16[256,512]{1,0:T(8,128)(2,1)S(1)}, bf16[256,512]{1,0:T(8,128)(2,1)S(1)}, u32[]{:S(2)}, u32[]{:S(2)}) collective-permute-start(bf16[256,512]{1,0:T(8,128)(2,1)S(1)} %get-tuple-element.108), channel_id=1, source_target_pairs={{0,1},{1,0},{2,3},{3,2},{4,5},{5,4},{6,7},{7,6},{8,9},{9,8},{10,11... | collective-permute-start | bytes 786440 | tf_op jit(solution)/shard_map/ppermute | solution.py:485
  74.3 1.9 %project.7 = (bf16[256,512]{1,0:T(8,128)(2,1)S(1)}, bf16[256,512]{1,0:T(8,128)(2,1)S(1)}) custom-call(s32[1]{0:T(128)} %bitcast.me_ref, bf16[256,512]{1,0:T(8,128)(2,1)S(1)} %recall.7.own_ref, bf16[256,512]{1,0:T(8,128)(2,1)S(1)} %collective-permute-done.13.side_ref, bf16[512,1024]{1,0:T(8,128)(2,1)S(1)} %bitcast.28, ...), custom_call_target="tpu_custom_call" | custom-call | flops 536870912 | tf_op jit(solution)/shard_map/project/pallas_call | solution.py:364
  76.8 1.6 %collective-permute-start.19 = (bf16[128,512]{1,0:T(8,128)(2,1)S(1)}, bf16[128,512]{1,0:T(8,128)(2,1)S(1)}, u32[]{:S(2)}, u32[]{:S(2)}) collective-permute-start(bf16[128,512]{1,0:T(8,128)(2,1)S(1)} %get-tuple-element.114), channel_id=1, source_target_pairs={{0,1},{1,0},{2,3},{3,2},{4,5},{5,4},{6,7},{7,6},{8,9},{9,8},{10,11... | collective-permute-start | bytes 393224 | tf_op jit(solution)/shard_map/ppermute | solution.py:485
  78.4 1.7 %project.6 = (bf16[128,512]{1,0:T(8,128)(2,1)S(1)}, bf16[128,512]{1,0:T(8,128)(2,1)S(1)}) custom-call(s32[1]{0:T(128)} %bitcast.me_ref, bf16[128,512]{1,0:T(8,128)(2,1)S(1)} %recall.6.own_ref, bf16[128,512]{1,0:T(8,128)(2,1)S(1)} %collective-permute-done.11.side_ref, bf16[512,1024]{1,0:T(8,128)(2,1)S(1)} %bitcast.29, ...), custom_call_target="tpu_custom_call" | custom-call | flops 268435456 | tf_op jit(solution)/shard_map/project/pallas_call | solution.py:364
  80.6 12.9 %collective-permute-done.19.refs_1_ = bf16[128,512]{1,0:T(8,128)(2,1)S(1)} collective-permute-done((bf16[128,512]{1,0:T(8,128)(2,1)S(1)}, bf16[128,512]{1,0:T(8,128)(2,1)S(1)}, u32[]{:S(2)}, u32[]{:S(2)}) %collective-permute-start.19) | collective-permute-done | bytes 131104 | tf_op jit(solution)/shard_map/ppermute | solution.py:485
  93.5 0.7 finish.5.refs_2_
  94.2 0.8 finish.6.refs_2_
  94.9 0.8 finish.7.refs_2_
  95.7 0.8 finish.8.refs_2_
  96.5 0.7 finish.9
  (132 shorter events, 7.4 us)
Async XLA Ops:
  2.0 18.0 %copy-start.33 = (bf16[256,512]{1,0:T(8,128)(2,1)}, bf16[256,512]{1,0:T(8,128)(2,1)S(1)}, u32[]{:S(2)}) copy-start(bf16[256,512]{1,0:T(8,128)(2,1)S(1)} %get-tuple-element.116.refs_0_) | copy-start | bytes 786436
  2.0 18.0 %collective-permute-start.1 = (bf16[256,512]{1,0:T(8,128)(2,1)S(1)}, bf16[256,512]{1,0:T(8,128)(2,1)}, u32[]{:S(2)}, u32[]{:S(2)}) collective-permute-start(bf16[256,512]{1,0:T(8,128)(2,1)S(1)} %get-tuple-element.116.refs_0_), channel_id=1, source_target_pairs={{1,0},{0,1},{3,2},{2,3},{5,4},{4,5},{7,6},{6,7},{9,8},{8,9},{11,10... | collective-permute-start | bytes 786440 | tf_op jit(solution)/shard_map/ppermute | solution.py:443
  4.9 18.4 %collective-permute-start.2 = (bf16[256,512]{1,0:T(8,128)(2,1)}, bf16[256,512]{1,0:T(8,128)(2,1)}, u32[]{:S(2)}, u32[]{:S(2)}) collective-permute-start(bf16[256,512]{1,0:T(8,128)(2,1)} %get-tuple-element.117.refs_1_), channel_id=1, source_target_pairs={{1,0},{0,1},{3,2},{2,3},{5,4},{4,5},{7,6},{6,7},{9,8},{8,9},{11,10... | collective-permute-start | bytes 786440 | tf_op jit(solution)/shard_map/ppermute | solution.py:443
  5.0 21.0 %collective-permute-start.3 = (bf16[256,512]{1,0:T(8,128)(2,1)}, bf16[256,512]{1,0:T(8,128)(2,1)}, u32[]{:S(2)}, u32[]{:S(2)}) collective-permute-start(bf16[256,512]{1,0:T(8,128)(2,1)} %get-tuple-element.115.refs_1_), channel_id=1, source_target_pairs={{1,0},{0,1},{3,2},{2,3},{5,4},{4,5},{7,6},{6,7},{9,8},{8,9},{11,10... | collective-permute-start | bytes 786440 | tf_op jit(solution)/shard_map/ppermute | solution.py:443
  15.4 13.3 %collective-permute-start.4 = (bf16[128,512]{1,0:T(8,128)(2,1)}, bf16[128,512]{1,0:T(8,128)(2,1)}, u32[]{:S(2)}, u32[]{:S(2)}) collective-permute-start(bf16[128,512]{1,0:T(8,128)(2,1)} %get-tuple-element.68.refs_1_), channel_id=1, source_target_pairs={{1,0},{0,1},{3,2},{2,3},{5,4},{4,5},{7,6},{6,7},{9,8},{8,9},{11,10... | collective-permute-start | bytes 393224 | tf_op jit(solution)/shard_map/ppermute | solution.py:443
  15.4 22.6 %collective-permute-start = (bf16[128,512]{1,0:T(8,128)(2,1)S(1)}, bf16[128,512]{1,0:T(8,128)(2,1)}, u32[]{:S(2)}, u32[]{:S(2)}) collective-permute-start(bf16[128,512]{1,0:T(8,128)(2,1)S(1)} %get-tuple-element.63.refs_0_), channel_id=1, source_target_pairs={{1,0},{0,1},{3,2},{2,3},{5,4},{4,5},{7,6},{6,7},{9,8},{8,9},{11,10... | collective-permute-start | bytes 393224 | tf_op jit(solution)/shard_map/ppermute | solution.py:443
  17.4 2.6 %copy-start.4 = (f32[1024,8]{1,0:T(8,128)S(1)}, f32[1024,8]{1,0:T(8,128)}, u32[]{:S(2)}) copy-start(f32[1024,8]{1,0:T(8,128)} %copy-done.3) | copy-start | bytes 98308
  17.4 2.6 %copy-start.49 = (f32[1,1024]{1,0:T(1,128)S(1)}, f32[1,1024]{1,0:T(1,128)}, u32[]{:S(2)}) copy-start(f32[1,1024]{1,0:T(1,128)} %gain_ref.11) | copy-start | bytes 12292
  19.9 44.4 %collective-permute-start.10 = (bf16[512,1024]{1,0:T(8,128)(2,1)}, bf16[512,1024]{1,0:T(8,128)(2,1)}, u32[]{:S(2)}, u32[]{:S(2)}) collective-permute-start(bf16[512,1024]{1,0:T(8,128)(2,1)} %bitcast.9), channel_id=1, source_target_pairs={{0,2},{2,0},{1,3},{3,1},{4,6},{6,4},{5,7},{7,5},{8,10},{10,8},{9,1... | collective-permute-start | bytes 3145736 | tf_op jit(solution)/shard_map/ppermute | solution.py:426
  23.3 9.0 %copy-start.13 = (bf16[256,512]{1,0:T(8,128)(2,1)}, bf16[256,512]{1,0:T(8,128)(2,1)S(1)}, u32[]{:S(2)}) copy-start(bf16[256,512]{1,0:T(8,128)(2,1)S(1)} %get-tuple-element.70.q_ref) | copy-start | bytes 786436
  23.3 13.0 %copy-start.1 = (bf16[256,512]{1,0:T(8,128)(2,1)}, bf16[256,512]{1,0:T(8,128)(2,1)S(1)}, u32[]{:S(2)}) copy-start(bf16[256,512]{1,0:T(8,128)(2,1)S(1)} %get-tuple-element.72.refs_1_.refs_2_.refs_3_.refs_4_.refs_5_) | copy-start | bytes 786436
  25.9 8.2 %copy-start.25 = (bf16[256,512]{1,0:T(8,128)(2,1)}, bf16[256,512]{1,0:T(8,128)(2,1)S(1)}, u32[]{:S(2)}) copy-start(bf16[256,512]{1,0:T(8,128)(2,1)S(1)} %get-tuple-element.73.q_ref) | copy-start | bytes 786436
  25.9 10.4 %copy-start.5 = (bf16[256,512]{1,0:T(8,128)(2,1)}, bf16[256,512]{1,0:T(8,128)(2,1)S(1)}, u32[]{:S(2)}) copy-start(bf16[256,512]{1,0:T(8,128)(2,1)S(1)} %get-tuple-element.74.refs_1_) | copy-start | bytes 786436
  25.9 10.3 %copy-start.7 = (bf16[256,512]{1,0:T(8,128)(2,1)}, bf16[256,512]{1,0:T(8,128)(2,1)S(1)}, u32[]{:S(2)}) copy-start(bf16[256,512]{1,0:T(8,128)(2,1)S(1)} %get-tuple-element.75.refs_3_.refs_4_.refs_5_.refs_6_) | copy-start | bytes 786436
  28.6 7.7 %copy-start.9 = (bf16[256,512]{1,0:T(8,128)(2,1)}, bf16[256,512]{1,0:T(8,128)(2,1)S(1)}, u32[]{:S(2)}) copy-start(bf16[256,512]{1,0:T(8,128)(2,1)S(1)} %get-tuple-element.77.refs_2_) | copy-start | bytes 786436
  28.6 7.7 %copy-start.11 = (bf16[256,512]{1,0:T(8,128)(2,1)}, bf16[256,512]{1,0:T(8,128)(2,1)S(1)}, u32[]{:S(2)}) copy-start(bf16[256,512]{1,0:T(8,128)(2,1)S(1)} %get-tuple-element.78.refs_5_.refs_6_.refs_7_) | copy-start | bytes 786436
  28.6 7.7 %copy-start.27 = (bf16[256,512]{1,0:T(8,128)(2,1)}, bf16[256,512]{1,0:T(8,128)(2,1)S(1)}, u32[]{:S(2)}) copy-start(bf16[256,512]{1,0:T(8,128)(2,1)S(1)} %get-tuple-element.76.q_ref) | copy-start | bytes 786436
  30.9 2.6 %copy-start.19 = (bf16[128,512]{1,0:T(8,128)(2,1)}, bf16[128,512]{1,0:T(8,128)(2,1)S(1)}, u32[]{:S(2)}) copy-start(bf16[128,512]{1,0:T(8,128)(2,1)S(1)} %get-tuple-element.81.refs_7_.refs_8_) | copy-start | bytes 393220
  30.9 7.1 %copy-start.17 = (bf16[128,512]{1,0:T(8,128)(2,1)}, bf16[128,512]{1,0:T(8,128)(2,1)S(1)}, u32[]{:S(2)}) copy-start(bf16[128,512]{1,0:T(8,128)(2,1)S(1)} %get-tuple-element.80.refs_3_) | copy-start | bytes 393220
  30.9 7.1 %copy-start.21 = (bf16[128,512]{1,0:T(8,128)(2,1)}, bf16[128,512]{1,0:T(8,128)(2,1)S(1)}, u32[]{:S(2)}) copy-start(bf16[128,512]{1,0:T(8,128)(2,1)S(1)} %get-tuple-element.79.q_ref) | copy-start | bytes 393220
  41.8 7.0 %collective-permute-start.5 = (bf16[528,128]{1,0:T(8,128)(2,1)}, bf16[528,128]{1,0:T(8,128)(2,1)}, u32[]{:S(2)}, u32[]{:S(2)}) collective-permute-start(bf16[528,128]{1,0:T(8,128)(2,1)} %get-tuple-element.88.refs_0_), channel_id=1, source_target_pairs={{0,4},{4,0},{8,12},{12,8},{16,20},{20,16},{24,28},{28,24},{1,5},{5... | collective-permute-start | bytes 405512 | tf_op jit(solution)/shard_map/ppermute | solution.py:465
  43.3 6.7 %collective-permute-start.6 = (bf16[528,128]{1,0:T(8,128)(2,1)}, bf16[528,128]{1,0:T(8,128)(2,1)}, u32[]{:S(2)}, u32[]{:S(2)}) collective-permute-start(bf16[528,128]{1,0:T(8,128)(2,1)} %get-tuple-element.88.refs_0_), channel_id=1, source_target_pairs={{0,8},{4,12},{8,0},{12,4},{16,24},{20,28},{24,16},{28,20},{1,9},{5... | collective-permute-start | bytes 405512 | tf_op jit(solution)/shard_map/ppermute | solution.py:465
  44.8 7.3 %collective-permute-start.7 = (bf16[528,128]{1,0:T(8,128)(2,1)}, bf16[528,128]{1,0:T(8,128)(2,1)}, u32[]{:S(2)}, u32[]{:S(2)}) collective-permute-start(bf16[528,128]{1,0:T(8,128)(2,1)} %get-tuple-element.88.refs_0_), channel_id=1, source_target_pairs={{0,12},{4,8},{8,4},{12,0},{16,28},{20,24},{24,20},{28,16},{1,13},{... | collective-permute-start | bytes 405512 | tf_op jit(solution)/shard_map/ppermute | solution.py:465
  45.3 17.3 %copy-start.22 = (bf16[128,512]{1,0:T(8,128)(2,1)S(1)}, bf16[128,512]{1,0:T(8,128)(2,1)}, u32[]{:S(2)}) copy-start(bf16[128,512]{1,0:T(8,128)(2,1)} %copy-done.21) | copy-start | bytes 393220
  45.3 17.3 %copy-start.24 = (bf16[128,512]{1,0:T(8,128)(2,1)S(1)}, bf16[128,512]{1,0:T(8,128)(2,1)}, u32[]{:S(2)}) copy-start(bf16[128,512]{1,0:T(8,128)(2,1)} %copy-done.23) | copy-start | bytes 393220
  45.3 17.3 %copy-start.48 = (f32[128,8]{1,0:T(8,128)S(1)}, f32[128,8]{1,0:T(8,128)}, u32[]{:S(2)}) copy-start(f32[128,8]{1,0:T(8,128)} %copy-done.47) | copy-start | bytes 12292
  45.3 19.0 %copy-start = (bf16[1,4,128,1024]{3,2,1,0:T(8,128)(2,1)S(1)}, bf16[1,4,128,1024]{3,2,1,0:T(8,128)(2,1)}, u32[]{:S(2)}) copy-start(bf16[1,4,128,1024]{3,2,1,0:T(8,128)(2,1)} %param.16) | copy-start | bytes 3145732
  47.1 18.9 %copy-start.14 = (bf16[256,512]{1,0:T(8,128)(2,1)S(1)}, bf16[256,512]{1,0:T(8,128)(2,1)}, u32[]{:S(2)}) copy-start(bf16[256,512]{1,0:T(8,128)(2,1)} %copy-done.13) | copy-start | bytes 786436
  47.1 18.9 %copy-start.16 = (bf16[256,512]{1,0:T(8,128)(2,1)S(1)}, bf16[256,512]{1,0:T(8,128)(2,1)}, u32[]{:S(2)}) copy-start(bf16[256,512]{1,0:T(8,128)(2,1)} %copy-done.15) | copy-start | bytes 786436
  47.1 18.9 %copy-start.44 = (f32[256,8]{1,0:T(8,128)S(1)}, f32[256,8]{1,0:T(8,128)}, u32[]{:S(2)}) copy-start(f32[256,8]{1,0:T(8,128)} %copy-done.43) | copy-start | bytes 24580
  48.7 17.8 %copy-start.26 = (bf16[256,512]{1,0:T(8,128)(2,1)S(1)}, bf16[256,512]{1,0:T(8,128)(2,1)}, u32[]{:S(2)}) copy-start(bf16[256,512]{1,0:T(8,128)(2,1)} %copy-done.25) | copy-start | bytes 786436
  48.7 17.8 %copy-start.32 = (bf16[256,512]{1,0:T(8,128)(2,1)S(1)}, bf16[256,512]{1,0:T(8,128)(2,1)}, u32[]{:S(2)}) copy-start(bf16[256,512]{1,0:T(8,128)(2,1)} %copy-done.31) | copy-start | bytes 786436
  48.7 17.8 %copy-start.42 = (f32[256,8]{1,0:T(8,128)S(1)}, f32[256,8]{1,0:T(8,128)}, u32[]{:S(2)}) copy-start(f32[256,8]{1,0:T(8,128)} %copy-done.41) | copy-start | bytes 24580
  48.7 18.4 %copy-start.28 = (bf16[256,512]{1,0:T(8,128)(2,1)S(1)}, bf16[256,512]{1,0:T(8,128)(2,1)}, u32[]{:S(2)}) copy-start(bf16[256,512]{1,0:T(8,128)(2,1)} %copy-done.27) | copy-start | bytes 786436
  48.7 18.4 %copy-start.30 = (bf16[256,512]{1,0:T(8,128)(2,1)S(1)}, bf16[256,512]{1,0:T(8,128)(2,1)}, u32[]{:S(2)}) copy-start(bf16[256,512]{1,0:T(8,128)(2,1)} %copy-done.29) | copy-start | bytes 786436
  48.8 18.4 %copy-start.40 = (f32[256,8]{1,0:T(8,128)S(1)}, f32[256,8]{1,0:T(8,128)}, u32[]{:S(2)}) copy-start(f32[256,8]{1,0:T(8,128)} %copy-done.39) | copy-start | bytes 24580
  53.7 8.8 %collective-permute-start.8 = (bf16[528,128]{1,0:T(8,128)(2,1)S(1)}, bf16[528,128]{1,0:T(8,128)(2,1)S(1)}, u32[]{:S(2)}, u32[]{:S(2)}) collective-permute-start(bf16[528,128]{1,0:T(8,128)(2,1)S(1)} %get-tuple-element.94.refs_0_), channel_id=1, source_target_pairs={{0,16},{4,20},{8,24},{12,28},{16,0},{20,4},{24,8},{28,12},{1,17},{... | collective-permute-start | bytes 405512 | tf_op jit(solution)/shard_map/ppermute | solution.py:472
  62.7 5.0 %copy-start.46 = (f32[128,8]{1,0:T(8,128)S(1)}, f32[128,8]{1,0:T(8,128)}, u32[]{:S(2)}) copy-start(f32[128,8]{1,0:T(8,128)} %copy-done.45) | copy-start | bytes 12292
  62.9 1.4 %collective-permute-start.9 = (bf16[128,512]{1,0:T(8,128)(2,1)S(1)}, bf16[128,512]{1,0:T(8,128)(2,1)S(1)}, u32[]{:S(2)}, u32[]{:S(2)}) collective-permute-start(bf16[128,512]{1,0:T(8,128)(2,1)S(1)} %recall.5.own_ref), channel_id=1, source_target_pairs={{0,2},{2,0},{1,3},{3,1},{4,6},{6,4},{5,7},{7,5},{8,10},{10,8},{9,1... | collective-permute-start | bytes 393224 | tf_op jit(solution)/shard_map/ppermute | solution.py:480
  66.3 2.0 %collective-permute-start.17 = (bf16[256,512]{1,0:T(8,128)(2,1)S(1)}, bf16[256,512]{1,0:T(8,128)(2,1)S(1)}, u32[]{:S(2)}, u32[]{:S(2)}) collective-permute-start(bf16[256,512]{1,0:T(8,128)(2,1)S(1)} %recall.9.own_ref), channel_id=1, source_target_pairs={{0,2},{2,0},{1,3},{3,1},{4,6},{6,4},{5,7},{7,5},{8,10},{10,8},{9,1... | collective-permute-start | bytes 786440 | tf_op jit(solution)/shard_map/ppermute | solution.py:480
  66.8 4.0 %collective-permute-start.15 = (bf16[256,512]{1,0:T(8,128)(2,1)S(1)}, bf16[256,512]{1,0:T(8,128)(2,1)S(1)}, u32[]{:S(2)}, u32[]{:S(2)}) collective-permute-start(bf16[256,512]{1,0:T(8,128)(2,1)S(1)} %recall.8.own_ref), channel_id=1, source_target_pairs={{0,2},{2,0},{1,3},{3,1},{4,6},{6,4},{5,7},{7,5},{8,10},{10,8},{9,1... | collective-permute-start | bytes 786440 | tf_op jit(solution)/shard_map/ppermute | solution.py:480
  67.4 6.9 %collective-permute-start.13 = (bf16[256,512]{1,0:T(8,128)(2,1)S(1)}, bf16[256,512]{1,0:T(8,128)(2,1)S(1)}, u32[]{:S(2)}, u32[]{:S(2)}) collective-permute-start(bf16[256,512]{1,0:T(8,128)(2,1)S(1)} %recall.7.own_ref), channel_id=1, source_target_pairs={{0,2},{2,0},{1,3},{3,1},{4,6},{6,4},{5,7},{7,5},{8,10},{10,8},{9,1... | collective-permute-start | bytes 786440 | tf_op jit(solution)/shard_map/ppermute | solution.py:480
  67.8 10.5 %collective-permute-start.11 = (bf16[128,512]{1,0:T(8,128)(2,1)S(1)}, bf16[128,512]{1,0:T(8,128)(2,1)S(1)}, u32[]{:S(2)}, u32[]{:S(2)}) collective-permute-start(bf16[128,512]{1,0:T(8,128)(2,1)S(1)} %recall.6.own_ref), channel_id=1, source_target_pairs={{0,2},{2,0},{1,3},{3,1},{4,6},{6,4},{5,7},{7,5},{8,10},{10,8},{9,1... | collective-permute-start | bytes 393224 | tf_op jit(solution)/shard_map/ppermute | solution.py:480
  70.2 23.9 %collective-permute-start.18 = (bf16[256,512]{1,0:T(8,128)(2,1)S(1)}, bf16[256,512]{1,0:T(8,128)(2,1)S(1)}, u32[]{:S(2)}, u32[]{:S(2)}) collective-permute-start(bf16[256,512]{1,0:T(8,128)(2,1)S(1)} %get-tuple-element.112), channel_id=1, source_target_pairs={{0,1},{1,0},{2,3},{3,2},{4,5},{5,4},{6,7},{7,6},{8,9},{9,8},{10,11... | collective-permute-start | bytes 786440 | tf_op jit(solution)/shard_map/ppermute | solution.py:485
  72.7 22.3 %collective-permute-start.16 = (bf16[256,512]{1,0:T(8,128)(2,1)S(1)}, bf16[256,512]{1,0:T(8,128)(2,1)S(1)}, u32[]{:S(2)}, u32[]{:S(2)}) collective-permute-start(bf16[256,512]{1,0:T(8,128)(2,1)S(1)} %get-tuple-element.108), channel_id=1, source_target_pairs={{0,1},{1,0},{2,3},{3,2},{4,5},{5,4},{6,7},{7,6},{8,9},{9,8},{10,11... | collective-permute-start | bytes 786440 | tf_op jit(solution)/shard_map/ppermute | solution.py:485
  76.3 19.4 %collective-permute-start.14 = (bf16[256,512]{1,0:T(8,128)(2,1)S(1)}, bf16[256,512]{1,0:T(8,128)(2,1)S(1)}, u32[]{:S(2)}, u32[]{:S(2)}) collective-permute-start(bf16[256,512]{1,0:T(8,128)(2,1)S(1)} %get-tuple-element.104), channel_id=1, source_target_pairs={{0,1},{1,0},{2,3},{3,2},{4,5},{5,4},{6,7},{7,6},{8,9},{9,8},{10,11... | collective-permute-start | bytes 786440 | tf_op jit(solution)/shard_map/ppermute | solution.py:485
  76.8 16.7 %collective-permute-start.19 = (bf16[128,512]{1,0:T(8,128)(2,1)S(1)}, bf16[128,512]{1,0:T(8,128)(2,1)S(1)}, u32[]{:S(2)}, u32[]{:S(2)}) collective-permute-start(bf16[128,512]{1,0:T(8,128)(2,1)S(1)} %get-tuple-element.114), channel_id=1, source_target_pairs={{0,1},{1,0},{2,3},{3,2},{4,5},{5,4},{6,7},{7,6},{8,9},{9,8},{10,11... | collective-permute-start | bytes 393224 | tf_op jit(solution)/shard_map/ppermute | solution.py:485
  80.1 16.4 %collective-permute-start.12 = (bf16[128,512]{1,0:T(8,128)(2,1)S(1)}, bf16[128,512]{1,0:T(8,128)(2,1)S(1)}, u32[]{:S(2)}, u32[]{:S(2)}) collective-permute-start(bf16[128,512]{1,0:T(8,128)(2,1)S(1)} %get-tuple-element.100), channel_id=1, source_target_pairs={{0,1},{1,0},{2,3},{3,2},{4,5},{5,4},{6,7},{7,6},{8,9},{9,8},{10,11... | collective-permute-start | bytes 393224 | tf_op jit(solution)/shard_map/ppermute | solution.py:485
  (26 other events, 34.0 us)

commit v8 on v7

--- a/solution.py
+++ b/solution.py
@@ -93,7 +93,8 @@
     )(logs, flags)
 
 
-def normed_parts(me, gain_ref, x_refs):
+def normed_parts(gain_ref, x_refs):
+    me = lax.axis_index("head")
     shards, width = len(x_refs), x_refs[0].shape[1]
     parts = [x[...].astype(F32) for x in x_refs]
     squares = sum(jnp.sum(p * p, axis=-1, keepdims=True) for p in parts)
@@ -119,7 +120,7 @@
     sum_ref[h] += dot_tn((key.astype(F32) * fade).astype(BF16), value)
 
 
-def qkv_kernel(heads, dim, first, me_ref, gain_ref, w_ref, fade_ref, *refs):
+def qkv_kernel(heads, dim, first, gain_ref, w_ref, fade_ref, *refs):
     refs, (q_ref, k_ref, v_ref, sum_ref) = refs[:-4], refs[-4:]
     if first == 0:
         sum_ref[...] = jnp.zeros_like(sum_ref)
@@ -127,7 +128,7 @@
     else:
         sum_ref[...] = refs[0][...]
         x_refs = refs[1:]
-    parts = normed_parts(me_ref[0], gain_ref, x_refs)
+    parts = normed_parts(gain_ref, x_refs)
     wide = heads * dim
     thirds = [projected(parts, w_ref, slice(i * wide, (i + 1) * wide)) for i in range(3)]
     taken = lambda at: thirds[at * dim // wide][:, at * dim % wide : at * dim % wide + dim]
@@ -141,24 +142,24 @@
         add_summary(sum_ref, h, key, value, fade_ref, first)
 
 
-def qkv(me, gain, w, fade, prev, xs, heads, dim, first):
+def qkv(gain, w, fade, prev, xs, heads, dim, first):
     rows = xs[0].shape[0]
     before = [prev] if first else []
     return pl.pallas_call(
         functools.partial(qkv_kernel, heads, dim, first),
-        in_specs=[SMEM] + [VMEM] * (3 + len(before) + len(xs)),
+        in_specs=[VMEM] * (3 + len(before) + len(xs)),
         out_specs=[VMEM] * 4,
         out_shape=[struct((rows, heads * dim))] * 3 + [struct((heads, dim, dim), F32)],
         compiler_params=params(),
         cost_estimate=cost(4 * rows * w.size, 0),
         name="qkv",
-    )(me, gain, w, fade, *before, *xs)
-
-
-def last_kernel(heads, dim, first, me_ref, gain_ref, w_ref, fade_ref, prev_ref, tail_ref, *refs):
+    )(gain, w, fade, *before, *xs)
+
+
+def last_kernel(heads, dim, first, gain_ref, w_ref, fade_ref, prev_ref, tail_ref, *refs):
     x_refs, (k_ref, v_ref, send_ref, sum_ref) = refs[:-4], refs[-4:]
     sum_ref[...] = prev_ref[...]
-    parts = normed_parts(me_ref[0], gain_ref, x_refs)
+    parts = normed_parts(gain_ref, x_refs)
     pairs = [
         projected(parts, w_ref, slice((3 * h + 1) * dim, (3 * h + 3) * dim)) for h in range(heads)
     ]
@@ -173,40 +174,40 @@
     send_ref[heads * dim :, :] = tail_ref[...]
 
 
-def last_keys_values(me, gain, w, fade, prev, tail, xs, heads, dim, first):
+def last_keys_values(gain, w, fade, prev, tail, xs, heads, dim, first):
     rows = xs[0].shape[0]
     return pl.pallas_call(
         functools.partial(last_kernel, heads, dim, first),
-        in_specs=[SMEM] + [VMEM] * (5 + len(xs)),
+        in_specs=[VMEM] * (5 + len(xs)),
         out_specs=[VMEM] * 3,
         out_shape=[struct((rows, heads * dim))] * 2 + [struct((heads * dim + TAIL, dim))],
         scratch_shapes=[pltpu.VMEM((heads, dim, dim), F32)],
         compiler_params=params(),
         cost_estimate=cost(3 * rows * w.size, 0),
         name="last_keys_values",
-    )(me, gain, w, fade, prev, tail, *xs)
-
-
-def queries_kernel(heads, dim, me_ref, gain_ref, w_ref, *refs):
+    )(gain, w, fade, prev, tail, *xs)
+
+
+def queries_kernel(heads, dim, gain_ref, w_ref, *refs):
     q_ref = refs[-1]
-    parts = normed_parts(me_ref[0], gain_ref, refs[:-1])
+    parts = normed_parts(gain_ref, refs[:-1])
     for h in range(heads):
         base = 3 * h * dim
         cols = slice(h * dim, (h + 1) * dim)
         q_ref[:, cols] = unit(projected(parts, w_ref, slice(base, base + dim))).astype(BF16)
 
 
-def last_queries(me, gain, w, xs, heads, dim):
+def last_queries(gain, w, xs, heads, dim):
     rows = xs[0].shape[0]
     return pl.pallas_call(
         functools.partial(queries_kernel, heads, dim),
-        in_specs=[SMEM] + [VMEM] * (2 + len(xs)),
+        in_specs=[VMEM] * (2 + len(xs)),
         out_specs=VMEM,
         out_shape=struct((rows, heads * dim)),
         compiler_params=params(),
         cost_estimate=cost(2 * rows * w.size, 0),
         name="last_queries",
-    )(me, gain, w, *xs)
+    )(gain, w, *xs)
 
 
 def attention_kernel(first, heads, dim, keep_ref, scale_ref, q_ref, *refs):
@@ -276,13 +277,14 @@
     return before, before_decay, state, since
 
 
-def quad_kernel(heads, dim, place_ref, *refs):
+def quad_kernel(heads, dim, *refs):
+    place = lax.rem(lax.axis_index("tm"), len(refs) - 3)
     refs, (before_ref, decay_ref, total_ref) = refs[:-3], refs[-3:]
     size = heads * dim
     total_ref[size:, :] = jnp.zeros((TAIL, total_ref.shape[1]), BF16)
     for h in range(heads):
         rows = slice(h * dim, (h + 1) * dim)
-        before, before_decay, state, since = scanned(place_ref[0], refs, h, dim)
+        before, before_decay, state, since = scanned(place, refs, h, dim)
         before_ref[rows, :] = before
         decay_ref[h : h + 1, :] = before_decay
         total_ref[rows, :] = state.astype(BF16)
@@ -292,11 +294,11 @@
         total_ref[size + TAIL // 2 + h : size + TAIL // 2 + h + 1, :] = low
 
 
-def quad(place, loads, heads, dim):
+def quad(loads, heads, dim):
     shape = loads[0].shape
     return pl.pallas_call(
         functools.partial(quad_kernel, heads, dim),
-        in_specs=[SMEM] + [VMEM] * len(loads),
+        in_specs=[VMEM] * len(loads),
         out_specs=[VMEM] * 3,
         out_shape=[
             struct((heads * dim, shape[1]), F32),
@@ -306,27 +308,28 @@
         compiler_params=params(),
         cost_estimate=cost(loads[0].size * 40, 0),
         name="quad",
-    )(place, *loads)
-
-
-def entering_kernel(heads, dim, place_ref, before_ref, decay_ref, *refs):
+    )(*loads)
+
+
+def entering_kernel(heads, dim, quad_size, before_ref, decay_ref, *refs):
     refs, out_ref = refs[:-1], refs[-1]
+    place = lax.div(lax.axis_index("tm"), quad_size)
     for h in range(heads):
         rows = slice(h * dim, (h + 1) * dim)
-        earlier = scanned(place_ref[0], refs, h, dim)[0]
+        earlier = scanned(place, refs, h, dim)[0]
         out_ref[rows, :] = (before_ref[rows, :] + decay_ref[h : h + 1, :] * earlier).astype(BF16)
 
 
-def entering(place, before, decay, totals, heads, dim):
-    return pl.pallas_call(
-        functools.partial(entering_kernel, heads, dim),
-        in_specs=[SMEM] + [VMEM] * (2 + len(totals)),
+def entering(quad_size, before, decay, totals, heads, dim):
+    return pl.pallas_call(
+        functools.partial(entering_kernel, heads, dim, quad_size),
+        in_specs=[VMEM] * (2 + len(totals)),
         out_specs=VMEM,
         out_shape=struct(before.shape),
         compiler_params=params(),
         cost_estimate=cost(before.size * 20, 0),
         name="entering",
-    )(place, before, decay, *totals)
+    )(before, decay, *totals)
 
 
 def recall_kernel(heads, dim, reading_ref, q_ref, local_ref, state_ref, out_ref):
@@ -348,28 +351,28 @@
     )(reading, q, local, state)
 
 
-def project_kernel(shards, me_ref, own_ref, side_ref, own_w_ref, side_w_ref, *out_refs):
+def project_kernel(shards, own_ref, side_ref, own_w_ref, side_w_ref, *out_refs):
     width = out_refs[0].shape[1]
     own, side = own_ref[...], side_ref[...]
     for k in reversed(range(shards)):
-        owner = lax.rem(me_ref[0] + k, shards)
+        owner = lax.rem(lax.axis_index("head") + k, shards)
         cols = pl.ds(pl.multiple_of(owner * width, width), width)
         out = dot(own, own_w_ref[:, cols]) + dot(side, side_w_ref[:, cols])
         out_refs[k][...] = out.astype(out_refs[k].dtype)
 
 
-def project(me, own, side, own_w, side_w, shards):
+def project(own, side, own_w, side_w, shards):
     rows = own.shape[0]
     width = own_w.shape[1] // shards
     return pl.pallas_call(
         functools.partial(project_kernel, shards),
-        in_specs=[SMEM] + [VMEM] * 4,
+        in_specs=[VMEM] * 4,
         out_specs=[VMEM] * shards,
         out_shape=[struct((rows, width))] * shards,
         compiler_params=params(),
         cost_estimate=cost(4 * rows * own_w.size, 0),
         name="project",
-    )(me, own, side, own_w, side_w)
+    )(own, side, own_w, side_w)
 
 
 def finish_kernel(count, *refs):
@@ -417,8 +420,6 @@
     blocks = lax.axis_size("tm")
     heads = triple_projector.shape[2]
     dim = emission_projector.shape[2]
-    me = lax.axis_index("head").astype(jnp.int32).reshape(1)
-    place = lax.axis_index("tm").astype(jnp.int32).reshape(1)
     swap_streams = [(0, 1), (1, 0)]
     tied = lambda *arrays: lax.optimization_barrier(arrays)
 
@@ -433,14 +434,16 @@
         1.0 / math.sqrt(dim * length * blocks),
         sizes,
     )
+    pieces = [x[first : first + size] for first, size in zip(firsts, sizes)]
     received = []
-    for first, size in zip(firsts, sizes):
-        piece = x[first : first + size]
-        if size < CHUNK:
-            piece, fade = tied(piece, fade)
-        xs = [piece]
+    for c in range(chunks):
+        if c == chunks - 2:
+            pieces[c], pieces[c + 1], received[0] = tied(pieces[c], pieces[c + 1], received[0])
+        xs = [pieces[c]]
         for k in range(1, shards):
-            xs.append(lax.ppermute(piece, "head", [((d + k) % shards, d) for d in range(shards)]))
+            xs.append(
+                lax.ppermute(pieces[c], "head", [((d + k) % shards, d) for d in range(shards)])
+            )
         received.append(xs)
     gain = prescale_amplifier
     w = triple_projector[0].reshape(-1, 3 * heads * dim)
@@ -448,14 +451,14 @@
     qs, ks, vs, locals_ = [], [], [], []
     summary = None
     for c, first in enumerate(firsts[:-1]):
-        q, k, v, summary = qkv(me, gain, w, fade, summary, received[c], heads, dim, first)
+        q, k, v, summary = qkv(gain, w, fade, summary, received[c], heads, dim, first)
         qs.append(q)
         ks.append(k)
         vs.append(v)
         locals_.append(attention(first, tile_retain_grid, score_scaler, q, ks, vs, heads, dim))
     summary, *locals_ = tied(summary, *locals_)
     k, v, sent = last_keys_values(
-        me, gain, w, fade, summary, tail, received[-1], heads, dim, firsts[-1]
+        gain, w, fade, summary, tail, received[-1], heads, dim, firsts[-1]
     )
     ks.append(k)
     vs.append(v)
@@ -464,21 +467,21 @@
     loads = [sent] + [
         lax.ppermute(sent, "tm", [(d, d ^ k) for d in range(blocks)]) for k in range(1, quad_size)
     ]
-    qs.append(last_queries(me, gain, w, received[-1], heads, dim))
+    qs.append(last_queries(gain, w, received[-1], heads, dim))
     locals_.append(attention(firsts[-1], tile_retain_grid, score_scaler, qs[-1], ks, vs, heads, dim))
     *loads, locals_[-1] = tied(*loads, locals_[-1])
-    before, decay, total = quad(lax.rem(place, quad_size), loads, heads, dim)
+    before, decay, total = quad(loads, heads, dim)
     totals = [total] + [
         lax.ppermute(total, "tm", [(d, d ^ (quad_size * k)) for d in range(blocks)])
         for k in range(1, blocks // quad_size)
     ]
-    state = entering(lax.div(place, quad_size), before, decay, totals, heads, dim)
+    state = entering(quad_size, before, decay, totals, heads, dim)
 
     result = None
     for c in [chunks - 2, *range(chunks - 2), chunks - 1]:
         head_out = recall(readings[c], qs[c], locals_[c], state, heads, dim)
         side = lax.ppermute(head_out, "stream", swap_streams)
-        outs = project(me, head_out, side, own_w, side_w, shards)
+        outs = project(head_out, side, own_w, side_w, shards)
         parts = [outs[0]]
         for k in range(1, shards):
             parts.append(

time: 97.8 us -> 81.1 us (0.83)
  Pallas kernels: 38 us -> 23.2 us
  local copies, waits for them, and re-layouts: 15.2 us -> 5.99 us
  waiting for transfers between devices: 23.8 us -> 29.7 us
  starting transfers between devices: 19.3 us -> 21.7 us
    pallas_call x8, Pallas kernels: 12.6 us -> 4.08 us  [the longest x5 3.07 us: project(): pl.pallas_call(functools.partial(project_kernel, shards), in_specs=[VMEM]...]
    unnamed x109 -> x13, local copies, waits for them, and re-layouts: 11.6 us -> 3.84 us
    ppermute x5, waiting for transfers between devices: 0.01 us -> 5.22 us  [per_device(): lax.ppermute(pieces[c], 'head', [((d + k) % shards, d) for d in range(sha...]
    pallas_call x4, Pallas kernels: 9.71 us -> 5.03 us  [qkv(): pl.pallas_call(functools.partial(qkv_kernel, heads, dim, first), in_specs...]
    ppermute x5, waiting for transfers between devices: 12.9 us -> 15.5 us  [per_device(): lax.ppermute(outs[k], 'head', [(d, (d + k) % shards) for d in range(shard...]
    ppermute x1, waiting for transfers between devices: 6.2 us -> 3.89 us  [per_device(): lax.ppermute(total, 'tm', [(d, d ^ quad_size * k) for d in range(blocks)])]
    pallas_call x1, Pallas kernels: 2.46 us -> 0.81 us  [last_keys_values(): pl.pallas_call(functools.partial(last_kernel, heads, dim, first), in_spec...]
    slice x2, local copies, waits for them, and re-layouts: 3.59 us -> 2.14 us  [per_device(): pieces = [x[first:first + size] for first, size in zip(firsts, sizes)]]
  transfers between devices with their start and end apart: 20 -> 20, of which waited for: 5 -> 8; matrix products, arithmetic and copies ran while one was open for 4% -> 4% of each run, Pallas kernels for 36% -> 27%
where the time goes in v8:
time: 81.1 us; the launch traced here: 80.9 us
  waiting for transfers between devices  29.7 us (37%)
  Pallas kernels  23.2 us (29%)
  starting transfers between devices  21.7 us (27%)
  local copies, waits for them, and re-layouts  5.99 us (7%)
    ppermute x5, waiting for transfers between devices, per_device(): lax.ppermute(outs[k], 'head', [(d, (d + k) % shards) for d in range(shard...  15.5 us
    pallas_call x5, Pallas kernels, attention(): pl.pallas_call(functools.partial(attention_kernel, first, heads, dim), in...  7.15 us
    ppermute x5, starting transfers between devices, per_device(): lax.ppermute(pieces[c], 'head', [((d + k) % shards, d) for d in range(sha...  7.15 us
    ppermute x5, starting transfers between devices, per_device(): lax.ppermute(outs[k], 'head', [(d, (d + k) % shards) for d in range(shard...  5.83 us
    ppermute x5, waiting for transfers between devices, per_device(): lax.ppermute(pieces[c], 'head', [((d + k) % shards, d) for d in range(sha...  5.22 us
    pallas_call x4, Pallas kernels, qkv(): pl.pallas_call(functools.partial(qkv_kernel, heads, dim, first), in_specs...  5.03 us
    ppermute x1, waiting for transfers between devices, per_device(): lax.ppermute(total, 'tm', [(d, d ^ quad_size * k) for d in range(blocks)])  3.89 us
    unnamed x13, local copies, waits for them, and re-layouts  3.84 us
  transfers between devices with their start and end apart: 20, of which 8 were waited for; matrix products, arithmetic and copies ran while one was open for 4% of the time, Pallas kernels for 27%

profile of v8, /device:TPU:0, one launch (start us, length us, event | category | flops | bytes accessed | tf_op | source)
XLA Modules:
  0.0 80.9 jit_solution(3282590811210627240)
XLA Ops:
  0.0 1.2 %slice_bitcast_fusion = (bf16[256,512]{1,0:T(8,128)(2,1)S(1)}, bf16[256,512]{1,0:T(8,128)(2,1)S(1)}, bf16[256,512]{1,0:T(8,128)(2,1)S(1)}) fusion(bf16[1,1024,512]{2,1,0:T(8,128)(2,1)} %param.9), kind=kLoop, calls=%fused_computation | loop fusion | bytes 1572864 | tf_op jit(solution)/shard_map/slice | solution.py:437
  1.2 3.0 %collective-permute-start = (bf16[256,512]{1,0:T(8,128)(2,1)S(1)}, bf16[256,512]{1,0:T(8,128)(2,1)S(1)}, u32[]{:S(2)}, u32[]{:S(2)}) collective-permute-start(bf16[256,512]{1,0:T(8,128)(2,1)S(1)} %get-tuple-element.63.refs_0_), channel_id=1, source_target_pairs={{1,0},{0,1},{3,2},{2,3},{5,4},{4,5},{7,6},{6,7},{9,8},{8,9},{11,10... | collective-permute-start | bytes 786440 | tf_op jit(solution)/shard_map/ppermute | solution.py:445
  4.3 1.9 %collective-permute-start.3 = (bf16[256,512]{1,0:T(8,128)(2,1)S(1)}, bf16[256,512]{1,0:T(8,128)(2,1)S(1)}, u32[]{:S(2)}, u32[]{:S(2)}) collective-permute-start(bf16[256,512]{1,0:T(8,128)(2,1)S(1)} %get-tuple-element.115.refs_1_), channel_id=1, source_target_pairs={{1,0},{0,1},{3,2},{2,3},{5,4},{4,5},{7,6},{6,7},{9,8},{8,9},{11,10... | collective-permute-start | bytes 786440 | tf_op jit(solution)/shard_map/ppermute | solution.py:445
  6.2 1.0 %slice_bitcast_fusion.3 = (bf16[128,512]{1,0:T(8,128)(2,1)S(1)}, bf16[128,512]{1,0:T(8,128)(2,1)S(1)}) fusion(bf16[1,1024,512]{2,1,0:T(8,128)(2,1)} %param.9), kind=kLoop, calls=%fused_computation.3 | loop fusion | bytes 524288 | tf_op jit(solution)/shard_map/slice | solution.py:437
  7.2 0.7 copy-done.2
  7.9 0.7 copy-done.5
  8.6 1.4 %prepare.1 = (f32[1024,8]{1,0:T(8,128)S(1)}, bf16[16,128]{1,0:T(8,128)(2,1)S(1)}, f32[256,8]{1,0:T(8,128)S(1)}, f32[256,8]{1,0:T(8,128)S(1)}, f32[256,8]{1,0:T(8...) custom-call(f32[4,1024]{1,0:T(4,128)S(1)} %bitcast.28, s32[2]{0:T(128)S(1)} %copy-done.5), custom_call_target="tpu_custom_call" | custom-call | flops 327680 | tf_op jit(solution)/shard_map/prepare/pallas_call | solution.py:83
  10.0 2.5 %copy.14 = bf16[128,8,4,384]{3,1,2,0:T(8,128)(2,1)S(1)} copy(bf16[128,8,4,384]{3,2,1,0:T(4,128)(2,1)} %bitcast.29) | data formatting | bytes 6291456
  12.5 0.9 %collective-permute-start.4 = (bf16[128,512]{1,0:T(8,128)(2,1)S(1)}, bf16[128,512]{1,0:T(8,128)(2,1)S(1)}, u32[]{:S(2)}, u32[]{:S(2)}) collective-permute-start(bf16[128,512]{1,0:T(8,128)(2,1)S(1)} %get-tuple-element.68.refs_1_), channel_id=1, source_target_pairs={{1,0},{0,1},{3,2},{2,3},{5,4},{4,5},{7,6},{6,7},{9,8},{8,9},{11,10... | collective-permute-start | bytes 393224 | tf_op jit(solution)/shard_map/ppermute | solution.py:445
  13.4 1.2 %collective-permute-start.1 = (bf16[128,512]{1,0:T(8,128)(2,1)S(1)}, bf16[128,512]{1,0:T(8,128)(2,1)S(1)}, u32[]{:S(2)}, u32[]{:S(2)}) collective-permute-start(bf16[128,512]{1,0:T(8,128)(2,1)S(1)} %get-tuple-element.61.refs_0_), channel_id=1, source_target_pairs={{1,0},{0,1},{3,2},{2,3},{5,4},{4,5},{7,6},{6,7},{9,8},{8,9},{11,10... | collective-permute-start | bytes 393224 | tf_op jit(solution)/shard_map/ppermute | solution.py:445
  14.6 1.4 %qkv.4 = (bf16[256,512]{1,0:T(8,128)(2,1)S(1)}, bf16[256,512]{1,0:T(8,128)(2,1)S(1)}, bf16[256,512]{1,0:T(8,128)(2,1)S(1)}, f32[4,128,128]{2,1,0:T(8,128)S(1)}) custom-call(f32[1,1024]{1,0:T(1,128)S(1)} %copy-done.1, bf16[1024,1536]{1,0:T(8,128)(2,1)S(1)} %bitcast.17, f32[1024,8]{1,0:T(8,128)S(1)} %get-tuple-element.62.fade_ref, ...), custom_call_target="tpu_custom_call" | custom-call | flops 1610612736 | tf_op jit(solution)/shard_map/qkv/pallas_call | solution.py:148
  15.9 1.0 %collective-permute-done.2.refs_2_ = bf16[256,512]{1,0:T(8,128)(2,1)S(1)} collective-permute-done((bf16[256,512]{1,0:T(8,128)(2,1)S(1)}, bf16[256,512]{1,0:T(8,128)(2,1)S(1)}, u32[]{:S(2)}, u32[]{:S(2)}) %collective-permute-start.2) | collective-permute-done | bytes 262176 | tf_op jit(solution)/shard_map/ppermute | solution.py:445
  16.9 1.4 %qkv.5 = (bf16[256,512]{1,0:T(8,128)(2,1)S(1)}, bf16[256,512]{1,0:T(8,128)(2,1)S(1)}, bf16[256,512]{1,0:T(8,128)(2,1)S(1)}, f32[4,128,128]{2,1,0:T(8,128)S(1)}) custom-call(f32[1,1024]{1,0:T(1,128)S(1)} %copy-done.1, bf16[1024,1536]{1,0:T(8,128)(2,1)S(1)} %bitcast.18, f32[1024,8]{1,0:T(8,128)S(1)} %get-tuple-element.62.fade_ref, ...), custom_call_target="tpu_custom_call" | custom-call | flops 1610612736 | tf_op jit(solution)/shard_map/qkv/pallas_call | solution.py:148
  18.3 4.2 %collective-permute-done.3.refs_2_ = bf16[256,512]{1,0:T(8,128)(2,1)S(1)} collective-permute-done((bf16[256,512]{1,0:T(8,128)(2,1)S(1)}, bf16[256,512]{1,0:T(8,128)(2,1)S(1)}, u32[]{:S(2)}, u32[]{:S(2)}) %collective-permute-start.3) | collective-permute-done | bytes 262176 | tf_op jit(solution)/shard_map/ppermute | solution.py:445
  22.6 1.4 %qkv.6 = (bf16[256,512]{1,0:T(8,128)(2,1)S(1)}, bf16[256,512]{1,0:T(8,128)(2,1)S(1)}, bf16[256,512]{1,0:T(8,128)(2,1)S(1)}, f32[4,128,128]{2,1,0:T(8,128)S(1)}) custom-call(f32[1,1024]{1,0:T(1,128)S(1)} %copy-done.1, bf16[1024,1536]{1,0:T(8,128)(2,1)S(1)} %bitcast.19, f32[1024,8]{1,0:T(8,128)S(1)} %get-tuple-element.62.fade_ref, ...), custom_call_target="tpu_custom_call" | custom-call | flops 1610612736 | tf_op jit(solution)/shard_map/qkv/pallas_call | solution.py:148
  24.0 1.4 %attention.6.local_ref = bf16[256,512]{1,0:T(8,128)(2,1)S(1)} custom-call(s32[2,2]{1,0:T(2,128)S(1)} %copy-done.3, f32[1,4]{1,0:T(1,128)S(1)} %copy-done.4, bf16[256,512]{1,0:T(8,128)(2,1)S(1)} %get-tuple-element.73.q_ref, bf16[256,512]{1,0:T(8,128)(2,1)S(1)} %get-tuple-element.71.refs_0_, bf16[256,512]{1,0:T(8,128)(2,1)S(1)} %get-tuple-element.74.refs_1_, ...), custom_call_target="tpu_custom_call" | custom-call | flops 536870912 | tf_op jit(solution)/shard_map/attention/pallas_call | solution.py:242
  25.4 1.7 %attention.7.local_ref = bf16[256,512]{1,0:T(8,128)(2,1)S(1)} custom-call(s32[2,2]{1,0:T(2,128)S(1)} %copy-done.3, f32[1,4]{1,0:T(1,128)S(1)} %copy-done.4, bf16[256,512]{1,0:T(8,128)(2,1)S(1)} %get-tuple-element.76.q_ref, bf16[256,512]{1,0:T(8,128)(2,1)S(1)} %get-tuple-element.71.refs_0_, bf16[256,512]{1,0:T(8,128)(2,1)S(1)} %get-tuple-element.74.refs_1_, ...), custom_call_target="tpu_custom_call" | custom-call | flops 805306368 | tf_op jit(solution)/shard_map/attention/pallas_call | solution.py:242
  27.1 1.1 %attention.5.local_ref = bf16[256,512]{1,0:T(8,128)(2,1)S(1)} custom-call(s32[2,2]{1,0:T(2,128)S(1)} %copy-done.3, f32[1,4]{1,0:T(1,128)S(1)} %copy-done.4, bf16[256,512]{1,0:T(8,128)(2,1)S(1)} %get-tuple-element.70.q_ref, bf16[256,512]{1,0:T(8,128)(2,1)S(1)} %get-tuple-element.71.refs_0_, ...), custom_call_target="tpu_custom_call" | custom-call | flops 268435456 | tf_op jit(solution)/shard_map/attention/pallas_call | solution.py:242
  28.2 0.9 %qkv.7 = (bf16[128,512]{1,0:T(8,128)(2,1)S(1)}, bf16[128,512]{1,0:T(8,128)(2,1)S(1)}, bf16[128,512]{1,0:T(8,128)(2,1)S(1)}, f32[4,128,128]{2,1,0:T(8,128)S(1)}) custom-call(f32[1,1024]{1,0:T(1,128)S(1)} %copy-done.1, bf16[1024,1536]{1,0:T(8,128)(2,1)S(1)} %bitcast.20, f32[1024,8]{1,0:T(8,128)S(1)} %get-tuple-element.62.fade_ref, ...), custom_call_target="tpu_custom_call" | custom-call | flops 805306368 | tf_op jit(solution)/shard_map/qkv/pallas_call | solution.py:148
  29.1 1.4 %attention.8.local_ref = bf16[128,512]{1,0:T(8,128)(2,1)S(1)} custom-call(s32[2,2]{1,0:T(2,128)S(1)} %copy-done.3, f32[1,4]{1,0:T(1,128)S(1)} %copy-done.4, bf16[128,512]{1,0:T(8,128)(2,1)S(1)} %get-tuple-element.79.q_ref, bf16[256,512]{1,0:T(8,128)(2,1)S(1)} %get-tuple-element.71.refs_0_, bf16[256,512]{1,0:T(8,128)(2,1)S(1)} %get-tuple-element.74.refs_1_, ...), custom_call_target="tpu_custom_call" | custom-call | flops 469762048 | tf_op jit(solution)/shard_map/attention/pallas_call | solution.py:242
  30.5 0.8 %last_keys_values.1 = (bf16[128,512]{1,0:T(8,128)(2,1)S(1)}, bf16[128,512]{1,0:T(8,128)(2,1)S(1)}, bf16[528,128]{1,0:T(8,128)(2,1)S(1)}) custom-call(f32[1,1024]{1,0:T(1,128)S(1)} %copy-done.1, bf16[1024,1536]{1,0:T(8,128)(2,1)S(1)} %bitcast.21, f32[1024,8]{1,0:T(8,128)S(1)} %get-tuple-element.62.fade_ref, f32[4,128,128]{2,1,0:T(8,128)S(1)} %get-tuple-element.82.prev_ref, ...), custom_call_target="tpu_custom_call" | custom-call | flops 603979776 | tf_op jit(solution)/shard_map/last_keys_values/pallas_call | solution.py:179
  31.4 2.1 %collective-permute-start.5 = (bf16[528,128]{1,0:T(8,128)(2,1)S(1)}, bf16[528,128]{1,0:T(8,128)(2,1)S(1)}, u32[]{:S(2)}, u32[]{:S(2)}) collective-permute-start(bf16[528,128]{1,0:T(8,128)(2,1)S(1)} %get-tuple-element.88.refs_0_), channel_id=1, source_target_pairs={{0,4},{4,0},{8,12},{12,8},{16,20},{20,16},{24,28},{28,24},{1,5},{5... | collective-permute-start | bytes 405512 | tf_op jit(solution)/shard_map/ppermute | solution.py:468
  33.5 1.6 %collective-permute-start.6 = (bf16[528,128]{1,0:T(8,128)(2,1)S(1)}, bf16[528,128]{1,0:T(8,128)(2,1)S(1)}, u32[]{:S(2)}, u32[]{:S(2)}) collective-permute-start(bf16[528,128]{1,0:T(8,128)(2,1)S(1)} %get-tuple-element.88.refs_0_), channel_id=1, source_target_pairs={{0,8},{4,12},{8,0},{12,4},{16,24},{20,28},{24,16},{28,20},{1,9},{5... | collective-permute-start | bytes 405512 | tf_op jit(solution)/shard_map/ppermute | solution.py:468
  35.0 0.6 last_queries.1.q_ref
  35.7 1.6 %attention.9.local_ref = bf16[128,512]{1,0:T(8,128)(2,1)S(1)} custom-call(s32[2,2]{1,0:T(2,128)S(1)} %copy-done.3, f32[1,4]{1,0:T(1,128)S(1)} %copy-done.4, bf16[128,512]{1,0:T(8,128)(2,1)S(1)} %last_queries.1.q_ref, bf16[256,512]{1,0:T(8,128)(2,1)S(1)} %get-tuple-element.71.refs_0_, bf16[256,512]{1,0:T(8,128)(2,1)S(1)} %get-tuple-element.74.refs_1_, ...), custom_call_target="tpu_custom_call" | custom-call | flops 536870912 | tf_op jit(solution)/shard_map/attention/pallas_call | solution.py:242
  37.2 0.6 collective-permute-done.5.refs_1_
  37.8 0.6 collective-permute-done.6.refs_2_
  38.5 2.5 %collective-permute-done.7.refs_3_ = bf16[528,128]{1,0:T(8,128)(2,1)S(1)} collective-permute-done((bf16[528,128]{1,0:T(8,128)(2,1)S(1)}, bf16[528,128]{1,0:T(8,128)(2,1)S(1)}, u32[]{:S(2)}, u32[]{:S(2)}) %collective-permute-start.7) | collective-permute-done | bytes 135200 | tf_op jit(solution)/shard_map/ppermute | solution.py:468
  41.3 3.5 %collective-permute-start.8 = (bf16[528,128]{1,0:T(8,128)(2,1)S(1)}, bf16[528,128]{1,0:T(8,128)(2,1)S(1)}, u32[]{:S(2)}, u32[]{:S(2)}) collective-permute-start(bf16[528,128]{1,0:T(8,128)(2,1)S(1)} %get-tuple-element.94.refs_0_), channel_id=1, source_target_pairs={{0,16},{4,20},{8,24},{12,28},{16,0},{20,4},{24,8},{28,12},{1,17},{... | collective-permute-start | bytes 405512 | tf_op jit(solution)/shard_map/ppermute | solution.py:475
  44.8 3.9 %collective-permute-done.8.refs_1_ = bf16[528,128]{1,0:T(8,128)(2,1)S(1)} collective-permute-done((bf16[528,128]{1,0:T(8,128)(2,1)S(1)}, bf16[528,128]{1,0:T(8,128)(2,1)S(1)}, u32[]{:S(2)}, u32[]{:S(2)}) %collective-permute-start.8) | collective-permute-done | bytes 135200 | tf_op jit(solution)/shard_map/ppermute | solution.py:475
  49.2 1.3 %collective-permute-done.9.side_ref = bf16[128,512]{1,0:T(8,128)(2,1)S(1)} collective-permute-done((bf16[128,512]{1,0:T(8,128)(2,1)S(1)}, bf16[128,512]{1,0:T(8,128)(2,1)S(1)}, u32[]{:S(2)}, u32[]{:S(2)}) %collective-permute-start.9) | collective-permute-done | bytes 131104 | tf_op jit(solution)/shard_map/ppermute | solution.py:483
  50.5 0.5 project.5
  51.7 0.4 collective-permute-start.15
  53.2 0.7 project.9
  53.9 1.6 %collective-permute-start.18 = (bf16[256,512]{1,0:T(8,128)(2,1)S(1)}, bf16[256,512]{1,0:T(8,128)(2,1)S(1)}, u32[]{:S(2)}, u32[]{:S(2)}) collective-permute-start(bf16[256,512]{1,0:T(8,128)(2,1)S(1)} %get-tuple-element.112), channel_id=1, source_target_pairs={{0,1},{1,0},{2,3},{3,2},{4,5},{5,4},{6,7},{7,6},{8,9},{9,8},{10,11... | collective-permute-start | bytes 786440 | tf_op jit(solution)/shard_map/ppermute | solution.py:488
  55.5 0.7 project.8
  56.2 0.6 collective-permute-start.16
  56.8 0.7 project.7
  57.5 1.6 %collective-permute-start.14 = (bf16[256,512]{1,0:T(8,128)(2,1)S(1)}, bf16[256,512]{1,0:T(8,128)(2,1)S(1)}, u32[]{:S(2)}, u32[]{:S(2)}) collective-permute-start(bf16[256,512]{1,0:T(8,128)(2,1)S(1)} %get-tuple-element.104), channel_id=1, source_target_pairs={{0,1},{1,0},{2,3},{3,2},{4,5},{5,4},{6,7},{7,6},{8,9},{9,8},{10,11... | collective-permute-start | bytes 786440 | tf_op jit(solution)/shard_map/ppermute | solution.py:488
  59.1 0.5 collective-permute-start.19
  59.6 0.5 project.6
  60.1 1.6 %collective-permute-start.12 = (bf16[128,512]{1,0:T(8,128)(2,1)S(1)}, bf16[128,512]{1,0:T(8,128)(2,1)S(1)}, u32[]{:S(2)}, u32[]{:S(2)}) collective-permute-start(bf16[128,512]{1,0:T(8,128)(2,1)S(1)} %get-tuple-element.100), channel_id=1, source_target_pairs={{0,1},{1,0},{2,3},{3,2},{4,5},{5,4},{6,7},{7,6},{8,9},{9,8},{10,11... | collective-permute-start | bytes 393224 | tf_op jit(solution)/shard_map/ppermute | solution.py:488
  61.7 15.5 %collective-permute-done.19.refs_1_ = bf16[128,512]{1,0:T(8,128)(2,1)S(1)} collective-permute-done((bf16[128,512]{1,0:T(8,128)(2,1)S(1)}, bf16[128,512]{1,0:T(8,128)(2,1)S(1)}, u32[]{:S(2)}, u32[]{:S(2)}) %collective-permute-start.19) | collective-permute-done | bytes 131104 | tf_op jit(solution)/shard_map/ppermute | solution.py:488
  77.2 0.7 finish.5.refs_2_
  77.9 0.8 finish.6.refs_2_
  78.6 0.8 finish.7.refs_2_
  79.4 0.8 finish.8.refs_2_
  80.2 0.7 finish.9
  (36 shorter events, 2.7 us)
Async XLA Ops:
  1.2 11.3 %collective-permute-start = (bf16[256,512]{1,0:T(8,128)(2,1)S(1)}, bf16[256,512]{1,0:T(8,128)(2,1)S(1)}, u32[]{:S(2)}, u32[]{:S(2)}) collective-permute-start(bf16[256,512]{1,0:T(8,128)(2,1)S(1)} %get-tuple-element.63.refs_0_), channel_id=1, source_target_pairs={{1,0},{0,1},{3,2},{2,3},{5,4},{4,5},{7,6},{6,7},{9,8},{8,9},{11,10... | collective-permute-start | bytes 786440 | tf_op jit(solution)/shard_map/ppermute | solution.py:445
  4.2 12.8 %collective-permute-start.2 = (bf16[256,512]{1,0:T(8,128)(2,1)S(1)}, bf16[256,512]{1,0:T(8,128)(2,1)S(1)}, u32[]{:S(2)}, u32[]{:S(2)}) collective-permute-start(bf16[256,512]{1,0:T(8,128)(2,1)S(1)} %get-tuple-element.117.refs_1_), channel_id=1, source_target_pairs={{1,0},{0,1},{3,2},{2,3},{5,4},{4,5},{7,6},{6,7},{9,8},{8,9},{11,10... | collective-permute-start | bytes 786440 | tf_op jit(solution)/shard_map/ppermute | solution.py:445
  4.3 18.3 %collective-permute-start.3 = (bf16[256,512]{1,0:T(8,128)(2,1)S(1)}, bf16[256,512]{1,0:T(8,128)(2,1)S(1)}, u32[]{:S(2)}, u32[]{:S(2)}) collective-permute-start(bf16[256,512]{1,0:T(8,128)(2,1)S(1)} %get-tuple-element.115.refs_1_), channel_id=1, source_target_pairs={{1,0},{0,1},{3,2},{2,3},{5,4},{4,5},{7,6},{6,7},{9,8},{8,9},{11,10... | collective-permute-start | bytes 786440 | tf_op jit(solution)/shard_map/ppermute | solution.py:445
  6.2 44.3 %collective-permute-start.10 = (bf16[512,1024]{1,0:T(8,128)(2,1)}, bf16[512,1024]{1,0:T(8,128)(2,1)S(1)}, u32[]{:S(2)}, u32[]{:S(2)}) collective-permute-start(bf16[512,1024]{1,0:T(8,128)(2,1)} %bitcast.30), channel_id=1, source_target_pairs={{0,2},{2,0},{1,3},{3,1},{4,6},{6,4},{5,7},{7,5},{8,10},{10,8},{9,1... | collective-permute-start | bytes 3145736 | tf_op jit(solution)/shard_map/ppermute | solution.py:427
  7.2 0.7 copy-start.2
  7.9 0.7 copy-start.5
  10.0 4.6 %copy-start.1 = (f32[1,1024]{1,0:T(1,128)S(1)}, f32[1,1024]{1,0:T(1,128)}, u32[]{:S(2)}) copy-start(f32[1,1024]{1,0:T(1,128)} %gain_ref.11) | copy-start | bytes 12292
  12.5 15.7 %collective-permute-start.4 = (bf16[128,512]{1,0:T(8,128)(2,1)S(1)}, bf16[128,512]{1,0:T(8,128)(2,1)S(1)}, u32[]{:S(2)}, u32[]{:S(2)}) collective-permute-start(bf16[128,512]{1,0:T(8,128)(2,1)S(1)} %get-tuple-element.68.refs_1_), channel_id=1, source_target_pairs={{1,0},{0,1},{3,2},{2,3},{5,4},{4,5},{7,6},{6,7},{9,8},{8,9},{11,10... | collective-permute-start | bytes 393224 | tf_op jit(solution)/shard_map/ppermute | solution.py:445
  13.4 17.2 %collective-permute-start.1 = (bf16[128,512]{1,0:T(8,128)(2,1)S(1)}, bf16[128,512]{1,0:T(8,128)(2,1)S(1)}, u32[]{:S(2)}, u32[]{:S(2)}) collective-permute-start(bf16[128,512]{1,0:T(8,128)(2,1)S(1)} %get-tuple-element.61.refs_0_), channel_id=1, source_target_pairs={{1,0},{0,1},{3,2},{2,3},{5,4},{4,5},{7,6},{6,7},{9,8},{8,9},{11,10... | collective-permute-start | bytes 393224 | tf_op jit(solution)/shard_map/ppermute | solution.py:445
  18.3 5.6 %copy-start.3 = (s32[2,2]{1,0:T(2,128)S(1)}, s32[2,2]{1,0:T(2,128)}, u32[]{:S(2)}) copy-start(s32[2,2]{1,0:T(2,128)} %keep_ref.9) | copy-start | bytes 52
  18.3 5.6 %copy-start.4 = (f32[1,4]{1,0:T(1,128)S(1)}, f32[1,4]{1,0:T(1,128)}, u32[]{:S(2)}) copy-start(f32[1,4]{1,0:T(1,128)} %scale_ref.9) | copy-start | bytes 52
  31.4 19.2 %copy-start = (bf16[1,4,128,1024]{3,2,1,0:T(8,128)(2,1)S(1)}, bf16[1,4,128,1024]{3,2,1,0:T(8,128)(2,1)}, u32[]{:S(2)}) copy-start(bf16[1,4,128,1024]{3,2,1,0:T(8,128)(2,1)} %param.16) | copy-start | bytes 3145732
  31.4 6.5 %collective-permute-start.5 = (bf16[528,128]{1,0:T(8,128)(2,1)S(1)}, bf16[528,128]{1,0:T(8,128)(2,1)S(1)}, u32[]{:S(2)}, u32[]{:S(2)}) collective-permute-start(bf16[528,128]{1,0:T(8,128)(2,1)S(1)} %get-tuple-element.88.refs_0_), channel_id=1, source_target_pairs={{0,4},{4,0},{8,12},{12,8},{16,20},{20,16},{24,28},{28,24},{1,5},{5... | collective-permute-start | bytes 405512 | tf_op jit(solution)/shard_map/ppermute | solution.py:468
  33.5 5.0 %collective-permute-start.6 = (bf16[528,128]{1,0:T(8,128)(2,1)S(1)}, bf16[528,128]{1,0:T(8,128)(2,1)S(1)}, u32[]{:S(2)}, u32[]{:S(2)}) collective-permute-start(bf16[528,128]{1,0:T(8,128)(2,1)S(1)} %get-tuple-element.88.refs_0_), channel_id=1, source_target_pairs={{0,8},{4,12},{8,0},{12,4},{16,24},{20,28},{24,16},{28,20},{1,9},{5... | collective-permute-start | bytes 405512 | tf_op jit(solution)/shard_map/ppermute | solution.py:468
  35.0 5.9 %collective-permute-start.7 = (bf16[528,128]{1,0:T(8,128)(2,1)S(1)}, bf16[528,128]{1,0:T(8,128)(2,1)S(1)}, u32[]{:S(2)}, u32[]{:S(2)}) collective-permute-start(bf16[528,128]{1,0:T(8,128)(2,1)S(1)} %get-tuple-element.88.refs_0_), channel_id=1, source_target_pairs={{0,12},{4,8},{8,4},{12,0},{16,28},{20,24},{24,20},{28,16},{1,13},{... | collective-permute-start | bytes 405512 | tf_op jit(solution)/shard_map/ppermute | solution.py:468
  41.3 7.4 %collective-permute-start.8 = (bf16[528,128]{1,0:T(8,128)(2,1)S(1)}, bf16[528,128]{1,0:T(8,128)(2,1)S(1)}, u32[]{:S(2)}, u32[]{:S(2)}) collective-permute-start(bf16[528,128]{1,0:T(8,128)(2,1)S(1)} %get-tuple-element.94.refs_0_), channel_id=1, source_target_pairs={{0,16},{4,20},{8,24},{12,28},{16,0},{20,4},{24,8},{28,12},{1,17},{... | collective-permute-start | bytes 405512 | tf_op jit(solution)/shard_map/ppermute | solution.py:475
  48.9 1.6 %collective-permute-start.9 = (bf16[128,512]{1,0:T(8,128)(2,1)S(1)}, bf16[128,512]{1,0:T(8,128)(2,1)S(1)}, u32[]{:S(2)}, u32[]{:S(2)}) collective-permute-start(bf16[128,512]{1,0:T(8,128)(2,1)S(1)} %recall.5.own_ref), channel_id=1, source_target_pairs={{0,2},{2,0},{1,3},{3,1},{4,6},{6,4},{5,7},{7,5},{8,10},{10,8},{9,1... | collective-permute-start | bytes 393224 | tf_op jit(solution)/shard_map/ppermute | solution.py:483
  51.2 2.0 %collective-permute-start.17 = (bf16[256,512]{1,0:T(8,128)(2,1)S(1)}, bf16[256,512]{1,0:T(8,128)(2,1)S(1)}, u32[]{:S(2)}, u32[]{:S(2)}) collective-permute-start(bf16[256,512]{1,0:T(8,128)(2,1)S(1)} %recall.9.own_ref), channel_id=1, source_target_pairs={{0,2},{2,0},{1,3},{3,1},{4,6},{6,4},{5,7},{7,5},{8,10},{10,8},{9,1... | collective-permute-start | bytes 786440 | tf_op jit(solution)/shard_map/ppermute | solution.py:483
  51.7 3.8 %collective-permute-start.15 = (bf16[256,512]{1,0:T(8,128)(2,1)S(1)}, bf16[256,512]{1,0:T(8,128)(2,1)S(1)}, u32[]{:S(2)}, u32[]{:S(2)}) collective-permute-start(bf16[256,512]{1,0:T(8,128)(2,1)S(1)} %recall.8.own_ref), channel_id=1, source_target_pairs={{0,2},{2,0},{1,3},{3,1},{4,6},{6,4},{5,7},{7,5},{8,10},{10,8},{9,1... | collective-permute-start | bytes 786440 | tf_op jit(solution)/shard_map/ppermute | solution.py:483
  52.4 4.5 %collective-permute-start.13 = (bf16[256,512]{1,0:T(8,128)(2,1)S(1)}, bf16[256,512]{1,0:T(8,128)(2,1)S(1)}, u32[]{:S(2)}, u32[]{:S(2)}) collective-permute-start(bf16[256,512]{1,0:T(8,128)(2,1)S(1)} %recall.7.own_ref), channel_id=1, source_target_pairs={{0,2},{2,0},{1,3},{3,1},{4,6},{6,4},{5,7},{7,5},{8,10},{10,8},{9,1... | collective-permute-start | bytes 786440 | tf_op jit(solution)/shard_map/ppermute | solution.py:483
  52.8 6.9 %collective-permute-start.11 = (bf16[128,512]{1,0:T(8,128)(2,1)S(1)}, bf16[128,512]{1,0:T(8,128)(2,1)S(1)}, u32[]{:S(2)}, u32[]{:S(2)}) collective-permute-start(bf16[128,512]{1,0:T(8,128)(2,1)S(1)} %recall.6.own_ref), channel_id=1, source_target_pairs={{0,2},{2,0},{1,3},{3,1},{4,6},{6,4},{5,7},{7,5},{8,10},{10,8},{9,1... | collective-permute-start | bytes 393224 | tf_op jit(solution)/shard_map/ppermute | solution.py:483
  53.9 24.0 %collective-permute-start.18 = (bf16[256,512]{1,0:T(8,128)(2,1)S(1)}, bf16[256,512]{1,0:T(8,128)(2,1)S(1)}, u32[]{:S(2)}, u32[]{:S(2)}) collective-permute-start(bf16[256,512]{1,0:T(8,128)(2,1)S(1)} %get-tuple-element.112), channel_id=1, source_target_pairs={{0,1},{1,0},{2,3},{3,2},{4,5},{5,4},{6,7},{7,6},{8,9},{9,8},{10,11... | collective-permute-start | bytes 786440 | tf_op jit(solution)/shard_map/ppermute | solution.py:488
  56.2 22.4 %collective-permute-start.16 = (bf16[256,512]{1,0:T(8,128)(2,1)S(1)}, bf16[256,512]{1,0:T(8,128)(2,1)S(1)}, u32[]{:S(2)}, u32[]{:S(2)}) collective-permute-start(bf16[256,512]{1,0:T(8,128)(2,1)S(1)} %get-tuple-element.108), channel_id=1, source_target_pairs={{0,1},{1,0},{2,3},{3,2},{4,5},{5,4},{6,7},{7,6},{8,9},{9,8},{10,11... | collective-permute-start | bytes 786440 | tf_op jit(solution)/shard_map/ppermute | solution.py:488
  57.5 21.9 %collective-permute-start.14 = (bf16[256,512]{1,0:T(8,128)(2,1)S(1)}, bf16[256,512]{1,0:T(8,128)(2,1)S(1)}, u32[]{:S(2)}, u32[]{:S(2)}) collective-permute-start(bf16[256,512]{1,0:T(8,128)(2,1)S(1)} %get-tuple-element.104), channel_id=1, source_target_pairs={{0,1},{1,0},{2,3},{3,2},{4,5},{5,4},{6,7},{7,6},{8,9},{9,8},{10,11... | collective-permute-start | bytes 786440 | tf_op jit(solution)/shard_map/ppermute | solution.py:488
  59.1 18.0 %collective-permute-start.19 = (bf16[128,512]{1,0:T(8,128)(2,1)S(1)}, bf16[128,512]{1,0:T(8,128)(2,1)S(1)}, u32[]{:S(2)}, u32[]{:S(2)}) collective-permute-start(bf16[128,512]{1,0:T(8,128)(2,1)S(1)} %get-tuple-element.114), channel_id=1, source_target_pairs={{0,1},{1,0},{2,3},{3,2},{4,5},{5,4},{6,7},{7,6},{8,9},{9,8},{10,11... | collective-permute-start | bytes 393224 | tf_op jit(solution)/shard_map/ppermute | solution.py:488
  60.1 20.1 %collective-permute-start.12 = (bf16[128,512]{1,0:T(8,128)(2,1)S(1)}, bf16[128,512]{1,0:T(8,128)(2,1)S(1)}, u32[]{:S(2)}, u32[]{:S(2)}) collective-permute-start(bf16[128,512]{1,0:T(8,128)(2,1)S(1)} %get-tuple-element.100), channel_id=1, source_target_pairs={{0,1},{1,0},{2,3},{3,2},{4,5},{5,4},{6,7},{7,6},{8,9},{9,8},{10,11... | collective-permute-start | bytes 393224 | tf_op jit(solution)/shard_map/ppermute | solution.py:488

commit v9 on v8

--- a/solution.py
+++ b/solution.py
@@ -455,8 +455,9 @@
         qs.append(q)
         ks.append(k)
         vs.append(v)
-        locals_.append(attention(first, tile_retain_grid, score_scaler, q, ks, vs, heads, dim))
-    summary, *locals_ = tied(summary, *locals_)
+        local = attention(first, tile_retain_grid, score_scaler, q, ks, vs, heads, dim)
+        summary, local = tied(summary, local)
+        locals_.append(local)
     k, v, sent = last_keys_values(
         gain, w, fade, summary, tail, received[-1], heads, dim, firsts[-1]
     )
@@ -478,7 +479,7 @@
     state = entering(quad_size, before, decay, totals, heads, dim)
 
     result = None
-    for c in [chunks - 2, *range(chunks - 2), chunks - 1]:
+    for c in range(chunks):
         head_out = recall(readings[c], qs[c], locals_[c], state, heads, dim)
         side = lax.ppermute(head_out, "stream", swap_streams)
         outs = project(head_out, side, own_w, side_w, shards)
@@ -487,8 +488,6 @@
             parts.append(
                 lax.ppermute(outs[k], "head", [(d, (d + k) % shards) for d in range(shards)])
             )
-        if result is None:
-            state, parts[0] = tied(state, parts[0])
         result = finish(parts, result, firsts[c], length)
     return result[None]
 

time: 81.1 us -> 76.1 us (0.938)
  waiting for transfers between devices: 29.7 us -> 24.6 us
    ppermute x5, waiting for transfers between devices: 5.22 us -> 2.85 us  [per_device(): lax.ppermute(pieces[c], 'head', [((d + k) % shards, d) for d in range(sha...]
    ppermute x5, waiting for transfers between devices: 1.35 us -> 0.01 us  [per_device(): side = lax.ppermute(head_out, 'stream', swap_streams)]
    ppermute x5, waiting for transfers between devices: 15.5 us -> 14.3 us  [per_device(): lax.ppermute(outs[k], 'head', [(d, (d + k) % shards) for d in range(shard...]
  transfers between devices with their start and end apart: 20 -> 20, of which waited for: 8 -> 12; matrix products, arithmetic and copies ran while one was open for 4% -> 5% of each run, Pallas kernels for 27% -> 30%
where the time goes in v9:
time: 76.1 us; the launch traced here: 75.8 us
  waiting for transfers between devices  24.6 us (32%)
  Pallas kernels  23.4 us (31%)
  starting transfers between devices  21.6 us (28%)
  local copies, waits for them, and re-layouts  5.99 us (8%)
    ppermute x5, waiting for transfers between devices, per_device(): lax.ppermute(outs[k], 'head', [(d, (d + k) % shards) for d in range(shard...  14.3 us
    ppermute x5, starting transfers between devices, per_device(): lax.ppermute(pieces[c], 'head', [((d + k) % shards, d) for d in range(sha...  7.26 us
    pallas_call x5, Pallas kernels, attention(): pl.pallas_call(functools.partial(attention_kernel, first, heads, dim), in...  7.16 us
    ppermute x5, starting transfers between devices, per_device(): lax.ppermute(outs[k], 'head', [(d, (d + k) % shards) for d in range(shard...  5.93 us
    pallas_call x4, Pallas kernels, qkv(): pl.pallas_call(functools.partial(qkv_kernel, heads, dim, first), in_specs...  5.03 us
    ppermute x1, waiting for transfers between devices, per_device(): lax.ppermute(total, 'tm', [(d, d ^ quad_size * k) for d in range(blocks)])  3.89 us
    unnamed x13, local copies, waits for them, and re-layouts  3.85 us
    pallas_call x5, Pallas kernels, finish(): pl.pallas_call(functools.partial(finish_kernel, len(parts)), grid=(1,), i...  3.67 us
  transfers between devices with their start and end apart: 20, of which 12 were waited for; matrix products, arithmetic and copies ran while one was open for 5% of the time, Pallas kernels for 30%

profile of v9, /device:TPU:0, one launch (start us, length us, event | category | flops | bytes accessed | tf_op | source)
XLA Modules:
  0.0 75.8 jit_solution(710905038885404915)
XLA Ops:
  0.0 1.2 %slice_bitcast_fusion = (bf16[256,512]{1,0:T(8,128)(2,1)S(1)}, bf16[256,512]{1,0:T(8,128)(2,1)S(1)}, bf16[256,512]{1,0:T(8,128)(2,1)S(1)}) fusion(bf16[1,1024,512]{2,1,0:T(8,128)(2,1)} %param.9), kind=kLoop, calls=%fused_computation | loop fusion | bytes 1572864 | tf_op jit(solution)/shard_map/slice | solution.py:437
  1.2 3.0 %collective-permute-start = (bf16[256,512]{1,0:T(8,128)(2,1)S(1)}, bf16[256,512]{1,0:T(8,128)(2,1)S(1)}, u32[]{:S(2)}, u32[]{:S(2)}) collective-permute-start(bf16[256,512]{1,0:T(8,128)(2,1)S(1)} %get-tuple-element.64.refs_0_), channel_id=1, source_target_pairs={{1,0},{0,1},{3,2},{2,3},{5,4},{4,5},{7,6},{6,7},{9,8},{8,9},{11,10... | collective-permute-start | bytes 786440 | tf_op jit(solution)/shard_map/ppermute | solution.py:445
  4.3 1.9 %collective-permute-start.3 = (bf16[256,512]{1,0:T(8,128)(2,1)S(1)}, bf16[256,512]{1,0:T(8,128)(2,1)S(1)}, u32[]{:S(2)}, u32[]{:S(2)}) collective-permute-start(bf16[256,512]{1,0:T(8,128)(2,1)S(1)} %get-tuple-element.117.refs_1_), channel_id=1, source_target_pairs={{1,0},{0,1},{3,2},{2,3},{5,4},{4,5},{7,6},{6,7},{9,8},{8,9},{11,10... | collective-permute-start | bytes 786440 | tf_op jit(solution)/shard_map/ppermute | solution.py:445
  6.2 1.0 %slice_bitcast_fusion.3 = (bf16[128,512]{1,0:T(8,128)(2,1)S(1)}, bf16[128,512]{1,0:T(8,128)(2,1)S(1)}) fusion(bf16[1,1024,512]{2,1,0:T(8,128)(2,1)} %param.9), kind=kLoop, calls=%fused_computation.3 | loop fusion | bytes 524288 | tf_op jit(solution)/shard_map/slice | solution.py:437
  7.2 0.7 copy-done.2
  7.9 0.7 copy-done.5
  8.6 1.4 %prepare.1 = (f32[1024,8]{1,0:T(8,128)S(1)}, bf16[16,128]{1,0:T(8,128)(2,1)S(1)}, f32[256,8]{1,0:T(8,128)S(1)}, f32[256,8]{1,0:T(8,128)S(1)}, f32[256,8]{1,0:T(8...) custom-call(f32[4,1024]{1,0:T(4,128)S(1)} %bitcast.28, s32[2]{0:T(128)S(1)} %copy-done.5), custom_call_target="tpu_custom_call" | custom-call | flops 327680 | tf_op jit(solution)/shard_map/prepare/pallas_call | solution.py:83
  10.0 2.5 %copy.14 = bf16[128,8,4,384]{3,1,2,0:T(8,128)(2,1)S(1)} copy(bf16[128,8,4,384]{3,2,1,0:T(4,128)(2,1)} %bitcast.29) | data formatting | bytes 6291456
  12.5 1.4 %qkv.4 = (bf16[256,512]{1,0:T(8,128)(2,1)S(1)}, bf16[256,512]{1,0:T(8,128)(2,1)S(1)}, bf16[256,512]{1,0:T(8,128)(2,1)S(1)}, f32[4,128,128]{2,1,0:T(8,128)S(1)}) custom-call(f32[1,1024]{1,0:T(1,128)S(1)} %copy-done.1, bf16[1024,1536]{1,0:T(8,128)(2,1)S(1)} %bitcast.17, f32[1024,8]{1,0:T(8,128)S(1)} %get-tuple-element.63.fade_ref, ...), custom_call_target="tpu_custom_call" | custom-call | flops 1610612736 | tf_op jit(solution)/shard_map/qkv/pallas_call | solution.py:148
  13.9 1.1 %attention.5.local_ref = bf16[256,512]{1,0:T(8,128)(2,1)S(1)} custom-call(s32[2,2]{1,0:T(2,128)S(1)} %copy-done.3, f32[1,4]{1,0:T(1,128)S(1)} %copy-done.4, bf16[256,512]{1,0:T(8,128)(2,1)S(1)} %get-tuple-element.67.q_ref, bf16[256,512]{1,0:T(8,128)(2,1)S(1)} %get-tuple-element.68.refs_0_, ...), custom_call_target="tpu_custom_call" | custom-call | flops 268435456 | tf_op jit(solution)/shard_map/attention/pallas_call | solution.py:242
  15.0 1.9 %collective-permute-done.2.refs_2_ = bf16[256,512]{1,0:T(8,128)(2,1)S(1)} collective-permute-done((bf16[256,512]{1,0:T(8,128)(2,1)S(1)}, bf16[256,512]{1,0:T(8,128)(2,1)S(1)}, u32[]{:S(2)}, u32[]{:S(2)}) %collective-permute-start.2) | collective-permute-done | bytes 262176 | tf_op jit(solution)/shard_map/ppermute | solution.py:445
  16.9 1.4 %qkv.5 = (bf16[256,512]{1,0:T(8,128)(2,1)S(1)}, bf16[256,512]{1,0:T(8,128)(2,1)S(1)}, bf16[256,512]{1,0:T(8,128)(2,1)S(1)}, f32[4,128,128]{2,1,0:T(8,128)S(1)}) custom-call(f32[1,1024]{1,0:T(1,128)S(1)} %copy-done.1, bf16[1024,1536]{1,0:T(8,128)(2,1)S(1)} %bitcast.18, f32[1024,8]{1,0:T(8,128)S(1)} %get-tuple-element.63.fade_ref, ...), custom_call_target="tpu_custom_call" | custom-call | flops 1610612736 | tf_op jit(solution)/shard_map/qkv/pallas_call | solution.py:148
  18.3 1.5 %attention.6.local_ref = bf16[256,512]{1,0:T(8,128)(2,1)S(1)} custom-call(s32[2,2]{1,0:T(2,128)S(1)} %copy-done.3, f32[1,4]{1,0:T(1,128)S(1)} %copy-done.4, bf16[256,512]{1,0:T(8,128)(2,1)S(1)} %get-tuple-element.72.q_ref, bf16[256,512]{1,0:T(8,128)(2,1)S(1)} %get-tuple-element.68.refs_0_, bf16[256,512]{1,0:T(8,128)(2,1)S(1)} %get-tuple-element.73.refs_1_, ...), custom_call_target="tpu_custom_call" | custom-call | flops 536870912 | tf_op jit(solution)/shard_map/attention/pallas_call | solution.py:242
  19.8 2.1 %collective-permute-start.4 = (bf16[128,512]{1,0:T(8,128)(2,1)S(1)}, bf16[128,512]{1,0:T(8,128)(2,1)S(1)}, u32[]{:S(2)}, u32[]{:S(2)}) collective-permute-start(bf16[128,512]{1,0:T(8,128)(2,1)S(1)} %get-tuple-element.81.refs_1_), channel_id=1, source_target_pairs={{1,0},{0,1},{3,2},{2,3},{5,4},{4,5},{7,6},{6,7},{9,8},{8,9},{11,10... | collective-permute-start | bytes 393224 | tf_op jit(solution)/shard_map/ppermute | solution.py:445
  22.4 1.4 %qkv.6 = (bf16[256,512]{1,0:T(8,128)(2,1)S(1)}, bf16[256,512]{1,0:T(8,128)(2,1)S(1)}, bf16[256,512]{1,0:T(8,128)(2,1)S(1)}, f32[4,128,128]{2,1,0:T(8,128)S(1)}) custom-call(f32[1,1024]{1,0:T(1,128)S(1)} %copy-done.1, bf16[1024,1536]{1,0:T(8,128)(2,1)S(1)} %bitcast.19, f32[1024,8]{1,0:T(8,128)S(1)} %get-tuple-element.63.fade_ref, ...), custom_call_target="tpu_custom_call" | custom-call | flops 1610612736 | tf_op jit(solution)/shard_map/qkv/pallas_call | solution.py:148
  23.7 1.7 %attention.7.local_ref = bf16[256,512]{1,0:T(8,128)(2,1)S(1)} custom-call(s32[2,2]{1,0:T(2,128)S(1)} %copy-done.3, f32[1,4]{1,0:T(1,128)S(1)} %copy-done.4, bf16[256,512]{1,0:T(8,128)(2,1)S(1)} %get-tuple-element.77.q_ref, bf16[256,512]{1,0:T(8,128)(2,1)S(1)} %get-tuple-element.68.refs_0_, bf16[256,512]{1,0:T(8,128)(2,1)S(1)} %get-tuple-element.73.refs_1_, ...), custom_call_target="tpu_custom_call" | custom-call | flops 805306368 | tf_op jit(solution)/shard_map/attention/pallas_call | solution.py:242
  25.4 0.5 collective-permute-done.4.refs_2_
  25.9 0.9 %qkv.7 = (bf16[128,512]{1,0:T(8,128)(2,1)S(1)}, bf16[128,512]{1,0:T(8,128)(2,1)S(1)}, bf16[128,512]{1,0:T(8,128)(2,1)S(1)}, f32[4,128,128]{2,1,0:T(8,128)S(1)}) custom-call(f32[1,1024]{1,0:T(1,128)S(1)} %copy-done.1, bf16[1024,1536]{1,0:T(8,128)(2,1)S(1)} %bitcast.20, f32[1024,8]{1,0:T(8,128)S(1)} %get-tuple-element.63.fade_ref, ...), custom_call_target="tpu_custom_call" | custom-call | flops 805306368 | tf_op jit(solution)/shard_map/qkv/pallas_call | solution.py:148
  26.9 1.4 %attention.8.local_ref = bf16[128,512]{1,0:T(8,128)(2,1)S(1)} custom-call(s32[2,2]{1,0:T(2,128)S(1)} %copy-done.3, f32[1,4]{1,0:T(1,128)S(1)} %copy-done.4, bf16[128,512]{1,0:T(8,128)(2,1)S(1)} %get-tuple-element.83.q_ref, bf16[256,512]{1,0:T(8,128)(2,1)S(1)} %get-tuple-element.68.refs_0_, bf16[256,512]{1,0:T(8,128)(2,1)S(1)} %get-tuple-element.73.refs_1_, ...), custom_call_target="tpu_custom_call" | custom-call | flops 469762048 | tf_op jit(solution)/shard_map/attention/pallas_call | solution.py:242
  28.3 0.8 %last_keys_values.1 = (bf16[128,512]{1,0:T(8,128)(2,1)S(1)}, bf16[128,512]{1,0:T(8,128)(2,1)S(1)}, bf16[528,128]{1,0:T(8,128)(2,1)S(1)}) custom-call(f32[1,1024]{1,0:T(1,128)S(1)} %copy-done.1, bf16[1024,1536]{1,0:T(8,128)(2,1)S(1)} %bitcast.21, f32[1024,8]{1,0:T(8,128)S(1)} %get-tuple-element.63.fade_ref, f32[4,128,128]{2,1,0:T(8,128)S(1)} %get-tuple-element.86.prev_ref, ...), custom_call_target="tpu_custom_call" | custom-call | flops 603979776 | tf_op jit(solution)/shard_map/last_keys_values/pallas_call | solution.py:179
  29.1 1.8 %collective-permute-start.5 = (bf16[528,128]{1,0:T(8,128)(2,1)S(1)}, bf16[528,128]{1,0:T(8,128)(2,1)S(1)}, u32[]{:S(2)}, u32[]{:S(2)}) collective-permute-start(bf16[528,128]{1,0:T(8,128)(2,1)S(1)} %get-tuple-element.92.refs_0_), channel_id=1, source_target_pairs={{0,4},{4,0},{8,12},{12,8},{16,20},{20,16},{24,28},{28,24},{1,5},{5... | collective-permute-start | bytes 405512 | tf_op jit(solution)/shard_map/ppermute | solution.py:469
  30.9 1.6 %collective-permute-start.6 = (bf16[528,128]{1,0:T(8,128)(2,1)S(1)}, bf16[528,128]{1,0:T(8,128)(2,1)S(1)}, u32[]{:S(2)}, u32[]{:S(2)}) collective-permute-start(bf16[528,128]{1,0:T(8,128)(2,1)S(1)} %get-tuple-element.92.refs_0_), channel_id=1, source_target_pairs={{0,8},{4,12},{8,0},{12,4},{16,24},{20,28},{24,16},{28,20},{1,9},{5... | collective-permute-start | bytes 405512 | tf_op jit(solution)/shard_map/ppermute | solution.py:469
  32.6 0.6 last_queries.1.q_ref
  33.3 1.6 %attention.9.local_ref = bf16[128,512]{1,0:T(8,128)(2,1)S(1)} custom-call(s32[2,2]{1,0:T(2,128)S(1)} %copy-done.3, f32[1,4]{1,0:T(1,128)S(1)} %copy-done.4, bf16[128,512]{1,0:T(8,128)(2,1)S(1)} %last_queries.1.q_ref, bf16[256,512]{1,0:T(8,128)(2,1)S(1)} %get-tuple-element.68.refs_0_, bf16[256,512]{1,0:T(8,128)(2,1)S(1)} %get-tuple-element.73.refs_1_, ...), custom_call_target="tpu_custom_call" | custom-call | flops 536870912 | tf_op jit(solution)/shard_map/attention/pallas_call | solution.py:242
  34.8 0.8 %collective-permute-done.5.refs_1_ = bf16[528,128]{1,0:T(8,128)(2,1)S(1)} collective-permute-done((bf16[528,128]{1,0:T(8,128)(2,1)S(1)}, bf16[528,128]{1,0:T(8,128)(2,1)S(1)}, u32[]{:S(2)}, u32[]{:S(2)}) %collective-permute-start.5) | collective-permute-done | bytes 135200 | tf_op jit(solution)/shard_map/ppermute | solution.py:469
  35.9 2.5 %collective-permute-done.7.refs_3_ = bf16[528,128]{1,0:T(8,128)(2,1)S(1)} collective-permute-done((bf16[528,128]{1,0:T(8,128)(2,1)S(1)}, bf16[528,128]{1,0:T(8,128)(2,1)S(1)}, u32[]{:S(2)}, u32[]{:S(2)}) %collective-permute-start.7) | collective-permute-done | bytes 135200 | tf_op jit(solution)/shard_map/ppermute | solution.py:469
  38.7 3.5 %collective-permute-start.8 = (bf16[528,128]{1,0:T(8,128)(2,1)S(1)}, bf16[528,128]{1,0:T(8,128)(2,1)S(1)}, u32[]{:S(2)}, u32[]{:S(2)}) collective-permute-start(bf16[528,128]{1,0:T(8,128)(2,1)S(1)} %get-tuple-element.98.refs_0_), channel_id=1, source_target_pairs={{0,16},{4,20},{8,24},{12,28},{16,0},{20,4},{24,8},{28,12},{1,17},{... | collective-permute-start | bytes 405512 | tf_op jit(solution)/shard_map/ppermute | solution.py:476
  42.2 3.9 %collective-permute-done.8.refs_1_ = bf16[528,128]{1,0:T(8,128)(2,1)S(1)} collective-permute-done((bf16[528,128]{1,0:T(8,128)(2,1)S(1)}, bf16[528,128]{1,0:T(8,128)(2,1)S(1)}, u32[]{:S(2)}, u32[]{:S(2)}) %collective-permute-start.8) | collective-permute-done | bytes 135200 | tf_op jit(solution)/shard_map/ppermute | solution.py:476
  46.9 0.6 collective-permute-start.16
  47.9 0.6 collective-permute-start.12
  48.8 0.7 project.9
  49.5 1.6 %collective-permute-start.19 = (bf16[256,512]{1,0:T(8,128)(2,1)S(1)}, bf16[256,512]{1,0:T(8,128)(2,1)S(1)}, u32[]{:S(2)}, u32[]{:S(2)}) collective-permute-start(bf16[256,512]{1,0:T(8,128)(2,1)S(1)} %get-tuple-element.116), channel_id=1, source_target_pairs={{0,1},{1,0},{2,3},{3,2},{4,5},{5,4},{6,7},{7,6},{8,9},{9,8},{10,11... | collective-permute-start | bytes 786440 | tf_op jit(solution)/shard_map/ppermute | solution.py:489
  51.1 0.7 project.8
  51.9 0.6 collective-permute-start.17
  52.4 0.7 project.7
  53.1 1.6 %collective-permute-start.15 = (bf16[256,512]{1,0:T(8,128)(2,1)S(1)}, bf16[256,512]{1,0:T(8,128)(2,1)S(1)}, u32[]{:S(2)}, u32[]{:S(2)}) collective-permute-start(bf16[256,512]{1,0:T(8,128)(2,1)S(1)} %get-tuple-element.108), channel_id=1, source_target_pairs={{0,1},{1,0},{2,3},{3,2},{4,5},{5,4},{6,7},{7,6},{8,9},{9,8},{10,11... | collective-permute-start | bytes 786440 | tf_op jit(solution)/shard_map/ppermute | solution.py:489
  55.2 0.6 collective-permute-start.13
  56.2 1.6 %collective-permute-start.11 = (bf16[128,512]{1,0:T(8,128)(2,1)S(1)}, bf16[128,512]{1,0:T(8,128)(2,1)S(1)}, u32[]{:S(2)}, u32[]{:S(2)}) collective-permute-start(bf16[128,512]{1,0:T(8,128)(2,1)S(1)} %get-tuple-element.100), channel_id=1, source_target_pairs={{0,1},{1,0},{2,3},{3,2},{4,5},{5,4},{6,7},{7,6},{8,9},{9,8},{10,11... | collective-permute-start | bytes 393224 | tf_op jit(solution)/shard_map/ppermute | solution.py:489
  57.8 0.9 %collective-permute-done.19.refs_1_ = bf16[256,512]{1,0:T(8,128)(2,1)S(1)} collective-permute-done((bf16[256,512]{1,0:T(8,128)(2,1)S(1)}, bf16[256,512]{1,0:T(8,128)(2,1)S(1)}, u32[]{:S(2)}, u32[]{:S(2)}) %collective-permute-start.19) | collective-permute-done | bytes 262176 | tf_op jit(solution)/shard_map/ppermute | solution.py:489
  58.7 0.8 %finish.5.refs_2_ = bf16[1024,512]{1,0:T(8,128)(2,1)} custom-call(bf16[256,512]{1,0:T(8,128)(2,1)S(1)} %get-tuple-element.115.refs_0_, bf16[256,512]{1,0:T(8,128)(2,1)S(1)} %collective-permute-done.19.refs_1_), custom_call_target="tpu_custom_call" | custom-call | flops 262144 | bytes 786432 | tf_op jit(solution)/shard_map/finish/pallas_call | solution.py:390
  59.5 4.9 %collective-permute-done.17.refs_1_ = bf16[256,512]{1,0:T(8,128)(2,1)S(1)} collective-permute-done((bf16[256,512]{1,0:T(8,128)(2,1)S(1)}, bf16[256,512]{1,0:T(8,128)(2,1)S(1)}, u32[]{:S(2)}, u32[]{:S(2)}) %collective-permute-start.17) | collective-permute-done | bytes 262176 | tf_op jit(solution)/shard_map/ppermute | solution.py:489
  64.3 0.8 %finish.6.refs_2_ = bf16[1024,512]{1,0:T(8,128)(2,1)} custom-call(bf16[256,512]{1,0:T(8,128)(2,1)S(1)} %get-tuple-element.111.refs_0_, bf16[256,512]{1,0:T(8,128)(2,1)S(1)} %collective-permute-done.17.refs_1_, bf16[1024,512]{1,0:T(8,128)(2,1)} %finish.5.refs_2_), custom_call_target="tpu_custom_call", output_to_operand_aliasing={{}: (2, {})} | custom-call | flops 262144 | bytes 786432 | tf_op jit(solution)/shard_map/finish/pallas_call | solution.py:390
  65.1 4.9 %collective-permute-done.15.refs_1_ = bf16[256,512]{1,0:T(8,128)(2,1)S(1)} collective-permute-done((bf16[256,512]{1,0:T(8,128)(2,1)S(1)}, bf16[256,512]{1,0:T(8,128)(2,1)S(1)}, u32[]{:S(2)}, u32[]{:S(2)}) %collective-permute-start.15) | collective-permute-done | bytes 262176 | tf_op jit(solution)/shard_map/ppermute | solution.py:489
  69.9 0.8 %finish.7.refs_2_ = bf16[1024,512]{1,0:T(8,128)(2,1)} custom-call(bf16[256,512]{1,0:T(8,128)(2,1)S(1)} %get-tuple-element.107.refs_0_, bf16[256,512]{1,0:T(8,128)(2,1)S(1)} %collective-permute-done.15.refs_1_, bf16[1024,512]{1,0:T(8,128)(2,1)} %finish.6.refs_2_), custom_call_target="tpu_custom_call", output_to_operand_aliasing={{}: (2, {})} | custom-call | flops 262144 | bytes 786432 | tf_op jit(solution)/shard_map/finish/pallas_call | solution.py:390
  70.7 2.0 %collective-permute-done.13.refs_1_ = bf16[128,512]{1,0:T(8,128)(2,1)S(1)} collective-permute-done((bf16[128,512]{1,0:T(8,128)(2,1)S(1)}, bf16[128,512]{1,0:T(8,128)(2,1)S(1)}, u32[]{:S(2)}, u32[]{:S(2)}) %collective-permute-start.13) | collective-permute-done | bytes 131104 | tf_op jit(solution)/shard_map/ppermute | solution.py:489
  72.8 0.7 finish.8.refs_2_
  73.4 1.7 %collective-permute-done.11.refs_1_ = bf16[128,512]{1,0:T(8,128)(2,1)S(1)} collective-permute-done((bf16[128,512]{1,0:T(8,128)(2,1)S(1)}, bf16[128,512]{1,0:T(8,128)(2,1)S(1)}, u32[]{:S(2)}, u32[]{:S(2)}) %collective-permute-start.11) | collective-permute-done | bytes 131104 | tf_op jit(solution)/shard_map/ppermute | solution.py:489
  75.1 0.7 finish.9
  (36 shorter events, 3.8 us)
Async XLA Ops:
  1.2 11.3 %collective-permute-start = (bf16[256,512]{1,0:T(8,128)(2,1)S(1)}, bf16[256,512]{1,0:T(8,128)(2,1)S(1)}, u32[]{:S(2)}, u32[]{:S(2)}) collective-permute-start(bf16[256,512]{1,0:T(8,128)(2,1)S(1)} %get-tuple-element.64.refs_0_), channel_id=1, source_target_pairs={{1,0},{0,1},{3,2},{2,3},{5,4},{4,5},{7,6},{6,7},{9,8},{8,9},{11,10... | collective-permute-start | bytes 786440 | tf_op jit(solution)/shard_map/ppermute | solution.py:445
  4.2 12.8 %collective-permute-start.2 = (bf16[256,512]{1,0:T(8,128)(2,1)S(1)}, bf16[256,512]{1,0:T(8,128)(2,1)S(1)}, u32[]{:S(2)}, u32[]{:S(2)}) collective-permute-start(bf16[256,512]{1,0:T(8,128)(2,1)S(1)} %get-tuple-element.119.refs_1_), channel_id=1, source_target_pairs={{1,0},{0,1},{3,2},{2,3},{5,4},{4,5},{7,6},{6,7},{9,8},{8,9},{11,10... | collective-permute-start | bytes 786440 | tf_op jit(solution)/shard_map/ppermute | solution.py:445
  4.3 18.1 %collective-permute-start.3 = (bf16[256,512]{1,0:T(8,128)(2,1)S(1)}, bf16[256,512]{1,0:T(8,128)(2,1)S(1)}, u32[]{:S(2)}, u32[]{:S(2)}) collective-permute-start(bf16[256,512]{1,0:T(8,128)(2,1)S(1)} %get-tuple-element.117.refs_1_), channel_id=1, source_target_pairs={{1,0},{0,1},{3,2},{2,3},{5,4},{4,5},{7,6},{6,7},{9,8},{8,9},{11,10... | collective-permute-start | bytes 786440 | tf_op jit(solution)/shard_map/ppermute | solution.py:445
  6.2 42.6 %collective-permute-start.10 = (bf16[512,1024]{1,0:T(8,128)(2,1)}, bf16[512,1024]{1,0:T(8,128)(2,1)S(1)}, u32[]{:S(2)}, u32[]{:S(2)}) collective-permute-start(bf16[512,1024]{1,0:T(8,128)(2,1)} %bitcast.30), channel_id=1, source_target_pairs={{0,2},{2,0},{1,3},{3,1},{4,6},{6,4},{5,7},{7,5},{8,10},{10,8},{9,1... | collective-permute-start | bytes 3145736 | tf_op jit(solution)/shard_map/ppermute | solution.py:427
  7.2 0.7 copy-start.2
  7.9 0.7 copy-start.5
  10.0 2.5 %copy-start.1 = (f32[1,1024]{1,0:T(1,128)S(1)}, f32[1,1024]{1,0:T(1,128)}, u32[]{:S(2)}) copy-start(f32[1,1024]{1,0:T(1,128)} %gain_ref.11) | copy-start | bytes 12292
  12.5 1.4 %copy-start.3 = (s32[2,2]{1,0:T(2,128)S(1)}, s32[2,2]{1,0:T(2,128)}, u32[]{:S(2)}) copy-start(s32[2,2]{1,0:T(2,128)} %keep_ref.9) | copy-start | bytes 52
  12.5 1.4 %copy-start.4 = (f32[1,4]{1,0:T(1,128)S(1)}, f32[1,4]{1,0:T(1,128)}, u32[]{:S(2)}) copy-start(f32[1,4]{1,0:T(1,128)} %scale_ref.9) | copy-start | bytes 52
  19.8 6.2 %collective-permute-start.4 = (bf16[128,512]{1,0:T(8,128)(2,1)S(1)}, bf16[128,512]{1,0:T(8,128)(2,1)S(1)}, u32[]{:S(2)}, u32[]{:S(2)}) collective-permute-start(bf16[128,512]{1,0:T(8,128)(2,1)S(1)} %get-tuple-element.81.refs_1_), channel_id=1, source_target_pairs={{1,0},{0,1},{3,2},{2,3},{5,4},{4,5},{7,6},{6,7},{9,8},{8,9},{11,10... | collective-permute-start | bytes 393224 | tf_op jit(solution)/shard_map/ppermute | solution.py:445
  21.9 6.4 %collective-permute-start.1 = (bf16[128,512]{1,0:T(8,128)(2,1)S(1)}, bf16[128,512]{1,0:T(8,128)(2,1)S(1)}, u32[]{:S(2)}, u32[]{:S(2)}) collective-permute-start(bf16[128,512]{1,0:T(8,128)(2,1)S(1)} %get-tuple-element.62.refs_0_), channel_id=1, source_target_pairs={{1,0},{0,1},{3,2},{2,3},{5,4},{4,5},{7,6},{6,7},{9,8},{8,9},{11,10... | collective-permute-start | bytes 393224 | tf_op jit(solution)/shard_map/ppermute | solution.py:445
  29.1 6.5 %collective-permute-start.5 = (bf16[528,128]{1,0:T(8,128)(2,1)S(1)}, bf16[528,128]{1,0:T(8,128)(2,1)S(1)}, u32[]{:S(2)}, u32[]{:S(2)}) collective-permute-start(bf16[528,128]{1,0:T(8,128)(2,1)S(1)} %get-tuple-element.92.refs_0_), channel_id=1, source_target_pairs={{0,4},{4,0},{8,12},{12,8},{16,20},{20,16},{24,28},{28,24},{1,5},{5... | collective-permute-start | bytes 405512 | tf_op jit(solution)/shard_map/ppermute | solution.py:469
  30.9 5.0 %collective-permute-start.6 = (bf16[528,128]{1,0:T(8,128)(2,1)S(1)}, bf16[528,128]{1,0:T(8,128)(2,1)S(1)}, u32[]{:S(2)}, u32[]{:S(2)}) collective-permute-start(bf16[528,128]{1,0:T(8,128)(2,1)S(1)} %get-tuple-element.92.refs_0_), channel_id=1, source_target_pairs={{0,8},{4,12},{8,0},{12,4},{16,24},{20,28},{24,16},{28,20},{1,9},{5... | collective-permute-start | bytes 405512 | tf_op jit(solution)/shard_map/ppermute | solution.py:469
  32.5 5.9 %collective-permute-start.7 = (bf16[528,128]{1,0:T(8,128)(2,1)S(1)}, bf16[528,128]{1,0:T(8,128)(2,1)S(1)}, u32[]{:S(2)}, u32[]{:S(2)}) collective-permute-start(bf16[528,128]{1,0:T(8,128)(2,1)S(1)} %get-tuple-element.92.refs_0_), channel_id=1, source_target_pairs={{0,12},{4,8},{8,4},{12,0},{16,28},{20,24},{24,20},{28,16},{1,13},{... | collective-permute-start | bytes 405512 | tf_op jit(solution)/shard_map/ppermute | solution.py:469
  34.8 14.0 %copy-start = (bf16[1,4,128,1024]{3,2,1,0:T(8,128)(2,1)S(1)}, bf16[1,4,128,1024]{3,2,1,0:T(8,128)(2,1)}, u32[]{:S(2)}) copy-start(bf16[1,4,128,1024]{3,2,1,0:T(8,128)(2,1)} %param.16) | copy-start | bytes 3145732
  38.7 7.4 %collective-permute-start.8 = (bf16[528,128]{1,0:T(8,128)(2,1)S(1)}, bf16[528,128]{1,0:T(8,128)(2,1)S(1)}, u32[]{:S(2)}, u32[]{:S(2)}) collective-permute-start(bf16[528,128]{1,0:T(8,128)(2,1)S(1)} %get-tuple-element.98.refs_0_), channel_id=1, source_target_pairs={{0,16},{4,20},{8,24},{12,28},{16,0},{20,4},{24,8},{28,12},{1,17},{... | collective-permute-start | bytes 405512 | tf_op jit(solution)/shard_map/ppermute | solution.py:476
  46.6 2.1 %collective-permute-start.18 = (bf16[256,512]{1,0:T(8,128)(2,1)S(1)}, bf16[256,512]{1,0:T(8,128)(2,1)S(1)}, u32[]{:S(2)}, u32[]{:S(2)}) collective-permute-start(bf16[256,512]{1,0:T(8,128)(2,1)S(1)} %recall.9.own_ref), channel_id=1, source_target_pairs={{0,2},{2,0},{1,3},{3,1},{4,6},{6,4},{5,7},{7,5},{8,10},{10,8},{9,1... | collective-permute-start | bytes 786440 | tf_op jit(solution)/shard_map/ppermute | solution.py:484
  46.9 4.3 %collective-permute-start.16 = (bf16[256,512]{1,0:T(8,128)(2,1)S(1)}, bf16[256,512]{1,0:T(8,128)(2,1)S(1)}, u32[]{:S(2)}, u32[]{:S(2)}) collective-permute-start(bf16[256,512]{1,0:T(8,128)(2,1)S(1)} %recall.8.own_ref), channel_id=1, source_target_pairs={{0,2},{2,0},{1,3},{3,1},{4,6},{6,4},{5,7},{7,5},{8,10},{10,8},{9,1... | collective-permute-start | bytes 786440 | tf_op jit(solution)/shard_map/ppermute | solution.py:484
  47.7 4.7 %collective-permute-start.14 = (bf16[256,512]{1,0:T(8,128)(2,1)S(1)}, bf16[256,512]{1,0:T(8,128)(2,1)S(1)}, u32[]{:S(2)}, u32[]{:S(2)}) collective-permute-start(bf16[256,512]{1,0:T(8,128)(2,1)S(1)} %recall.7.own_ref), channel_id=1, source_target_pairs={{0,2},{2,0},{1,3},{3,1},{4,6},{6,4},{5,7},{7,5},{8,10},{10,8},{9,1... | collective-permute-start | bytes 786440 | tf_op jit(solution)/shard_map/ppermute | solution.py:484
  47.9 6.8 %collective-permute-start.12 = (bf16[128,512]{1,0:T(8,128)(2,1)S(1)}, bf16[128,512]{1,0:T(8,128)(2,1)S(1)}, u32[]{:S(2)}, u32[]{:S(2)}) collective-permute-start(bf16[128,512]{1,0:T(8,128)(2,1)S(1)} %recall.6.own_ref), channel_id=1, source_target_pairs={{0,2},{2,0},{1,3},{3,1},{4,6},{6,4},{5,7},{7,5},{8,10},{10,8},{9,1... | collective-permute-start | bytes 393224 | tf_op jit(solution)/shard_map/ppermute | solution.py:484
  48.7 7.1 %collective-permute-start.9 = (bf16[128,512]{1,0:T(8,128)(2,1)S(1)}, bf16[128,512]{1,0:T(8,128)(2,1)S(1)}, u32[]{:S(2)}, u32[]{:S(2)}) collective-permute-start(bf16[128,512]{1,0:T(8,128)(2,1)S(1)} %recall.5.own_ref), channel_id=1, source_target_pairs={{0,2},{2,0},{1,3},{3,1},{4,6},{6,4},{5,7},{7,5},{8,10},{10,8},{9,1... | collective-permute-start | bytes 393224 | tf_op jit(solution)/shard_map/ppermute | solution.py:484
  49.5 9.2 %collective-permute-start.19 = (bf16[256,512]{1,0:T(8,128)(2,1)S(1)}, bf16[256,512]{1,0:T(8,128)(2,1)S(1)}, u32[]{:S(2)}, u32[]{:S(2)}) collective-permute-start(bf16[256,512]{1,0:T(8,128)(2,1)S(1)} %get-tuple-element.116), channel_id=1, source_target_pairs={{0,1},{1,0},{2,3},{3,2},{4,5},{5,4},{6,7},{7,6},{8,9},{9,8},{10,11... | collective-permute-start | bytes 786440 | tf_op jit(solution)/shard_map/ppermute | solution.py:489
  51.9 12.5 %collective-permute-start.17 = (bf16[256,512]{1,0:T(8,128)(2,1)S(1)}, bf16[256,512]{1,0:T(8,128)(2,1)S(1)}, u32[]{:S(2)}, u32[]{:S(2)}) collective-permute-start(bf16[256,512]{1,0:T(8,128)(2,1)S(1)} %get-tuple-element.112), channel_id=1, source_target_pairs={{0,1},{1,0},{2,3},{3,2},{4,5},{5,4},{6,7},{7,6},{8,9},{9,8},{10,11... | collective-permute-start | bytes 786440 | tf_op jit(solution)/shard_map/ppermute | solution.py:489
  53.1 16.8 %collective-permute-start.15 = (bf16[256,512]{1,0:T(8,128)(2,1)S(1)}, bf16[256,512]{1,0:T(8,128)(2,1)S(1)}, u32[]{:S(2)}, u32[]{:S(2)}) collective-permute-start(bf16[256,512]{1,0:T(8,128)(2,1)S(1)} %get-tuple-element.108), channel_id=1, source_target_pairs={{0,1},{1,0},{2,3},{3,2},{4,5},{5,4},{6,7},{7,6},{8,9},{9,8},{10,11... | collective-permute-start | bytes 786440 | tf_op jit(solution)/shard_map/ppermute | solution.py:489
  55.2 17.5 %collective-permute-start.13 = (bf16[128,512]{1,0:T(8,128)(2,1)S(1)}, bf16[128,512]{1,0:T(8,128)(2,1)S(1)}, u32[]{:S(2)}, u32[]{:S(2)}) collective-permute-start(bf16[128,512]{1,0:T(8,128)(2,1)S(1)} %get-tuple-element.104), channel_id=1, source_target_pairs={{0,1},{1,0},{2,3},{3,2},{4,5},{5,4},{6,7},{7,6},{8,9},{9,8},{10,11... | collective-permute-start | bytes 393224 | tf_op jit(solution)/shard_map/ppermute | solution.py:489
  56.2 18.9 %collective-permute-start.11 = (bf16[128,512]{1,0:T(8,128)(2,1)S(1)}, bf16[128,512]{1,0:T(8,128)(2,1)S(1)}, u32[]{:S(2)}, u32[]{:S(2)}) collective-permute-start(bf16[128,512]{1,0:T(8,128)(2,1)S(1)} %get-tuple-element.100), channel_id=1, source_target_pairs={{0,1},{1,0},{2,3},{3,2},{4,5},{5,4},{6,7},{7,6},{8,9},{9,8},{10,11... | collective-permute-start | bytes 393224 | tf_op jit(solution)/shard_map/ppermute | solution.py:489

commit v10 on v9

--- a/solution.py
+++ b/solution.py
@@ -438,7 +438,7 @@
     received = []
     for c in range(chunks):
         if c == chunks - 2:
-            pieces[c], pieces[c + 1], received[0] = tied(pieces[c], pieces[c + 1], received[0])
+            pieces[c], pieces[c + 1], tail = tied(pieces[c], pieces[c + 1], tail)
         xs = [pieces[c]]
         for k in range(1, shards):
             xs.append(
@@ -455,9 +455,10 @@
         qs.append(q)
         ks.append(k)
         vs.append(v)
-        local = attention(first, tile_retain_grid, score_scaler, q, ks, vs, heads, dim)
-        summary, local = tied(summary, local)
-        locals_.append(local)
+        if c < chunks - 2:
+            local = attention(first, tile_retain_grid, score_scaler, q, ks, vs, heads, dim)
+            summary, local = tied(summary, local)
+            locals_.append(local)
     k, v, sent = last_keys_values(
         gain, w, fade, summary, tail, received[-1], heads, dim, firsts[-1]
     )
@@ -469,13 +470,19 @@
         lax.ppermute(sent, "tm", [(d, d ^ k) for d in range(blocks)]) for k in range(1, quad_size)
     ]
     qs.append(last_queries(gain, w, received[-1], heads, dim))
-    locals_.append(attention(firsts[-1], tile_retain_grid, score_scaler, qs[-1], ks, vs, heads, dim))
-    *loads, locals_[-1] = tied(*loads, locals_[-1])
+    for c in range(chunks - 2, chunks):
+        locals_.append(
+            attention(
+                firsts[c], tile_retain_grid, score_scaler, qs[c], ks[: c + 1], vs[: c + 1], heads, dim
+            )
+        )
+    *loads, locals_[-2] = tied(*loads, locals_[-2])
     before, decay, total = quad(loads, heads, dim)
     totals = [total] + [
         lax.ppermute(total, "tm", [(d, d ^ (quad_size * k)) for d in range(blocks)])
         for k in range(1, blocks // quad_size)
     ]
+    *totals, locals_[-1] = tied(*totals, locals_[-1])
     state = entering(quad_size, before, decay, totals, heads, dim)
 
     result = None

time: 76.1 us -> 75.4 us (level)
    ppermute x1, waiting for transfers between devices: 3.89 us -> 2.42 us  [per_device(): lax.ppermute(total, 'tm', [(d, d ^ quad_size * k) for d in range(blocks)])]
    ppermute x3, waiting for transfers between devices: 3.54 us -> 4.49 us  [per_device(): lax.ppermute(sent, 'tm', [(d, d ^ k) for d in range(blocks)])]
    unnamed x13 -> x15, local copies, waits for them, and re-layouts: 3.85 us -> 3.92 us
  transfers between devices with their start and end apart: 20 -> 20, of which waited for: 12 -> 11; matrix products, arithmetic and copies ran while one was open for 5% -> 5% of each run, Pallas kernels for 30% -> 30%
where the time goes in v10:
time: 75.4 us; the launch traced here: 75.1 us
  waiting for transfers between devices  24.3 us (32%)
  Pallas kernels  23.4 us (31%)
  starting transfers between devices  21 us (28%)
  local copies, waits for them, and re-layouts  6.06 us (8%)
    ppermute x5, waiting for transfers between devices, per_device(): lax.ppermute(outs[k], 'head', [(d, (d + k) % shards) for d in range(shard...  14.2 us
    pallas_call x5, Pallas kernels, attention(): pl.pallas_call(functools.partial(attention_kernel, first, heads, dim), in...  7.15 us
    ppermute x5, starting transfers between devices, per_device(): lax.ppermute(pieces[c], 'head', [((d + k) % shards, d) for d in range(sha...  7.14 us
    ppermute x5, starting transfers between devices, per_device(): lax.ppermute(outs[k], 'head', [(d, (d + k) % shards) for d in range(shard...  6.06 us
    pallas_call x4, Pallas kernels, qkv(): pl.pallas_call(functools.partial(qkv_kernel, heads, dim, first), in_specs...  5.04 us
    ppermute x3, waiting for transfers between devices, per_device(): lax.ppermute(sent, 'tm', [(d, d ^ k) for d in range(blocks)])  4.49 us
    unnamed x15, local copies, waits for them, and re-layouts  3.92 us
    pallas_call x5, Pallas kernels, finish(): pl.pallas_call(functools.partial(finish_kernel, len(parts)), grid=(1,), i...  3.67 us
  transfers between devices with their start and end apart: 20, of which 11 were waited for; matrix products, arithmetic and copies ran while one was open for 5% of the time, Pallas kernels for 30%

profile of v10, /device:TPU:0, one launch (start us, length us, event | category | flops | bytes accessed | tf_op | source)
XLA Modules:
  0.0 75.1 jit_solution(2176358171216780440)
XLA Ops:
  0.0 1.2 %slice_bitcast_fusion = (bf16[256,512]{1,0:T(8,128)(2,1)S(1)}, bf16[256,512]{1,0:T(8,128)(2,1)S(1)}, bf16[256,512]{1,0:T(8,128)(2,1)S(1)}) fusion(bf16[1,1024,512]{2,1,0:T(8,128)(2,1)} %param.9), kind=kLoop, calls=%fused_computation | loop fusion | bytes 1572864 | tf_op jit(solution)/shard_map/slice | solution.py:437
  1.2 3.0 %collective-permute-start.1 = (bf16[256,512]{1,0:T(8,128)(2,1)S(1)}, bf16[256,512]{1,0:T(8,128)(2,1)S(1)}, u32[]{:S(2)}, u32[]{:S(2)}) collective-permute-start(bf16[256,512]{1,0:T(8,128)(2,1)S(1)} %get-tuple-element.118.refs_0_), channel_id=1, source_target_pairs={{1,0},{0,1},{3,2},{2,3},{5,4},{4,5},{7,6},{6,7},{9,8},{8,9},{11,10... | collective-permute-start | bytes 786440 | tf_op jit(solution)/shard_map/ppermute | solution.py:445
  4.3 1.9 %collective-permute-start.3 = (bf16[256,512]{1,0:T(8,128)(2,1)S(1)}, bf16[256,512]{1,0:T(8,128)(2,1)S(1)}, u32[]{:S(2)}, u32[]{:S(2)}) collective-permute-start(bf16[256,512]{1,0:T(8,128)(2,1)S(1)} %get-tuple-element.117.refs_1_), channel_id=1, source_target_pairs={{1,0},{0,1},{3,2},{2,3},{5,4},{4,5},{7,6},{6,7},{9,8},{8,9},{11,10... | collective-permute-start | bytes 786440 | tf_op jit(solution)/shard_map/ppermute | solution.py:445
  6.2 1.0 %slice_bitcast_fusion.3 = (bf16[128,512]{1,0:T(8,128)(2,1)S(1)}, bf16[128,512]{1,0:T(8,128)(2,1)S(1)}) fusion(bf16[1,1024,512]{2,1,0:T(8,128)(2,1)} %param.9), kind=kLoop, calls=%fused_computation.3 | loop fusion | bytes 524288 | tf_op jit(solution)/shard_map/slice | solution.py:437
  7.2 0.7 copy-done.2
  7.9 0.7 copy-done.5
  8.6 1.4 %prepare.1 = (f32[1024,8]{1,0:T(8,128)S(1)}, bf16[16,128]{1,0:T(8,128)(2,1)S(1)}, f32[256,8]{1,0:T(8,128)S(1)}, f32[256,8]{1,0:T(8,128)S(1)}, f32[256,8]{1,0:T(8...) custom-call(f32[4,1024]{1,0:T(4,128)S(1)} %bitcast.28, s32[2]{0:T(128)S(1)} %copy-done.5), custom_call_target="tpu_custom_call" | custom-call | flops 327680 | tf_op jit(solution)/shard_map/prepare/pallas_call | solution.py:83
  10.1 1.9 %collective-permute-start = (bf16[128,512]{1,0:T(8,128)(2,1)S(1)}, bf16[128,512]{1,0:T(8,128)(2,1)S(1)}, u32[]{:S(2)}, u32[]{:S(2)}) collective-permute-start(bf16[128,512]{1,0:T(8,128)(2,1)S(1)} %get-tuple-element.63.refs_0_), channel_id=1, source_target_pairs={{1,0},{0,1},{3,2},{2,3},{5,4},{4,5},{7,6},{6,7},{9,8},{8,9},{11,10... | collective-permute-start | bytes 393224 | tf_op jit(solution)/shard_map/ppermute | solution.py:445
  12.1 2.5 %copy.14 = bf16[128,8,4,384]{3,1,2,0:T(8,128)(2,1)S(1)} copy(bf16[128,8,4,384]{3,2,1,0:T(4,128)(2,1)} %bitcast.29) | data formatting | bytes 6291456
  14.8 1.4 %qkv.4 = (bf16[256,512]{1,0:T(8,128)(2,1)S(1)}, bf16[256,512]{1,0:T(8,128)(2,1)S(1)}, bf16[256,512]{1,0:T(8,128)(2,1)S(1)}, f32[4,128,128]{2,1,0:T(8,128)S(1)}) custom-call(f32[1,1024]{1,0:T(1,128)S(1)} %copy-done.1, bf16[1024,1536]{1,0:T(8,128)(2,1)S(1)} %bitcast.17, f32[1024,8]{1,0:T(8,128)S(1)} %get-tuple-element.64.fade_ref, ...), custom_call_target="tpu_custom_call" | custom-call | flops 1610612736 | tf_op jit(solution)/shard_map/qkv/pallas_call | solution.py:148
  16.1 1.1 %attention.5.local_ref = bf16[256,512]{1,0:T(8,128)(2,1)S(1)} custom-call(s32[2,2]{1,0:T(2,128)S(1)} %copy-done.3, f32[1,4]{1,0:T(1,128)S(1)} %copy-done.4, bf16[256,512]{1,0:T(8,128)(2,1)S(1)} %get-tuple-element.66.q_ref, bf16[256,512]{1,0:T(8,128)(2,1)S(1)} %get-tuple-element.67.refs_0_, ...), custom_call_target="tpu_custom_call" | custom-call | flops 268435456 | tf_op jit(solution)/shard_map/attention/pallas_call | solution.py:242
  17.3 1.4 %qkv.5 = (bf16[256,512]{1,0:T(8,128)(2,1)S(1)}, bf16[256,512]{1,0:T(8,128)(2,1)S(1)}, bf16[256,512]{1,0:T(8,128)(2,1)S(1)}, f32[4,128,128]{2,1,0:T(8,128)S(1)}) custom-call(f32[1,1024]{1,0:T(1,128)S(1)} %copy-done.1, bf16[1024,1536]{1,0:T(8,128)(2,1)S(1)} %bitcast.18, f32[1024,8]{1,0:T(8,128)S(1)} %get-tuple-element.64.fade_ref, ...), custom_call_target="tpu_custom_call" | custom-call | flops 1610612736 | tf_op jit(solution)/shard_map/qkv/pallas_call | solution.py:148
  18.6 1.4 %attention.6.local_ref = bf16[256,512]{1,0:T(8,128)(2,1)S(1)} custom-call(s32[2,2]{1,0:T(2,128)S(1)} %copy-done.3, f32[1,4]{1,0:T(1,128)S(1)} %copy-done.4, bf16[256,512]{1,0:T(8,128)(2,1)S(1)} %get-tuple-element.71.q_ref, bf16[256,512]{1,0:T(8,128)(2,1)S(1)} %get-tuple-element.67.refs_0_, bf16[256,512]{1,0:T(8,128)(2,1)S(1)} %get-tuple-element.72.refs_1_, ...), custom_call_target="tpu_custom_call" | custom-call | flops 536870912 | tf_op jit(solution)/shard_map/attention/pallas_call | solution.py:242
  20.1 2.5 %collective-permute-done.3.refs_2_ = bf16[256,512]{1,0:T(8,128)(2,1)S(1)} collective-permute-done((bf16[256,512]{1,0:T(8,128)(2,1)S(1)}, bf16[256,512]{1,0:T(8,128)(2,1)S(1)}, u32[]{:S(2)}, u32[]{:S(2)}) %collective-permute-start.3) | collective-permute-done | bytes 262176 | tf_op jit(solution)/shard_map/ppermute | solution.py:445
  22.6 1.4 %qkv.6 = (bf16[256,512]{1,0:T(8,128)(2,1)S(1)}, bf16[256,512]{1,0:T(8,128)(2,1)S(1)}, bf16[256,512]{1,0:T(8,128)(2,1)S(1)}, f32[4,128,128]{2,1,0:T(8,128)S(1)}) custom-call(f32[1,1024]{1,0:T(1,128)S(1)} %copy-done.1, bf16[1024,1536]{1,0:T(8,128)(2,1)S(1)} %bitcast.19, f32[1024,8]{1,0:T(8,128)S(1)} %get-tuple-element.64.fade_ref, ...), custom_call_target="tpu_custom_call" | custom-call | flops 1610612736 | tf_op jit(solution)/shard_map/qkv/pallas_call | solution.py:148
  23.9 1.7 %attention.7.local_ref = bf16[256,512]{1,0:T(8,128)(2,1)S(1)} custom-call(s32[2,2]{1,0:T(2,128)S(1)} %copy-done.3, f32[1,4]{1,0:T(1,128)S(1)} %copy-done.4, bf16[256,512]{1,0:T(8,128)(2,1)S(1)} %get-tuple-element.76.q_ref, bf16[256,512]{1,0:T(8,128)(2,1)S(1)} %get-tuple-element.67.refs_0_, bf16[256,512]{1,0:T(8,128)(2,1)S(1)} %get-tuple-element.72.refs_1_, ...), custom_call_target="tpu_custom_call" | custom-call | flops 805306368 | tf_op jit(solution)/shard_map/attention/pallas_call | solution.py:242
  25.6 0.9 %qkv.7 = (bf16[128,512]{1,0:T(8,128)(2,1)S(1)}, bf16[128,512]{1,0:T(8,128)(2,1)S(1)}, bf16[128,512]{1,0:T(8,128)(2,1)S(1)}, f32[4,128,128]{2,1,0:T(8,128)S(1)}) custom-call(f32[1,1024]{1,0:T(1,128)S(1)} %copy-done.1, bf16[1024,1536]{1,0:T(8,128)(2,1)S(1)} %bitcast.20, f32[1024,8]{1,0:T(8,128)S(1)} %get-tuple-element.64.fade_ref, ...), custom_call_target="tpu_custom_call" | custom-call | flops 805306368 | tf_op jit(solution)/shard_map/qkv/pallas_call | solution.py:148
  26.6 0.8 %collective-permute-done.refs_1_ = bf16[128,512]{1,0:T(8,128)(2,1)S(1)} collective-permute-done((bf16[128,512]{1,0:T(8,128)(2,1)S(1)}, bf16[128,512]{1,0:T(8,128)(2,1)S(1)}, u32[]{:S(2)}, u32[]{:S(2)}) %collective-permute-start) | collective-permute-done | bytes 131104 | tf_op jit(solution)/shard_map/ppermute | solution.py:445
  27.4 0.8 %last_keys_values.1 = (bf16[128,512]{1,0:T(8,128)(2,1)S(1)}, bf16[128,512]{1,0:T(8,128)(2,1)S(1)}, bf16[528,128]{1,0:T(8,128)(2,1)S(1)}) custom-call(f32[1,1024]{1,0:T(1,128)S(1)} %copy-done.1, bf16[1024,1536]{1,0:T(8,128)(2,1)S(1)} %bitcast.21, f32[1024,8]{1,0:T(8,128)S(1)} %get-tuple-element.64.fade_ref, f32[4,128,128]{2,1,0:T(8,128)S(1)} %get-tuple-element.81.prev_ref, ...), custom_call_target="tpu_custom_call" | custom-call | flops 603979776 | tf_op jit(solution)/shard_map/last_keys_values/pallas_call | solution.py:179
  28.2 1.8 %collective-permute-start.5 = (bf16[528,128]{1,0:T(8,128)(2,1)S(1)}, bf16[528,128]{1,0:T(8,128)(2,1)S(1)}, u32[]{:S(2)}, u32[]{:S(2)}) collective-permute-start(bf16[528,128]{1,0:T(8,128)(2,1)S(1)} %get-tuple-element.87.refs_0_), channel_id=1, source_target_pairs={{0,4},{4,0},{8,12},{12,8},{16,20},{20,16},{24,28},{28,24},{1,5},{5... | collective-permute-start | bytes 405512 | tf_op jit(solution)/shard_map/ppermute | solution.py:470
  29.9 1.6 %collective-permute-start.6 = (bf16[528,128]{1,0:T(8,128)(2,1)S(1)}, bf16[528,128]{1,0:T(8,128)(2,1)S(1)}, u32[]{:S(2)}, u32[]{:S(2)}) collective-permute-start(bf16[528,128]{1,0:T(8,128)(2,1)S(1)} %get-tuple-element.87.refs_0_), channel_id=1, source_target_pairs={{0,8},{4,12},{8,0},{12,4},{16,24},{20,28},{24,16},{28,20},{1,9},{5... | collective-permute-start | bytes 405512 | tf_op jit(solution)/shard_map/ppermute | solution.py:470
  31.7 1.4 %attention.8.local_ref = bf16[128,512]{1,0:T(8,128)(2,1)S(1)} custom-call(s32[2,2]{1,0:T(2,128)S(1)} %copy-done.3, f32[1,4]{1,0:T(1,128)S(1)} %copy-done.4, bf16[128,512]{1,0:T(8,128)(2,1)S(1)} %get-tuple-element.84.q_ref, bf16[256,512]{1,0:T(8,128)(2,1)S(1)} %get-tuple-element.67.refs_0_, bf16[256,512]{1,0:T(8,128)(2,1)S(1)} %get-tuple-element.72.refs_1_, ...), custom_call_target="tpu_custom_call" | custom-call | flops 469762048 | tf_op jit(solution)/shard_map/attention/pallas_call | solution.py:242
  33.1 0.8 %collective-permute-done.5.refs_1_ = bf16[528,128]{1,0:T(8,128)(2,1)S(1)} collective-permute-done((bf16[528,128]{1,0:T(8,128)(2,1)S(1)}, bf16[528,128]{1,0:T(8,128)(2,1)S(1)}, u32[]{:S(2)}, u32[]{:S(2)}) %collective-permute-start.5) | collective-permute-done | bytes 135200 | tf_op jit(solution)/shard_map/ppermute | solution.py:470
  33.9 1.6 %collective-permute-done.6.refs_2_ = bf16[528,128]{1,0:T(8,128)(2,1)S(1)} collective-permute-done((bf16[528,128]{1,0:T(8,128)(2,1)S(1)}, bf16[528,128]{1,0:T(8,128)(2,1)S(1)}, u32[]{:S(2)}, u32[]{:S(2)}) %collective-permute-start.6) | collective-permute-done | bytes 135200 | tf_op jit(solution)/shard_map/ppermute | solution.py:470
  35.6 2.0 %collective-permute-done.7.refs_3_ = bf16[528,128]{1,0:T(8,128)(2,1)S(1)} collective-permute-done((bf16[528,128]{1,0:T(8,128)(2,1)S(1)}, bf16[528,128]{1,0:T(8,128)(2,1)S(1)}, u32[]{:S(2)}, u32[]{:S(2)}) %collective-permute-start.7) | collective-permute-done | bytes 135200 | tf_op jit(solution)/shard_map/ppermute | solution.py:470
  37.9 2.8 %collective-permute-start.8 = (bf16[528,128]{1,0:T(8,128)(2,1)S(1)}, bf16[528,128]{1,0:T(8,128)(2,1)S(1)}, u32[]{:S(2)}, u32[]{:S(2)}) collective-permute-start(bf16[528,128]{1,0:T(8,128)(2,1)S(1)} %get-tuple-element.97.refs_0_), channel_id=1, source_target_pairs={{0,16},{4,20},{8,24},{12,28},{16,0},{20,4},{24,8},{28,12},{1,17},{... | collective-permute-start | bytes 405512 | tf_op jit(solution)/shard_map/ppermute | solution.py:482
  40.7 0.6 last_queries.1.q_ref
  41.4 1.5 %attention.9.local_ref = bf16[128,512]{1,0:T(8,128)(2,1)S(1)} custom-call(s32[2,2]{1,0:T(2,128)S(1)} %copy-done.3, f32[1,4]{1,0:T(1,128)S(1)} %copy-done.4, bf16[128,512]{1,0:T(8,128)(2,1)S(1)} %last_queries.1.q_ref, bf16[256,512]{1,0:T(8,128)(2,1)S(1)} %get-tuple-element.67.refs_0_, bf16[256,512]{1,0:T(8,128)(2,1)S(1)} %get-tuple-element.72.refs_1_, ...), custom_call_target="tpu_custom_call" | custom-call | flops 536870912 | tf_op jit(solution)/shard_map/attention/pallas_call | solution.py:242
  42.9 2.4 %collective-permute-done.8.refs_1_ = bf16[528,128]{1,0:T(8,128)(2,1)S(1)} collective-permute-done((bf16[528,128]{1,0:T(8,128)(2,1)S(1)}, bf16[528,128]{1,0:T(8,128)(2,1)S(1)}, u32[]{:S(2)}, u32[]{:S(2)}) %collective-permute-start.8) | collective-permute-done | bytes 135200 | tf_op jit(solution)/shard_map/ppermute | solution.py:482
  46.2 0.6 collective-permute-start.16
  47.2 0.6 collective-permute-start.12
  48.1 0.7 project.9
  48.8 1.7 %collective-permute-start.19 = (bf16[256,512]{1,0:T(8,128)(2,1)S(1)}, bf16[256,512]{1,0:T(8,128)(2,1)S(1)}, u32[]{:S(2)}, u32[]{:S(2)}) collective-permute-start(bf16[256,512]{1,0:T(8,128)(2,1)S(1)} %get-tuple-element.116), channel_id=1, source_target_pairs={{0,1},{1,0},{2,3},{3,2},{4,5},{5,4},{6,7},{7,6},{8,9},{9,8},{10,11... | collective-permute-start | bytes 786440 | tf_op jit(solution)/shard_map/ppermute | solution.py:496
  50.6 0.7 project.8
  51.7 0.7 project.7
  52.4 1.7 %collective-permute-start.15 = (bf16[256,512]{1,0:T(8,128)(2,1)S(1)}, bf16[256,512]{1,0:T(8,128)(2,1)S(1)}, u32[]{:S(2)}, u32[]{:S(2)}) collective-permute-start(bf16[256,512]{1,0:T(8,128)(2,1)S(1)} %get-tuple-element.108), channel_id=1, source_target_pairs={{0,1},{1,0},{2,3},{3,2},{4,5},{5,4},{6,7},{7,6},{8,9},{9,8},{10,11... | collective-permute-start | bytes 786440 | tf_op jit(solution)/shard_map/ppermute | solution.py:496
  55.1 0.5 project.5
  55.5 1.7 %collective-permute-start.11 = (bf16[128,512]{1,0:T(8,128)(2,1)S(1)}, bf16[128,512]{1,0:T(8,128)(2,1)S(1)}, u32[]{:S(2)}, u32[]{:S(2)}) collective-permute-start(bf16[128,512]{1,0:T(8,128)(2,1)S(1)} %get-tuple-element.100), channel_id=1, source_target_pairs={{0,1},{1,0},{2,3},{3,2},{4,5},{5,4},{6,7},{7,6},{8,9},{9,8},{10,11... | collective-permute-start | bytes 393224 | tf_op jit(solution)/shard_map/ppermute | solution.py:496
  57.3 0.7 collective-permute-done.19.refs_1_
  58.0 0.8 %finish.5.refs_2_ = bf16[1024,512]{1,0:T(8,128)(2,1)} custom-call(bf16[256,512]{1,0:T(8,128)(2,1)S(1)} %get-tuple-element.115.refs_0_, bf16[256,512]{1,0:T(8,128)(2,1)S(1)} %collective-permute-done.19.refs_1_), custom_call_target="tpu_custom_call" | custom-call | flops 262144 | bytes 786432 | tf_op jit(solution)/shard_map/finish/pallas_call | solution.py:390
  58.8 4.9 %collective-permute-done.17.refs_1_ = bf16[256,512]{1,0:T(8,128)(2,1)S(1)} collective-permute-done((bf16[256,512]{1,0:T(8,128)(2,1)S(1)}, bf16[256,512]{1,0:T(8,128)(2,1)S(1)}, u32[]{:S(2)}, u32[]{:S(2)}) %collective-permute-start.17) | collective-permute-done | bytes 262176 | tf_op jit(solution)/shard_map/ppermute | solution.py:496
  63.6 0.8 %finish.6.refs_2_ = bf16[1024,512]{1,0:T(8,128)(2,1)} custom-call(bf16[256,512]{1,0:T(8,128)(2,1)S(1)} %get-tuple-element.111.refs_0_, bf16[256,512]{1,0:T(8,128)(2,1)S(1)} %collective-permute-done.17.refs_1_, bf16[1024,512]{1,0:T(8,128)(2,1)} %finish.5.refs_2_), custom_call_target="tpu_custom_call", output_to_operand_aliasing={{}: (2, {})} | custom-call | flops 262144 | bytes 786432 | tf_op jit(solution)/shard_map/finish/pallas_call | solution.py:390
  64.4 4.9 %collective-permute-done.15.refs_1_ = bf16[256,512]{1,0:T(8,128)(2,1)S(1)} collective-permute-done((bf16[256,512]{1,0:T(8,128)(2,1)S(1)}, bf16[256,512]{1,0:T(8,128)(2,1)S(1)}, u32[]{:S(2)}, u32[]{:S(2)}) %collective-permute-start.15) | collective-permute-done | bytes 262176 | tf_op jit(solution)/shard_map/ppermute | solution.py:496
  69.2 0.8 %finish.7.refs_2_ = bf16[1024,512]{1,0:T(8,128)(2,1)} custom-call(bf16[256,512]{1,0:T(8,128)(2,1)S(1)} %get-tuple-element.107.refs_0_, bf16[256,512]{1,0:T(8,128)(2,1)S(1)} %collective-permute-done.15.refs_1_, bf16[1024,512]{1,0:T(8,128)(2,1)} %finish.6.refs_2_), custom_call_target="tpu_custom_call", output_to_operand_aliasing={{}: (2, {})} | custom-call | flops 262144 | bytes 786432 | tf_op jit(solution)/shard_map/finish/pallas_call | solution.py:390
  70.0 2.0 %collective-permute-done.13.refs_1_ = bf16[128,512]{1,0:T(8,128)(2,1)S(1)} collective-permute-done((bf16[128,512]{1,0:T(8,128)(2,1)S(1)}, bf16[128,512]{1,0:T(8,128)(2,1)S(1)}, u32[]{:S(2)}, u32[]{:S(2)}) %collective-permute-start.13) | collective-permute-done | bytes 131104 | tf_op jit(solution)/shard_map/ppermute | solution.py:496
  72.0 0.7 finish.8.refs_2_
  72.7 1.7 %collective-permute-done.11.refs_1_ = bf16[128,512]{1,0:T(8,128)(2,1)S(1)} collective-permute-done((bf16[128,512]{1,0:T(8,128)(2,1)S(1)}, bf16[128,512]{1,0:T(8,128)(2,1)S(1)}, u32[]{:S(2)}, u32[]{:S(2)}) %collective-permute-start.11) | collective-permute-done | bytes 131104 | tf_op jit(solution)/shard_map/ppermute | solution.py:496
  74.4 0.7 finish.9
  (38 shorter events, 3.7 us)
Async XLA Ops:
  1.2 13.5 %collective-permute-start.1 = (bf16[256,512]{1,0:T(8,128)(2,1)S(1)}, bf16[256,512]{1,0:T(8,128)(2,1)S(1)}, u32[]{:S(2)}, u32[]{:S(2)}) collective-permute-start(bf16[256,512]{1,0:T(8,128)(2,1)S(1)} %get-tuple-element.118.refs_0_), channel_id=1, source_target_pairs={{1,0},{0,1},{3,2},{2,3},{5,4},{4,5},{7,6},{6,7},{9,8},{8,9},{11,10... | collective-permute-start | bytes 786440 | tf_op jit(solution)/shard_map/ppermute | solution.py:445
  4.2 13.1 %collective-permute-start.2 = (bf16[256,512]{1,0:T(8,128)(2,1)S(1)}, bf16[256,512]{1,0:T(8,128)(2,1)S(1)}, u32[]{:S(2)}, u32[]{:S(2)}) collective-permute-start(bf16[256,512]{1,0:T(8,128)(2,1)S(1)} %get-tuple-element.119.refs_1_), channel_id=1, source_target_pairs={{1,0},{0,1},{3,2},{2,3},{5,4},{4,5},{7,6},{6,7},{9,8},{8,9},{11,10... | collective-permute-start | bytes 786440 | tf_op jit(solution)/shard_map/ppermute | solution.py:445
  4.3 18.3 %collective-permute-start.3 = (bf16[256,512]{1,0:T(8,128)(2,1)S(1)}, bf16[256,512]{1,0:T(8,128)(2,1)S(1)}, u32[]{:S(2)}, u32[]{:S(2)}) collective-permute-start(bf16[256,512]{1,0:T(8,128)(2,1)S(1)} %get-tuple-element.117.refs_1_), channel_id=1, source_target_pairs={{1,0},{0,1},{3,2},{2,3},{5,4},{4,5},{7,6},{6,7},{9,8},{8,9},{11,10... | collective-permute-start | bytes 786440 | tf_op jit(solution)/shard_map/ppermute | solution.py:445
  7.2 0.7 copy-start.2
  7.9 0.7 copy-start.5
  10.0 15.6 %collective-permute-start.4 = (bf16[128,512]{1,0:T(8,128)(2,1)S(1)}, bf16[128,512]{1,0:T(8,128)(2,1)S(1)}, u32[]{:S(2)}, u32[]{:S(2)}) collective-permute-start(bf16[128,512]{1,0:T(8,128)(2,1)S(1)} %get-tuple-element.80.refs_1_), channel_id=1, source_target_pairs={{1,0},{0,1},{3,2},{2,3},{5,4},{4,5},{7,6},{6,7},{9,8},{8,9},{11,10... | collective-permute-start | bytes 393224 | tf_op jit(solution)/shard_map/ppermute | solution.py:445
  10.1 17.2 %collective-permute-start = (bf16[128,512]{1,0:T(8,128)(2,1)S(1)}, bf16[128,512]{1,0:T(8,128)(2,1)S(1)}, u32[]{:S(2)}, u32[]{:S(2)}) collective-permute-start(bf16[128,512]{1,0:T(8,128)(2,1)S(1)} %get-tuple-element.63.refs_0_), channel_id=1, source_target_pairs={{1,0},{0,1},{3,2},{2,3},{5,4},{4,5},{7,6},{6,7},{9,8},{8,9},{11,10... | collective-permute-start | bytes 393224 | tf_op jit(solution)/shard_map/ppermute | solution.py:445
  12.1 2.6 %copy-start.6 = (bf16[1,4,128,1024]{3,2,1,0:T(8,128)(2,1)S(1)}, bf16[1,4,128,1024]{3,2,1,0:T(8,128)(2,1)}, u32[]{:S(2)}) copy-start(bf16[1,4,128,1024]{3,2,1,0:T(8,128)(2,1)} %param.17) | copy-start | bytes 3145732
  12.1 2.7 %copy-start.1 = (f32[1,1024]{1,0:T(1,128)S(1)}, f32[1,1024]{1,0:T(1,128)}, u32[]{:S(2)}) copy-start(f32[1,1024]{1,0:T(1,128)} %gain_ref.11) | copy-start | bytes 12292
  14.6 1.5 %copy-start.3 = (s32[2,2]{1,0:T(2,128)S(1)}, s32[2,2]{1,0:T(2,128)}, u32[]{:S(2)}) copy-start(s32[2,2]{1,0:T(2,128)} %keep_ref.9) | copy-start | bytes 52
  14.6 1.5 %copy-start.4 = (f32[1,4]{1,0:T(1,128)S(1)}, f32[1,4]{1,0:T(1,128)}, u32[]{:S(2)}) copy-start(f32[1,4]{1,0:T(1,128)} %scale_ref.9) | copy-start | bytes 52
  14.7 33.4 %collective-permute-start.10 = (bf16[512,1024]{1,0:T(8,128)(2,1)S(1)}, bf16[512,1024]{1,0:T(8,128)(2,1)S(1)}, u32[]{:S(2)}, u32[]{:S(2)}) collective-permute-start(bf16[512,1024]{1,0:T(8,128)(2,1)S(1)} %bitcast.30), channel_id=1, source_target_pairs={{0,2},{2,0},{1,3},{3,1},{4,6},{6,4},{5,7},{7,5},{8,10},{10,8},{9,1... | collective-permute-start | bytes 3145736 | tf_op jit(solution)/shard_map/ppermute | solution.py:427
  28.2 5.8 %collective-permute-start.5 = (bf16[528,128]{1,0:T(8,128)(2,1)S(1)}, bf16[528,128]{1,0:T(8,128)(2,1)S(1)}, u32[]{:S(2)}, u32[]{:S(2)}) collective-permute-start(bf16[528,128]{1,0:T(8,128)(2,1)S(1)} %get-tuple-element.87.refs_0_), channel_id=1, source_target_pairs={{0,4},{4,0},{8,12},{12,8},{16,20},{20,16},{24,28},{28,24},{1,5},{5... | collective-permute-start | bytes 405512 | tf_op jit(solution)/shard_map/ppermute | solution.py:470
  29.9 5.6 %collective-permute-start.6 = (bf16[528,128]{1,0:T(8,128)(2,1)S(1)}, bf16[528,128]{1,0:T(8,128)(2,1)S(1)}, u32[]{:S(2)}, u32[]{:S(2)}) collective-permute-start(bf16[528,128]{1,0:T(8,128)(2,1)S(1)} %get-tuple-element.87.refs_0_), channel_id=1, source_target_pairs={{0,8},{4,12},{8,0},{12,4},{16,24},{20,28},{24,16},{28,20},{1,9},{5... | collective-permute-start | bytes 405512 | tf_op jit(solution)/shard_map/ppermute | solution.py:470
  31.5 6.1 %collective-permute-start.7 = (bf16[528,128]{1,0:T(8,128)(2,1)S(1)}, bf16[528,128]{1,0:T(8,128)(2,1)S(1)}, u32[]{:S(2)}, u32[]{:S(2)}) collective-permute-start(bf16[528,128]{1,0:T(8,128)(2,1)S(1)} %get-tuple-element.87.refs_0_), channel_id=1, source_target_pairs={{0,12},{4,8},{8,4},{12,0},{16,28},{20,24},{24,20},{28,16},{1,13},{... | collective-permute-start | bytes 405512 | tf_op jit(solution)/shard_map/ppermute | solution.py:470
  37.9 7.4 %collective-permute-start.8 = (bf16[528,128]{1,0:T(8,128)(2,1)S(1)}, bf16[528,128]{1,0:T(8,128)(2,1)S(1)}, u32[]{:S(2)}, u32[]{:S(2)}) collective-permute-start(bf16[528,128]{1,0:T(8,128)(2,1)S(1)} %get-tuple-element.97.refs_0_), channel_id=1, source_target_pairs={{0,16},{4,20},{8,24},{12,28},{16,0},{20,4},{24,8},{28,12},{1,17},{... | collective-permute-start | bytes 405512 | tf_op jit(solution)/shard_map/ppermute | solution.py:482
  41.3 6.7 %copy-start = (bf16[1,4,128,1024]{3,2,1,0:T(8,128)(2,1)S(1)}, bf16[1,4,128,1024]{3,2,1,0:T(8,128)(2,1)}, u32[]{:S(2)}) copy-start(bf16[1,4,128,1024]{3,2,1,0:T(8,128)(2,1)} %param.16) | copy-start | bytes 3145732
  45.8 2.1 %collective-permute-start.18 = (bf16[256,512]{1,0:T(8,128)(2,1)S(1)}, bf16[256,512]{1,0:T(8,128)(2,1)S(1)}, u32[]{:S(2)}, u32[]{:S(2)}) collective-permute-start(bf16[256,512]{1,0:T(8,128)(2,1)S(1)} %recall.9.own_ref), channel_id=1, source_target_pairs={{0,2},{2,0},{1,3},{3,1},{4,6},{6,4},{5,7},{7,5},{8,10},{10,8},{9,1... | collective-permute-start | bytes 786440 | tf_op jit(solution)/shard_map/ppermute | solution.py:491
  46.2 4.4 %collective-permute-start.16 = (bf16[256,512]{1,0:T(8,128)(2,1)S(1)}, bf16[256,512]{1,0:T(8,128)(2,1)S(1)}, u32[]{:S(2)}, u32[]{:S(2)}) collective-permute-start(bf16[256,512]{1,0:T(8,128)(2,1)S(1)} %recall.8.own_ref), channel_id=1, source_target_pairs={{0,2},{2,0},{1,3},{3,1},{4,6},{6,4},{5,7},{7,5},{8,10},{10,8},{9,1... | collective-permute-start | bytes 786440 | tf_op jit(solution)/shard_map/ppermute | solution.py:491
  47.0 4.7 %collective-permute-start.14 = (bf16[256,512]{1,0:T(8,128)(2,1)S(1)}, bf16[256,512]{1,0:T(8,128)(2,1)S(1)}, u32[]{:S(2)}, u32[]{:S(2)}) collective-permute-start(bf16[256,512]{1,0:T(8,128)(2,1)S(1)} %recall.7.own_ref), channel_id=1, source_target_pairs={{0,2},{2,0},{1,3},{3,1},{4,6},{6,4},{5,7},{7,5},{8,10},{10,8},{9,1... | collective-permute-start | bytes 786440 | tf_op jit(solution)/shard_map/ppermute | solution.py:491
  47.2 6.9 %collective-permute-start.12 = (bf16[128,512]{1,0:T(8,128)(2,1)S(1)}, bf16[128,512]{1,0:T(8,128)(2,1)S(1)}, u32[]{:S(2)}, u32[]{:S(2)}) collective-permute-start(bf16[128,512]{1,0:T(8,128)(2,1)S(1)} %recall.6.own_ref), channel_id=1, source_target_pairs={{0,2},{2,0},{1,3},{3,1},{4,6},{6,4},{5,7},{7,5},{8,10},{10,8},{9,1... | collective-permute-start | bytes 393224 | tf_op jit(solution)/shard_map/ppermute | solution.py:491
  48.0 7.1 %collective-permute-start.9 = (bf16[128,512]{1,0:T(8,128)(2,1)S(1)}, bf16[128,512]{1,0:T(8,128)(2,1)S(1)}, u32[]{:S(2)}, u32[]{:S(2)}) collective-permute-start(bf16[128,512]{1,0:T(8,128)(2,1)S(1)} %recall.5.own_ref), channel_id=1, source_target_pairs={{0,2},{2,0},{1,3},{3,1},{4,6},{6,4},{5,7},{7,5},{8,10},{10,8},{9,1... | collective-permute-start | bytes 393224 | tf_op jit(solution)/shard_map/ppermute | solution.py:491
  48.8 9.2 %collective-permute-start.19 = (bf16[256,512]{1,0:T(8,128)(2,1)S(1)}, bf16[256,512]{1,0:T(8,128)(2,1)S(1)}, u32[]{:S(2)}, u32[]{:S(2)}) collective-permute-start(bf16[256,512]{1,0:T(8,128)(2,1)S(1)} %get-tuple-element.116), channel_id=1, source_target_pairs={{0,1},{1,0},{2,3},{3,2},{4,5},{5,4},{6,7},{7,6},{8,9},{9,8},{10,11... | collective-permute-start | bytes 786440 | tf_op jit(solution)/shard_map/ppermute | solution.py:496
  51.3 12.3 %collective-permute-start.17 = (bf16[256,512]{1,0:T(8,128)(2,1)S(1)}, bf16[256,512]{1,0:T(8,128)(2,1)S(1)}, u32[]{:S(2)}, u32[]{:S(2)}) collective-permute-start(bf16[256,512]{1,0:T(8,128)(2,1)S(1)} %get-tuple-element.112), channel_id=1, source_target_pairs={{0,1},{1,0},{2,3},{3,2},{4,5},{5,4},{6,7},{7,6},{8,9},{9,8},{10,11... | collective-permute-start | bytes 786440 | tf_op jit(solution)/shard_map/ppermute | solution.py:496
  52.4 16.8 %collective-permute-start.15 = (bf16[256,512]{1,0:T(8,128)(2,1)S(1)}, bf16[256,512]{1,0:T(8,128)(2,1)S(1)}, u32[]{:S(2)}, u32[]{:S(2)}) collective-permute-start(bf16[256,512]{1,0:T(8,128)(2,1)S(1)} %get-tuple-element.108), channel_id=1, source_target_pairs={{0,1},{1,0},{2,3},{3,2},{4,5},{5,4},{6,7},{7,6},{8,9},{9,8},{10,11... | collective-permute-start | bytes 786440 | tf_op jit(solution)/shard_map/ppermute | solution.py:496
  54.6 17.4 %collective-permute-start.13 = (bf16[128,512]{1,0:T(8,128)(2,1)S(1)}, bf16[128,512]{1,0:T(8,128)(2,1)S(1)}, u32[]{:S(2)}, u32[]{:S(2)}) collective-permute-start(bf16[128,512]{1,0:T(8,128)(2,1)S(1)} %get-tuple-element.104), channel_id=1, source_target_pairs={{0,1},{1,0},{2,3},{3,2},{4,5},{5,4},{6,7},{7,6},{8,9},{9,8},{10,11... | collective-permute-start | bytes 393224 | tf_op jit(solution)/shard_map/ppermute | solution.py:496
  55.5 18.9 %collective-permute-start.11 = (bf16[128,512]{1,0:T(8,128)(2,1)S(1)}, bf16[128,512]{1,0:T(8,128)(2,1)S(1)}, u32[]{:S(2)}, u32[]{:S(2)}) collective-permute-start(bf16[128,512]{1,0:T(8,128)(2,1)S(1)} %get-tuple-element.100), channel_id=1, source_target_pairs={{0,1},{1,0},{2,3},{3,2},{4,5},{5,4},{6,7},{7,6},{8,9},{9,8},{10,11... | collective-permute-start | bytes 393224 | tf_op jit(solution)/shard_map/ppermute | solution.py:496

commit v11 on v10

--- a/solution.py
+++ b/solution.py
@@ -210,7 +210,7 @@
     )(gain, w, *xs)
 
 
-def attention_kernel(first, heads, dim, keep_ref, scale_ref, q_ref, *refs):
+def attention_kernel(first, heads, dim, keep_ref, scale_ref, reading_ref, q_ref, *refs):
     count = len(refs) // 2
     k_refs, v_refs, out_ref = refs[:count], refs[count:-1], refs[-1]
     rows = q_ref.shape[0]
@@ -234,22 +234,23 @@
                 part = jnp.where(keep_ref[block, at // BLOCK] == 1, part, 0.0)
             total = part if total is None else total + part
             at += keys
-        out_ref[:, cols] = (total[:, :dim] / total[:, dim:]).astype(BF16)
-
-
-def attention(first, keep, scale, q, ks, vs, heads, dim):
+        out_ref[:rows, cols] = (query.astype(F32) * reading_ref[:, h : h + 1]).astype(BF16)
+        out_ref[rows:, cols] = (total[:, :dim] / total[:, dim:]).astype(BF16)
+
+
+def attention(first, keep, scale, reading, q, ks, vs, heads, dim):
     rows = q.shape[0]
     return pl.pallas_call(
         functools.partial(attention_kernel, first, heads, dim),
-        in_specs=[SMEM, SMEM] + [VMEM] * (1 + len(ks) + len(vs)),
+        in_specs=[SMEM, SMEM] + [VMEM] * (2 + len(ks) + len(vs)),
         out_specs=VMEM,
-        out_shape=struct(q.shape),
+        out_shape=struct((2 * rows, heads * dim)),
         compiler_params=params(),
         cost_estimate=cost(
             heads * 8 * rows * (first + rows) * dim, 0, heads * rows * (first + rows)
         ),
         name="attention",
-    )(keep, scale, q, *ks, *vs)
+    )(keep, scale, reading, q, *ks, *vs)
 
 
 def body_and_decay(ref, h, dim):
@@ -332,28 +333,18 @@
     )(before, decay, *totals)
 
 
-def recall_kernel(heads, dim, reading_ref, q_ref, local_ref, state_ref, out_ref):
-    for h in range(heads):
-        cols = slice(h * dim, (h + 1) * dim)
-        recalled = dot(q_ref[:, cols], state_ref[cols, :]) * reading_ref[:, h : h + 1]
-        out_ref[:, cols] = (local_ref[:, cols].astype(F32) + recalled).astype(BF16)
-
-
-def recall(reading, q, local, state, heads, dim):
-    return pl.pallas_call(
-        functools.partial(recall_kernel, heads, dim),
-        in_specs=[VMEM] * 4,
-        out_specs=VMEM,
-        out_shape=struct(q.shape),
-        compiler_params=params(),
-        cost_estimate=cost(4 * q.size * dim, 0),
-        name="recall",
-    )(reading, q, local, state)
-
-
-def project_kernel(shards, own_ref, side_ref, own_w_ref, side_w_ref, *out_refs):
-    width = out_refs[0].shape[1]
-    own, side = own_ref[...], side_ref[...]
+def respond_kernel(shards, heads, dim, own_ref, side_ref, own_state_ref, side_state_ref, *refs):
+    own_w_ref, side_w_ref, *out_refs = refs
+    rows, width = out_refs[0].shape
+    head_outs = []
+    for pack_ref, state_ref in ((own_ref, own_state_ref), (side_ref, side_state_ref)):
+        parts = []
+        for h in range(heads):
+            cols = slice(h * dim, (h + 1) * dim)
+            recalled = dot(pack_ref[:rows, cols], state_ref[cols, :])
+            parts.append((pack_ref[rows:, cols].astype(F32) + recalled).astype(BF16))
+        head_outs.append(jnp.concatenate(parts, axis=1))
+    own, side = head_outs
     for k in reversed(range(shards)):
         owner = lax.rem(lax.axis_index("head") + k, shards)
         cols = pl.ds(pl.multiple_of(owner * width, width), width)
@@ -361,18 +352,18 @@
         out_refs[k][...] = out.astype(out_refs[k].dtype)
 
 
-def project(own, side, own_w, side_w, shards):
-    rows = own.shape[0]
+def respond(own, side, own_state, side_state, own_w, side_w, shards, heads, dim):
+    rows = own.shape[0] // 2
     width = own_w.shape[1] // shards
     return pl.pallas_call(
-        functools.partial(project_kernel, shards),
-        in_specs=[VMEM] * 4,
+        functools.partial(respond_kernel, shards, heads, dim),
+        in_specs=[VMEM] * 6,
         out_specs=[VMEM] * shards,
         out_shape=[struct((rows, width))] * shards,
         compiler_params=params(),
         cost_estimate=cost(4 * rows * own_w.size, 0),
-        name="project",
-    )(own, side, own_w, side_w)
+        name="respond",
+    )(own, side, own_state, side_state, own_w, side_w)
 
 
 def finish_kernel(count, *refs):
@@ -448,7 +439,7 @@
     gain = prescale_amplifier
     w = triple_projector[0].reshape(-1, 3 * heads * dim)
 
-    qs, ks, vs, locals_ = [], [], [], []
+    qs, ks, vs, packs, sides = [], [], [], [], []
     summary = None
     for c, first in enumerate(firsts[:-1]):
         q, k, v, summary = qkv(gain, w, fade, summary, received[c], heads, dim, first)
@@ -456,9 +447,15 @@
         ks.append(k)
         vs.append(v)
         if c < chunks - 2:
-            local = attention(first, tile_retain_grid, score_scaler, q, ks, vs, heads, dim)
-            summary, local = tied(summary, local)
-            locals_.append(local)
+            pack = attention(
+                first, tile_retain_grid, score_scaler, readings[c], q, ks, vs, heads, dim
+            )
+            if c == 0:
+                pack, side_w = tied(pack, side_w)
+            summary, pack = tied(summary, pack)
+            packs.append(pack)
+            if c < 2:
+                sides.append(lax.ppermute(pack, "stream", swap_streams))
     k, v, sent = last_keys_values(
         gain, w, fade, summary, tail, received[-1], heads, dim, firsts[-1]
     )
@@ -471,25 +468,35 @@
     ]
     qs.append(last_queries(gain, w, received[-1], heads, dim))
     for c in range(chunks - 2, chunks):
-        locals_.append(
+        packs.append(
             attention(
-                firsts[c], tile_retain_grid, score_scaler, qs[c], ks[: c + 1], vs[: c + 1], heads, dim
+                firsts[c],
+                tile_retain_grid,
+                score_scaler,
+                readings[c],
+                qs[c],
+                ks[: c + 1],
+                vs[: c + 1],
+                heads,
+                dim,
             )
         )
-    *loads, locals_[-2] = tied(*loads, locals_[-2])
+    *loads, packs[-2] = tied(*loads, packs[-2])
     before, decay, total = quad(loads, heads, dim)
     totals = [total] + [
         lax.ppermute(total, "tm", [(d, d ^ (quad_size * k)) for d in range(blocks)])
         for k in range(1, blocks // quad_size)
     ]
-    *totals, locals_[-1] = tied(*totals, locals_[-1])
+    sides += [lax.ppermute(pack, "stream", swap_streams) for pack in packs[2:]]
+    *totals, sides[2], sides[3], packs[-1] = tied(*totals, sides[2], sides[3], packs[-1])
     state = entering(quad_size, before, decay, totals, heads, dim)
 
+    side_state = lax.ppermute(state, "stream", swap_streams)
     result = None
     for c in range(chunks):
-        head_out = recall(readings[c], qs[c], locals_[c], state, heads, dim)
-        side = lax.ppermute(head_out, "stream", swap_streams)
-        outs = project(head_out, side, own_w, side_w, shards)
+        outs = respond(
+            packs[c], sides[c], state, side_state, own_w, side_w, shards, heads, dim
+        )
         parts = [outs[0]]
         for k in range(1, shards):
             parts.append(

time: 75.4 us -> 77.3 us (1.025)
  waiting for transfers between devices: 24.3 us -> 27.5 us
  starting transfers between devices: 21 us -> 20.1 us
    ppermute x1, waiting for transfers between devices: 2.42 us -> 4.8 us  [per_device(): lax.ppermute(total, 'tm', [(d, d ^ quad_size * k) for d in range(blocks)])]
    ppermute x5, waiting for transfers between devices: 14.2 us -> 13.3 us  [per_device(): lax.ppermute(outs[k], 'head', [(d, (d + k) % shards) for d in range(shard...]
    ppermute x5 -> x6, waiting for transfers between devices: 0.01 us -> 0.85 us  [the longest x1 0.83 us: per_device(): side_state = lax.ppermute(state, 'stream', swap_streams)]
    pallas_call x10 -> x5, Pallas kernels: 4.32 us -> 3.94 us  [respond(): pl.pallas_call(functools.partial(respond_kernel, shards, heads, dim), in_...]
    unnamed x15 -> x13, local copies, waits for them, and re-layouts: 3.92 us -> 3.84 us
  transfers between devices with their start and end apart: 20 -> 21, of which waited for: 11 -> 12; matrix products, arithmetic and copies ran while one was open for 5% -> 6% of each run, Pallas kernels for 30% -> 29%
where the time goes in v11:
time: 77.3 us; the launch traced here: 77 us
  waiting for transfers between devices  27.5 us (36%)
  Pallas kernels  23.2 us (30%)
  starting transfers between devices  20.1 us (26%)
  local copies, waits for them, and re-layouts  5.98 us (8%)
    ppermute x5, waiting for transfers between devices, per_device(): lax.ppermute(outs[k], 'head', [(d, (d + k) % shards) for d in range(shard...  13.3 us
    pallas_call x5, Pallas kernels, attention(): pl.pallas_call(functools.partial(attention_kernel, first, heads, dim), in...  7.35 us
    ppermute x5, starting transfers between devices, per_device(): lax.ppermute(pieces[c], 'head', [((d + k) % shards, d) for d in range(sha...  6.75 us
    ppermute x5, starting transfers between devices, per_device(): lax.ppermute(outs[k], 'head', [(d, (d + k) % shards) for d in range(shard...  5.97 us
    pallas_call x4, Pallas kernels, qkv(): pl.pallas_call(functools.partial(qkv_kernel, heads, dim, first), in_specs...  5.03 us
    ppermute x1, waiting for transfers between devices, per_device(): lax.ppermute(total, 'tm', [(d, d ^ quad_size * k) for d in range(blocks)])  4.8 us
    ppermute x3, waiting for transfers between devices, per_device(): lax.ppermute(sent, 'tm', [(d, d ^ k) for d in range(blocks)])  4.61 us
    ppermute x5, waiting for transfers between devices, per_device(): lax.ppermute(pieces[c], 'head', [((d + k) % shards, d) for d in range(sha...  3.95 us
  transfers between devices with their start and end apart: 21, of which 12 were waited for; matrix products, arithmetic and copies ran while one was open for 6% of the time, Pallas kernels for 29%

profile of v11, /device:TPU:0, one launch (start us, length us, event | category | flops | bytes accessed | tf_op | source)
XLA Modules:
  0.0 77.0 jit_solution(15159960644098543899)
XLA Ops:
  0.5 1.2 %slice_bitcast_fusion = (bf16[256,512]{1,0:T(8,128)(2,1)S(1)}, bf16[256,512]{1,0:T(8,128)(2,1)S(1)}, bf16[256,512]{1,0:T(8,128)(2,1)S(1)}) fusion(bf16[1,1024,512]{2,1,0:T(8,128)(2,1)} %param.9), kind=kLoop, calls=%fused_computation | loop fusion | bytes 1572864 | tf_op jit(solution)/shard_map/slice | solution.py:428
  1.6 2.6 %collective-permute-start = (bf16[256,512]{1,0:T(8,128)(2,1)S(1)}, bf16[256,512]{1,0:T(8,128)(2,1)S(1)}, u32[]{:S(2)}, u32[]{:S(2)}) collective-permute-start(bf16[256,512]{1,0:T(8,128)(2,1)S(1)} %get-tuple-element.129.refs_0_), channel_id=1, source_target_pairs={{1,0},{0,1},{3,2},{2,3},{5,4},{4,5},{7,6},{6,7},{9,8},{8,9},{11,10... | collective-permute-start | bytes 786440 | tf_op jit(solution)/shard_map/ppermute | solution.py:436
  4.3 1.9 %collective-permute-start.3 = (bf16[256,512]{1,0:T(8,128)(2,1)S(1)}, bf16[256,512]{1,0:T(8,128)(2,1)S(1)}, u32[]{:S(2)}, u32[]{:S(2)}) collective-permute-start(bf16[256,512]{1,0:T(8,128)(2,1)S(1)} %get-tuple-element.127.refs_1_), channel_id=1, source_target_pairs={{1,0},{0,1},{3,2},{2,3},{5,4},{4,5},{7,6},{6,7},{9,8},{8,9},{11,10... | collective-permute-start | bytes 786440 | tf_op jit(solution)/shard_map/ppermute | solution.py:436
  6.2 1.0 %slice_bitcast_fusion.3 = (bf16[128,512]{1,0:T(8,128)(2,1)S(1)}, bf16[128,512]{1,0:T(8,128)(2,1)S(1)}) fusion(bf16[1,1024,512]{2,1,0:T(8,128)(2,1)} %param.9), kind=kLoop, calls=%fused_computation.3 | loop fusion | bytes 524288 | tf_op jit(solution)/shard_map/slice | solution.py:428
  7.2 0.7 copy-done.2
  7.9 0.7 copy-done.5
  8.6 1.4 %prepare.1 = (f32[1024,8]{1,0:T(8,128)S(1)}, bf16[16,128]{1,0:T(8,128)(2,1)S(1)}, f32[256,8]{1,0:T(8,128)S(1)}, f32[256,8]{1,0:T(8,128)S(1)}, f32[256,8]{1,0:T(8...) custom-call(f32[4,1024]{1,0:T(4,128)S(1)} %bitcast.28, s32[2]{0:T(128)S(1)} %copy-done.5), custom_call_target="tpu_custom_call" | custom-call | flops 327680 | tf_op jit(solution)/shard_map/prepare/pallas_call | solution.py:83
  10.1 2.4 %copy.14 = bf16[128,8,4,384]{3,1,2,0:T(8,128)(2,1)S(1)} copy(bf16[128,8,4,384]{3,2,1,0:T(4,128)(2,1)} %bitcast.29) | data formatting | bytes 6291456
  12.6 2.0 %collective-permute-start.5 = (bf16[128,512]{1,0:T(8,128)(2,1)S(1)}, bf16[128,512]{1,0:T(8,128)(2,1)S(1)}, u32[]{:S(2)}, u32[]{:S(2)}) collective-permute-start(bf16[128,512]{1,0:T(8,128)(2,1)S(1)} %get-tuple-element.89.refs_0_), channel_id=1, source_target_pairs={{1,0},{0,1},{3,2},{2,3},{5,4},{4,5},{7,6},{6,7},{9,8},{8,9},{11,10... | collective-permute-start | bytes 393224 | tf_op jit(solution)/shard_map/ppermute | solution.py:436
  14.7 1.4 %qkv.4 = (bf16[256,512]{1,0:T(8,128)(2,1)S(1)}, bf16[256,512]{1,0:T(8,128)(2,1)S(1)}, bf16[256,512]{1,0:T(8,128)(2,1)S(1)}, f32[4,128,128]{2,1,0:T(8,128)S(1)}) custom-call(f32[1,1024]{1,0:T(1,128)S(1)} %copy-done.1, bf16[1024,1536]{1,0:T(8,128)(2,1)S(1)} %bitcast.17, f32[1024,8]{1,0:T(8,128)S(1)} %get-tuple-element.65.fade_ref, ...), custom_call_target="tpu_custom_call" | custom-call | flops 1610612736 | tf_op jit(solution)/shard_map/qkv/pallas_call | solution.py:148
  16.0 1.1 %attention.5.own_ref = bf16[512,512]{1,0:T(8,128)(2,1)S(1)} custom-call(s32[2,2]{1,0:T(2,128)S(1)} %copy-done.3, f32[1,4]{1,0:T(1,128)S(1)} %copy-done.4, f32[256,8]{1,0:T(8,128)S(1)} %get-tuple-element.67.reading_ref, bf16[256,512]{1,0:T(8,128)(2,1)S(1)} %get-tuple-element.68.q_ref, bf16[256,512]{1,0:T(8,128)(2,1)S(1)} %get-tuple-element.69.refs_0_, ...), custom_call_target="tpu_custom_call" | custom-call | flops 268435456 | tf_op jit(solution)/shard_map/attention/pallas_call | solution.py:243
  17.2 1.4 %qkv.5 = (bf16[256,512]{1,0:T(8,128)(2,1)S(1)}, bf16[256,512]{1,0:T(8,128)(2,1)S(1)}, bf16[256,512]{1,0:T(8,128)(2,1)S(1)}, f32[4,128,128]{2,1,0:T(8,128)S(1)}) custom-call(f32[1,1024]{1,0:T(1,128)S(1)} %copy-done.1, bf16[1024,1536]{1,0:T(8,128)(2,1)S(1)} %bitcast.18, f32[1024,8]{1,0:T(8,128)S(1)} %get-tuple-element.65.fade_ref, ...), custom_call_target="tpu_custom_call" | custom-call | flops 1610612736 | tf_op jit(solution)/shard_map/qkv/pallas_call | solution.py:148
  18.6 1.5 %attention.6.own_ref = bf16[512,512]{1,0:T(8,128)(2,1)S(1)} custom-call(s32[2,2]{1,0:T(2,128)S(1)} %copy-done.3, f32[1,4]{1,0:T(1,128)S(1)} %copy-done.4, f32[256,8]{1,0:T(8,128)S(1)} %get-tuple-element.74.reading_ref, bf16[256,512]{1,0:T(8,128)(2,1)S(1)} %get-tuple-element.75.q_ref, bf16[256,512]{1,0:T(8,128)(2,1)S(1)} %get-tuple-element.69.refs_0_, ...), custom_call_target="tpu_custom_call" | custom-call | flops 536870912 | tf_op jit(solution)/shard_map/attention/pallas_call | solution.py:243
  20.0 2.6 %collective-permute-done.3.refs_2_ = bf16[256,512]{1,0:T(8,128)(2,1)S(1)} collective-permute-done((bf16[256,512]{1,0:T(8,128)(2,1)S(1)}, bf16[256,512]{1,0:T(8,128)(2,1)S(1)}, u32[]{:S(2)}, u32[]{:S(2)}) %collective-permute-start.3) | collective-permute-done | bytes 262176 | tf_op jit(solution)/shard_map/ppermute | solution.py:436
  22.6 1.4 %qkv.6 = (bf16[256,512]{1,0:T(8,128)(2,1)S(1)}, bf16[256,512]{1,0:T(8,128)(2,1)S(1)}, bf16[256,512]{1,0:T(8,128)(2,1)S(1)}, f32[4,128,128]{2,1,0:T(8,128)S(1)}) custom-call(f32[1,1024]{1,0:T(1,128)S(1)} %copy-done.1, bf16[1024,1536]{1,0:T(8,128)(2,1)S(1)} %bitcast.19, f32[1024,8]{1,0:T(8,128)S(1)} %get-tuple-element.65.fade_ref, ...), custom_call_target="tpu_custom_call" | custom-call | flops 1610612736 | tf_op jit(solution)/shard_map/qkv/pallas_call | solution.py:148
  24.0 1.7 %attention.7.own_ref = bf16[512,512]{1,0:T(8,128)(2,1)S(1)} custom-call(s32[2,2]{1,0:T(2,128)S(1)} %copy-done.3, f32[1,4]{1,0:T(1,128)S(1)} %copy-done.4, f32[256,8]{1,0:T(8,128)S(1)} %get-tuple-element.80.reading_ref, bf16[256,512]{1,0:T(8,128)(2,1)S(1)} %get-tuple-element.81.q_ref, bf16[256,512]{1,0:T(8,128)(2,1)S(1)} %get-tuple-element.69.refs_0_, ...), custom_call_target="tpu_custom_call" | custom-call | flops 805306368 | tf_op jit(solution)/shard_map/attention/pallas_call | solution.py:243
  25.7 0.9 %qkv.7 = (bf16[128,512]{1,0:T(8,128)(2,1)S(1)}, bf16[128,512]{1,0:T(8,128)(2,1)S(1)}, bf16[128,512]{1,0:T(8,128)(2,1)S(1)}, f32[4,128,128]{2,1,0:T(8,128)S(1)}) custom-call(f32[1,1024]{1,0:T(1,128)S(1)} %copy-done.1, bf16[1024,1536]{1,0:T(8,128)(2,1)S(1)} %bitcast.20, f32[1024,8]{1,0:T(8,128)S(1)} %get-tuple-element.65.fade_ref, ...), custom_call_target="tpu_custom_call" | custom-call | flops 805306368 | tf_op jit(solution)/shard_map/qkv/pallas_call | solution.py:148
  26.7 1.4 %collective-permute-done.5.refs_1_ = bf16[128,512]{1,0:T(8,128)(2,1)S(1)} collective-permute-done((bf16[128,512]{1,0:T(8,128)(2,1)S(1)}, bf16[128,512]{1,0:T(8,128)(2,1)S(1)}, u32[]{:S(2)}, u32[]{:S(2)}) %collective-permute-start.5) | collective-permute-done | bytes 131104 | tf_op jit(solution)/shard_map/ppermute | solution.py:436
  28.0 0.8 %last_keys_values.1 = (bf16[128,512]{1,0:T(8,128)(2,1)S(1)}, bf16[128,512]{1,0:T(8,128)(2,1)S(1)}, bf16[528,128]{1,0:T(8,128)(2,1)S(1)}) custom-call(f32[1,1024]{1,0:T(1,128)S(1)} %copy-done.1, bf16[1024,1536]{1,0:T(8,128)(2,1)S(1)} %bitcast.21, f32[1024,8]{1,0:T(8,128)S(1)} %get-tuple-element.65.fade_ref, f32[4,128,128]{2,1,0:T(8,128)S(1)} %get-tuple-element.87.prev_ref, ...), custom_call_target="tpu_custom_call" | custom-call | flops 603979776 | tf_op jit(solution)/shard_map/last_keys_values/pallas_call | solution.py:179
  28.8 1.8 %collective-permute-start.6 = (bf16[528,128]{1,0:T(8,128)(2,1)S(1)}, bf16[528,128]{1,0:T(8,128)(2,1)S(1)}, u32[]{:S(2)}, u32[]{:S(2)}) collective-permute-start(bf16[528,128]{1,0:T(8,128)(2,1)S(1)} %get-tuple-element.95.refs_0_), channel_id=1, source_target_pairs={{0,4},{4,0},{8,12},{12,8},{16,20},{20,16},{24,28},{28,24},{1,5},{5... | collective-permute-start | bytes 405512 | tf_op jit(solution)/shard_map/ppermute | solution.py:467
  30.6 1.6 %collective-permute-start.7 = (bf16[528,128]{1,0:T(8,128)(2,1)S(1)}, bf16[528,128]{1,0:T(8,128)(2,1)S(1)}, u32[]{:S(2)}, u32[]{:S(2)}) collective-permute-start(bf16[528,128]{1,0:T(8,128)(2,1)S(1)} %get-tuple-element.95.refs_0_), channel_id=1, source_target_pairs={{0,8},{4,12},{8,0},{12,4},{16,24},{20,28},{24,16},{28,20},{1,9},{5... | collective-permute-start | bytes 405512 | tf_op jit(solution)/shard_map/ppermute | solution.py:467
  32.4 1.9 %collective-permute-done.6.refs_1_ = bf16[528,128]{1,0:T(8,128)(2,1)S(1)} collective-permute-done((bf16[528,128]{1,0:T(8,128)(2,1)S(1)}, bf16[528,128]{1,0:T(8,128)(2,1)S(1)}, u32[]{:S(2)}, u32[]{:S(2)}) %collective-permute-start.6) | collective-permute-done | bytes 135200 | tf_op jit(solution)/shard_map/ppermute | solution.py:467
  34.3 1.4 %attention.8.own_ref = bf16[256,512]{1,0:T(8,128)(2,1)S(1)} custom-call(s32[2,2]{1,0:T(2,128)S(1)} %copy-done.3, f32[1,4]{1,0:T(1,128)S(1)} %copy-done.4, f32[128,8]{1,0:T(8,128)S(1)} %get-tuple-element.91.reading_ref, bf16[128,512]{1,0:T(8,128)(2,1)S(1)} %get-tuple-element.92.q_ref, bf16[256,512]{1,0:T(8,128)(2,1)S(1)} %get-tuple-element.69.refs_0_, ...), custom_call_target="tpu_custom_call" | custom-call | flops 469762048 | tf_op jit(solution)/shard_map/attention/pallas_call | solution.py:243
  35.7 1.3 %collective-permute-done.7.refs_2_ = bf16[528,128]{1,0:T(8,128)(2,1)S(1)} collective-permute-done((bf16[528,128]{1,0:T(8,128)(2,1)S(1)}, bf16[528,128]{1,0:T(8,128)(2,1)S(1)}, u32[]{:S(2)}, u32[]{:S(2)}) %collective-permute-start.7) | collective-permute-done | bytes 135200 | tf_op jit(solution)/shard_map/ppermute | solution.py:467
  37.0 1.4 %collective-permute-done.8.refs_3_ = bf16[528,128]{1,0:T(8,128)(2,1)S(1)} collective-permute-done((bf16[528,128]{1,0:T(8,128)(2,1)S(1)}, bf16[528,128]{1,0:T(8,128)(2,1)S(1)}, u32[]{:S(2)}, u32[]{:S(2)}) %collective-permute-start.8) | collective-permute-done | bytes 135200 | tf_op jit(solution)/shard_map/ppermute | solution.py:467
  38.7 2.7 %collective-permute-start.9 = (bf16[528,128]{1,0:T(8,128)(2,1)S(1)}, bf16[528,128]{1,0:T(8,128)(2,1)S(1)}, u32[]{:S(2)}, u32[]{:S(2)}) collective-permute-start(bf16[528,128]{1,0:T(8,128)(2,1)S(1)} %get-tuple-element.108.refs_0_), channel_id=1, source_target_pairs={{0,16},{4,20},{8,24},{12,28},{16,0},{20,4},{24,8},{28,12},{1,17},{... | collective-permute-start | bytes 405512 | tf_op jit(solution)/shard_map/ppermute | solution.py:487
  41.5 0.6 last_queries.1.q_ref
  42.1 1.7 %attention.9.own_ref = bf16[256,512]{1,0:T(8,128)(2,1)S(1)} custom-call(s32[2,2]{1,0:T(2,128)S(1)} %copy-done.3, f32[1,4]{1,0:T(1,128)S(1)} %copy-done.4, f32[128,8]{1,0:T(8,128)S(1)} %get-tuple-element.102.reading_ref, bf16[128,512]{1,0:T(8,128)(2,1)S(1)} %last_queries.1.q_ref, bf16[256,512]{1,0:T(8,128)(2,1)S(1)} %get-tuple-element.69.refs_0_, ...), custom_call_target="tpu_custom_call" | custom-call | flops 536870912 | tf_op jit(solution)/shard_map/attention/pallas_call | solution.py:243
  43.8 4.8 %collective-permute-done.9.refs_1_ = bf16[528,128]{1,0:T(8,128)(2,1)S(1)} collective-permute-done((bf16[528,128]{1,0:T(8,128)(2,1)S(1)}, bf16[528,128]{1,0:T(8,128)(2,1)S(1)}, u32[]{:S(2)}, u32[]{:S(2)}) %collective-permute-start.9) | collective-permute-done | bytes 135200 | tf_op jit(solution)/shard_map/ppermute | solution.py:487
  49.3 0.8 %collective-permute-done.13.side_state_ref = bf16[512,128]{1,0:T(8,128)(2,1)S(1)} collective-permute-done((bf16[512,128]{1,0:T(8,128)(2,1)S(1)}, bf16[512,128]{1,0:T(8,128)(2,1)S(1)}, u32[]{:S(2)}, u32[]{:S(2)}) %collective-permute-start.13) | collective-permute-done | bytes 131104 | tf_op jit(solution)/shard_map/ppermute | solution.py:494
  50.1 0.9 %respond.9 = (bf16[256,512]{1,0:T(8,128)(2,1)S(1)}, bf16[256,512]{1,0:T(8,128)(2,1)S(1)}) custom-call(bf16[512,512]{1,0:T(8,128)(2,1)S(1)} %attention.5.own_ref, bf16[512,512]{1,0:T(8,128)(2,1)S(1)} %collective-permute-done.19.side_ref, bf16[512,128]{1,0:T(8,128)(2,1)S(1)} %entering.1.own_state_ref, ...), custom_call_target="tpu_custom_call" | custom-call | flops 536870912 | tf_op jit(solution)/shard_map/respond/pallas_call | solution.py:358
  51.1 1.6 %collective-permute-start.20 = (bf16[256,512]{1,0:T(8,128)(2,1)S(1)}, bf16[256,512]{1,0:T(8,128)(2,1)S(1)}, u32[]{:S(2)}, u32[]{:S(2)}) collective-permute-start(bf16[256,512]{1,0:T(8,128)(2,1)S(1)} %get-tuple-element.124), channel_id=1, source_target_pairs={{0,1},{1,0},{2,3},{3,2},{4,5},{5,4},{6,7},{7,6},{8,9},{9,8},{10,11... | collective-permute-start | bytes 786440 | tf_op jit(solution)/shard_map/ppermute | solution.py:503
  52.7 0.9 %respond.8 = (bf16[256,512]{1,0:T(8,128)(2,1)S(1)}, bf16[256,512]{1,0:T(8,128)(2,1)S(1)}) custom-call(bf16[512,512]{1,0:T(8,128)(2,1)S(1)} %attention.6.own_ref, bf16[512,512]{1,0:T(8,128)(2,1)S(1)} %collective-permute-done.17.side_ref, bf16[512,128]{1,0:T(8,128)(2,1)S(1)} %entering.1.own_state_ref, ...), custom_call_target="tpu_custom_call" | custom-call | flops 536870912 | tf_op jit(solution)/shard_map/respond/pallas_call | solution.py:358
  53.6 0.5 collective-permute-start.18
  54.1 0.9 %respond.7 = (bf16[256,512]{1,0:T(8,128)(2,1)S(1)}, bf16[256,512]{1,0:T(8,128)(2,1)S(1)}) custom-call(bf16[512,512]{1,0:T(8,128)(2,1)S(1)} %attention.7.own_ref, bf16[512,512]{1,0:T(8,128)(2,1)S(1)} %collective-permute-done.10.side_ref, bf16[512,128]{1,0:T(8,128)(2,1)S(1)} %entering.1.own_state_ref, ...), custom_call_target="tpu_custom_call" | custom-call | flops 536870912 | tf_op jit(solution)/shard_map/respond/pallas_call | solution.py:358
  55.1 1.7 %collective-permute-start.16 = (bf16[256,512]{1,0:T(8,128)(2,1)S(1)}, bf16[256,512]{1,0:T(8,128)(2,1)S(1)}, u32[]{:S(2)}, u32[]{:S(2)}) collective-permute-start(bf16[256,512]{1,0:T(8,128)(2,1)S(1)} %get-tuple-element.118), channel_id=1, source_target_pairs={{0,1},{1,0},{2,3},{3,2},{4,5},{5,4},{6,7},{7,6},{8,9},{9,8},{10,11... | collective-permute-start | bytes 786440 | tf_op jit(solution)/shard_map/ppermute | solution.py:503
  56.7 0.6 respond.6
  57.8 0.6 respond.5
  58.4 1.7 %collective-permute-start.14 = (bf16[128,512]{1,0:T(8,128)(2,1)S(1)}, bf16[128,512]{1,0:T(8,128)(2,1)S(1)}, u32[]{:S(2)}, u32[]{:S(2)}) collective-permute-start(bf16[128,512]{1,0:T(8,128)(2,1)S(1)} %get-tuple-element.112), channel_id=1, source_target_pairs={{0,1},{1,0},{2,3},{3,2},{4,5},{5,4},{6,7},{7,6},{8,9},{9,8},{10,11... | collective-permute-start | bytes 393224 | tf_op jit(solution)/shard_map/ppermute | solution.py:503
  60.3 0.8 finish.5.refs_2_
  61.0 4.8 %collective-permute-done.18.refs_1_ = bf16[256,512]{1,0:T(8,128)(2,1)S(1)} collective-permute-done((bf16[256,512]{1,0:T(8,128)(2,1)S(1)}, bf16[256,512]{1,0:T(8,128)(2,1)S(1)}, u32[]{:S(2)}, u32[]{:S(2)}) %collective-permute-start.18) | collective-permute-done | bytes 262176 | tf_op jit(solution)/shard_map/ppermute | solution.py:503
  65.9 0.8 finish.6.refs_2_
  66.7 4.9 %collective-permute-done.16.refs_1_ = bf16[256,512]{1,0:T(8,128)(2,1)S(1)} collective-permute-done((bf16[256,512]{1,0:T(8,128)(2,1)S(1)}, bf16[256,512]{1,0:T(8,128)(2,1)S(1)}, u32[]{:S(2)}, u32[]{:S(2)}) %collective-permute-start.16) | collective-permute-done | bytes 262176 | tf_op jit(solution)/shard_map/ppermute | solution.py:503
  71.5 0.8 finish.7.refs_2_
  72.3 2.0 %collective-permute-done.15.refs_1_ = bf16[128,512]{1,0:T(8,128)(2,1)S(1)} collective-permute-done((bf16[128,512]{1,0:T(8,128)(2,1)S(1)}, bf16[128,512]{1,0:T(8,128)(2,1)S(1)}, u32[]{:S(2)}, u32[]{:S(2)}) %collective-permute-start.15) | collective-permute-done | bytes 131104 | tf_op jit(solution)/shard_map/ppermute | solution.py:503
  74.3 0.7 finish.8.refs_2_
  75.0 1.3 %collective-permute-done.14.refs_1_ = bf16[128,512]{1,0:T(8,128)(2,1)S(1)} collective-permute-done((bf16[128,512]{1,0:T(8,128)(2,1)S(1)}, bf16[128,512]{1,0:T(8,128)(2,1)S(1)}, u32[]{:S(2)}, u32[]{:S(2)}) %collective-permute-start.14) | collective-permute-done | bytes 131104 | tf_op jit(solution)/shard_map/ppermute | solution.py:503
  76.3 0.7 finish.9
  (33 shorter events, 2.6 us)
Async XLA Ops:
  0.0 17.2 %collective-permute-start.1 = (bf16[512,1024]{1,0:T(8,128)(2,1)}, bf16[512,1024]{1,0:T(8,128)(2,1)S(1)}, u32[]{:S(2)}, u32[]{:S(2)}) collective-permute-start(bf16[512,1024]{1,0:T(8,128)(2,1)} %bitcast.30), channel_id=1, source_target_pairs={{0,2},{2,0},{1,3},{3,1},{4,6},{6,4},{5,7},{7,5},{8,10},{10,8},{9,1... | collective-permute-start | bytes 3145736 | tf_op jit(solution)/shard_map/ppermute | solution.py:418
  1.6 11.0 %collective-permute-start = (bf16[256,512]{1,0:T(8,128)(2,1)S(1)}, bf16[256,512]{1,0:T(8,128)(2,1)S(1)}, u32[]{:S(2)}, u32[]{:S(2)}) collective-permute-start(bf16[256,512]{1,0:T(8,128)(2,1)S(1)} %get-tuple-element.129.refs_0_), channel_id=1, source_target_pairs={{1,0},{0,1},{3,2},{2,3},{5,4},{4,5},{7,6},{6,7},{9,8},{8,9},{11,10... | collective-permute-start | bytes 786440 | tf_op jit(solution)/shard_map/ppermute | solution.py:436
  4.2 13.0 %collective-permute-start.2 = (bf16[256,512]{1,0:T(8,128)(2,1)S(1)}, bf16[256,512]{1,0:T(8,128)(2,1)S(1)}, u32[]{:S(2)}, u32[]{:S(2)}) collective-permute-start(bf16[256,512]{1,0:T(8,128)(2,1)S(1)} %get-tuple-element.128.refs_1_), channel_id=1, source_target_pairs={{1,0},{0,1},{3,2},{2,3},{5,4},{4,5},{7,6},{6,7},{9,8},{8,9},{11,10... | collective-permute-start | bytes 786440 | tf_op jit(solution)/shard_map/ppermute | solution.py:436
  4.3 18.3 %collective-permute-start.3 = (bf16[256,512]{1,0:T(8,128)(2,1)S(1)}, bf16[256,512]{1,0:T(8,128)(2,1)S(1)}, u32[]{:S(2)}, u32[]{:S(2)}) collective-permute-start(bf16[256,512]{1,0:T(8,128)(2,1)S(1)} %get-tuple-element.127.refs_1_), channel_id=1, source_target_pairs={{1,0},{0,1},{3,2},{2,3},{5,4},{4,5},{7,6},{6,7},{9,8},{8,9},{11,10... | collective-permute-start | bytes 786440 | tf_op jit(solution)/shard_map/ppermute | solution.py:436
  7.2 0.7 copy-start.2
  7.9 0.7 copy-start.5
  10.0 15.7 %collective-permute-start.4 = (bf16[128,512]{1,0:T(8,128)(2,1)S(1)}, bf16[128,512]{1,0:T(8,128)(2,1)S(1)}, u32[]{:S(2)}, u32[]{:S(2)}) collective-permute-start(bf16[128,512]{1,0:T(8,128)(2,1)S(1)} %get-tuple-element.86.refs_1_), channel_id=1, source_target_pairs={{1,0},{0,1},{3,2},{2,3},{5,4},{4,5},{7,6},{6,7},{9,8},{8,9},{11,10... | collective-permute-start | bytes 393224 | tf_op jit(solution)/shard_map/ppermute | solution.py:436
  10.1 4.5 %copy-start.1 = (f32[1,1024]{1,0:T(1,128)S(1)}, f32[1,1024]{1,0:T(1,128)}, u32[]{:S(2)}) copy-start(f32[1,1024]{1,0:T(1,128)} %gain_ref.11) | copy-start | bytes 12292
  12.6 3.4 %copy-start.3 = (s32[2,2]{1,0:T(2,128)S(1)}, s32[2,2]{1,0:T(2,128)}, u32[]{:S(2)}) copy-start(s32[2,2]{1,0:T(2,128)} %keep_ref.9) | copy-start | bytes 52
  12.6 3.4 %copy-start.4 = (f32[1,4]{1,0:T(1,128)S(1)}, f32[1,4]{1,0:T(1,128)}, u32[]{:S(2)}) copy-start(f32[1,4]{1,0:T(1,128)} %scale_ref.9) | copy-start | bytes 52
  12.6 15.4 %collective-permute-start.5 = (bf16[128,512]{1,0:T(8,128)(2,1)S(1)}, bf16[128,512]{1,0:T(8,128)(2,1)S(1)}, u32[]{:S(2)}, u32[]{:S(2)}) collective-permute-start(bf16[128,512]{1,0:T(8,128)(2,1)S(1)} %get-tuple-element.89.refs_0_), channel_id=1, source_target_pairs={{1,0},{0,1},{3,2},{2,3},{5,4},{4,5},{7,6},{6,7},{9,8},{8,9},{11,10... | collective-permute-start | bytes 393224 | tf_op jit(solution)/shard_map/ppermute | solution.py:436
  25.6 23.0 %collective-permute-start.10 = (bf16[512,512]{1,0:T(8,128)(2,1)S(1)}, bf16[512,512]{1,0:T(8,128)(2,1)S(1)}, u32[]{:S(2)}, u32[]{:S(2)}) collective-permute-start(bf16[512,512]{1,0:T(8,128)(2,1)S(1)} %attention.7.own_ref), channel_id=1, source_target_pairs={{0,2},{2,0},{1,3},{3,1},{4,6},{6,4},{5,7},{7,5},{8,10},{10,8},{9,1... | collective-permute-start | bytes 1572872 | tf_op jit(solution)/shard_map/ppermute | solution.py:490
  28.8 5.5 %collective-permute-start.6 = (bf16[528,128]{1,0:T(8,128)(2,1)S(1)}, bf16[528,128]{1,0:T(8,128)(2,1)S(1)}, u32[]{:S(2)}, u32[]{:S(2)}) collective-permute-start(bf16[528,128]{1,0:T(8,128)(2,1)S(1)} %get-tuple-element.95.refs_0_), channel_id=1, source_target_pairs={{0,4},{4,0},{8,12},{12,8},{16,20},{20,16},{24,28},{28,24},{1,5},{5... | collective-permute-start | bytes 405512 | tf_op jit(solution)/shard_map/ppermute | solution.py:467
  30.6 6.4 %collective-permute-start.7 = (bf16[528,128]{1,0:T(8,128)(2,1)S(1)}, bf16[528,128]{1,0:T(8,128)(2,1)S(1)}, u32[]{:S(2)}, u32[]{:S(2)}) collective-permute-start(bf16[528,128]{1,0:T(8,128)(2,1)S(1)} %get-tuple-element.95.refs_0_), channel_id=1, source_target_pairs={{0,8},{4,12},{8,0},{12,4},{16,24},{20,28},{24,16},{28,20},{1,9},{5... | collective-permute-start | bytes 405512 | tf_op jit(solution)/shard_map/ppermute | solution.py:467
  32.2 6.2 %collective-permute-start.8 = (bf16[528,128]{1,0:T(8,128)(2,1)S(1)}, bf16[528,128]{1,0:T(8,128)(2,1)S(1)}, u32[]{:S(2)}, u32[]{:S(2)}) collective-permute-start(bf16[528,128]{1,0:T(8,128)(2,1)S(1)} %get-tuple-element.95.refs_0_), channel_id=1, source_target_pairs={{0,12},{4,8},{8,4},{12,0},{16,28},{20,24},{24,20},{28,16},{1,13},{... | collective-permute-start | bytes 405512 | tf_op jit(solution)/shard_map/ppermute | solution.py:467
  32.4 16.9 %collective-permute-start.19 = (bf16[512,512]{1,0:T(8,128)(2,1)S(1)}, bf16[512,512]{1,0:T(8,128)(2,1)S(1)}, u32[]{:S(2)}, u32[]{:S(2)}) collective-permute-start(bf16[512,512]{1,0:T(8,128)(2,1)S(1)} %attention.5.own_ref), channel_id=1, source_target_pairs={{0,2},{2,0},{1,3},{3,1},{4,6},{6,4},{5,7},{7,5},{8,10},{10,8},{9,1... | collective-permute-start | bytes 1572872 | tf_op jit(solution)/shard_map/ppermute | solution.py:458
  34.3 18.4 %collective-permute-start.17 = (bf16[512,512]{1,0:T(8,128)(2,1)S(1)}, bf16[512,512]{1,0:T(8,128)(2,1)S(1)}, u32[]{:S(2)}, u32[]{:S(2)}) collective-permute-start(bf16[512,512]{1,0:T(8,128)(2,1)S(1)} %attention.6.own_ref), channel_id=1, source_target_pairs={{0,2},{2,0},{1,3},{3,1},{4,6},{6,4},{5,7},{7,5},{8,10},{10,8},{9,1... | collective-permute-start | bytes 1572872 | tf_op jit(solution)/shard_map/ppermute | solution.py:458
  38.4 10.2 %collective-permute-start.11 = (bf16[256,512]{1,0:T(8,128)(2,1)S(1)}, bf16[256,512]{1,0:T(8,128)(2,1)S(1)}, u32[]{:S(2)}, u32[]{:S(2)}) collective-permute-start(bf16[256,512]{1,0:T(8,128)(2,1)S(1)} %attention.8.own_ref), channel_id=1, source_target_pairs={{0,2},{2,0},{1,3},{3,1},{4,6},{6,4},{5,7},{7,5},{8,10},{10,8},{9,1... | collective-permute-start | bytes 786440 | tf_op jit(solution)/shard_map/ppermute | solution.py:490
  38.7 11.4 %copy-start = (bf16[1,4,128,1024]{3,2,1,0:T(8,128)(2,1)S(1)}, bf16[1,4,128,1024]{3,2,1,0:T(8,128)(2,1)}, u32[]{:S(2)}) copy-start(bf16[1,4,128,1024]{3,2,1,0:T(8,128)(2,1)} %param.16) | copy-start | bytes 3145732
  38.7 9.9 %collective-permute-start.9 = (bf16[528,128]{1,0:T(8,128)(2,1)S(1)}, bf16[528,128]{1,0:T(8,128)(2,1)S(1)}, u32[]{:S(2)}, u32[]{:S(2)}) collective-permute-start(bf16[528,128]{1,0:T(8,128)(2,1)S(1)} %get-tuple-element.108.refs_0_), channel_id=1, source_target_pairs={{0,16},{4,20},{8,24},{12,28},{16,0},{20,4},{24,8},{28,12},{1,17},{... | collective-permute-start | bytes 405512 | tf_op jit(solution)/shard_map/ppermute | solution.py:487
  48.7 1.4 %collective-permute-start.13 = (bf16[512,128]{1,0:T(8,128)(2,1)S(1)}, bf16[512,128]{1,0:T(8,128)(2,1)S(1)}, u32[]{:S(2)}, u32[]{:S(2)}) collective-permute-start(bf16[512,128]{1,0:T(8,128)(2,1)S(1)} %entering.1.own_state_ref), channel_id=1, source_target_pairs={{0,2},{2,0},{1,3},{3,1},{4,6},{6,4},{5,7},{7,5},{8,10},{10,8},{9,1... | collective-permute-start | bytes 393224 | tf_op jit(solution)/shard_map/ppermute | solution.py:494
  48.8 9.0 %collective-permute-start.12 = (bf16[256,512]{1,0:T(8,128)(2,1)S(1)}, bf16[256,512]{1,0:T(8,128)(2,1)S(1)}, u32[]{:S(2)}, u32[]{:S(2)}) collective-permute-start(bf16[256,512]{1,0:T(8,128)(2,1)S(1)} %attention.9.own_ref), channel_id=1, source_target_pairs={{0,2},{2,0},{1,3},{3,1},{4,6},{6,4},{5,7},{7,5},{8,10},{10,8},{9,1... | collective-permute-start | bytes 786440 | tf_op jit(solution)/shard_map/ppermute | solution.py:490
  51.1 9.2 %collective-permute-start.20 = (bf16[256,512]{1,0:T(8,128)(2,1)S(1)}, bf16[256,512]{1,0:T(8,128)(2,1)S(1)}, u32[]{:S(2)}, u32[]{:S(2)}) collective-permute-start(bf16[256,512]{1,0:T(8,128)(2,1)S(1)} %get-tuple-element.124), channel_id=1, source_target_pairs={{0,1},{1,0},{2,3},{3,2},{4,5},{5,4},{6,7},{7,6},{8,9},{9,8},{10,11... | collective-permute-start | bytes 786440 | tf_op jit(solution)/shard_map/ppermute | solution.py:503
  53.6 12.3 %collective-permute-start.18 = (bf16[256,512]{1,0:T(8,128)(2,1)S(1)}, bf16[256,512]{1,0:T(8,128)(2,1)S(1)}, u32[]{:S(2)}, u32[]{:S(2)}) collective-permute-start(bf16[256,512]{1,0:T(8,128)(2,1)S(1)} %get-tuple-element.121), channel_id=1, source_target_pairs={{0,1},{1,0},{2,3},{3,2},{4,5},{5,4},{6,7},{7,6},{8,9},{9,8},{10,11... | collective-permute-start | bytes 786440 | tf_op jit(solution)/shard_map/ppermute | solution.py:503
  55.1 16.5 %collective-permute-start.16 = (bf16[256,512]{1,0:T(8,128)(2,1)S(1)}, bf16[256,512]{1,0:T(8,128)(2,1)S(1)}, u32[]{:S(2)}, u32[]{:S(2)}) collective-permute-start(bf16[256,512]{1,0:T(8,128)(2,1)S(1)} %get-tuple-element.118), channel_id=1, source_target_pairs={{0,1},{1,0},{2,3},{3,2},{4,5},{5,4},{6,7},{7,6},{8,9},{9,8},{10,11... | collective-permute-start | bytes 786440 | tf_op jit(solution)/shard_map/ppermute | solution.py:503
  57.3 17.0 %collective-permute-start.15 = (bf16[128,512]{1,0:T(8,128)(2,1)S(1)}, bf16[128,512]{1,0:T(8,128)(2,1)S(1)}, u32[]{:S(2)}, u32[]{:S(2)}) collective-permute-start(bf16[128,512]{1,0:T(8,128)(2,1)S(1)} %get-tuple-element.115), channel_id=1, source_target_pairs={{0,1},{1,0},{2,3},{3,2},{4,5},{5,4},{6,7},{7,6},{8,9},{9,8},{10,11... | collective-permute-start | bytes 393224 | tf_op jit(solution)/shard_map/ppermute | solution.py:503
  58.4 17.9 %collective-permute-start.14 = (bf16[128,512]{1,0:T(8,128)(2,1)S(1)}, bf16[128,512]{1,0:T(8,128)(2,1)S(1)}, u32[]{:S(2)}, u32[]{:S(2)}) collective-permute-start(bf16[128,512]{1,0:T(8,128)(2,1)S(1)} %get-tuple-element.112), channel_id=1, source_target_pairs={{0,1},{1,0},{2,3},{3,2},{4,5},{5,4},{6,7},{7,6},{8,9},{9,8},{10,11... | collective-permute-start | bytes 393224 | tf_op jit(solution)/shard_map/ppermute | solution.py:503

commit v12 on v10

--- a/solution.py
+++ b/solution.py
@@ -311,18 +311,20 @@
     )(*loads)
 
 
-def entering_kernel(heads, dim, quad_size, before_ref, decay_ref, *refs):
+def entering_kernel(heads, dim, before_ref, decay_ref, *refs):
     refs, out_ref = refs[:-1], refs[-1]
-    place = lax.div(lax.axis_index("tm"), quad_size)
     for h in range(heads):
         rows = slice(h * dim, (h + 1) * dim)
-        earlier = scanned(place, refs, h, dim)[0]
+        earlier = jnp.zeros((dim, out_ref.shape[1]), F32)
+        for ref in reversed(refs):
+            body, decay = body_and_decay(ref, h, dim)
+            earlier = body + decay * earlier
         out_ref[rows, :] = (before_ref[rows, :] + decay_ref[h : h + 1, :] * earlier).astype(BF16)
 
 
-def entering(quad_size, before, decay, totals, heads, dim):
-    return pl.pallas_call(
-        functools.partial(entering_kernel, heads, dim, quad_size),
+def entering(before, decay, totals, heads, dim):
+    return pl.pallas_call(
+        functools.partial(entering_kernel, heads, dim),
         in_specs=[VMEM] * (2 + len(totals)),
         out_specs=VMEM,
         out_shape=struct(before.shape),
@@ -478,12 +480,12 @@
         )
     *loads, locals_[-2] = tied(*loads, locals_[-2])
     before, decay, total = quad(loads, heads, dim)
-    totals = [total] + [
-        lax.ppermute(total, "tm", [(d, d ^ (quad_size * k)) for d in range(blocks)])
+    totals = [
+        lax.ppermute(total, "tm", [(d, d + quad_size * k) for d in range(blocks - quad_size * k)])
         for k in range(1, blocks // quad_size)
     ]
     *totals, locals_[-1] = tied(*totals, locals_[-1])
-    state = entering(quad_size, before, decay, totals, heads, dim)
+    state = entering(before, decay, totals, heads, dim)
 
     result = None
     for c in range(chunks):

time: 75.4 us -> 74.9 us (level)
  waiting for transfers between devices: 24.3 us -> 22.2 us
  starting transfers between devices: 21 us -> 22.9 us
    ppermute x1, waiting for transfers between devices: 2.42 us -> 0.18 us  [per_device(): lax.ppermute(total, 'tm', [(d, d + quad_size * k) for d in range(blocks -...]
    ppermute x1, starting transfers between devices: 2.81 us -> 4.84 us  [per_device(): lax.ppermute(total, 'tm', [(d, d + quad_size * k) for d in range(blocks -...]
where the time goes in v12:
time: 74.9 us; the launch traced here: 74.7 us
  Pallas kernels  23.2 us (31%)
  starting transfers between devices  22.9 us (31%)
  waiting for transfers between devices  22.2 us (30%)
  local copies, waits for them, and re-layouts  6.06 us (8%)
    ppermute x5, waiting for transfers between devices, per_device(): lax.ppermute(outs[k], 'head', [(d, (d + k) % shards) for d in range(shard...  14.3 us
    pallas_call x5, Pallas kernels, attention(): pl.pallas_call(functools.partial(attention_kernel, first, heads, dim), in...  7.15 us
    ppermute x5, starting transfers between devices, per_device(): lax.ppermute(pieces[c], 'head', [((d + k) % shards, d) for d in range(sha...  7.14 us
    ppermute x5, starting transfers between devices, per_device(): lax.ppermute(outs[k], 'head', [(d, (d + k) % shards) for d in range(shard...  5.92 us
    pallas_call x4, Pallas kernels, qkv(): pl.pallas_call(functools.partial(qkv_kernel, heads, dim, first), in_specs...  5.04 us
    ppermute x1, starting transfers between devices, per_device(): lax.ppermute(total, 'tm', [(d, d + quad_size * k) for d in range(blocks -...  4.84 us
    ppermute x3, waiting for transfers between devices, per_device(): lax.ppermute(sent, 'tm', [(d, d ^ k) for d in range(blocks)])  4.49 us
    unnamed x15, local copies, waits for them, and re-layouts  3.92 us
  transfers between devices with their start and end apart: 20, of which 11 were waited for; matrix products, arithmetic and copies ran while one was open for 5% of the time, Pallas kernels for 30%

profile of v12, /device:TPU:0, one launch (start us, length us, event | category | flops | bytes accessed | tf_op | source)
XLA Modules:
  0.0 74.7 jit_solution(4436236294682208635)
XLA Ops:
  0.0 1.2 %slice_bitcast_fusion = (bf16[256,512]{1,0:T(8,128)(2,1)S(1)}, bf16[256,512]{1,0:T(8,128)(2,1)S(1)}, bf16[256,512]{1,0:T(8,128)(2,1)S(1)}) fusion(bf16[1,1024,512]{2,1,0:T(8,128)(2,1)} %param.9), kind=kLoop, calls=%fused_computation | loop fusion | bytes 1572864 | tf_op jit(solution)/shard_map/slice | solution.py:439
  1.2 3.0 %collective-permute-start.1 = (bf16[256,512]{1,0:T(8,128)(2,1)S(1)}, bf16[256,512]{1,0:T(8,128)(2,1)S(1)}, u32[]{:S(2)}, u32[]{:S(2)}) collective-permute-start(bf16[256,512]{1,0:T(8,128)(2,1)S(1)} %get-tuple-element.116.refs_0_), channel_id=1, source_target_pairs={{1,0},{0,1},{3,2},{2,3},{5,4},{4,5},{7,6},{6,7},{9,8},{8,9},{11,10... | collective-permute-start | bytes 786440 | tf_op jit(solution)/shard_map/ppermute | solution.py:447
  4.3 1.9 %collective-permute-start.3 = (bf16[256,512]{1,0:T(8,128)(2,1)S(1)}, bf16[256,512]{1,0:T(8,128)(2,1)S(1)}, u32[]{:S(2)}, u32[]{:S(2)}) collective-permute-start(bf16[256,512]{1,0:T(8,128)(2,1)S(1)} %get-tuple-element.115.refs_1_), channel_id=1, source_target_pairs={{1,0},{0,1},{3,2},{2,3},{5,4},{4,5},{7,6},{6,7},{9,8},{8,9},{11,10... | collective-permute-start | bytes 786440 | tf_op jit(solution)/shard_map/ppermute | solution.py:447
  6.2 1.0 %slice_bitcast_fusion.3 = (bf16[128,512]{1,0:T(8,128)(2,1)S(1)}, bf16[128,512]{1,0:T(8,128)(2,1)S(1)}) fusion(bf16[1,1024,512]{2,1,0:T(8,128)(2,1)} %param.9), kind=kLoop, calls=%fused_computation.3 | loop fusion | bytes 524288 | tf_op jit(solution)/shard_map/slice | solution.py:439
  7.2 0.7 copy-done.2
  7.9 0.7 copy-done.5
  8.6 1.4 %prepare.1 = (f32[1024,8]{1,0:T(8,128)S(1)}, bf16[16,128]{1,0:T(8,128)(2,1)S(1)}, f32[256,8]{1,0:T(8,128)S(1)}, f32[256,8]{1,0:T(8,128)S(1)}, f32[256,8]{1,0:T(8...) custom-call(f32[4,1024]{1,0:T(4,128)S(1)} %bitcast.28, s32[2]{0:T(128)S(1)} %copy-done.5), custom_call_target="tpu_custom_call" | custom-call | flops 327680 | tf_op jit(solution)/shard_map/prepare/pallas_call | solution.py:83
  10.1 1.9 %collective-permute-start = (bf16[128,512]{1,0:T(8,128)(2,1)S(1)}, bf16[128,512]{1,0:T(8,128)(2,1)S(1)}, u32[]{:S(2)}, u32[]{:S(2)}) collective-permute-start(bf16[128,512]{1,0:T(8,128)(2,1)S(1)} %get-tuple-element.62.refs_0_), channel_id=1, source_target_pairs={{1,0},{0,1},{3,2},{2,3},{5,4},{4,5},{7,6},{6,7},{9,8},{8,9},{11,10... | collective-permute-start | bytes 393224 | tf_op jit(solution)/shard_map/ppermute | solution.py:447
  12.1 2.5 %copy.14 = bf16[128,8,4,384]{3,1,2,0:T(8,128)(2,1)S(1)} copy(bf16[128,8,4,384]{3,2,1,0:T(4,128)(2,1)} %bitcast.29) | data formatting | bytes 6291456
  14.8 1.4 %qkv.4 = (bf16[256,512]{1,0:T(8,128)(2,1)S(1)}, bf16[256,512]{1,0:T(8,128)(2,1)S(1)}, bf16[256,512]{1,0:T(8,128)(2,1)S(1)}, f32[4,128,128]{2,1,0:T(8,128)S(1)}) custom-call(f32[1,1024]{1,0:T(1,128)S(1)} %copy-done.1, bf16[1024,1536]{1,0:T(8,128)(2,1)S(1)} %bitcast.17, f32[1024,8]{1,0:T(8,128)S(1)} %get-tuple-element.63.fade_ref, ...), custom_call_target="tpu_custom_call" | custom-call | flops 1610612736 | tf_op jit(solution)/shard_map/qkv/pallas_call | solution.py:148
  16.1 1.1 %attention.5.local_ref = bf16[256,512]{1,0:T(8,128)(2,1)S(1)} custom-call(s32[2,2]{1,0:T(2,128)S(1)} %copy-done.3, f32[1,4]{1,0:T(1,128)S(1)} %copy-done.4, bf16[256,512]{1,0:T(8,128)(2,1)S(1)} %get-tuple-element.65.q_ref, bf16[256,512]{1,0:T(8,128)(2,1)S(1)} %get-tuple-element.66.refs_0_, ...), custom_call_target="tpu_custom_call" | custom-call | flops 268435456 | tf_op jit(solution)/shard_map/attention/pallas_call | solution.py:242
  17.3 1.4 %qkv.5 = (bf16[256,512]{1,0:T(8,128)(2,1)S(1)}, bf16[256,512]{1,0:T(8,128)(2,1)S(1)}, bf16[256,512]{1,0:T(8,128)(2,1)S(1)}, f32[4,128,128]{2,1,0:T(8,128)S(1)}) custom-call(f32[1,1024]{1,0:T(1,128)S(1)} %copy-done.1, bf16[1024,1536]{1,0:T(8,128)(2,1)S(1)} %bitcast.18, f32[1024,8]{1,0:T(8,128)S(1)} %get-tuple-element.63.fade_ref, ...), custom_call_target="tpu_custom_call" | custom-call | flops 1610612736 | tf_op jit(solution)/shard_map/qkv/pallas_call | solution.py:148
  18.6 1.4 %attention.6.local_ref = bf16[256,512]{1,0:T(8,128)(2,1)S(1)} custom-call(s32[2,2]{1,0:T(2,128)S(1)} %copy-done.3, f32[1,4]{1,0:T(1,128)S(1)} %copy-done.4, bf16[256,512]{1,0:T(8,128)(2,1)S(1)} %get-tuple-element.70.q_ref, bf16[256,512]{1,0:T(8,128)(2,1)S(1)} %get-tuple-element.66.refs_0_, bf16[256,512]{1,0:T(8,128)(2,1)S(1)} %get-tuple-element.71.refs_1_, ...), custom_call_target="tpu_custom_call" | custom-call | flops 536870912 | tf_op jit(solution)/shard_map/attention/pallas_call | solution.py:242
  20.1 2.5 %collective-permute-done.3.refs_2_ = bf16[256,512]{1,0:T(8,128)(2,1)S(1)} collective-permute-done((bf16[256,512]{1,0:T(8,128)(2,1)S(1)}, bf16[256,512]{1,0:T(8,128)(2,1)S(1)}, u32[]{:S(2)}, u32[]{:S(2)}) %collective-permute-start.3) | collective-permute-done | bytes 262176 | tf_op jit(solution)/shard_map/ppermute | solution.py:447
  22.6 1.4 %qkv.6 = (bf16[256,512]{1,0:T(8,128)(2,1)S(1)}, bf16[256,512]{1,0:T(8,128)(2,1)S(1)}, bf16[256,512]{1,0:T(8,128)(2,1)S(1)}, f32[4,128,128]{2,1,0:T(8,128)S(1)}) custom-call(f32[1,1024]{1,0:T(1,128)S(1)} %copy-done.1, bf16[1024,1536]{1,0:T(8,128)(2,1)S(1)} %bitcast.19, f32[1024,8]{1,0:T(8,128)S(1)} %get-tuple-element.63.fade_ref, ...), custom_call_target="tpu_custom_call" | custom-call | flops 1610612736 | tf_op jit(solution)/shard_map/qkv/pallas_call | solution.py:148
  23.9 1.7 %attention.7.local_ref = bf16[256,512]{1,0:T(8,128)(2,1)S(1)} custom-call(s32[2,2]{1,0:T(2,128)S(1)} %copy-done.3, f32[1,4]{1,0:T(1,128)S(1)} %copy-done.4, bf16[256,512]{1,0:T(8,128)(2,1)S(1)} %get-tuple-element.75.q_ref, bf16[256,512]{1,0:T(8,128)(2,1)S(1)} %get-tuple-element.66.refs_0_, bf16[256,512]{1,0:T(8,128)(2,1)S(1)} %get-tuple-element.71.refs_1_, ...), custom_call_target="tpu_custom_call" | custom-call | flops 805306368 | tf_op jit(solution)/shard_map/attention/pallas_call | solution.py:242
  25.6 0.9 %qkv.7 = (bf16[128,512]{1,0:T(8,128)(2,1)S(1)}, bf16[128,512]{1,0:T(8,128)(2,1)S(1)}, bf16[128,512]{1,0:T(8,128)(2,1)S(1)}, f32[4,128,128]{2,1,0:T(8,128)S(1)}) custom-call(f32[1,1024]{1,0:T(1,128)S(1)} %copy-done.1, bf16[1024,1536]{1,0:T(8,128)(2,1)S(1)} %bitcast.20, f32[1024,8]{1,0:T(8,128)S(1)} %get-tuple-element.63.fade_ref, ...), custom_call_target="tpu_custom_call" | custom-call | flops 805306368 | tf_op jit(solution)/shard_map/qkv/pallas_call | solution.py:148
  26.6 0.8 %collective-permute-done.refs_1_ = bf16[128,512]{1,0:T(8,128)(2,1)S(1)} collective-permute-done((bf16[128,512]{1,0:T(8,128)(2,1)S(1)}, bf16[128,512]{1,0:T(8,128)(2,1)S(1)}, u32[]{:S(2)}, u32[]{:S(2)}) %collective-permute-start) | collective-permute-done | bytes 131104 | tf_op jit(solution)/shard_map/ppermute | solution.py:447
  27.4 0.8 %last_keys_values.1 = (bf16[128,512]{1,0:T(8,128)(2,1)S(1)}, bf16[128,512]{1,0:T(8,128)(2,1)S(1)}, bf16[528,128]{1,0:T(8,128)(2,1)S(1)}) custom-call(f32[1,1024]{1,0:T(1,128)S(1)} %copy-done.1, bf16[1024,1536]{1,0:T(8,128)(2,1)S(1)} %bitcast.21, f32[1024,8]{1,0:T(8,128)S(1)} %get-tuple-element.63.fade_ref, f32[4,128,128]{2,1,0:T(8,128)S(1)} %get-tuple-element.80.prev_ref, ...), custom_call_target="tpu_custom_call" | custom-call | flops 603979776 | tf_op jit(solution)/shard_map/last_keys_values/pallas_call | solution.py:179
  28.2 1.8 %collective-permute-start.5 = (bf16[528,128]{1,0:T(8,128)(2,1)S(1)}, bf16[528,128]{1,0:T(8,128)(2,1)S(1)}, u32[]{:S(2)}, u32[]{:S(2)}) collective-permute-start(bf16[528,128]{1,0:T(8,128)(2,1)S(1)} %get-tuple-element.86.refs_0_), channel_id=1, source_target_pairs={{0,4},{4,0},{8,12},{12,8},{16,20},{20,16},{24,28},{28,24},{1,5},{5... | collective-permute-start | bytes 405512 | tf_op jit(solution)/shard_map/ppermute | solution.py:472
  29.9 1.6 %collective-permute-start.6 = (bf16[528,128]{1,0:T(8,128)(2,1)S(1)}, bf16[528,128]{1,0:T(8,128)(2,1)S(1)}, u32[]{:S(2)}, u32[]{:S(2)}) collective-permute-start(bf16[528,128]{1,0:T(8,128)(2,1)S(1)} %get-tuple-element.86.refs_0_), channel_id=1, source_target_pairs={{0,8},{4,12},{8,0},{12,4},{16,24},{20,28},{24,16},{28,20},{1,9},{5... | collective-permute-start | bytes 405512 | tf_op jit(solution)/shard_map/ppermute | solution.py:472
  31.7 1.4 %attention.8.local_ref = bf16[128,512]{1,0:T(8,128)(2,1)S(1)} custom-call(s32[2,2]{1,0:T(2,128)S(1)} %copy-done.3, f32[1,4]{1,0:T(1,128)S(1)} %copy-done.4, bf16[128,512]{1,0:T(8,128)(2,1)S(1)} %get-tuple-element.83.q_ref, bf16[256,512]{1,0:T(8,128)(2,1)S(1)} %get-tuple-element.66.refs_0_, bf16[256,512]{1,0:T(8,128)(2,1)S(1)} %get-tuple-element.71.refs_1_, ...), custom_call_target="tpu_custom_call" | custom-call | flops 469762048 | tf_op jit(solution)/shard_map/attention/pallas_call | solution.py:242
  33.1 0.8 %collective-permute-done.5.refs_1_ = bf16[528,128]{1,0:T(8,128)(2,1)S(1)} collective-permute-done((bf16[528,128]{1,0:T(8,128)(2,1)S(1)}, bf16[528,128]{1,0:T(8,128)(2,1)S(1)}, u32[]{:S(2)}, u32[]{:S(2)}) %collective-permute-start.5) | collective-permute-done | bytes 135200 | tf_op jit(solution)/shard_map/ppermute | solution.py:472
  33.9 1.6 %collective-permute-done.6.refs_2_ = bf16[528,128]{1,0:T(8,128)(2,1)S(1)} collective-permute-done((bf16[528,128]{1,0:T(8,128)(2,1)S(1)}, bf16[528,128]{1,0:T(8,128)(2,1)S(1)}, u32[]{:S(2)}, u32[]{:S(2)}) %collective-permute-start.6) | collective-permute-done | bytes 135200 | tf_op jit(solution)/shard_map/ppermute | solution.py:472
  35.6 2.0 %collective-permute-done.7.refs_3_ = bf16[528,128]{1,0:T(8,128)(2,1)S(1)} collective-permute-done((bf16[528,128]{1,0:T(8,128)(2,1)S(1)}, bf16[528,128]{1,0:T(8,128)(2,1)S(1)}, u32[]{:S(2)}, u32[]{:S(2)}) %collective-permute-start.7) | collective-permute-done | bytes 135200 | tf_op jit(solution)/shard_map/ppermute | solution.py:472
  37.9 4.8 %collective-permute-start.8 = (bf16[528,128]{1,0:T(8,128)(2,1)S(1)}, bf16[528,128]{1,0:T(8,128)(2,1)S(1)}, u32[]{:S(2)}, u32[]{:S(2)}) collective-permute-start(bf16[528,128]{1,0:T(8,128)(2,1)S(1)} %get-tuple-element.90), channel_id=1, source_target_pairs={{0,16},{4,20},{8,24},{12,28},{1,17},{5,21},{9,25},{13,29},{2,18},{... | collective-permute-start | bytes 405512 | tf_op jit(solution)/shard_map/ppermute | solution.py:484
  42.8 0.6 last_queries.1.q_ref
  43.4 1.6 %attention.9.local_ref = bf16[128,512]{1,0:T(8,128)(2,1)S(1)} custom-call(s32[2,2]{1,0:T(2,128)S(1)} %copy-done.3, f32[1,4]{1,0:T(1,128)S(1)} %copy-done.4, bf16[128,512]{1,0:T(8,128)(2,1)S(1)} %last_queries.1.q_ref, bf16[256,512]{1,0:T(8,128)(2,1)S(1)} %get-tuple-element.66.refs_0_, bf16[256,512]{1,0:T(8,128)(2,1)S(1)} %get-tuple-element.71.refs_1_, ...), custom_call_target="tpu_custom_call" | custom-call | flops 536870912 | tf_op jit(solution)/shard_map/attention/pallas_call | solution.py:242
  45.7 0.6 collective-permute-start.16
  46.8 0.6 collective-permute-start.12
  47.7 0.7 project.9
  48.4 1.6 %collective-permute-start.19 = (bf16[256,512]{1,0:T(8,128)(2,1)S(1)}, bf16[256,512]{1,0:T(8,128)(2,1)S(1)}, u32[]{:S(2)}, u32[]{:S(2)}) collective-permute-start(bf16[256,512]{1,0:T(8,128)(2,1)S(1)} %get-tuple-element.114), channel_id=1, source_target_pairs={{0,1},{1,0},{2,3},{3,2},{4,5},{5,4},{6,7},{7,6},{8,9},{9,8},{10,11... | collective-permute-start | bytes 786440 | tf_op jit(solution)/shard_map/ppermute | solution.py:498
  50.0 0.7 project.8
  50.7 0.6 collective-permute-start.17
  51.3 0.7 project.7
  52.0 1.6 %collective-permute-start.15 = (bf16[256,512]{1,0:T(8,128)(2,1)S(1)}, bf16[256,512]{1,0:T(8,128)(2,1)S(1)}, u32[]{:S(2)}, u32[]{:S(2)}) collective-permute-start(bf16[256,512]{1,0:T(8,128)(2,1)S(1)} %get-tuple-element.106), channel_id=1, source_target_pairs={{0,1},{1,0},{2,3},{3,2},{4,5},{5,4},{6,7},{7,6},{8,9},{9,8},{10,11... | collective-permute-start | bytes 786440 | tf_op jit(solution)/shard_map/ppermute | solution.py:498
  54.1 0.6 collective-permute-start.13
  55.1 1.6 %collective-permute-start.11 = (bf16[128,512]{1,0:T(8,128)(2,1)S(1)}, bf16[128,512]{1,0:T(8,128)(2,1)S(1)}, u32[]{:S(2)}, u32[]{:S(2)}) collective-permute-start(bf16[128,512]{1,0:T(8,128)(2,1)S(1)} %get-tuple-element.98), channel_id=1, source_target_pairs={{0,1},{1,0},{2,3},{3,2},{4,5},{5,4},{6,7},{7,6},{8,9},{9,8},{10,11... | collective-permute-start | bytes 393224 | tf_op jit(solution)/shard_map/ppermute | solution.py:498
  56.7 0.8 %collective-permute-done.19.refs_1_ = bf16[256,512]{1,0:T(8,128)(2,1)S(1)} collective-permute-done((bf16[256,512]{1,0:T(8,128)(2,1)S(1)}, bf16[256,512]{1,0:T(8,128)(2,1)S(1)}, u32[]{:S(2)}, u32[]{:S(2)}) %collective-permute-start.19) | collective-permute-done | bytes 262176 | tf_op jit(solution)/shard_map/ppermute | solution.py:498
  57.6 0.8 %finish.5.refs_2_ = bf16[1024,512]{1,0:T(8,128)(2,1)} custom-call(bf16[256,512]{1,0:T(8,128)(2,1)S(1)} %get-tuple-element.113.refs_0_, bf16[256,512]{1,0:T(8,128)(2,1)S(1)} %collective-permute-done.19.refs_1_), custom_call_target="tpu_custom_call" | custom-call | flops 262144 | bytes 786432 | tf_op jit(solution)/shard_map/finish/pallas_call | solution.py:392
  58.3 4.9 %collective-permute-done.17.refs_1_ = bf16[256,512]{1,0:T(8,128)(2,1)S(1)} collective-permute-done((bf16[256,512]{1,0:T(8,128)(2,1)S(1)}, bf16[256,512]{1,0:T(8,128)(2,1)S(1)}, u32[]{:S(2)}, u32[]{:S(2)}) %collective-permute-start.17) | collective-permute-done | bytes 262176 | tf_op jit(solution)/shard_map/ppermute | solution.py:498
  63.2 0.8 %finish.6.refs_2_ = bf16[1024,512]{1,0:T(8,128)(2,1)} custom-call(bf16[256,512]{1,0:T(8,128)(2,1)S(1)} %get-tuple-element.109.refs_0_, bf16[256,512]{1,0:T(8,128)(2,1)S(1)} %collective-permute-done.17.refs_1_, bf16[1024,512]{1,0:T(8,128)(2,1)} %finish.5.refs_2_), custom_call_target="tpu_custom_call", output_to_operand_aliasing={{}: (2, {})} | custom-call | flops 262144 | bytes 786432 | tf_op jit(solution)/shard_map/finish/pallas_call | solution.py:392
  64.0 4.9 %collective-permute-done.15.refs_1_ = bf16[256,512]{1,0:T(8,128)(2,1)S(1)} collective-permute-done((bf16[256,512]{1,0:T(8,128)(2,1)S(1)}, bf16[256,512]{1,0:T(8,128)(2,1)S(1)}, u32[]{:S(2)}, u32[]{:S(2)}) %collective-permute-start.15) | collective-permute-done | bytes 262176 | tf_op jit(solution)/shard_map/ppermute | solution.py:498
  68.8 0.8 %finish.7.refs_2_ = bf16[1024,512]{1,0:T(8,128)(2,1)} custom-call(bf16[256,512]{1,0:T(8,128)(2,1)S(1)} %get-tuple-element.105.refs_0_, bf16[256,512]{1,0:T(8,128)(2,1)S(1)} %collective-permute-done.15.refs_1_, bf16[1024,512]{1,0:T(8,128)(2,1)} %finish.6.refs_2_), custom_call_target="tpu_custom_call", output_to_operand_aliasing={{}: (2, {})} | custom-call | flops 262144 | bytes 786432 | tf_op jit(solution)/shard_map/finish/pallas_call | solution.py:392
  69.6 2.0 %collective-permute-done.13.refs_1_ = bf16[128,512]{1,0:T(8,128)(2,1)S(1)} collective-permute-done((bf16[128,512]{1,0:T(8,128)(2,1)S(1)}, bf16[128,512]{1,0:T(8,128)(2,1)S(1)}, u32[]{:S(2)}, u32[]{:S(2)}) %collective-permute-start.13) | collective-permute-done | bytes 131104 | tf_op jit(solution)/shard_map/ppermute | solution.py:498
  71.6 0.7 finish.8.refs_2_
  72.3 1.7 %collective-permute-done.11.refs_1_ = bf16[128,512]{1,0:T(8,128)(2,1)S(1)} collective-permute-done((bf16[128,512]{1,0:T(8,128)(2,1)S(1)}, bf16[128,512]{1,0:T(8,128)(2,1)S(1)}, u32[]{:S(2)}, u32[]{:S(2)}) %collective-permute-start.11) | collective-permute-done | bytes 131104 | tf_op jit(solution)/shard_map/ppermute | solution.py:498
  74.0 0.7 finish.9
  (38 shorter events, 3.3 us)
Async XLA Ops:
  1.2 13.5 %collective-permute-start.1 = (bf16[256,512]{1,0:T(8,128)(2,1)S(1)}, bf16[256,512]{1,0:T(8,128)(2,1)S(1)}, u32[]{:S(2)}, u32[]{:S(2)}) collective-permute-start(bf16[256,512]{1,0:T(8,128)(2,1)S(1)} %get-tuple-element.116.refs_0_), channel_id=1, source_target_pairs={{1,0},{0,1},{3,2},{2,3},{5,4},{4,5},{7,6},{6,7},{9,8},{8,9},{11,10... | collective-permute-start | bytes 786440 | tf_op jit(solution)/shard_map/ppermute | solution.py:447
  4.2 13.1 %collective-permute-start.2 = (bf16[256,512]{1,0:T(8,128)(2,1)S(1)}, bf16[256,512]{1,0:T(8,128)(2,1)S(1)}, u32[]{:S(2)}, u32[]{:S(2)}) collective-permute-start(bf16[256,512]{1,0:T(8,128)(2,1)S(1)} %get-tuple-element.117.refs_1_), channel_id=1, source_target_pairs={{1,0},{0,1},{3,2},{2,3},{5,4},{4,5},{7,6},{6,7},{9,8},{8,9},{11,10... | collective-permute-start | bytes 786440 | tf_op jit(solution)/shard_map/ppermute | solution.py:447
  4.3 18.3 %collective-permute-start.3 = (bf16[256,512]{1,0:T(8,128)(2,1)S(1)}, bf16[256,512]{1,0:T(8,128)(2,1)S(1)}, u32[]{:S(2)}, u32[]{:S(2)}) collective-permute-start(bf16[256,512]{1,0:T(8,128)(2,1)S(1)} %get-tuple-element.115.refs_1_), channel_id=1, source_target_pairs={{1,0},{0,1},{3,2},{2,3},{5,4},{4,5},{7,6},{6,7},{9,8},{8,9},{11,10... | collective-permute-start | bytes 786440 | tf_op jit(solution)/shard_map/ppermute | solution.py:447
  7.2 0.7 copy-start.2
  7.9 0.7 copy-start.5
  10.0 15.6 %collective-permute-start.4 = (bf16[128,512]{1,0:T(8,128)(2,1)S(1)}, bf16[128,512]{1,0:T(8,128)(2,1)S(1)}, u32[]{:S(2)}, u32[]{:S(2)}) collective-permute-start(bf16[128,512]{1,0:T(8,128)(2,1)S(1)} %get-tuple-element.79.refs_1_), channel_id=1, source_target_pairs={{1,0},{0,1},{3,2},{2,3},{5,4},{4,5},{7,6},{6,7},{9,8},{8,9},{11,10... | collective-permute-start | bytes 393224 | tf_op jit(solution)/shard_map/ppermute | solution.py:447
  10.1 17.2 %collective-permute-start = (bf16[128,512]{1,0:T(8,128)(2,1)S(1)}, bf16[128,512]{1,0:T(8,128)(2,1)S(1)}, u32[]{:S(2)}, u32[]{:S(2)}) collective-permute-start(bf16[128,512]{1,0:T(8,128)(2,1)S(1)} %get-tuple-element.62.refs_0_), channel_id=1, source_target_pairs={{1,0},{0,1},{3,2},{2,3},{5,4},{4,5},{7,6},{6,7},{9,8},{8,9},{11,10... | collective-permute-start | bytes 393224 | tf_op jit(solution)/shard_map/ppermute | solution.py:447
  12.1 2.6 %copy-start.6 = (bf16[1,4,128,1024]{3,2,1,0:T(8,128)(2,1)S(1)}, bf16[1,4,128,1024]{3,2,1,0:T(8,128)(2,1)}, u32[]{:S(2)}) copy-start(bf16[1,4,128,1024]{3,2,1,0:T(8,128)(2,1)} %param.17) | copy-start | bytes 3145732
  12.1 2.7 %copy-start.1 = (f32[1,1024]{1,0:T(1,128)S(1)}, f32[1,1024]{1,0:T(1,128)}, u32[]{:S(2)}) copy-start(f32[1,1024]{1,0:T(1,128)} %gain_ref.11) | copy-start | bytes 12292
  14.6 1.5 %copy-start.3 = (s32[2,2]{1,0:T(2,128)S(1)}, s32[2,2]{1,0:T(2,128)}, u32[]{:S(2)}) copy-start(s32[2,2]{1,0:T(2,128)} %keep_ref.9) | copy-start | bytes 52
  14.6 1.5 %copy-start.4 = (f32[1,4]{1,0:T(1,128)S(1)}, f32[1,4]{1,0:T(1,128)}, u32[]{:S(2)}) copy-start(f32[1,4]{1,0:T(1,128)} %scale_ref.9) | copy-start | bytes 52
  14.7 33.0 %collective-permute-start.10 = (bf16[512,1024]{1,0:T(8,128)(2,1)S(1)}, bf16[512,1024]{1,0:T(8,128)(2,1)S(1)}, u32[]{:S(2)}, u32[]{:S(2)}) collective-permute-start(bf16[512,1024]{1,0:T(8,128)(2,1)S(1)} %bitcast.30), channel_id=1, source_target_pairs={{0,2},{2,0},{1,3},{3,1},{4,6},{6,4},{5,7},{7,5},{8,10},{10,8},{9,1... | collective-permute-start | bytes 3145736 | tf_op jit(solution)/shard_map/ppermute | solution.py:429
  28.2 5.8 %collective-permute-start.5 = (bf16[528,128]{1,0:T(8,128)(2,1)S(1)}, bf16[528,128]{1,0:T(8,128)(2,1)S(1)}, u32[]{:S(2)}, u32[]{:S(2)}) collective-permute-start(bf16[528,128]{1,0:T(8,128)(2,1)S(1)} %get-tuple-element.86.refs_0_), channel_id=1, source_target_pairs={{0,4},{4,0},{8,12},{12,8},{16,20},{20,16},{24,28},{28,24},{1,5},{5... | collective-permute-start | bytes 405512 | tf_op jit(solution)/shard_map/ppermute | solution.py:472
  29.9 5.6 %collective-permute-start.6 = (bf16[528,128]{1,0:T(8,128)(2,1)S(1)}, bf16[528,128]{1,0:T(8,128)(2,1)S(1)}, u32[]{:S(2)}, u32[]{:S(2)}) collective-permute-start(bf16[528,128]{1,0:T(8,128)(2,1)S(1)} %get-tuple-element.86.refs_0_), channel_id=1, source_target_pairs={{0,8},{4,12},{8,0},{12,4},{16,24},{20,28},{24,16},{28,20},{1,9},{5... | collective-permute-start | bytes 405512 | tf_op jit(solution)/shard_map/ppermute | solution.py:472
  31.5 6.1 %collective-permute-start.7 = (bf16[528,128]{1,0:T(8,128)(2,1)S(1)}, bf16[528,128]{1,0:T(8,128)(2,1)S(1)}, u32[]{:S(2)}, u32[]{:S(2)}) collective-permute-start(bf16[528,128]{1,0:T(8,128)(2,1)S(1)} %get-tuple-element.86.refs_0_), channel_id=1, source_target_pairs={{0,12},{4,8},{8,4},{12,0},{16,28},{20,24},{24,20},{28,16},{1,13},{... | collective-permute-start | bytes 405512 | tf_op jit(solution)/shard_map/ppermute | solution.py:472
  37.9 7.2 %collective-permute-start.8 = (bf16[528,128]{1,0:T(8,128)(2,1)S(1)}, bf16[528,128]{1,0:T(8,128)(2,1)S(1)}, u32[]{:S(2)}, u32[]{:S(2)}) collective-permute-start(bf16[528,128]{1,0:T(8,128)(2,1)S(1)} %get-tuple-element.90), channel_id=1, source_target_pairs={{0,16},{4,20},{8,24},{12,28},{1,17},{5,21},{9,25},{13,29},{2,18},{... | collective-permute-start | bytes 405512 | tf_op jit(solution)/shard_map/ppermute | solution.py:484
  43.4 4.3 %copy-start = (bf16[1,4,128,1024]{3,2,1,0:T(8,128)(2,1)S(1)}, bf16[1,4,128,1024]{3,2,1,0:T(8,128)(2,1)}, u32[]{:S(2)}) copy-start(bf16[1,4,128,1024]{3,2,1,0:T(8,128)(2,1)} %param.16) | copy-start | bytes 3145732
  45.4 2.1 %collective-permute-start.18 = (bf16[256,512]{1,0:T(8,128)(2,1)S(1)}, bf16[256,512]{1,0:T(8,128)(2,1)S(1)}, u32[]{:S(2)}, u32[]{:S(2)}) collective-permute-start(bf16[256,512]{1,0:T(8,128)(2,1)S(1)} %recall.9.own_ref), channel_id=1, source_target_pairs={{0,2},{2,0},{1,3},{3,1},{4,6},{6,4},{5,7},{7,5},{8,10},{10,8},{9,1... | collective-permute-start | bytes 786440 | tf_op jit(solution)/shard_map/ppermute | solution.py:493
  45.7 4.2 %collective-permute-start.16 = (bf16[256,512]{1,0:T(8,128)(2,1)S(1)}, bf16[256,512]{1,0:T(8,128)(2,1)S(1)}, u32[]{:S(2)}, u32[]{:S(2)}) collective-permute-start(bf16[256,512]{1,0:T(8,128)(2,1)S(1)} %recall.8.own_ref), channel_id=1, source_target_pairs={{0,2},{2,0},{1,3},{3,1},{4,6},{6,4},{5,7},{7,5},{8,10},{10,8},{9,1... | collective-permute-start | bytes 786440 | tf_op jit(solution)/shard_map/ppermute | solution.py:493
  46.5 4.7 %collective-permute-start.14 = (bf16[256,512]{1,0:T(8,128)(2,1)S(1)}, bf16[256,512]{1,0:T(8,128)(2,1)S(1)}, u32[]{:S(2)}, u32[]{:S(2)}) collective-permute-start(bf16[256,512]{1,0:T(8,128)(2,1)S(1)} %recall.7.own_ref), channel_id=1, source_target_pairs={{0,2},{2,0},{1,3},{3,1},{4,6},{6,4},{5,7},{7,5},{8,10},{10,8},{9,1... | collective-permute-start | bytes 786440 | tf_op jit(solution)/shard_map/ppermute | solution.py:493
  46.8 6.8 %collective-permute-start.12 = (bf16[128,512]{1,0:T(8,128)(2,1)S(1)}, bf16[128,512]{1,0:T(8,128)(2,1)S(1)}, u32[]{:S(2)}, u32[]{:S(2)}) collective-permute-start(bf16[128,512]{1,0:T(8,128)(2,1)S(1)} %recall.6.own_ref), channel_id=1, source_target_pairs={{0,2},{2,0},{1,3},{3,1},{4,6},{6,4},{5,7},{7,5},{8,10},{10,8},{9,1... | collective-permute-start | bytes 393224 | tf_op jit(solution)/shard_map/ppermute | solution.py:493
  47.6 7.1 %collective-permute-start.9 = (bf16[128,512]{1,0:T(8,128)(2,1)S(1)}, bf16[128,512]{1,0:T(8,128)(2,1)S(1)}, u32[]{:S(2)}, u32[]{:S(2)}) collective-permute-start(bf16[128,512]{1,0:T(8,128)(2,1)S(1)} %recall.5.own_ref), channel_id=1, source_target_pairs={{0,2},{2,0},{1,3},{3,1},{4,6},{6,4},{5,7},{7,5},{8,10},{10,8},{9,1... | collective-permute-start | bytes 393224 | tf_op jit(solution)/shard_map/ppermute | solution.py:493
  48.4 9.2 %collective-permute-start.19 = (bf16[256,512]{1,0:T(8,128)(2,1)S(1)}, bf16[256,512]{1,0:T(8,128)(2,1)S(1)}, u32[]{:S(2)}, u32[]{:S(2)}) collective-permute-start(bf16[256,512]{1,0:T(8,128)(2,1)S(1)} %get-tuple-element.114), channel_id=1, source_target_pairs={{0,1},{1,0},{2,3},{3,2},{4,5},{5,4},{6,7},{7,6},{8,9},{9,8},{10,11... | collective-permute-start | bytes 786440 | tf_op jit(solution)/shard_map/ppermute | solution.py:498
  50.7 12.5 %collective-permute-start.17 = (bf16[256,512]{1,0:T(8,128)(2,1)S(1)}, bf16[256,512]{1,0:T(8,128)(2,1)S(1)}, u32[]{:S(2)}, u32[]{:S(2)}) collective-permute-start(bf16[256,512]{1,0:T(8,128)(2,1)S(1)} %get-tuple-element.110), channel_id=1, source_target_pairs={{0,1},{1,0},{2,3},{3,2},{4,5},{5,4},{6,7},{7,6},{8,9},{9,8},{10,11... | collective-permute-start | bytes 786440 | tf_op jit(solution)/shard_map/ppermute | solution.py:498
  52.0 16.8 %collective-permute-start.15 = (bf16[256,512]{1,0:T(8,128)(2,1)S(1)}, bf16[256,512]{1,0:T(8,128)(2,1)S(1)}, u32[]{:S(2)}, u32[]{:S(2)}) collective-permute-start(bf16[256,512]{1,0:T(8,128)(2,1)S(1)} %get-tuple-element.106), channel_id=1, source_target_pairs={{0,1},{1,0},{2,3},{3,2},{4,5},{5,4},{6,7},{7,6},{8,9},{9,8},{10,11... | collective-permute-start | bytes 786440 | tf_op jit(solution)/shard_map/ppermute | solution.py:498
  54.1 17.5 %collective-permute-start.13 = (bf16[128,512]{1,0:T(8,128)(2,1)S(1)}, bf16[128,512]{1,0:T(8,128)(2,1)S(1)}, u32[]{:S(2)}, u32[]{:S(2)}) collective-permute-start(bf16[128,512]{1,0:T(8,128)(2,1)S(1)} %get-tuple-element.102), channel_id=1, source_target_pairs={{0,1},{1,0},{2,3},{3,2},{4,5},{5,4},{6,7},{7,6},{8,9},{9,8},{10,11... | collective-permute-start | bytes 393224 | tf_op jit(solution)/shard_map/ppermute | solution.py:498
  55.1 18.9 %collective-permute-start.11 = (bf16[128,512]{1,0:T(8,128)(2,1)S(1)}, bf16[128,512]{1,0:T(8,128)(2,1)S(1)}, u32[]{:S(2)}, u32[]{:S(2)}) collective-permute-start(bf16[128,512]{1,0:T(8,128)(2,1)S(1)} %get-tuple-element.98), channel_id=1, source_target_pairs={{0,1},{1,0},{2,3},{3,2},{4,5},{5,4},{6,7},{7,6},{8,9},{9,8},{10,11... | collective-permute-start | bytes 393224 | tf_op jit(solution)/shard_map/ppermute | solution.py:498

commit v13 on v10

--- a/solution.py
+++ b/solution.py
@@ -259,16 +259,14 @@
     return ref[h * dim : (h + 1) * dim, :].astype(F32), high + low
 
 
-def scanned(place, refs, h, dim):
-    count = len(refs)
-    loaded = [body_and_decay(ref, h, dim) for ref in refs]
-    state, since = jnp.zeros((dim, refs[0].shape[1]), F32), jnp.ones((1, refs[0].shape[1]), F32)
+def scanned(place, loaded):
+    state, since = jnp.zeros_like(loaded[0][0]), jnp.ones_like(loaded[0][1])
     before, before_decay = state, since
-    for j in range(count):
+    for j in range(len(loaded)):
         before = jnp.where(place == j, state, before)
         before_decay = jnp.where(place == j, since, before_decay)
         body, decay = loaded[0]
-        for k in range(1, count):
+        for k in range(1, len(loaded)):
             here = place == (j ^ k)
             body = jnp.where(here, loaded[k][0], body)
             decay = jnp.where(here, loaded[k][1], decay)
@@ -284,7 +282,8 @@
     total_ref[size:, :] = jnp.zeros((TAIL, total_ref.shape[1]), BF16)
     for h in range(heads):
         rows = slice(h * dim, (h + 1) * dim)
-        before, before_decay, state, since = scanned(place, refs, h, dim)
+        loaded = [body_and_decay(ref, h, dim) for ref in refs]
+        before, before_decay, state, since = scanned(place, loaded)
         before_ref[rows, :] = before
         decay_ref[h : h + 1, :] = before_decay
         total_ref[rows, :] = state.astype(BF16)
@@ -311,12 +310,18 @@
     )(*loads)
 
 
-def entering_kernel(heads, dim, quad_size, before_ref, decay_ref, *refs):
+def entering_kernel(heads, dim, quad_size, before_ref, decay_ref, total_ref, *refs):
     refs, out_ref = refs[:-1], refs[-1]
     place = lax.div(lax.axis_index("tm"), quad_size)
+    near = lax.rem(lax.axis_index("tm"), quad_size) < quad_size // 2
+    near_refs, far_refs = refs[: len(refs) // 2], refs[len(refs) // 2 :]
     for h in range(heads):
         rows = slice(h * dim, (h + 1) * dim)
-        earlier = scanned(place, refs, h, dim)[0]
+        loaded = [body_and_decay(total_ref, h, dim)]
+        for near_ref, far_ref in zip(near_refs, far_refs):
+            pair = zip(body_and_decay(near_ref, h, dim), body_and_decay(far_ref, h, dim))
+            loaded.append([jnp.where(near, a, b) for a, b in pair])
+        earlier = scanned(place, loaded)[0]
         out_ref[rows, :] = (before_ref[rows, :] + decay_ref[h : h + 1, :] * earlier).astype(BF16)
 
 
@@ -478,10 +483,16 @@
         )
     *loads, locals_[-2] = tied(*loads, locals_[-2])
     before, decay, total = quad(loads, heads, dim)
-    totals = [total] + [
-        lax.ppermute(total, "tm", [(d, d ^ (quad_size * k)) for d in range(blocks)])
-        for k in range(1, blocks // quad_size)
-    ]
+    totals, half = [total], quad_size // 2
+    for into in (0, half):
+        for k in range(1, blocks // quad_size):
+            pairs = {d: d for d in range(blocks)}
+            for d in range(blocks):
+                later = d ^ (quad_size * k)
+                if d % quad_size >= half and later > d:
+                    later += into - half
+                    pairs[d], pairs[later] = later, d
+            totals.append(lax.ppermute(total, "tm", list(pairs.items())))
     *totals, locals_[-1] = tied(*totals, locals_[-1])
     state = entering(quad_size, before, decay, totals, heads, dim)
 

time: 75.4 us -> 77.8 us (1.032)
  the two profiles are of different devices: /device:TPU:0 before, /device:TPU:8 now
where the time goes in v13:
time: 77.8 us; the launch traced here: 77.5 us
  waiting for transfers between devices  24.9 us (32%)
  Pallas kernels  23.3 us (30%)
  starting transfers between devices  22.9 us (29%)
  local copies, waits for them, and re-layouts  6.06 us (8%)
    ppermute x5, waiting for transfers between devices, per_device(): lax.ppermute(outs[k], 'head', [(d, (d + k) % shards) for d in range(shard...  14.3 us
    pallas_call x5, Pallas kernels, attention(): pl.pallas_call(functools.partial(attention_kernel, first, heads, dim), in...  7.17 us
    ppermute x2, starting transfers between devices, per_device(): totals.append(lax.ppermute(total, 'tm', list(pairs.items())))  6.36 us
    ppermute x5, starting transfers between devices, per_device(): lax.ppermute(outs[k], 'head', [(d, (d + k) % shards) for d in range(shard...  5.91 us
    ppermute x5, starting transfers between devices, per_device(): lax.ppermute(pieces[c], 'head', [((d + k) % shards, d) for d in range(sha...  5.69 us
    pallas_call x4, Pallas kernels, qkv(): pl.pallas_call(functools.partial(qkv_kernel, heads, dim, first), in_specs...  5.04 us
    unnamed x15, local copies, waits for them, and re-layouts  3.92 us
    pallas_call x5, Pallas kernels, finish(): pl.pallas_call(functools.partial(finish_kernel, len(parts)), grid=(1,), i...  3.67 us
  transfers between devices with their start and end apart: 21, of which 12 were waited for; matrix products, arithmetic and copies ran while one was open for 5% of the time, Pallas kernels for 29%

profile of v13, /device:TPU:8, one launch (start us, length us, event | category | flops | bytes accessed | tf_op | source)
XLA Modules:
  0.0 77.5 jit_solution(14092571843869818906)
XLA Ops:
  0.0 1.2 %slice_bitcast_fusion = (bf16[256,512]{1,0:T(8,128)(2,1)S(1)}, bf16[256,512]{1,0:T(8,128)(2,1)S(1)}, bf16[256,512]{1,0:T(8,128)(2,1)S(1)}) fusion(bf16[1,1024,512]{2,1,0:T(8,128)(2,1)} %param.9), kind=kLoop, calls=%fused_computation | loop fusion | bytes 1572864 | tf_op jit(solution)/shard_map/slice | solution.py:442
  1.2 1.6 %collective-permute-start.1 = (bf16[256,512]{1,0:T(8,128)(2,1)S(1)}, bf16[256,512]{1,0:T(8,128)(2,1)S(1)}, u32[]{:S(2)}, u32[]{:S(2)}) collective-permute-start(bf16[256,512]{1,0:T(8,128)(2,1)S(1)} %get-tuple-element.120.refs_0_), channel_id=1, source_target_pairs={{1,0},{0,1},{3,2},{2,3},{5,4},{4,5},{7,6},{6,7},{9,8},{8,9},{11,10... | collective-permute-start | bytes 786440 | tf_op jit(solution)/shard_map/ppermute | solution.py:450
  3.3 1.5 %collective-permute-start.3 = (bf16[256,512]{1,0:T(8,128)(2,1)S(1)}, bf16[256,512]{1,0:T(8,128)(2,1)S(1)}, u32[]{:S(2)}, u32[]{:S(2)}) collective-permute-start(bf16[256,512]{1,0:T(8,128)(2,1)S(1)} %get-tuple-element.119.refs_1_), channel_id=1, source_target_pairs={{1,0},{0,1},{3,2},{2,3},{5,4},{4,5},{7,6},{6,7},{9,8},{8,9},{11,10... | collective-permute-start | bytes 786440 | tf_op jit(solution)/shard_map/ppermute | solution.py:450
  4.8 1.0 %slice_bitcast_fusion.3 = (bf16[128,512]{1,0:T(8,128)(2,1)S(1)}, bf16[128,512]{1,0:T(8,128)(2,1)S(1)}) fusion(bf16[1,1024,512]{2,1,0:T(8,128)(2,1)} %param.9), kind=kLoop, calls=%fused_computation.3 | loop fusion | bytes 524288 | tf_op jit(solution)/shard_map/slice | solution.py:442
  5.8 0.7 copy-done.2
  6.5 0.7 copy-done.5
  7.1 1.4 %prepare.1 = (f32[1024,8]{1,0:T(8,128)S(1)}, bf16[16,128]{1,0:T(8,128)(2,1)S(1)}, f32[256,8]{1,0:T(8,128)S(1)}, f32[256,8]{1,0:T(8,128)S(1)}, f32[256,8]{1,0:T(8...) custom-call(f32[4,1024]{1,0:T(4,128)S(1)} %bitcast.28, s32[2]{0:T(128)S(1)} %copy-done.5), custom_call_target="tpu_custom_call" | custom-call | flops 327680 | tf_op jit(solution)/shard_map/prepare/pallas_call | solution.py:83
  8.6 0.6 collective-permute-start.4
  9.1 1.5 %collective-permute-start = (bf16[128,512]{1,0:T(8,128)(2,1)S(1)}, bf16[128,512]{1,0:T(8,128)(2,1)S(1)}, u32[]{:S(2)}, u32[]{:S(2)}) collective-permute-start(bf16[128,512]{1,0:T(8,128)(2,1)S(1)} %get-tuple-element.64.refs_0_), channel_id=1, source_target_pairs={{1,0},{0,1},{3,2},{2,3},{5,4},{4,5},{7,6},{6,7},{9,8},{8,9},{11,10... | collective-permute-start | bytes 393224 | tf_op jit(solution)/shard_map/ppermute | solution.py:450
  10.6 2.5 %copy.14 = bf16[128,8,4,384]{3,1,2,0:T(8,128)(2,1)S(1)} copy(bf16[128,8,4,384]{3,2,1,0:T(4,128)(2,1)} %bitcast.29) | data formatting | bytes 6291456
  13.3 1.4 %qkv.4 = (bf16[256,512]{1,0:T(8,128)(2,1)S(1)}, bf16[256,512]{1,0:T(8,128)(2,1)S(1)}, bf16[256,512]{1,0:T(8,128)(2,1)S(1)}, f32[4,128,128]{2,1,0:T(8,128)S(1)}) custom-call(f32[1,1024]{1,0:T(1,128)S(1)} %copy-done.1, bf16[1024,1536]{1,0:T(8,128)(2,1)S(1)} %bitcast.17, f32[1024,8]{1,0:T(8,128)S(1)} %get-tuple-element.65.fade_ref, ...), custom_call_target="tpu_custom_call" | custom-call | flops 1610612736 | tf_op jit(solution)/shard_map/qkv/pallas_call | solution.py:148
  14.7 1.1 %attention.5.local_ref = bf16[256,512]{1,0:T(8,128)(2,1)S(1)} custom-call(s32[2,2]{1,0:T(2,128)S(1)} %copy-done.3, f32[1,4]{1,0:T(1,128)S(1)} %copy-done.4, bf16[256,512]{1,0:T(8,128)(2,1)S(1)} %get-tuple-element.67.q_ref, bf16[256,512]{1,0:T(8,128)(2,1)S(1)} %get-tuple-element.68.refs_0_, ...), custom_call_target="tpu_custom_call" | custom-call | flops 268435456 | tf_op jit(solution)/shard_map/attention/pallas_call | solution.py:242
  16.0 1.4 %qkv.5 = (bf16[256,512]{1,0:T(8,128)(2,1)S(1)}, bf16[256,512]{1,0:T(8,128)(2,1)S(1)}, bf16[256,512]{1,0:T(8,128)(2,1)S(1)}, f32[4,128,128]{2,1,0:T(8,128)S(1)}) custom-call(f32[1,1024]{1,0:T(1,128)S(1)} %copy-done.1, bf16[1024,1536]{1,0:T(8,128)(2,1)S(1)} %bitcast.18, f32[1024,8]{1,0:T(8,128)S(1)} %get-tuple-element.65.fade_ref, ...), custom_call_target="tpu_custom_call" | custom-call | flops 1610612736 | tf_op jit(solution)/shard_map/qkv/pallas_call | solution.py:148
  17.4 1.4 %attention.6.local_ref = bf16[256,512]{1,0:T(8,128)(2,1)S(1)} custom-call(s32[2,2]{1,0:T(2,128)S(1)} %copy-done.3, f32[1,4]{1,0:T(1,128)S(1)} %copy-done.4, bf16[256,512]{1,0:T(8,128)(2,1)S(1)} %get-tuple-element.72.q_ref, bf16[256,512]{1,0:T(8,128)(2,1)S(1)} %get-tuple-element.68.refs_0_, bf16[256,512]{1,0:T(8,128)(2,1)S(1)} %get-tuple-element.73.refs_1_, ...), custom_call_target="tpu_custom_call" | custom-call | flops 536870912 | tf_op jit(solution)/shard_map/attention/pallas_call | solution.py:242
  18.9 2.8 %collective-permute-done.3.refs_2_ = bf16[256,512]{1,0:T(8,128)(2,1)S(1)} collective-permute-done((bf16[256,512]{1,0:T(8,128)(2,1)S(1)}, bf16[256,512]{1,0:T(8,128)(2,1)S(1)}, u32[]{:S(2)}, u32[]{:S(2)}) %collective-permute-start.3) | collective-permute-done | bytes 262176 | tf_op jit(solution)/shard_map/ppermute | solution.py:450
  21.7 1.4 %qkv.6 = (bf16[256,512]{1,0:T(8,128)(2,1)S(1)}, bf16[256,512]{1,0:T(8,128)(2,1)S(1)}, bf16[256,512]{1,0:T(8,128)(2,1)S(1)}, f32[4,128,128]{2,1,0:T(8,128)S(1)}) custom-call(f32[1,1024]{1,0:T(1,128)S(1)} %copy-done.1, bf16[1024,1536]{1,0:T(8,128)(2,1)S(1)} %bitcast.19, f32[1024,8]{1,0:T(8,128)S(1)} %get-tuple-element.65.fade_ref, ...), custom_call_target="tpu_custom_call" | custom-call | flops 1610612736 | tf_op jit(solution)/shard_map/qkv/pallas_call | solution.py:148
  23.0 1.7 %attention.7.local_ref = bf16[256,512]{1,0:T(8,128)(2,1)S(1)} custom-call(s32[2,2]{1,0:T(2,128)S(1)} %copy-done.3, f32[1,4]{1,0:T(1,128)S(1)} %copy-done.4, bf16[256,512]{1,0:T(8,128)(2,1)S(1)} %get-tuple-element.77.q_ref, bf16[256,512]{1,0:T(8,128)(2,1)S(1)} %get-tuple-element.68.refs_0_, bf16[256,512]{1,0:T(8,128)(2,1)S(1)} %get-tuple-element.73.refs_1_, ...), custom_call_target="tpu_custom_call" | custom-call | flops 805306368 | tf_op jit(solution)/shard_map/attention/pallas_call | solution.py:242
  24.7 0.9 %qkv.7 = (bf16[128,512]{1,0:T(8,128)(2,1)S(1)}, bf16[128,512]{1,0:T(8,128)(2,1)S(1)}, bf16[128,512]{1,0:T(8,128)(2,1)S(1)}, f32[4,128,128]{2,1,0:T(8,128)S(1)}) custom-call(f32[1,1024]{1,0:T(1,128)S(1)} %copy-done.1, bf16[1024,1536]{1,0:T(8,128)(2,1)S(1)} %bitcast.20, f32[1024,8]{1,0:T(8,128)S(1)} %get-tuple-element.65.fade_ref, ...), custom_call_target="tpu_custom_call" | custom-call | flops 805306368 | tf_op jit(solution)/shard_map/qkv/pallas_call | solution.py:148
  26.1 0.8 %last_keys_values.1 = (bf16[128,512]{1,0:T(8,128)(2,1)S(1)}, bf16[128,512]{1,0:T(8,128)(2,1)S(1)}, bf16[528,128]{1,0:T(8,128)(2,1)S(1)}) custom-call(f32[1,1024]{1,0:T(1,128)S(1)} %copy-done.1, bf16[1024,1536]{1,0:T(8,128)(2,1)S(1)} %bitcast.21, f32[1024,8]{1,0:T(8,128)S(1)} %get-tuple-element.65.fade_ref, f32[4,128,128]{2,1,0:T(8,128)S(1)} %get-tuple-element.82.prev_ref, ...), custom_call_target="tpu_custom_call" | custom-call | flops 603979776 | tf_op jit(solution)/shard_map/last_keys_values/pallas_call | solution.py:179
  26.9 1.6 %collective-permute-start.5 = (bf16[528,128]{1,0:T(8,128)(2,1)S(1)}, bf16[528,128]{1,0:T(8,128)(2,1)S(1)}, u32[]{:S(2)}, u32[]{:S(2)}) collective-permute-start(bf16[528,128]{1,0:T(8,128)(2,1)S(1)} %get-tuple-element.88.refs_0_), channel_id=1, source_target_pairs={{0,4},{4,0},{8,12},{12,8},{16,20},{20,16},{24,28},{28,24},{1,5},{5... | collective-permute-start | bytes 405512 | tf_op jit(solution)/shard_map/ppermute | solution.py:475
  28.9 1.6 %collective-permute-start.7 = (bf16[528,128]{1,0:T(8,128)(2,1)S(1)}, bf16[528,128]{1,0:T(8,128)(2,1)S(1)}, u32[]{:S(2)}, u32[]{:S(2)}) collective-permute-start(bf16[528,128]{1,0:T(8,128)(2,1)S(1)} %get-tuple-element.88.refs_0_), channel_id=1, source_target_pairs={{0,12},{4,8},{8,4},{12,0},{16,28},{20,24},{24,20},{28,16},{1,13},{... | collective-permute-start | bytes 405512 | tf_op jit(solution)/shard_map/ppermute | solution.py:475
  30.5 1.4 %attention.8.local_ref = bf16[128,512]{1,0:T(8,128)(2,1)S(1)} custom-call(s32[2,2]{1,0:T(2,128)S(1)} %copy-done.3, f32[1,4]{1,0:T(1,128)S(1)} %copy-done.4, bf16[128,512]{1,0:T(8,128)(2,1)S(1)} %get-tuple-element.85.q_ref, bf16[256,512]{1,0:T(8,128)(2,1)S(1)} %get-tuple-element.68.refs_0_, bf16[256,512]{1,0:T(8,128)(2,1)S(1)} %get-tuple-element.73.refs_1_, ...), custom_call_target="tpu_custom_call" | custom-call | flops 469762048 | tf_op jit(solution)/shard_map/attention/pallas_call | solution.py:242
  31.9 1.6 %collective-permute-done.5.refs_1_ = bf16[528,128]{1,0:T(8,128)(2,1)S(1)} collective-permute-done((bf16[528,128]{1,0:T(8,128)(2,1)S(1)}, bf16[528,128]{1,0:T(8,128)(2,1)S(1)}, u32[]{:S(2)}, u32[]{:S(2)}) %collective-permute-start.5) | collective-permute-done | bytes 135200 | tf_op jit(solution)/shard_map/ppermute | solution.py:475
  33.5 0.7 collective-permute-done.6.refs_2_
  34.1 1.4 %collective-permute-done.7.refs_3_ = bf16[528,128]{1,0:T(8,128)(2,1)S(1)} collective-permute-done((bf16[528,128]{1,0:T(8,128)(2,1)S(1)}, bf16[528,128]{1,0:T(8,128)(2,1)S(1)}, u32[]{:S(2)}, u32[]{:S(2)}) %collective-permute-start.7) | collective-permute-done | bytes 135200 | tf_op jit(solution)/shard_map/ppermute | solution.py:475
  35.8 4.3 %collective-permute-start.8 = (bf16[528,128]{1,0:T(8,128)(2,1)S(1)}, bf16[528,128]{1,0:T(8,128)(2,1)S(1)}, u32[]{:S(2)}, u32[]{:S(2)}) collective-permute-start(bf16[528,128]{1,0:T(8,128)(2,1)S(1)} %get-tuple-element.98.total_ref), channel_id=1, source_target_pairs={{0,0},{4,4},{8,16},{12,20},{16,8},{20,12},{24,24},{28,28},{1,1},{5... | collective-permute-start | bytes 405512 | tf_op jit(solution)/shard_map/ppermute | solution.py:495
  40.1 2.1 %collective-permute-start.9 = (bf16[528,128]{1,0:T(8,128)(2,1)S(1)}, bf16[528,128]{1,0:T(8,128)(2,1)S(1)}, u32[]{:S(2)}, u32[]{:S(2)}) collective-permute-start(bf16[528,128]{1,0:T(8,128)(2,1)S(1)} %get-tuple-element.98.total_ref), channel_id=1, source_target_pairs={{0,0},{4,4},{8,24},{12,28},{16,16},{20,20},{24,8},{28,12},{1,1},{5... | collective-permute-start | bytes 405512 | tf_op jit(solution)/shard_map/ppermute | solution.py:495
  42.2 0.6 last_queries.1.q_ref
  42.8 1.6 %attention.9.local_ref = bf16[128,512]{1,0:T(8,128)(2,1)S(1)} custom-call(s32[2,2]{1,0:T(2,128)S(1)} %copy-done.3, f32[1,4]{1,0:T(1,128)S(1)} %copy-done.4, bf16[128,512]{1,0:T(8,128)(2,1)S(1)} %last_queries.1.q_ref, bf16[256,512]{1,0:T(8,128)(2,1)S(1)} %get-tuple-element.68.refs_0_, bf16[256,512]{1,0:T(8,128)(2,1)S(1)} %get-tuple-element.73.refs_1_, ...), custom_call_target="tpu_custom_call" | custom-call | flops 536870912 | tf_op jit(solution)/shard_map/attention/pallas_call | solution.py:242
  44.4 3.5 %collective-permute-done.9.refs_1_ = bf16[528,128]{1,0:T(8,128)(2,1)S(1)} collective-permute-done((bf16[528,128]{1,0:T(8,128)(2,1)S(1)}, bf16[528,128]{1,0:T(8,128)(2,1)S(1)}, u32[]{:S(2)}, u32[]{:S(2)}) %collective-permute-start.9) | collective-permute-done | bytes 135200 | tf_op jit(solution)/shard_map/ppermute | solution.py:495
  50.5 0.7 project.9
  51.2 1.6 %collective-permute-start.20 = (bf16[256,512]{1,0:T(8,128)(2,1)S(1)}, bf16[256,512]{1,0:T(8,128)(2,1)S(1)}, u32[]{:S(2)}, u32[]{:S(2)}) collective-permute-start(bf16[256,512]{1,0:T(8,128)(2,1)S(1)} %get-tuple-element.118), channel_id=1, source_target_pairs={{0,1},{1,0},{2,3},{3,2},{4,5},{5,4},{6,7},{7,6},{8,9},{9,8},{10,11... | collective-permute-start | bytes 786440 | tf_op jit(solution)/shard_map/ppermute | solution.py:507
  52.8 0.7 project.8
  53.6 0.6 collective-permute-start.18
  54.1 0.7 project.7
  54.9 1.6 %collective-permute-start.16 = (bf16[256,512]{1,0:T(8,128)(2,1)S(1)}, bf16[256,512]{1,0:T(8,128)(2,1)S(1)}, u32[]{:S(2)}, u32[]{:S(2)}) collective-permute-start(bf16[256,512]{1,0:T(8,128)(2,1)S(1)} %get-tuple-element.110), channel_id=1, source_target_pairs={{0,1},{1,0},{2,3},{3,2},{4,5},{5,4},{6,7},{7,6},{8,9},{9,8},{10,11... | collective-permute-start | bytes 786440 | tf_op jit(solution)/shard_map/ppermute | solution.py:507
  56.9 0.6 collective-permute-start.14
  58.0 1.6 %collective-permute-start.12 = (bf16[128,512]{1,0:T(8,128)(2,1)S(1)}, bf16[128,512]{1,0:T(8,128)(2,1)S(1)}, u32[]{:S(2)}, u32[]{:S(2)}) collective-permute-start(bf16[128,512]{1,0:T(8,128)(2,1)S(1)} %get-tuple-element.102), channel_id=1, source_target_pairs={{0,1},{1,0},{2,3},{3,2},{4,5},{5,4},{6,7},{7,6},{8,9},{9,8},{10,11... | collective-permute-start | bytes 393224 | tf_op jit(solution)/shard_map/ppermute | solution.py:507
  59.6 0.8 %collective-permute-done.20.refs_1_ = bf16[256,512]{1,0:T(8,128)(2,1)S(1)} collective-permute-done((bf16[256,512]{1,0:T(8,128)(2,1)S(1)}, bf16[256,512]{1,0:T(8,128)(2,1)S(1)}, u32[]{:S(2)}, u32[]{:S(2)}) %collective-permute-start.20) | collective-permute-done | bytes 262176 | tf_op jit(solution)/shard_map/ppermute | solution.py:507
  60.4 0.8 finish.5.refs_2_
  61.2 4.9 %collective-permute-done.18.refs_1_ = bf16[256,512]{1,0:T(8,128)(2,1)S(1)} collective-permute-done((bf16[256,512]{1,0:T(8,128)(2,1)S(1)}, bf16[256,512]{1,0:T(8,128)(2,1)S(1)}, u32[]{:S(2)}, u32[]{:S(2)}) %collective-permute-start.18) | collective-permute-done | bytes 262176 | tf_op jit(solution)/shard_map/ppermute | solution.py:507
  66.0 0.8 finish.6.refs_2_
  66.8 4.9 %collective-permute-done.16.refs_1_ = bf16[256,512]{1,0:T(8,128)(2,1)S(1)} collective-permute-done((bf16[256,512]{1,0:T(8,128)(2,1)S(1)}, bf16[256,512]{1,0:T(8,128)(2,1)S(1)}, u32[]{:S(2)}, u32[]{:S(2)}) %collective-permute-start.16) | collective-permute-done | bytes 262176 | tf_op jit(solution)/shard_map/ppermute | solution.py:507
  71.7 0.8 finish.7.refs_2_
  72.4 2.0 %collective-permute-done.14.refs_1_ = bf16[128,512]{1,0:T(8,128)(2,1)S(1)} collective-permute-done((bf16[128,512]{1,0:T(8,128)(2,1)S(1)}, bf16[128,512]{1,0:T(8,128)(2,1)S(1)}, u32[]{:S(2)}, u32[]{:S(2)}) %collective-permute-start.14) | collective-permute-done | bytes 131104 | tf_op jit(solution)/shard_map/ppermute | solution.py:507
  74.5 0.7 finish.8.refs_2_
  75.2 1.7 %collective-permute-done.12.refs_1_ = bf16[128,512]{1,0:T(8,128)(2,1)S(1)} collective-permute-done((bf16[128,512]{1,0:T(8,128)(2,1)S(1)}, bf16[128,512]{1,0:T(8,128)(2,1)S(1)}, u32[]{:S(2)}, u32[]{:S(2)}) %collective-permute-start.12) | collective-permute-done | bytes 131104 | tf_op jit(solution)/shard_map/ppermute | solution.py:507
  76.9 0.7 finish.9
  (40 shorter events, 5.5 us)
Async XLA Ops:
  1.2 12.0 %collective-permute-start.1 = (bf16[256,512]{1,0:T(8,128)(2,1)S(1)}, bf16[256,512]{1,0:T(8,128)(2,1)S(1)}, u32[]{:S(2)}, u32[]{:S(2)}) collective-permute-start(bf16[256,512]{1,0:T(8,128)(2,1)S(1)} %get-tuple-element.120.refs_0_), channel_id=1, source_target_pairs={{1,0},{0,1},{3,2},{2,3},{5,4},{4,5},{7,6},{6,7},{9,8},{8,9},{11,10... | collective-permute-start | bytes 786440 | tf_op jit(solution)/shard_map/ppermute | solution.py:450
  2.7 13.3 %collective-permute-start.2 = (bf16[256,512]{1,0:T(8,128)(2,1)S(1)}, bf16[256,512]{1,0:T(8,128)(2,1)S(1)}, u32[]{:S(2)}, u32[]{:S(2)}) collective-permute-start(bf16[256,512]{1,0:T(8,128)(2,1)S(1)} %get-tuple-element.121.refs_1_), channel_id=1, source_target_pairs={{1,0},{0,1},{3,2},{2,3},{5,4},{4,5},{7,6},{6,7},{9,8},{8,9},{11,10... | collective-permute-start | bytes 786440 | tf_op jit(solution)/shard_map/ppermute | solution.py:450
  3.3 18.4 %collective-permute-start.3 = (bf16[256,512]{1,0:T(8,128)(2,1)S(1)}, bf16[256,512]{1,0:T(8,128)(2,1)S(1)}, u32[]{:S(2)}, u32[]{:S(2)}) collective-permute-start(bf16[256,512]{1,0:T(8,128)(2,1)S(1)} %get-tuple-element.119.refs_1_), channel_id=1, source_target_pairs={{1,0},{0,1},{3,2},{2,3},{5,4},{4,5},{7,6},{6,7},{9,8},{8,9},{11,10... | collective-permute-start | bytes 786440 | tf_op jit(solution)/shard_map/ppermute | solution.py:450
  5.8 0.7 copy-start.2
  6.5 0.7 copy-start.5
  8.6 16.1 %collective-permute-start.4 = (bf16[128,512]{1,0:T(8,128)(2,1)S(1)}, bf16[128,512]{1,0:T(8,128)(2,1)S(1)}, u32[]{:S(2)}, u32[]{:S(2)}) collective-permute-start(bf16[128,512]{1,0:T(8,128)(2,1)S(1)} %get-tuple-element.81.refs_1_), channel_id=1, source_target_pairs={{1,0},{0,1},{3,2},{2,3},{5,4},{4,5},{7,6},{6,7},{9,8},{8,9},{11,10... | collective-permute-start | bytes 393224 | tf_op jit(solution)/shard_map/ppermute | solution.py:450
  9.1 17.0 %collective-permute-start = (bf16[128,512]{1,0:T(8,128)(2,1)S(1)}, bf16[128,512]{1,0:T(8,128)(2,1)S(1)}, u32[]{:S(2)}, u32[]{:S(2)}) collective-permute-start(bf16[128,512]{1,0:T(8,128)(2,1)S(1)} %get-tuple-element.64.refs_0_), channel_id=1, source_target_pairs={{1,0},{0,1},{3,2},{2,3},{5,4},{4,5},{7,6},{6,7},{9,8},{8,9},{11,10... | collective-permute-start | bytes 393224 | tf_op jit(solution)/shard_map/ppermute | solution.py:450
  10.6 2.6 %copy-start.6 = (bf16[1,4,128,1024]{3,2,1,0:T(8,128)(2,1)S(1)}, bf16[1,4,128,1024]{3,2,1,0:T(8,128)(2,1)}, u32[]{:S(2)}) copy-start(bf16[1,4,128,1024]{3,2,1,0:T(8,128)(2,1)} %param.17) | copy-start | bytes 3145732
  10.6 2.7 %copy-start.1 = (f32[1,1024]{1,0:T(1,128)S(1)}, f32[1,1024]{1,0:T(1,128)}, u32[]{:S(2)}) copy-start(f32[1,1024]{1,0:T(1,128)} %gain_ref.11) | copy-start | bytes 12292
  13.2 1.5 %copy-start.3 = (s32[2,2]{1,0:T(2,128)S(1)}, s32[2,2]{1,0:T(2,128)}, u32[]{:S(2)}) copy-start(s32[2,2]{1,0:T(2,128)} %keep_ref.9) | copy-start | bytes 52
  13.2 1.5 %copy-start.4 = (f32[1,4]{1,0:T(1,128)S(1)}, f32[1,4]{1,0:T(1,128)}, u32[]{:S(2)}) copy-start(f32[1,4]{1,0:T(1,128)} %scale_ref.9) | copy-start | bytes 52
  13.2 37.3 %collective-permute-start.11 = (bf16[512,1024]{1,0:T(8,128)(2,1)S(1)}, bf16[512,1024]{1,0:T(8,128)(2,1)S(1)}, u32[]{:S(2)}, u32[]{:S(2)}) collective-permute-start(bf16[512,1024]{1,0:T(8,128)(2,1)S(1)} %bitcast.30), channel_id=1, source_target_pairs={{0,2},{2,0},{1,3},{3,1},{4,6},{6,4},{5,7},{7,5},{8,10},{10,8},{9,1... | collective-permute-start | bytes 3145736 | tf_op jit(solution)/shard_map/ppermute | solution.py:432
  26.9 6.5 %collective-permute-start.5 = (bf16[528,128]{1,0:T(8,128)(2,1)S(1)}, bf16[528,128]{1,0:T(8,128)(2,1)S(1)}, u32[]{:S(2)}, u32[]{:S(2)}) collective-permute-start(bf16[528,128]{1,0:T(8,128)(2,1)S(1)} %get-tuple-element.88.refs_0_), channel_id=1, source_target_pairs={{0,4},{4,0},{8,12},{12,8},{16,20},{20,16},{24,28},{28,24},{1,5},{5... | collective-permute-start | bytes 405512 | tf_op jit(solution)/shard_map/ppermute | solution.py:475
  28.5 5.6 %collective-permute-start.6 = (bf16[528,128]{1,0:T(8,128)(2,1)S(1)}, bf16[528,128]{1,0:T(8,128)(2,1)S(1)}, u32[]{:S(2)}, u32[]{:S(2)}) collective-permute-start(bf16[528,128]{1,0:T(8,128)(2,1)S(1)} %get-tuple-element.88.refs_0_), channel_id=1, source_target_pairs={{0,8},{4,12},{8,0},{12,4},{16,24},{20,28},{24,16},{28,20},{1,9},{5... | collective-permute-start | bytes 405512 | tf_op jit(solution)/shard_map/ppermute | solution.py:475
  28.9 6.6 %collective-permute-start.7 = (bf16[528,128]{1,0:T(8,128)(2,1)S(1)}, bf16[528,128]{1,0:T(8,128)(2,1)S(1)}, u32[]{:S(2)}, u32[]{:S(2)}) collective-permute-start(bf16[528,128]{1,0:T(8,128)(2,1)S(1)} %get-tuple-element.88.refs_0_), channel_id=1, source_target_pairs={{0,12},{4,8},{8,4},{12,0},{16,28},{20,24},{24,20},{28,16},{1,13},{... | collective-permute-start | bytes 405512 | tf_op jit(solution)/shard_map/ppermute | solution.py:475
  35.8 8.6 %collective-permute-start.8 = (bf16[528,128]{1,0:T(8,128)(2,1)S(1)}, bf16[528,128]{1,0:T(8,128)(2,1)S(1)}, u32[]{:S(2)}, u32[]{:S(2)}) collective-permute-start(bf16[528,128]{1,0:T(8,128)(2,1)S(1)} %get-tuple-element.98.total_ref), channel_id=1, source_target_pairs={{0,0},{4,4},{8,16},{12,20},{16,8},{20,12},{24,24},{28,28},{1,1},{5... | collective-permute-start | bytes 405512 | tf_op jit(solution)/shard_map/ppermute | solution.py:495
  40.1 7.8 %collective-permute-start.9 = (bf16[528,128]{1,0:T(8,128)(2,1)S(1)}, bf16[528,128]{1,0:T(8,128)(2,1)S(1)}, u32[]{:S(2)}, u32[]{:S(2)}) collective-permute-start(bf16[528,128]{1,0:T(8,128)(2,1)S(1)} %get-tuple-element.98.total_ref), channel_id=1, source_target_pairs={{0,0},{4,4},{8,24},{12,28},{16,16},{20,20},{24,8},{28,12},{1,1},{5... | collective-permute-start | bytes 405512 | tf_op jit(solution)/shard_map/ppermute | solution.py:495
  44.4 6.1 %copy-start = (bf16[1,4,128,1024]{3,2,1,0:T(8,128)(2,1)S(1)}, bf16[1,4,128,1024]{3,2,1,0:T(8,128)(2,1)}, u32[]{:S(2)}) copy-start(bf16[1,4,128,1024]{3,2,1,0:T(8,128)(2,1)} %param.16) | copy-start | bytes 3145732
  48.3 2.1 %collective-permute-start.19 = (bf16[256,512]{1,0:T(8,128)(2,1)S(1)}, bf16[256,512]{1,0:T(8,128)(2,1)S(1)}, u32[]{:S(2)}, u32[]{:S(2)}) collective-permute-start(bf16[256,512]{1,0:T(8,128)(2,1)S(1)} %recall.9.own_ref), channel_id=1, source_target_pairs={{0,2},{2,0},{1,3},{3,1},{4,6},{6,4},{5,7},{7,5},{8,10},{10,8},{9,1... | collective-permute-start | bytes 786440 | tf_op jit(solution)/shard_map/ppermute | solution.py:502
  48.6 4.2 %collective-permute-start.17 = (bf16[256,512]{1,0:T(8,128)(2,1)S(1)}, bf16[256,512]{1,0:T(8,128)(2,1)S(1)}, u32[]{:S(2)}, u32[]{:S(2)}) collective-permute-start(bf16[256,512]{1,0:T(8,128)(2,1)S(1)} %recall.8.own_ref), channel_id=1, source_target_pairs={{0,2},{2,0},{1,3},{3,1},{4,6},{6,4},{5,7},{7,5},{8,10},{10,8},{9,1... | collective-permute-start | bytes 786440 | tf_op jit(solution)/shard_map/ppermute | solution.py:502
  49.4 4.7 %collective-permute-start.15 = (bf16[256,512]{1,0:T(8,128)(2,1)S(1)}, bf16[256,512]{1,0:T(8,128)(2,1)S(1)}, u32[]{:S(2)}, u32[]{:S(2)}) collective-permute-start(bf16[256,512]{1,0:T(8,128)(2,1)S(1)} %recall.7.own_ref), channel_id=1, source_target_pairs={{0,2},{2,0},{1,3},{3,1},{4,6},{6,4},{5,7},{7,5},{8,10},{10,8},{9,1... | collective-permute-start | bytes 786440 | tf_op jit(solution)/shard_map/ppermute | solution.py:502
  49.7 6.8 %collective-permute-start.13 = (bf16[128,512]{1,0:T(8,128)(2,1)S(1)}, bf16[128,512]{1,0:T(8,128)(2,1)S(1)}, u32[]{:S(2)}, u32[]{:S(2)}) collective-permute-start(bf16[128,512]{1,0:T(8,128)(2,1)S(1)} %recall.6.own_ref), channel_id=1, source_target_pairs={{0,2},{2,0},{1,3},{3,1},{4,6},{6,4},{5,7},{7,5},{8,10},{10,8},{9,1... | collective-permute-start | bytes 393224 | tf_op jit(solution)/shard_map/ppermute | solution.py:502
  50.4 7.1 %collective-permute-start.10 = (bf16[128,512]{1,0:T(8,128)(2,1)S(1)}, bf16[128,512]{1,0:T(8,128)(2,1)S(1)}, u32[]{:S(2)}, u32[]{:S(2)}) collective-permute-start(bf16[128,512]{1,0:T(8,128)(2,1)S(1)} %recall.5.own_ref), channel_id=1, source_target_pairs={{0,2},{2,0},{1,3},{3,1},{4,6},{6,4},{5,7},{7,5},{8,10},{10,8},{9,1... | collective-permute-start | bytes 393224 | tf_op jit(solution)/shard_map/ppermute | solution.py:502
  51.2 9.2 %collective-permute-start.20 = (bf16[256,512]{1,0:T(8,128)(2,1)S(1)}, bf16[256,512]{1,0:T(8,128)(2,1)S(1)}, u32[]{:S(2)}, u32[]{:S(2)}) collective-permute-start(bf16[256,512]{1,0:T(8,128)(2,1)S(1)} %get-tuple-element.118), channel_id=1, source_target_pairs={{0,1},{1,0},{2,3},{3,2},{4,5},{5,4},{6,7},{7,6},{8,9},{9,8},{10,11... | collective-permute-start | bytes 786440 | tf_op jit(solution)/shard_map/ppermute | solution.py:507
  53.6 12.5 %collective-permute-start.18 = (bf16[256,512]{1,0:T(8,128)(2,1)S(1)}, bf16[256,512]{1,0:T(8,128)(2,1)S(1)}, u32[]{:S(2)}, u32[]{:S(2)}) collective-permute-start(bf16[256,512]{1,0:T(8,128)(2,1)S(1)} %get-tuple-element.114), channel_id=1, source_target_pairs={{0,1},{1,0},{2,3},{3,2},{4,5},{5,4},{6,7},{7,6},{8,9},{9,8},{10,11... | collective-permute-start | bytes 786440 | tf_op jit(solution)/shard_map/ppermute | solution.py:507
  54.9 16.8 %collective-permute-start.16 = (bf16[256,512]{1,0:T(8,128)(2,1)S(1)}, bf16[256,512]{1,0:T(8,128)(2,1)S(1)}, u32[]{:S(2)}, u32[]{:S(2)}) collective-permute-start(bf16[256,512]{1,0:T(8,128)(2,1)S(1)} %get-tuple-element.110), channel_id=1, source_target_pairs={{0,1},{1,0},{2,3},{3,2},{4,5},{5,4},{6,7},{7,6},{8,9},{9,8},{10,11... | collective-permute-start | bytes 786440 | tf_op jit(solution)/shard_map/ppermute | solution.py:507
  56.9 17.5 %collective-permute-start.14 = (bf16[128,512]{1,0:T(8,128)(2,1)S(1)}, bf16[128,512]{1,0:T(8,128)(2,1)S(1)}, u32[]{:S(2)}, u32[]{:S(2)}) collective-permute-start(bf16[128,512]{1,0:T(8,128)(2,1)S(1)} %get-tuple-element.106), channel_id=1, source_target_pairs={{0,1},{1,0},{2,3},{3,2},{4,5},{5,4},{6,7},{7,6},{8,9},{9,8},{10,11... | collective-permute-start | bytes 393224 | tf_op jit(solution)/shard_map/ppermute | solution.py:507
  58.0 18.9 %collective-permute-start.12 = (bf16[128,512]{1,0:T(8,128)(2,1)S(1)}, bf16[128,512]{1,0:T(8,128)(2,1)S(1)}, u32[]{:S(2)}, u32[]{:S(2)}) collective-permute-start(bf16[128,512]{1,0:T(8,128)(2,1)S(1)} %get-tuple-element.102), channel_id=1, source_target_pairs={{0,1},{1,0},{2,3},{3,2},{4,5},{5,4},{6,7},{7,6},{8,9},{9,8},{10,11... | collective-permute-start | bytes 393224 | tf_op jit(solution)/shard_map/ppermute | solution.py:507

commit v14 on v12

--- a/solution.py
+++ b/solution.py
@@ -10,7 +10,7 @@
 
 BLOCK = 512
 CHUNK = 256
-LAST = 128
+LAST = 64
 TAIL = 16
 EPSILON = 1e-06
 F32 = jnp.float32
@@ -415,7 +415,7 @@
 ):
     x = residual_signal[0]
     length = x.shape[0]
-    sizes = [CHUNK] * (length // CHUNK - 1) + [LAST] * (CHUNK // LAST)
+    sizes = [CHUNK] * (length // CHUNK - 1) + [CHUNK - LAST, LAST]
     firsts = [sum(sizes[:c]) for c in range(len(sizes))]
     chunks = len(sizes)
     shards = lax.axis_size("head")

time: 74.9 us -> 74.6 us (level)
  waiting for transfers between devices: 22.2 us -> 20.2 us
  Pallas kernels: 23.2 us -> 24.2 us
  local copies, waits for them, and re-layouts: 6.06 us -> 6.87 us
    ppermute x5, waiting for transfers between devices: 14.3 us -> 12.2 us  [per_device(): lax.ppermute(outs[k], 'head', [(d, (d + k) % shards) for d in range(shard...]
    ppermute x5, waiting for transfers between devices: 0.01 us -> 1.25 us  [per_device(): side = lax.ppermute(head_out, 'stream', swap_streams)]
    slice x2 -> x3, local copies, waits for them, and re-layouts: 2.14 us -> 2.95 us  [per_device(): pieces = [x[first:first + size] for first, size in zip(firsts, sizes)]]
  transfers between devices with their start and end apart: 20 -> 20, of which waited for: 11 -> 9; matrix products, arithmetic and copies ran while one was open for 5% -> 6% of each run, Pallas kernels for 30% -> 32%
where the time goes in v14:
time: 74.6 us; the launch traced here: 74.3 us
  Pallas kernels  24.2 us (32%)
  starting transfers between devices  22.7 us (30%)
  waiting for transfers between devices  20.2 us (27%)
  local copies, waits for them, and re-layouts  6.87 us (9%)
    ppermute x5, waiting for transfers between devices, per_device(): lax.ppermute(outs[k], 'head', [(d, (d + k) % shards) for d in range(shard...  12.2 us
    pallas_call x5, Pallas kernels, attention(): pl.pallas_call(functools.partial(attention_kernel, first, heads, dim), in...  7.86 us
    ppermute x5, starting transfers between devices, per_device(): lax.ppermute(pieces[c], 'head', [((d + k) % shards, d) for d in range(sha...  7.14 us
    ppermute x5, starting transfers between devices, per_device(): lax.ppermute(outs[k], 'head', [(d, (d + k) % shards) for d in range(shard...  5.91 us
    pallas_call x4, Pallas kernels, qkv(): pl.pallas_call(functools.partial(qkv_kernel, heads, dim, first), in_specs...  5.3 us
    ppermute x1, starting transfers between devices, per_device(): lax.ppermute(total, 'tm', [(d, d + quad_size * k) for d in range(blocks -...  4.69 us
    ppermute x3, waiting for transfers between devices, per_device(): lax.ppermute(sent, 'tm', [(d, d ^ k) for d in range(blocks)])  4.06 us
    unnamed x15, local copies, waits for them, and re-layouts  3.92 us
  transfers between devices with their start and end apart: 20, of which 9 were waited for; matrix products, arithmetic and copies ran while one was open for 6% of the time, Pallas kernels for 32%

profile of v14, /device:TPU:0, one launch (start us, length us, event | category | flops | bytes accessed | tf_op | source)
XLA Modules:
  0.0 74.3 jit_solution(3619117740707703939)
XLA Ops:
  0.0 1.2 %slice_bitcast_fusion = (bf16[256,512]{1,0:T(8,128)(2,1)S(1)}, bf16[256,512]{1,0:T(8,128)(2,1)S(1)}, bf16[256,512]{1,0:T(8,128)(2,1)S(1)}) fusion(bf16[1,1024,512]{2,1,0:T(8,128)(2,1)} %param.9), kind=kLoop, calls=%fused_computation | loop fusion | bytes 1572864 | tf_op jit(solution)/shard_map/slice | solution.py:439
  1.2 3.0 %collective-permute-start.1 = (bf16[256,512]{1,0:T(8,128)(2,1)S(1)}, bf16[256,512]{1,0:T(8,128)(2,1)S(1)}, u32[]{:S(2)}, u32[]{:S(2)}) collective-permute-start(bf16[256,512]{1,0:T(8,128)(2,1)S(1)} %get-tuple-element.116.refs_0_), channel_id=1, source_target_pairs={{1,0},{0,1},{3,2},{2,3},{5,4},{4,5},{7,6},{6,7},{9,8},{8,9},{11,10... | collective-permute-start | bytes 786440 | tf_op jit(solution)/shard_map/ppermute | solution.py:447
  4.3 1.9 %collective-permute-start.3 = (bf16[256,512]{1,0:T(8,128)(2,1)S(1)}, bf16[256,512]{1,0:T(8,128)(2,1)S(1)}, u32[]{:S(2)}, u32[]{:S(2)}) collective-permute-start(bf16[256,512]{1,0:T(8,128)(2,1)S(1)} %get-tuple-element.115.refs_1_), channel_id=1, source_target_pairs={{1,0},{0,1},{3,2},{2,3},{5,4},{4,5},{7,6},{6,7},{9,8},{8,9},{11,10... | collective-permute-start | bytes 786440 | tf_op jit(solution)/shard_map/ppermute | solution.py:447
  6.2 0.9 %slice_bitcast_fusion.3.refs_1_ = bf16[192,512]{1,0:T(8,128)(2,1)S(1)} fusion(bf16[1,1024,512]{2,1,0:T(8,128)(2,1)} %param.9), kind=kLoop, calls=%fused_computation.3 | loop fusion | bytes 393216 | tf_op jit(solution)/shard_map/slice | solution.py:439
  7.2 0.8 %slice_bitcast_fusion.4.refs_0_ = bf16[64,512]{1,0:T(8,128)(2,1)S(1)} fusion(bf16[1,1024,512]{2,1,0:T(8,128)(2,1)} %param.9), kind=kLoop, calls=%fused_computation.4 | loop fusion | bytes 131072 | tf_op jit(solution)/shard_map/slice | solution.py:439
  8.0 0.7 copy-done.1
  8.7 0.7 copy-done.5
  9.4 1.4 %prepare.1 = (f32[1024,8]{1,0:T(8,128)S(1)}, bf16[16,128]{1,0:T(8,128)(2,1)S(1)}, f32[256,8]{1,0:T(8,128)S(1)}, f32[256,8]{1,0:T(8,128)S(1)}, f32[256,8]{1,0:T(8...) custom-call(f32[4,1024]{1,0:T(4,128)S(1)} %bitcast.28, s32[2]{0:T(128)S(1)} %copy-done.5), custom_call_target="tpu_custom_call" | custom-call | flops 327680 | tf_op jit(solution)/shard_map/prepare/pallas_call | solution.py:83
  10.9 1.9 %collective-permute-start = (bf16[64,512]{1,0:T(8,128)(2,1)S(1)}, bf16[64,512]{1,0:T(8,128)(2,1)S(1)}, u32[]{:S(2)}, u32[]{:S(2)}) collective-permute-start(bf16[64,512]{1,0:T(8,128)(2,1)S(1)} %slice_bitcast_fusion.4.refs_0_), channel_id=1, source_target_pairs={{1,0},{0,1},{3,2},{2,3},{5,4},{4,5},{7,6},{6,7},{9,8},{8,9},{11,10... | collective-permute-start | bytes 196616 | tf_op jit(solution)/shard_map/ppermute | solution.py:447
  12.9 2.5 %copy.14 = bf16[128,8,4,384]{3,1,2,0:T(8,128)(2,1)S(1)} copy(bf16[128,8,4,384]{3,2,1,0:T(4,128)(2,1)} %bitcast.29) | data formatting | bytes 6291456
  15.6 1.4 %qkv.4 = (bf16[256,512]{1,0:T(8,128)(2,1)S(1)}, bf16[256,512]{1,0:T(8,128)(2,1)S(1)}, bf16[256,512]{1,0:T(8,128)(2,1)S(1)}, f32[4,128,128]{2,1,0:T(8,128)S(1)}) custom-call(f32[1,1024]{1,0:T(1,128)S(1)} %copy-done.2, bf16[1024,1536]{1,0:T(8,128)(2,1)S(1)} %bitcast.17, f32[1024,8]{1,0:T(8,128)S(1)} %get-tuple-element.63.fade_ref, ...), custom_call_target="tpu_custom_call" | custom-call | flops 1610612736 | tf_op jit(solution)/shard_map/qkv/pallas_call | solution.py:148
  16.9 1.1 %attention.5.local_ref = bf16[256,512]{1,0:T(8,128)(2,1)S(1)} custom-call(s32[2,2]{1,0:T(2,128)S(1)} %copy-done.3, f32[1,4]{1,0:T(1,128)S(1)} %copy-done.4, bf16[256,512]{1,0:T(8,128)(2,1)S(1)} %get-tuple-element.65.q_ref, bf16[256,512]{1,0:T(8,128)(2,1)S(1)} %get-tuple-element.66.refs_0_, ...), custom_call_target="tpu_custom_call" | custom-call | flops 268435456 | tf_op jit(solution)/shard_map/attention/pallas_call | solution.py:242
  18.1 1.4 %qkv.5 = (bf16[256,512]{1,0:T(8,128)(2,1)S(1)}, bf16[256,512]{1,0:T(8,128)(2,1)S(1)}, bf16[256,512]{1,0:T(8,128)(2,1)S(1)}, f32[4,128,128]{2,1,0:T(8,128)S(1)}) custom-call(f32[1,1024]{1,0:T(1,128)S(1)} %copy-done.2, bf16[1024,1536]{1,0:T(8,128)(2,1)S(1)} %bitcast.18, f32[1024,8]{1,0:T(8,128)S(1)} %get-tuple-element.63.fade_ref, ...), custom_call_target="tpu_custom_call" | custom-call | flops 1610612736 | tf_op jit(solution)/shard_map/qkv/pallas_call | solution.py:148
  19.4 1.4 %attention.6.local_ref = bf16[256,512]{1,0:T(8,128)(2,1)S(1)} custom-call(s32[2,2]{1,0:T(2,128)S(1)} %copy-done.3, f32[1,4]{1,0:T(1,128)S(1)} %copy-done.4, bf16[256,512]{1,0:T(8,128)(2,1)S(1)} %get-tuple-element.70.q_ref, bf16[256,512]{1,0:T(8,128)(2,1)S(1)} %get-tuple-element.66.refs_0_, bf16[256,512]{1,0:T(8,128)(2,1)S(1)} %get-tuple-element.71.refs_1_, ...), custom_call_target="tpu_custom_call" | custom-call | flops 536870912 | tf_op jit(solution)/shard_map/attention/pallas_call | solution.py:242
  20.9 1.7 %collective-permute-done.3.refs_2_ = bf16[256,512]{1,0:T(8,128)(2,1)S(1)} collective-permute-done((bf16[256,512]{1,0:T(8,128)(2,1)S(1)}, bf16[256,512]{1,0:T(8,128)(2,1)S(1)}, u32[]{:S(2)}, u32[]{:S(2)}) %collective-permute-start.3) | collective-permute-done | bytes 262176 | tf_op jit(solution)/shard_map/ppermute | solution.py:447
  22.6 1.4 %qkv.6 = (bf16[256,512]{1,0:T(8,128)(2,1)S(1)}, bf16[256,512]{1,0:T(8,128)(2,1)S(1)}, bf16[256,512]{1,0:T(8,128)(2,1)S(1)}, f32[4,128,128]{2,1,0:T(8,128)S(1)}) custom-call(f32[1,1024]{1,0:T(1,128)S(1)} %copy-done.2, bf16[1024,1536]{1,0:T(8,128)(2,1)S(1)} %bitcast.19, f32[1024,8]{1,0:T(8,128)S(1)} %get-tuple-element.63.fade_ref, ...), custom_call_target="tpu_custom_call" | custom-call | flops 1610612736 | tf_op jit(solution)/shard_map/qkv/pallas_call | solution.py:148
  23.9 1.7 %attention.7.local_ref = bf16[256,512]{1,0:T(8,128)(2,1)S(1)} custom-call(s32[2,2]{1,0:T(2,128)S(1)} %copy-done.3, f32[1,4]{1,0:T(1,128)S(1)} %copy-done.4, bf16[256,512]{1,0:T(8,128)(2,1)S(1)} %get-tuple-element.75.q_ref, bf16[256,512]{1,0:T(8,128)(2,1)S(1)} %get-tuple-element.66.refs_0_, bf16[256,512]{1,0:T(8,128)(2,1)S(1)} %get-tuple-element.71.refs_1_, ...), custom_call_target="tpu_custom_call" | custom-call | flops 805306368 | tf_op jit(solution)/shard_map/attention/pallas_call | solution.py:242
  25.6 1.1 %collective-permute-done.4.refs_2_ = bf16[192,512]{1,0:T(8,128)(2,1)S(1)} collective-permute-done((bf16[192,512]{1,0:T(8,128)(2,1)S(1)}, bf16[192,512]{1,0:T(8,128)(2,1)S(1)}, u32[]{:S(2)}, u32[]{:S(2)}) %collective-permute-start.4) | collective-permute-done | bytes 196640 | tf_op jit(solution)/shard_map/ppermute | solution.py:447
  26.7 1.2 %qkv.7 = (bf16[192,512]{1,0:T(8,128)(2,1)S(1)}, bf16[192,512]{1,0:T(8,128)(2,1)S(1)}, bf16[192,512]{1,0:T(8,128)(2,1)S(1)}, f32[4,128,128]{2,1,0:T(8,128)S(1)}) custom-call(f32[1,1024]{1,0:T(1,128)S(1)} %copy-done.2, bf16[1024,1536]{1,0:T(8,128)(2,1)S(1)} %bitcast.20, f32[1024,8]{1,0:T(8,128)S(1)} %get-tuple-element.63.fade_ref, ...), custom_call_target="tpu_custom_call" | custom-call | flops 1207959552 | tf_op jit(solution)/shard_map/qkv/pallas_call | solution.py:148
  27.9 0.8 %last_keys_values.1 = (bf16[64,512]{1,0:T(8,128)(2,1)S(1)}, bf16[64,512]{1,0:T(8,128)(2,1)S(1)}, bf16[528,128]{1,0:T(8,128)(2,1)S(1)}) custom-call(f32[1,1024]{1,0:T(1,128)S(1)} %copy-done.2, bf16[1024,1536]{1,0:T(8,128)(2,1)S(1)} %bitcast.21, f32[1024,8]{1,0:T(8,128)S(1)} %get-tuple-element.63.fade_ref, f32[4,128,128]{2,1,0:T(8,128)S(1)} %get-tuple-element.80.prev_ref, ...), custom_call_target="tpu_custom_call" | custom-call | flops 301989888 | tf_op jit(solution)/shard_map/last_keys_values/pallas_call | solution.py:179
  28.7 1.8 %collective-permute-start.5 = (bf16[528,128]{1,0:T(8,128)(2,1)S(1)}, bf16[528,128]{1,0:T(8,128)(2,1)S(1)}, u32[]{:S(2)}, u32[]{:S(2)}) collective-permute-start(bf16[528,128]{1,0:T(8,128)(2,1)S(1)} %get-tuple-element.86.refs_0_), channel_id=1, source_target_pairs={{0,4},{4,0},{8,12},{12,8},{16,20},{20,16},{24,28},{28,24},{1,5},{5... | collective-permute-start | bytes 405512 | tf_op jit(solution)/shard_map/ppermute | solution.py:472
  30.5 1.6 %collective-permute-start.6 = (bf16[528,128]{1,0:T(8,128)(2,1)S(1)}, bf16[528,128]{1,0:T(8,128)(2,1)S(1)}, u32[]{:S(2)}, u32[]{:S(2)}) collective-permute-start(bf16[528,128]{1,0:T(8,128)(2,1)S(1)} %get-tuple-element.86.refs_0_), channel_id=1, source_target_pairs={{0,8},{4,12},{8,0},{12,4},{16,24},{20,28},{24,16},{28,20},{1,9},{5... | collective-permute-start | bytes 405512 | tf_op jit(solution)/shard_map/ppermute | solution.py:472
  32.2 1.7 %attention.8.local_ref = bf16[192,512]{1,0:T(8,128)(2,1)S(1)} custom-call(s32[2,2]{1,0:T(2,128)S(1)} %copy-done.3, f32[1,4]{1,0:T(1,128)S(1)} %copy-done.4, bf16[192,512]{1,0:T(8,128)(2,1)S(1)} %get-tuple-element.83.q_ref, bf16[256,512]{1,0:T(8,128)(2,1)S(1)} %get-tuple-element.66.refs_0_, bf16[256,512]{1,0:T(8,128)(2,1)S(1)} %get-tuple-element.71.refs_1_, ...), custom_call_target="tpu_custom_call" | custom-call | flops 754974720 | tf_op jit(solution)/shard_map/attention/pallas_call | solution.py:242
  33.9 0.5 collective-permute-done.5.refs_1_
  34.5 1.2 %collective-permute-done.6.refs_2_ = bf16[528,128]{1,0:T(8,128)(2,1)S(1)} collective-permute-done((bf16[528,128]{1,0:T(8,128)(2,1)S(1)}, bf16[528,128]{1,0:T(8,128)(2,1)S(1)}, u32[]{:S(2)}, u32[]{:S(2)}) %collective-permute-start.6) | collective-permute-done | bytes 135200 | tf_op jit(solution)/shard_map/ppermute | solution.py:472
  35.6 2.3 %collective-permute-done.7.refs_3_ = bf16[528,128]{1,0:T(8,128)(2,1)S(1)} collective-permute-done((bf16[528,128]{1,0:T(8,128)(2,1)S(1)}, bf16[528,128]{1,0:T(8,128)(2,1)S(1)}, u32[]{:S(2)}, u32[]{:S(2)}) %collective-permute-start.7) | collective-permute-done | bytes 135200 | tf_op jit(solution)/shard_map/ppermute | solution.py:472
  38.3 4.7 %collective-permute-start.8 = (bf16[528,128]{1,0:T(8,128)(2,1)S(1)}, bf16[528,128]{1,0:T(8,128)(2,1)S(1)}, u32[]{:S(2)}, u32[]{:S(2)}) collective-permute-start(bf16[528,128]{1,0:T(8,128)(2,1)S(1)} %get-tuple-element.90), channel_id=1, source_target_pairs={{0,16},{4,20},{8,24},{12,28},{1,17},{5,21},{9,25},{13,29},{2,18},{... | collective-permute-start | bytes 405512 | tf_op jit(solution)/shard_map/ppermute | solution.py:484
  43.5 2.0 %attention.9.local_ref = bf16[64,512]{1,0:T(8,128)(2,1)S(1)} custom-call(s32[2,2]{1,0:T(2,128)S(1)} %copy-done.3, f32[1,4]{1,0:T(1,128)S(1)} %copy-done.4, bf16[64,512]{1,0:T(8,128)(2,1)S(1)} %last_queries.1.q_ref, bf16[256,512]{1,0:T(8,128)(2,1)S(1)} %get-tuple-element.66.refs_0_, bf16[256,512]{1,0:T(8,128)(2,1)S(1)} %get-tuple-element.71.refs_1_, ...), custom_call_target="tpu_custom_call" | custom-call | flops 268435456 | tf_op jit(solution)/shard_map/attention/pallas_call | solution.py:242
  46.1 0.6 collective-permute-start.16
  47.2 0.6 collective-permute-start.12
  47.7 0.7 project.9
  48.5 1.6 %collective-permute-start.19 = (bf16[256,512]{1,0:T(8,128)(2,1)S(1)}, bf16[256,512]{1,0:T(8,128)(2,1)S(1)}, u32[]{:S(2)}, u32[]{:S(2)}) collective-permute-start(bf16[256,512]{1,0:T(8,128)(2,1)S(1)} %get-tuple-element.114), channel_id=1, source_target_pairs={{0,1},{1,0},{2,3},{3,2},{4,5},{5,4},{6,7},{7,6},{8,9},{9,8},{10,11... | collective-permute-start | bytes 786440 | tf_op jit(solution)/shard_map/ppermute | solution.py:498
  50.1 0.7 project.8
  50.8 0.6 collective-permute-start.17
  51.4 0.7 project.7
  52.1 1.6 %collective-permute-start.15 = (bf16[256,512]{1,0:T(8,128)(2,1)S(1)}, bf16[256,512]{1,0:T(8,128)(2,1)S(1)}, u32[]{:S(2)}, u32[]{:S(2)}) collective-permute-start(bf16[256,512]{1,0:T(8,128)(2,1)S(1)} %get-tuple-element.106), channel_id=1, source_target_pairs={{0,1},{1,0},{2,3},{3,2},{4,5},{5,4},{6,7},{7,6},{8,9},{9,8},{10,11... | collective-permute-start | bytes 786440 | tf_op jit(solution)/shard_map/ppermute | solution.py:498
  53.7 0.6 project.6
  54.3 0.6 collective-permute-start.13
  55.1 1.2 %collective-permute-done.9.side_ref = bf16[64,512]{1,0:T(8,128)(2,1)S(1)} collective-permute-done((bf16[64,512]{1,0:T(8,128)(2,1)S(1)}, bf16[64,512]{1,0:T(8,128)(2,1)S(1)}, u32[]{:S(2)}, u32[]{:S(2)}) %collective-permute-start.9) | collective-permute-done | bytes 65568 | tf_op jit(solution)/shard_map/ppermute | solution.py:493
  56.9 1.6 %collective-permute-start.11 = (bf16[64,512]{1,0:T(8,128)(2,1)S(1)}, bf16[64,512]{1,0:T(8,128)(2,1)S(1)}, u32[]{:S(2)}, u32[]{:S(2)}) collective-permute-start(bf16[64,512]{1,0:T(8,128)(2,1)S(1)} %get-tuple-element.98), channel_id=1, source_target_pairs={{0,1},{1,0},{2,3},{3,2},{4,5},{5,4},{6,7},{7,6},{8,9},{9,8},{10,11... | collective-permute-start | bytes 196616 | tf_op jit(solution)/shard_map/ppermute | solution.py:498
  58.5 0.8 %finish.5.refs_2_ = bf16[1024,512]{1,0:T(8,128)(2,1)} custom-call(bf16[256,512]{1,0:T(8,128)(2,1)S(1)} %get-tuple-element.113.refs_0_, bf16[256,512]{1,0:T(8,128)(2,1)S(1)} %collective-permute-done.19.refs_1_), custom_call_target="tpu_custom_call" | custom-call | flops 262144 | bytes 786432 | tf_op jit(solution)/shard_map/finish/pallas_call | solution.py:392
  59.2 4.1 %collective-permute-done.17.refs_1_ = bf16[256,512]{1,0:T(8,128)(2,1)S(1)} collective-permute-done((bf16[256,512]{1,0:T(8,128)(2,1)S(1)}, bf16[256,512]{1,0:T(8,128)(2,1)S(1)}, u32[]{:S(2)}, u32[]{:S(2)}) %collective-permute-start.17) | collective-permute-done | bytes 262176 | tf_op jit(solution)/shard_map/ppermute | solution.py:498
  63.3 0.8 %finish.6.refs_2_ = bf16[1024,512]{1,0:T(8,128)(2,1)} custom-call(bf16[256,512]{1,0:T(8,128)(2,1)S(1)} %get-tuple-element.109.refs_0_, bf16[256,512]{1,0:T(8,128)(2,1)S(1)} %collective-permute-done.17.refs_1_, bf16[1024,512]{1,0:T(8,128)(2,1)} %finish.5.refs_2_), custom_call_target="tpu_custom_call", output_to_operand_aliasing={{}: (2, {})} | custom-call | flops 262144 | bytes 786432 | tf_op jit(solution)/shard_map/finish/pallas_call | solution.py:392
  64.1 4.9 %collective-permute-done.15.refs_1_ = bf16[256,512]{1,0:T(8,128)(2,1)S(1)} collective-permute-done((bf16[256,512]{1,0:T(8,128)(2,1)S(1)}, bf16[256,512]{1,0:T(8,128)(2,1)S(1)}, u32[]{:S(2)}, u32[]{:S(2)}) %collective-permute-start.15) | collective-permute-done | bytes 262176 | tf_op jit(solution)/shard_map/ppermute | solution.py:498
  68.9 0.8 %finish.7.refs_2_ = bf16[1024,512]{1,0:T(8,128)(2,1)} custom-call(bf16[256,512]{1,0:T(8,128)(2,1)S(1)} %get-tuple-element.105.refs_0_, bf16[256,512]{1,0:T(8,128)(2,1)S(1)} %collective-permute-done.15.refs_1_, bf16[1024,512]{1,0:T(8,128)(2,1)} %finish.6.refs_2_), custom_call_target="tpu_custom_call", output_to_operand_aliasing={{}: (2, {})} | custom-call | flops 262144 | bytes 786432 | tf_op jit(solution)/shard_map/finish/pallas_call | solution.py:392
  69.7 3.2 %collective-permute-done.13.refs_1_ = bf16[192,512]{1,0:T(8,128)(2,1)S(1)} collective-permute-done((bf16[192,512]{1,0:T(8,128)(2,1)S(1)}, bf16[192,512]{1,0:T(8,128)(2,1)S(1)}, u32[]{:S(2)}, u32[]{:S(2)}) %collective-permute-start.13) | collective-permute-done | bytes 196640 | tf_op jit(solution)/shard_map/ppermute | solution.py:498
  72.9 0.7 finish.8.refs_2_
  73.7 0.6 finish.9
  (39 shorter events, 3.1 us)
Async XLA Ops:
  1.2 14.3 %collective-permute-start.1 = (bf16[256,512]{1,0:T(8,128)(2,1)S(1)}, bf16[256,512]{1,0:T(8,128)(2,1)S(1)}, u32[]{:S(2)}, u32[]{:S(2)}) collective-permute-start(bf16[256,512]{1,0:T(8,128)(2,1)S(1)} %get-tuple-element.116.refs_0_), channel_id=1, source_target_pairs={{1,0},{0,1},{3,2},{2,3},{5,4},{4,5},{7,6},{6,7},{9,8},{8,9},{11,10... | collective-permute-start | bytes 786440 | tf_op jit(solution)/shard_map/ppermute | solution.py:447
  4.2 13.9 %collective-permute-start.2 = (bf16[256,512]{1,0:T(8,128)(2,1)S(1)}, bf16[256,512]{1,0:T(8,128)(2,1)S(1)}, u32[]{:S(2)}, u32[]{:S(2)}) collective-permute-start(bf16[256,512]{1,0:T(8,128)(2,1)S(1)} %get-tuple-element.117.refs_1_), channel_id=1, source_target_pairs={{1,0},{0,1},{3,2},{2,3},{5,4},{4,5},{7,6},{6,7},{9,8},{8,9},{11,10... | collective-permute-start | bytes 786440 | tf_op jit(solution)/shard_map/ppermute | solution.py:447
  4.3 18.3 %collective-permute-start.3 = (bf16[256,512]{1,0:T(8,128)(2,1)S(1)}, bf16[256,512]{1,0:T(8,128)(2,1)S(1)}, u32[]{:S(2)}, u32[]{:S(2)}) collective-permute-start(bf16[256,512]{1,0:T(8,128)(2,1)S(1)} %get-tuple-element.115.refs_1_), channel_id=1, source_target_pairs={{1,0},{0,1},{3,2},{2,3},{5,4},{4,5},{7,6},{6,7},{9,8},{8,9},{11,10... | collective-permute-start | bytes 786440 | tf_op jit(solution)/shard_map/ppermute | solution.py:447
  8.0 0.7 copy-start.1
  8.7 0.7 copy-start.5
  10.8 15.8 %collective-permute-start.4 = (bf16[192,512]{1,0:T(8,128)(2,1)S(1)}, bf16[192,512]{1,0:T(8,128)(2,1)S(1)}, u32[]{:S(2)}, u32[]{:S(2)}) collective-permute-start(bf16[192,512]{1,0:T(8,128)(2,1)S(1)} %slice_bitcast_fusion.3.refs_1_), channel_id=1, source_target_pairs={{1,0},{0,1},{3,2},{2,3},{5,4},{4,5},{7,6},{6,7},{9,8},{8,9},{11,10... | collective-permute-start | bytes 589832 | tf_op jit(solution)/shard_map/ppermute | solution.py:447
  10.9 16.9 %collective-permute-start = (bf16[64,512]{1,0:T(8,128)(2,1)S(1)}, bf16[64,512]{1,0:T(8,128)(2,1)S(1)}, u32[]{:S(2)}, u32[]{:S(2)}) collective-permute-start(bf16[64,512]{1,0:T(8,128)(2,1)S(1)} %slice_bitcast_fusion.4.refs_0_), channel_id=1, source_target_pairs={{1,0},{0,1},{3,2},{2,3},{5,4},{4,5},{7,6},{6,7},{9,8},{8,9},{11,10... | collective-permute-start | bytes 196616 | tf_op jit(solution)/shard_map/ppermute | solution.py:447
  12.9 2.6 %copy-start.6 = (bf16[1,4,128,1024]{3,2,1,0:T(8,128)(2,1)S(1)}, bf16[1,4,128,1024]{3,2,1,0:T(8,128)(2,1)}, u32[]{:S(2)}) copy-start(bf16[1,4,128,1024]{3,2,1,0:T(8,128)(2,1)} %param.17) | copy-start | bytes 3145732
  12.9 2.7 %copy-start.2 = (f32[1,1024]{1,0:T(1,128)S(1)}, f32[1,1024]{1,0:T(1,128)}, u32[]{:S(2)}) copy-start(f32[1,1024]{1,0:T(1,128)} %gain_ref.11) | copy-start | bytes 12292
  15.4 1.5 %copy-start.3 = (s32[2,2]{1,0:T(2,128)S(1)}, s32[2,2]{1,0:T(2,128)}, u32[]{:S(2)}) copy-start(s32[2,2]{1,0:T(2,128)} %keep_ref.9) | copy-start | bytes 52
  15.4 1.5 %copy-start.4 = (f32[1,4]{1,0:T(1,128)S(1)}, f32[1,4]{1,0:T(1,128)}, u32[]{:S(2)}) copy-start(f32[1,4]{1,0:T(1,128)} %scale_ref.9) | copy-start | bytes 52
  15.5 32.3 %collective-permute-start.10 = (bf16[512,1024]{1,0:T(8,128)(2,1)S(1)}, bf16[512,1024]{1,0:T(8,128)(2,1)S(1)}, u32[]{:S(2)}, u32[]{:S(2)}) collective-permute-start(bf16[512,1024]{1,0:T(8,128)(2,1)S(1)} %bitcast.30), channel_id=1, source_target_pairs={{0,2},{2,0},{1,3},{3,1},{4,6},{6,4},{5,7},{7,5},{8,10},{10,8},{9,1... | collective-permute-start | bytes 3145736 | tf_op jit(solution)/shard_map/ppermute | solution.py:429
  28.7 5.8 %collective-permute-start.5 = (bf16[528,128]{1,0:T(8,128)(2,1)S(1)}, bf16[528,128]{1,0:T(8,128)(2,1)S(1)}, u32[]{:S(2)}, u32[]{:S(2)}) collective-permute-start(bf16[528,128]{1,0:T(8,128)(2,1)S(1)} %get-tuple-element.86.refs_0_), channel_id=1, source_target_pairs={{0,4},{4,0},{8,12},{12,8},{16,20},{20,16},{24,28},{28,24},{1,5},{5... | collective-permute-start | bytes 405512 | tf_op jit(solution)/shard_map/ppermute | solution.py:472
  30.5 5.1 %collective-permute-start.6 = (bf16[528,128]{1,0:T(8,128)(2,1)S(1)}, bf16[528,128]{1,0:T(8,128)(2,1)S(1)}, u32[]{:S(2)}, u32[]{:S(2)}) collective-permute-start(bf16[528,128]{1,0:T(8,128)(2,1)S(1)} %get-tuple-element.86.refs_0_), channel_id=1, source_target_pairs={{0,8},{4,12},{8,0},{12,4},{16,24},{20,28},{24,16},{28,20},{1,9},{5... | collective-permute-start | bytes 405512 | tf_op jit(solution)/shard_map/ppermute | solution.py:472
  32.1 5.9 %collective-permute-start.7 = (bf16[528,128]{1,0:T(8,128)(2,1)S(1)}, bf16[528,128]{1,0:T(8,128)(2,1)S(1)}, u32[]{:S(2)}, u32[]{:S(2)}) collective-permute-start(bf16[528,128]{1,0:T(8,128)(2,1)S(1)} %get-tuple-element.86.refs_0_), channel_id=1, source_target_pairs={{0,12},{4,8},{8,4},{12,0},{16,28},{20,24},{24,20},{28,16},{1,13},{... | collective-permute-start | bytes 405512 | tf_op jit(solution)/shard_map/ppermute | solution.py:472
  38.3 7.2 %collective-permute-start.8 = (bf16[528,128]{1,0:T(8,128)(2,1)S(1)}, bf16[528,128]{1,0:T(8,128)(2,1)S(1)}, u32[]{:S(2)}, u32[]{:S(2)}) collective-permute-start(bf16[528,128]{1,0:T(8,128)(2,1)S(1)} %get-tuple-element.90), channel_id=1, source_target_pairs={{0,16},{4,20},{8,24},{12,28},{1,17},{5,21},{9,25},{13,29},{2,18},{... | collective-permute-start | bytes 405512 | tf_op jit(solution)/shard_map/ppermute | solution.py:484
  43.4 4.3 %copy-start = (bf16[1,4,128,1024]{3,2,1,0:T(8,128)(2,1)S(1)}, bf16[1,4,128,1024]{3,2,1,0:T(8,128)(2,1)}, u32[]{:S(2)}) copy-start(bf16[1,4,128,1024]{3,2,1,0:T(8,128)(2,1)} %param.16) | copy-start | bytes 3145732
  45.8 2.0 %collective-permute-start.18 = (bf16[256,512]{1,0:T(8,128)(2,1)S(1)}, bf16[256,512]{1,0:T(8,128)(2,1)S(1)}, u32[]{:S(2)}, u32[]{:S(2)}) collective-permute-start(bf16[256,512]{1,0:T(8,128)(2,1)S(1)} %recall.9.own_ref), channel_id=1, source_target_pairs={{0,2},{2,0},{1,3},{3,1},{4,6},{6,4},{5,7},{7,5},{8,10},{10,8},{9,1... | collective-permute-start | bytes 786440 | tf_op jit(solution)/shard_map/ppermute | solution.py:493
  46.1 4.0 %collective-permute-start.16 = (bf16[256,512]{1,0:T(8,128)(2,1)S(1)}, bf16[256,512]{1,0:T(8,128)(2,1)S(1)}, u32[]{:S(2)}, u32[]{:S(2)}) collective-permute-start(bf16[256,512]{1,0:T(8,128)(2,1)S(1)} %recall.8.own_ref), channel_id=1, source_target_pairs={{0,2},{2,0},{1,3},{3,1},{4,6},{6,4},{5,7},{7,5},{8,10},{10,8},{9,1... | collective-permute-start | bytes 786440 | tf_op jit(solution)/shard_map/ppermute | solution.py:493
  46.9 4.5 %collective-permute-start.14 = (bf16[256,512]{1,0:T(8,128)(2,1)S(1)}, bf16[256,512]{1,0:T(8,128)(2,1)S(1)}, u32[]{:S(2)}, u32[]{:S(2)}) collective-permute-start(bf16[256,512]{1,0:T(8,128)(2,1)S(1)} %recall.7.own_ref), channel_id=1, source_target_pairs={{0,2},{2,0},{1,3},{3,1},{4,6},{6,4},{5,7},{7,5},{8,10},{10,8},{9,1... | collective-permute-start | bytes 786440 | tf_op jit(solution)/shard_map/ppermute | solution.py:493
  47.2 6.5 %collective-permute-start.12 = (bf16[192,512]{1,0:T(8,128)(2,1)S(1)}, bf16[192,512]{1,0:T(8,128)(2,1)S(1)}, u32[]{:S(2)}, u32[]{:S(2)}) collective-permute-start(bf16[192,512]{1,0:T(8,128)(2,1)S(1)} %recall.6.own_ref), channel_id=1, source_target_pairs={{0,2},{2,0},{1,3},{3,1},{4,6},{6,4},{5,7},{7,5},{8,10},{10,8},{9,1... | collective-permute-start | bytes 589832 | tf_op jit(solution)/shard_map/ppermute | solution.py:493
  48.5 10.0 %collective-permute-start.19 = (bf16[256,512]{1,0:T(8,128)(2,1)S(1)}, bf16[256,512]{1,0:T(8,128)(2,1)S(1)}, u32[]{:S(2)}, u32[]{:S(2)}) collective-permute-start(bf16[256,512]{1,0:T(8,128)(2,1)S(1)} %get-tuple-element.114), channel_id=1, source_target_pairs={{0,1},{1,0},{2,3},{3,2},{4,5},{5,4},{6,7},{7,6},{8,9},{9,8},{10,11... | collective-permute-start | bytes 786440 | tf_op jit(solution)/shard_map/ppermute | solution.py:498
  50.8 12.5 %collective-permute-start.17 = (bf16[256,512]{1,0:T(8,128)(2,1)S(1)}, bf16[256,512]{1,0:T(8,128)(2,1)S(1)}, u32[]{:S(2)}, u32[]{:S(2)}) collective-permute-start(bf16[256,512]{1,0:T(8,128)(2,1)S(1)} %get-tuple-element.110), channel_id=1, source_target_pairs={{0,1},{1,0},{2,3},{3,2},{4,5},{5,4},{6,7},{7,6},{8,9},{9,8},{10,11... | collective-permute-start | bytes 786440 | tf_op jit(solution)/shard_map/ppermute | solution.py:498
  52.1 16.8 %collective-permute-start.15 = (bf16[256,512]{1,0:T(8,128)(2,1)S(1)}, bf16[256,512]{1,0:T(8,128)(2,1)S(1)}, u32[]{:S(2)}, u32[]{:S(2)}) collective-permute-start(bf16[256,512]{1,0:T(8,128)(2,1)S(1)} %get-tuple-element.106), channel_id=1, source_target_pairs={{0,1},{1,0},{2,3},{3,2},{4,5},{5,4},{6,7},{7,6},{8,9},{9,8},{10,11... | collective-permute-start | bytes 786440 | tf_op jit(solution)/shard_map/ppermute | solution.py:498
  54.3 18.6 %collective-permute-start.13 = (bf16[192,512]{1,0:T(8,128)(2,1)S(1)}, bf16[192,512]{1,0:T(8,128)(2,1)S(1)}, u32[]{:S(2)}, u32[]{:S(2)}) collective-permute-start(bf16[192,512]{1,0:T(8,128)(2,1)S(1)} %get-tuple-element.102), channel_id=1, source_target_pairs={{0,1},{1,0},{2,3},{3,2},{4,5},{5,4},{6,7},{7,6},{8,9},{9,8},{10,11... | collective-permute-start | bytes 589832 | tf_op jit(solution)/shard_map/ppermute | solution.py:498
  55.0 1.3 %collective-permute-start.9 = (bf16[64,512]{1,0:T(8,128)(2,1)S(1)}, bf16[64,512]{1,0:T(8,128)(2,1)S(1)}, u32[]{:S(2)}, u32[]{:S(2)}) collective-permute-start(bf16[64,512]{1,0:T(8,128)(2,1)S(1)} %recall.5.own_ref), channel_id=1, source_target_pairs={{0,2},{2,0},{1,3},{3,1},{4,6},{6,4},{5,7},{7,5},{8,10},{10,8},{9,1... | collective-permute-start | bytes 196616 | tf_op jit(solution)/shard_map/ppermute | solution.py:493
  56.9 16.8 %collective-permute-start.11 = (bf16[64,512]{1,0:T(8,128)(2,1)S(1)}, bf16[64,512]{1,0:T(8,128)(2,1)S(1)}, u32[]{:S(2)}, u32[]{:S(2)}) collective-permute-start(bf16[64,512]{1,0:T(8,128)(2,1)S(1)} %get-tuple-element.98), channel_id=1, source_target_pairs={{0,1},{1,0},{2,3},{3,2},{4,5},{5,4},{6,7},{7,6},{8,9},{9,8},{10,11... | collective-permute-start | bytes 196616 | tf_op jit(solution)/shard_map/ppermute | solution.py:498

commit v15 on v14

--- a/solution.py
+++ b/solution.py
@@ -156,13 +156,45 @@
     )(gain, w, fade, *before, *xs)
 
 
-def last_kernel(heads, dim, first, gain_ref, w_ref, fade_ref, prev_ref, tail_ref, *refs):
+def own_part_kernel(heads, dim, gain_ref, w_ref, x_ref, out_ref):
+    width = x_ref.shape[1]
+    rows = pl.ds(pl.multiple_of(lax.axis_index("head") * width, width), width)
+    part = (x_ref[...].astype(F32) * gain_ref[:, rows]).astype(BF16)
+    for h in range(heads):
+        cols = slice((3 * h + 1) * dim, (3 * h + 3) * dim)
+        out_ref[:, 2 * h * dim : 2 * (h + 1) * dim] = dot(part, w_ref[rows, cols])
+
+
+def own_part(gain, w, x, heads, dim):
+    return pl.pallas_call(
+        functools.partial(own_part_kernel, heads, dim),
+        in_specs=[VMEM] * 3,
+        out_specs=VMEM,
+        out_shape=struct((x.shape[0], 2 * heads * dim), F32),
+        compiler_params=params(),
+        cost_estimate=cost(x.shape[0] * w.size, 0),
+        name="own_part",
+    )(gain, w, x)
+
+
+def last_kernel(heads, dim, first, acc_ref, gain_ref, w_ref, fade_ref, prev_ref, tail_ref, *refs):
     x_refs, (k_ref, v_ref, send_ref, sum_ref) = refs[:-4], refs[-4:]
     sum_ref[...] = prev_ref[...]
-    parts = normed_parts(gain_ref, x_refs)
-    pairs = [
-        projected(parts, w_ref, slice((3 * h + 1) * dim, (3 * h + 3) * dim)) for h in range(heads)
-    ]
+    shards, width = len(x_refs), x_refs[0].shape[1]
+    xs = [x[...].astype(F32) for x in x_refs]
+    squares = sum(jnp.sum(x * x, axis=-1, keepdims=True) for x in xs)
+    scale = lax.rsqrt(squares * (1.0 / (width * shards)) + EPSILON)
+    parts = []
+    for k in range(1, shards):
+        owner = lax.rem(lax.axis_index("head") + k, shards)
+        span = pl.ds(pl.multiple_of(owner * width, width), width)
+        parts.append(((xs[k] * gain_ref[:, span]).astype(BF16), span))
+    pairs = []
+    for h in range(heads):
+        total = acc_ref[:, 2 * h * dim : 2 * (h + 1) * dim]
+        if parts:
+            total += projected(parts, w_ref, slice((3 * h + 1) * dim, (3 * h + 3) * dim))
+        pairs.append(total * scale)
     for h in range(heads):
         cols = slice(h * dim, (h + 1) * dim)
         key = unit(pairs[h][:, :dim]).astype(BF16)
@@ -174,18 +206,18 @@
     send_ref[heads * dim :, :] = tail_ref[...]
 
 
-def last_keys_values(gain, w, fade, prev, tail, xs, heads, dim, first):
+def last_keys_values(acc, gain, w, fade, prev, tail, xs, heads, dim, first):
     rows = xs[0].shape[0]
     return pl.pallas_call(
         functools.partial(last_kernel, heads, dim, first),
-        in_specs=[VMEM] * (5 + len(xs)),
+        in_specs=[VMEM] * (6 + len(xs)),
         out_specs=[VMEM] * 3,
         out_shape=[struct((rows, heads * dim))] * 2 + [struct((heads * dim + TAIL, dim))],
         scratch_shapes=[pltpu.VMEM((heads, dim, dim), F32)],
         compiler_params=params(),
         cost_estimate=cost(3 * rows * w.size, 0),
         name="last_keys_values",
-    )(gain, w, fade, prev, tail, *xs)
+    )(acc, gain, w, fade, prev, tail, *xs)
 
 
 def queries_kernel(heads, dim, gain_ref, w_ref, *refs):
@@ -461,8 +493,10 @@
             local = attention(first, tile_retain_grid, score_scaler, q, ks, vs, heads, dim)
             summary, local = tied(summary, local)
             locals_.append(local)
+    acc = own_part(gain, w, received[-1][0], heads, dim)
+    summary, acc = tied(summary, acc)
     k, v, sent = last_keys_values(
-        gain, w, fade, summary, tail, received[-1], heads, dim, firsts[-1]
+        acc, gain, w, fade, summary, tail, received[-1], heads, dim, firsts[-1]
     )
     ks.append(k)
     vs.append(v)

time: 74.6 us -> 74.4 us (level)
  waiting for transfers between devices: 20.2 us -> 19.2 us
  local copies, waits for them, and re-layouts: 6.87 us -> 7.66 us
    ppermute x5, waiting for transfers between devices: 2.72 us -> 1.7 us  [per_device(): lax.ppermute(pieces[c], 'head', [((d + k) % shards, d) for d in range(sha...]
    unnamed x15, local copies, waits for them, and re-layouts: 3.92 us -> 4.71 us
where the time goes in v15:
time: 74.4 us; the launch traced here: 74.1 us
  Pallas kernels  24.3 us (33%)
  starting transfers between devices  22.6 us (30%)
  waiting for transfers between devices  19.2 us (26%)
  local copies, waits for them, and re-layouts  7.66 us (10%)
    ppermute x5, waiting for transfers between devices, per_device(): lax.ppermute(outs[k], 'head', [(d, (d + k) % shards) for d in range(shard...  12.2 us
    pallas_call x5, Pallas kernels, attention(): pl.pallas_call(functools.partial(attention_kernel, first, heads, dim), in...  7.87 us
    ppermute x5, starting transfers between devices, per_device(): lax.ppermute(pieces[c], 'head', [((d + k) % shards, d) for d in range(sha...  7.14 us
    ppermute x5, starting transfers between devices, per_device(): lax.ppermute(outs[k], 'head', [(d, (d + k) % shards) for d in range(shard...  5.91 us
    pallas_call x4, Pallas kernels, qkv(): pl.pallas_call(functools.partial(qkv_kernel, heads, dim, first), in_specs...  5.3 us
    unnamed x15, local copies, waits for them, and re-layouts  4.71 us
    ppermute x1, starting transfers between devices, per_device(): lax.ppermute(total, 'tm', [(d, d + quad_size * k) for d in range(blocks -...  4.68 us
    ppermute x3, waiting for transfers between devices, per_device(): lax.ppermute(sent, 'tm', [(d, d ^ k) for d in range(blocks)])  4.05 us
  transfers between devices with their start and end apart: 20, of which 9 were waited for; matrix products, arithmetic and copies ran while one was open for 6% of the time, Pallas kernels for 32%

profile of v15, /device:TPU:0, one launch (start us, length us, event | category | flops | bytes accessed | tf_op | source)
XLA Modules:
  0.0 74.1 jit_solution(17422552281245985355)
XLA Ops:
  0.0 1.2 %slice_bitcast_fusion = (bf16[256,512]{1,0:T(8,128)(2,1)S(1)}, bf16[256,512]{1,0:T(8,128)(2,1)S(1)}, bf16[256,512]{1,0:T(8,128)(2,1)S(1)}) fusion(bf16[1,1024,512]{2,1,0:T(8,128)(2,1)} %param.9), kind=kLoop, calls=%fused_computation | loop fusion | bytes 1572864 | tf_op jit(solution)/shard_map/slice | solution.py:471
  1.2 3.0 %collective-permute-start.1 = (bf16[256,512]{1,0:T(8,128)(2,1)S(1)}, bf16[256,512]{1,0:T(8,128)(2,1)S(1)}, u32[]{:S(2)}, u32[]{:S(2)}) collective-permute-start(bf16[256,512]{1,0:T(8,128)(2,1)S(1)} %get-tuple-element.120.refs_0_), channel_id=1, source_target_pairs={{1,0},{0,1},{3,2},{2,3},{5,4},{4,5},{7,6},{6,7},{9,8},{8,9},{11,10... | collective-permute-start | bytes 786440 | tf_op jit(solution)/shard_map/ppermute | solution.py:479
  4.3 1.9 %collective-permute-start.3 = (bf16[256,512]{1,0:T(8,128)(2,1)S(1)}, bf16[256,512]{1,0:T(8,128)(2,1)S(1)}, u32[]{:S(2)}, u32[]{:S(2)}) collective-permute-start(bf16[256,512]{1,0:T(8,128)(2,1)S(1)} %get-tuple-element.119.refs_1_), channel_id=1, source_target_pairs={{1,0},{0,1},{3,2},{2,3},{5,4},{4,5},{7,6},{6,7},{9,8},{8,9},{11,10... | collective-permute-start | bytes 786440 | tf_op jit(solution)/shard_map/ppermute | solution.py:479
  6.2 0.9 %slice_bitcast_fusion.3.refs_1_ = bf16[192,512]{1,0:T(8,128)(2,1)S(1)} fusion(bf16[1,1024,512]{2,1,0:T(8,128)(2,1)} %param.9), kind=kLoop, calls=%fused_computation.3 | loop fusion | bytes 393216 | tf_op jit(solution)/shard_map/slice | solution.py:471
  7.2 0.8 %slice_bitcast_fusion.4.refs_0_.x_ref = bf16[64,512]{1,0:T(8,128)(2,1)S(1)} fusion(bf16[1,1024,512]{2,1,0:T(8,128)(2,1)} %param.9), kind=kLoop, calls=%fused_computation.4 | loop fusion | bytes 131072 | tf_op jit(solution)/shard_map/slice | solution.py:471
  8.0 0.7 copy-done.2
  8.7 0.7 copy-done.5
  9.4 1.4 %prepare.1 = (f32[1024,8]{1,0:T(8,128)S(1)}, bf16[16,128]{1,0:T(8,128)(2,1)S(1)}, f32[256,8]{1,0:T(8,128)S(1)}, f32[256,8]{1,0:T(8,128)S(1)}, f32[256,8]{1,0:T(8...) custom-call(f32[4,1024]{1,0:T(4,128)S(1)} %bitcast.29, s32[2]{0:T(128)S(1)} %copy-done.5), custom_call_target="tpu_custom_call" | custom-call | flops 327680 | tf_op jit(solution)/shard_map/prepare/pallas_call | solution.py:83
  10.9 1.9 %collective-permute-start = (bf16[64,512]{1,0:T(8,128)(2,1)S(1)}, bf16[64,512]{1,0:T(8,128)(2,1)S(1)}, u32[]{:S(2)}, u32[]{:S(2)}) collective-permute-start(bf16[64,512]{1,0:T(8,128)(2,1)S(1)} %slice_bitcast_fusion.4.refs_0_.x_ref), channel_id=1, source_target_pairs={{1,0},{0,1},{3,2},{2,3},{5,4},{4,5},{7,6},{6,7},{9,8},{8,9},{11,10... | collective-permute-start | bytes 196616 | tf_op jit(solution)/shard_map/ppermute | solution.py:479
  12.9 2.4 %copy.14 = bf16[128,8,4,384]{3,1,2,0:T(8,128)(2,1)S(1)} copy(bf16[128,8,4,384]{3,2,1,0:T(4,128)(2,1)} %bitcast.30) | data formatting | bytes 6291456
  15.7 0.9 %copy-done.6 = bf16[1,4,128,1024]{3,2,1,0:T(8,128)(2,1)S(1)} copy-done((bf16[1,4,128,1024]{3,2,1,0:T(8,128)(2,1)S(1)}, bf16[1,4,128,1024]{3,2,1,0:T(8,128)(2,1)}, u32[]{:S(2)}) %copy-start.6) | copy-done | bytes 1048600
  16.6 1.4 %qkv.4 = (bf16[256,512]{1,0:T(8,128)(2,1)S(1)}, bf16[256,512]{1,0:T(8,128)(2,1)S(1)}, bf16[256,512]{1,0:T(8,128)(2,1)S(1)}, f32[4,128,128]{2,1,0:T(8,128)S(1)}) custom-call(f32[1,1024]{1,0:T(1,128)S(1)} %copy-done.1, bf16[1024,1536]{1,0:T(8,128)(2,1)S(1)} %bitcast.18, f32[1024,8]{1,0:T(8,128)S(1)} %get-tuple-element.65.fade_ref, ...), custom_call_target="tpu_custom_call" | custom-call | flops 1610612736 | tf_op jit(solution)/shard_map/qkv/pallas_call | solution.py:148
  18.0 1.1 %attention.5.local_ref = bf16[256,512]{1,0:T(8,128)(2,1)S(1)} custom-call(s32[2,2]{1,0:T(2,128)S(1)} %copy-done.3, f32[1,4]{1,0:T(1,128)S(1)} %copy-done.4, bf16[256,512]{1,0:T(8,128)(2,1)S(1)} %get-tuple-element.67.q_ref, bf16[256,512]{1,0:T(8,128)(2,1)S(1)} %get-tuple-element.68.refs_0_, ...), custom_call_target="tpu_custom_call" | custom-call | flops 268435456 | tf_op jit(solution)/shard_map/attention/pallas_call | solution.py:274
  19.1 1.4 %qkv.5 = (bf16[256,512]{1,0:T(8,128)(2,1)S(1)}, bf16[256,512]{1,0:T(8,128)(2,1)S(1)}, bf16[256,512]{1,0:T(8,128)(2,1)S(1)}, f32[4,128,128]{2,1,0:T(8,128)S(1)}) custom-call(f32[1,1024]{1,0:T(1,128)S(1)} %copy-done.1, bf16[1024,1536]{1,0:T(8,128)(2,1)S(1)} %bitcast.19, f32[1024,8]{1,0:T(8,128)S(1)} %get-tuple-element.65.fade_ref, ...), custom_call_target="tpu_custom_call" | custom-call | flops 1610612736 | tf_op jit(solution)/shard_map/qkv/pallas_call | solution.py:148
  20.5 1.5 %attention.6.local_ref = bf16[256,512]{1,0:T(8,128)(2,1)S(1)} custom-call(s32[2,2]{1,0:T(2,128)S(1)} %copy-done.3, f32[1,4]{1,0:T(1,128)S(1)} %copy-done.4, bf16[256,512]{1,0:T(8,128)(2,1)S(1)} %get-tuple-element.72.q_ref, bf16[256,512]{1,0:T(8,128)(2,1)S(1)} %get-tuple-element.68.refs_0_, bf16[256,512]{1,0:T(8,128)(2,1)S(1)} %get-tuple-element.73.refs_1_, ...), custom_call_target="tpu_custom_call" | custom-call | flops 536870912 | tf_op jit(solution)/shard_map/attention/pallas_call | solution.py:274
  21.9 0.6 collective-permute-done.3.refs_2_
  22.6 1.4 %qkv.6 = (bf16[256,512]{1,0:T(8,128)(2,1)S(1)}, bf16[256,512]{1,0:T(8,128)(2,1)S(1)}, bf16[256,512]{1,0:T(8,128)(2,1)S(1)}, f32[4,128,128]{2,1,0:T(8,128)S(1)}) custom-call(f32[1,1024]{1,0:T(1,128)S(1)} %copy-done.1, bf16[1024,1536]{1,0:T(8,128)(2,1)S(1)} %bitcast.20, f32[1024,8]{1,0:T(8,128)S(1)} %get-tuple-element.65.fade_ref, ...), custom_call_target="tpu_custom_call" | custom-call | flops 1610612736 | tf_op jit(solution)/shard_map/qkv/pallas_call | solution.py:148
  23.9 1.7 %attention.7.local_ref = bf16[256,512]{1,0:T(8,128)(2,1)S(1)} custom-call(s32[2,2]{1,0:T(2,128)S(1)} %copy-done.3, f32[1,4]{1,0:T(1,128)S(1)} %copy-done.4, bf16[256,512]{1,0:T(8,128)(2,1)S(1)} %get-tuple-element.77.q_ref, bf16[256,512]{1,0:T(8,128)(2,1)S(1)} %get-tuple-element.68.refs_0_, bf16[256,512]{1,0:T(8,128)(2,1)S(1)} %get-tuple-element.73.refs_1_, ...), custom_call_target="tpu_custom_call" | custom-call | flops 805306368 | tf_op jit(solution)/shard_map/attention/pallas_call | solution.py:274
  25.6 1.0 %collective-permute-done.4.refs_2_ = bf16[192,512]{1,0:T(8,128)(2,1)S(1)} collective-permute-done((bf16[192,512]{1,0:T(8,128)(2,1)S(1)}, bf16[192,512]{1,0:T(8,128)(2,1)S(1)}, u32[]{:S(2)}, u32[]{:S(2)}) %collective-permute-start.4) | collective-permute-done | bytes 196640 | tf_op jit(solution)/shard_map/ppermute | solution.py:479
  26.7 1.2 %qkv.7 = (bf16[192,512]{1,0:T(8,128)(2,1)S(1)}, bf16[192,512]{1,0:T(8,128)(2,1)S(1)}, bf16[192,512]{1,0:T(8,128)(2,1)S(1)}, f32[4,128,128]{2,1,0:T(8,128)S(1)}) custom-call(f32[1,1024]{1,0:T(1,128)S(1)} %copy-done.1, bf16[1024,1536]{1,0:T(8,128)(2,1)S(1)} %bitcast.21, f32[1024,8]{1,0:T(8,128)S(1)} %get-tuple-element.65.fade_ref, ...), custom_call_target="tpu_custom_call" | custom-call | flops 1207959552 | tf_op jit(solution)/shard_map/qkv/pallas_call | solution.py:148
  27.9 0.6 last_keys_values.1
  28.5 1.8 %collective-permute-start.5 = (bf16[528,128]{1,0:T(8,128)(2,1)S(1)}, bf16[528,128]{1,0:T(8,128)(2,1)S(1)}, u32[]{:S(2)}, u32[]{:S(2)}) collective-permute-start(bf16[528,128]{1,0:T(8,128)(2,1)S(1)} %get-tuple-element.90.refs_0_), channel_id=1, source_target_pairs={{0,4},{4,0},{8,12},{12,8},{16,20},{20,16},{24,28},{28,24},{1,5},{5... | collective-permute-start | bytes 405512 | tf_op jit(solution)/shard_map/ppermute | solution.py:506
  30.2 1.6 %collective-permute-start.6 = (bf16[528,128]{1,0:T(8,128)(2,1)S(1)}, bf16[528,128]{1,0:T(8,128)(2,1)S(1)}, u32[]{:S(2)}, u32[]{:S(2)}) collective-permute-start(bf16[528,128]{1,0:T(8,128)(2,1)S(1)} %get-tuple-element.90.refs_0_), channel_id=1, source_target_pairs={{0,8},{4,12},{8,0},{12,4},{16,24},{20,28},{24,16},{28,20},{1,9},{5... | collective-permute-start | bytes 405512 | tf_op jit(solution)/shard_map/ppermute | solution.py:506
  32.0 1.7 %attention.8.local_ref = bf16[192,512]{1,0:T(8,128)(2,1)S(1)} custom-call(s32[2,2]{1,0:T(2,128)S(1)} %copy-done.3, f32[1,4]{1,0:T(1,128)S(1)} %copy-done.4, bf16[192,512]{1,0:T(8,128)(2,1)S(1)} %get-tuple-element.87.q_ref, bf16[256,512]{1,0:T(8,128)(2,1)S(1)} %get-tuple-element.68.refs_0_, bf16[256,512]{1,0:T(8,128)(2,1)S(1)} %get-tuple-element.73.refs_1_, ...), custom_call_target="tpu_custom_call" | custom-call | flops 754974720 | tf_op jit(solution)/shard_map/attention/pallas_call | solution.py:274
  34.2 1.3 %collective-permute-done.6.refs_2_ = bf16[528,128]{1,0:T(8,128)(2,1)S(1)} collective-permute-done((bf16[528,128]{1,0:T(8,128)(2,1)S(1)}, bf16[528,128]{1,0:T(8,128)(2,1)S(1)}, u32[]{:S(2)}, u32[]{:S(2)}) %collective-permute-start.6) | collective-permute-done | bytes 135200 | tf_op jit(solution)/shard_map/ppermute | solution.py:506
  35.6 2.2 %collective-permute-done.7.refs_3_ = bf16[528,128]{1,0:T(8,128)(2,1)S(1)} collective-permute-done((bf16[528,128]{1,0:T(8,128)(2,1)S(1)}, bf16[528,128]{1,0:T(8,128)(2,1)S(1)}, u32[]{:S(2)}, u32[]{:S(2)}) %collective-permute-start.7) | collective-permute-done | bytes 135200 | tf_op jit(solution)/shard_map/ppermute | solution.py:506
  38.0 4.7 %collective-permute-start.8 = (bf16[528,128]{1,0:T(8,128)(2,1)S(1)}, bf16[528,128]{1,0:T(8,128)(2,1)S(1)}, u32[]{:S(2)}, u32[]{:S(2)}) collective-permute-start(bf16[528,128]{1,0:T(8,128)(2,1)S(1)} %get-tuple-element.94), channel_id=1, source_target_pairs={{0,16},{4,20},{8,24},{12,28},{1,17},{5,21},{9,25},{13,29},{2,18},{... | collective-permute-start | bytes 405512 | tf_op jit(solution)/shard_map/ppermute | solution.py:518
  43.2 2.0 %attention.9.local_ref = bf16[64,512]{1,0:T(8,128)(2,1)S(1)} custom-call(s32[2,2]{1,0:T(2,128)S(1)} %copy-done.3, f32[1,4]{1,0:T(1,128)S(1)} %copy-done.4, bf16[64,512]{1,0:T(8,128)(2,1)S(1)} %last_queries.1.q_ref, bf16[256,512]{1,0:T(8,128)(2,1)S(1)} %get-tuple-element.68.refs_0_, bf16[256,512]{1,0:T(8,128)(2,1)S(1)} %get-tuple-element.73.refs_1_, ...), custom_call_target="tpu_custom_call" | custom-call | flops 268435456 | tf_op jit(solution)/shard_map/attention/pallas_call | solution.py:274
  45.8 0.6 collective-permute-start.16
  46.9 0.6 collective-permute-start.12
  47.5 0.7 project.9
  48.2 1.6 %collective-permute-start.19 = (bf16[256,512]{1,0:T(8,128)(2,1)S(1)}, bf16[256,512]{1,0:T(8,128)(2,1)S(1)}, u32[]{:S(2)}, u32[]{:S(2)}) collective-permute-start(bf16[256,512]{1,0:T(8,128)(2,1)S(1)} %get-tuple-element.118), channel_id=1, source_target_pairs={{0,1},{1,0},{2,3},{3,2},{4,5},{5,4},{6,7},{7,6},{8,9},{9,8},{10,11... | collective-permute-start | bytes 786440 | tf_op jit(solution)/shard_map/ppermute | solution.py:532
  49.8 0.7 project.8
  50.6 0.6 collective-permute-start.17
  51.1 0.7 project.7
  51.9 1.6 %collective-permute-start.15 = (bf16[256,512]{1,0:T(8,128)(2,1)S(1)}, bf16[256,512]{1,0:T(8,128)(2,1)S(1)}, u32[]{:S(2)}, u32[]{:S(2)}) collective-permute-start(bf16[256,512]{1,0:T(8,128)(2,1)S(1)} %get-tuple-element.110), channel_id=1, source_target_pairs={{0,1},{1,0},{2,3},{3,2},{4,5},{5,4},{6,7},{7,6},{8,9},{9,8},{10,11... | collective-permute-start | bytes 786440 | tf_op jit(solution)/shard_map/ppermute | solution.py:532
  53.5 0.6 project.6
  54.1 0.6 collective-permute-start.13
  54.9 1.2 %collective-permute-done.9.side_ref = bf16[64,512]{1,0:T(8,128)(2,1)S(1)} collective-permute-done((bf16[64,512]{1,0:T(8,128)(2,1)S(1)}, bf16[64,512]{1,0:T(8,128)(2,1)S(1)}, u32[]{:S(2)}, u32[]{:S(2)}) %collective-permute-start.9) | collective-permute-done | bytes 65568 | tf_op jit(solution)/shard_map/ppermute | solution.py:527
  56.6 1.6 %collective-permute-start.11 = (bf16[64,512]{1,0:T(8,128)(2,1)S(1)}, bf16[64,512]{1,0:T(8,128)(2,1)S(1)}, u32[]{:S(2)}, u32[]{:S(2)}) collective-permute-start(bf16[64,512]{1,0:T(8,128)(2,1)S(1)} %get-tuple-element.102), channel_id=1, source_target_pairs={{0,1},{1,0},{2,3},{3,2},{4,5},{5,4},{6,7},{7,6},{8,9},{9,8},{10,11... | collective-permute-start | bytes 196616 | tf_op jit(solution)/shard_map/ppermute | solution.py:532
  58.2 0.8 %finish.5.refs_2_ = bf16[1024,512]{1,0:T(8,128)(2,1)} custom-call(bf16[256,512]{1,0:T(8,128)(2,1)S(1)} %get-tuple-element.117.refs_0_, bf16[256,512]{1,0:T(8,128)(2,1)S(1)} %collective-permute-done.19.refs_1_), custom_call_target="tpu_custom_call" | custom-call | flops 262144 | bytes 786432 | tf_op jit(solution)/shard_map/finish/pallas_call | solution.py:424
  59.0 4.1 %collective-permute-done.17.refs_1_ = bf16[256,512]{1,0:T(8,128)(2,1)S(1)} collective-permute-done((bf16[256,512]{1,0:T(8,128)(2,1)S(1)}, bf16[256,512]{1,0:T(8,128)(2,1)S(1)}, u32[]{:S(2)}, u32[]{:S(2)}) %collective-permute-start.17) | collective-permute-done | bytes 262176 | tf_op jit(solution)/shard_map/ppermute | solution.py:532
  63.1 0.8 %finish.6.refs_2_ = bf16[1024,512]{1,0:T(8,128)(2,1)} custom-call(bf16[256,512]{1,0:T(8,128)(2,1)S(1)} %get-tuple-element.113.refs_0_, bf16[256,512]{1,0:T(8,128)(2,1)S(1)} %collective-permute-done.17.refs_1_, bf16[1024,512]{1,0:T(8,128)(2,1)} %finish.5.refs_2_), custom_call_target="tpu_custom_call", output_to_operand_aliasing={{}: (2, {})} | custom-call | flops 262144 | bytes 786432 | tf_op jit(solution)/shard_map/finish/pallas_call | solution.py:424
  63.9 4.9 %collective-permute-done.15.refs_1_ = bf16[256,512]{1,0:T(8,128)(2,1)S(1)} collective-permute-done((bf16[256,512]{1,0:T(8,128)(2,1)S(1)}, bf16[256,512]{1,0:T(8,128)(2,1)S(1)}, u32[]{:S(2)}, u32[]{:S(2)}) %collective-permute-start.15) | collective-permute-done | bytes 262176 | tf_op jit(solution)/shard_map/ppermute | solution.py:532
  68.7 0.8 %finish.7.refs_2_ = bf16[1024,512]{1,0:T(8,128)(2,1)} custom-call(bf16[256,512]{1,0:T(8,128)(2,1)S(1)} %get-tuple-element.109.refs_0_, bf16[256,512]{1,0:T(8,128)(2,1)S(1)} %collective-permute-done.15.refs_1_, bf16[1024,512]{1,0:T(8,128)(2,1)} %finish.6.refs_2_), custom_call_target="tpu_custom_call", output_to_operand_aliasing={{}: (2, {})} | custom-call | flops 262144 | bytes 786432 | tf_op jit(solution)/shard_map/finish/pallas_call | solution.py:424
  69.5 3.2 %collective-permute-done.13.refs_1_ = bf16[192,512]{1,0:T(8,128)(2,1)S(1)} collective-permute-done((bf16[192,512]{1,0:T(8,128)(2,1)S(1)}, bf16[192,512]{1,0:T(8,128)(2,1)S(1)}, u32[]{:S(2)}, u32[]{:S(2)}) %collective-permute-start.13) | collective-permute-done | bytes 196640 | tf_op jit(solution)/shard_map/ppermute | solution.py:532
  72.7 0.7 finish.8.refs_2_
  73.4 0.6 finish.9
  (40 shorter events, 3.9 us)
Async XLA Ops:
  1.2 14.5 %collective-permute-start.1 = (bf16[256,512]{1,0:T(8,128)(2,1)S(1)}, bf16[256,512]{1,0:T(8,128)(2,1)S(1)}, u32[]{:S(2)}, u32[]{:S(2)}) collective-permute-start(bf16[256,512]{1,0:T(8,128)(2,1)S(1)} %get-tuple-element.120.refs_0_), channel_id=1, source_target_pairs={{1,0},{0,1},{3,2},{2,3},{5,4},{4,5},{7,6},{6,7},{9,8},{8,9},{11,10... | collective-permute-start | bytes 786440 | tf_op jit(solution)/shard_map/ppermute | solution.py:479
  4.2 14.9 %collective-permute-start.2 = (bf16[256,512]{1,0:T(8,128)(2,1)S(1)}, bf16[256,512]{1,0:T(8,128)(2,1)S(1)}, u32[]{:S(2)}, u32[]{:S(2)}) collective-permute-start(bf16[256,512]{1,0:T(8,128)(2,1)S(1)} %get-tuple-element.121.refs_1_), channel_id=1, source_target_pairs={{1,0},{0,1},{3,2},{2,3},{5,4},{4,5},{7,6},{6,7},{9,8},{8,9},{11,10... | collective-permute-start | bytes 786440 | tf_op jit(solution)/shard_map/ppermute | solution.py:479
  4.3 18.3 %collective-permute-start.3 = (bf16[256,512]{1,0:T(8,128)(2,1)S(1)}, bf16[256,512]{1,0:T(8,128)(2,1)S(1)}, u32[]{:S(2)}, u32[]{:S(2)}) collective-permute-start(bf16[256,512]{1,0:T(8,128)(2,1)S(1)} %get-tuple-element.119.refs_1_), channel_id=1, source_target_pairs={{1,0},{0,1},{3,2},{2,3},{5,4},{4,5},{7,6},{6,7},{9,8},{8,9},{11,10... | collective-permute-start | bytes 786440 | tf_op jit(solution)/shard_map/ppermute | solution.py:479
  8.0 0.7 copy-start.2
  8.7 0.7 copy-start.5
  10.8 15.8 %collective-permute-start.4 = (bf16[192,512]{1,0:T(8,128)(2,1)S(1)}, bf16[192,512]{1,0:T(8,128)(2,1)S(1)}, u32[]{:S(2)}, u32[]{:S(2)}) collective-permute-start(bf16[192,512]{1,0:T(8,128)(2,1)S(1)} %slice_bitcast_fusion.3.refs_1_), channel_id=1, source_target_pairs={{1,0},{0,1},{3,2},{2,3},{5,4},{4,5},{7,6},{6,7},{9,8},{8,9},{11,10... | collective-permute-start | bytes 589832 | tf_op jit(solution)/shard_map/ppermute | solution.py:479
  10.9 16.9 %collective-permute-start = (bf16[64,512]{1,0:T(8,128)(2,1)S(1)}, bf16[64,512]{1,0:T(8,128)(2,1)S(1)}, u32[]{:S(2)}, u32[]{:S(2)}) collective-permute-start(bf16[64,512]{1,0:T(8,128)(2,1)S(1)} %slice_bitcast_fusion.4.refs_0_.x_ref), channel_id=1, source_target_pairs={{1,0},{0,1},{3,2},{2,3},{5,4},{4,5},{7,6},{6,7},{9,8},{8,9},{11,10... | collective-permute-start | bytes 196616 | tf_op jit(solution)/shard_map/ppermute | solution.py:479
  12.9 2.5 %copy-start.1 = (f32[1,1024]{1,0:T(1,128)S(1)}, f32[1,1024]{1,0:T(1,128)}, u32[]{:S(2)}) copy-start(f32[1,1024]{1,0:T(1,128)} %gain_ref.13) | copy-start | bytes 12292
  15.3 1.2 %copy-start.6 = (bf16[1,4,128,1024]{3,2,1,0:T(8,128)(2,1)S(1)}, bf16[1,4,128,1024]{3,2,1,0:T(8,128)(2,1)}, u32[]{:S(2)}) copy-start(bf16[1,4,128,1024]{3,2,1,0:T(8,128)(2,1)} %param.17) | copy-start | bytes 3145732
  15.7 2.3 %copy-start.3 = (s32[2,2]{1,0:T(2,128)S(1)}, s32[2,2]{1,0:T(2,128)}, u32[]{:S(2)}) copy-start(s32[2,2]{1,0:T(2,128)} %keep_ref.9) | copy-start | bytes 52
  15.7 2.3 %copy-start.4 = (f32[1,4]{1,0:T(1,128)S(1)}, f32[1,4]{1,0:T(1,128)}, u32[]{:S(2)}) copy-start(f32[1,4]{1,0:T(1,128)} %scale_ref.9) | copy-start | bytes 52
  16.6 30.9 %collective-permute-start.10 = (bf16[512,1024]{1,0:T(8,128)(2,1)S(1)}, bf16[512,1024]{1,0:T(8,128)(2,1)S(1)}, u32[]{:S(2)}, u32[]{:S(2)}) collective-permute-start(bf16[512,1024]{1,0:T(8,128)(2,1)S(1)} %bitcast.31), channel_id=1, source_target_pairs={{0,2},{2,0},{1,3},{3,1},{4,6},{6,4},{5,7},{7,5},{8,10},{10,8},{9,1... | collective-permute-start | bytes 3145736 | tf_op jit(solution)/shard_map/ppermute | solution.py:461
  28.5 5.8 %collective-permute-start.5 = (bf16[528,128]{1,0:T(8,128)(2,1)S(1)}, bf16[528,128]{1,0:T(8,128)(2,1)S(1)}, u32[]{:S(2)}, u32[]{:S(2)}) collective-permute-start(bf16[528,128]{1,0:T(8,128)(2,1)S(1)} %get-tuple-element.90.refs_0_), channel_id=1, source_target_pairs={{0,4},{4,0},{8,12},{12,8},{16,20},{20,16},{24,28},{28,24},{1,5},{5... | collective-permute-start | bytes 405512 | tf_op jit(solution)/shard_map/ppermute | solution.py:506
  30.2 5.3 %collective-permute-start.6 = (bf16[528,128]{1,0:T(8,128)(2,1)S(1)}, bf16[528,128]{1,0:T(8,128)(2,1)S(1)}, u32[]{:S(2)}, u32[]{:S(2)}) collective-permute-start(bf16[528,128]{1,0:T(8,128)(2,1)S(1)} %get-tuple-element.90.refs_0_), channel_id=1, source_target_pairs={{0,8},{4,12},{8,0},{12,4},{16,24},{20,28},{24,16},{28,20},{1,9},{5... | collective-permute-start | bytes 405512 | tf_op jit(solution)/shard_map/ppermute | solution.py:506
  31.8 5.9 %collective-permute-start.7 = (bf16[528,128]{1,0:T(8,128)(2,1)S(1)}, bf16[528,128]{1,0:T(8,128)(2,1)S(1)}, u32[]{:S(2)}, u32[]{:S(2)}) collective-permute-start(bf16[528,128]{1,0:T(8,128)(2,1)S(1)} %get-tuple-element.90.refs_0_), channel_id=1, source_target_pairs={{0,12},{4,8},{8,4},{12,0},{16,28},{20,24},{24,20},{28,16},{1,13},{... | collective-permute-start | bytes 405512 | tf_op jit(solution)/shard_map/ppermute | solution.py:506
  38.0 7.2 %collective-permute-start.8 = (bf16[528,128]{1,0:T(8,128)(2,1)S(1)}, bf16[528,128]{1,0:T(8,128)(2,1)S(1)}, u32[]{:S(2)}, u32[]{:S(2)}) collective-permute-start(bf16[528,128]{1,0:T(8,128)(2,1)S(1)} %get-tuple-element.94), channel_id=1, source_target_pairs={{0,16},{4,20},{8,24},{12,28},{1,17},{5,21},{9,25},{13,29},{2,18},{... | collective-permute-start | bytes 405512 | tf_op jit(solution)/shard_map/ppermute | solution.py:518
  43.2 4.3 %copy-start = (bf16[1,4,128,1024]{3,2,1,0:T(8,128)(2,1)S(1)}, bf16[1,4,128,1024]{3,2,1,0:T(8,128)(2,1)}, u32[]{:S(2)}) copy-start(bf16[1,4,128,1024]{3,2,1,0:T(8,128)(2,1)} %param.16) | copy-start | bytes 3145732
  45.5 2.0 %collective-permute-start.18 = (bf16[256,512]{1,0:T(8,128)(2,1)S(1)}, bf16[256,512]{1,0:T(8,128)(2,1)S(1)}, u32[]{:S(2)}, u32[]{:S(2)}) collective-permute-start(bf16[256,512]{1,0:T(8,128)(2,1)S(1)} %recall.9.own_ref), channel_id=1, source_target_pairs={{0,2},{2,0},{1,3},{3,1},{4,6},{6,4},{5,7},{7,5},{8,10},{10,8},{9,1... | collective-permute-start | bytes 786440 | tf_op jit(solution)/shard_map/ppermute | solution.py:527
  45.8 4.0 %collective-permute-start.16 = (bf16[256,512]{1,0:T(8,128)(2,1)S(1)}, bf16[256,512]{1,0:T(8,128)(2,1)S(1)}, u32[]{:S(2)}, u32[]{:S(2)}) collective-permute-start(bf16[256,512]{1,0:T(8,128)(2,1)S(1)} %recall.8.own_ref), channel_id=1, source_target_pairs={{0,2},{2,0},{1,3},{3,1},{4,6},{6,4},{5,7},{7,5},{8,10},{10,8},{9,1... | collective-permute-start | bytes 786440 | tf_op jit(solution)/shard_map/ppermute | solution.py:527
  46.7 4.5 %collective-permute-start.14 = (bf16[256,512]{1,0:T(8,128)(2,1)S(1)}, bf16[256,512]{1,0:T(8,128)(2,1)S(1)}, u32[]{:S(2)}, u32[]{:S(2)}) collective-permute-start(bf16[256,512]{1,0:T(8,128)(2,1)S(1)} %recall.7.own_ref), channel_id=1, source_target_pairs={{0,2},{2,0},{1,3},{3,1},{4,6},{6,4},{5,7},{7,5},{8,10},{10,8},{9,1... | collective-permute-start | bytes 786440 | tf_op jit(solution)/shard_map/ppermute | solution.py:527
  46.9 6.5 %collective-permute-start.12 = (bf16[192,512]{1,0:T(8,128)(2,1)S(1)}, bf16[192,512]{1,0:T(8,128)(2,1)S(1)}, u32[]{:S(2)}, u32[]{:S(2)}) collective-permute-start(bf16[192,512]{1,0:T(8,128)(2,1)S(1)} %recall.6.own_ref), channel_id=1, source_target_pairs={{0,2},{2,0},{1,3},{3,1},{4,6},{6,4},{5,7},{7,5},{8,10},{10,8},{9,1... | collective-permute-start | bytes 589832 | tf_op jit(solution)/shard_map/ppermute | solution.py:527
  48.2 10.0 %collective-permute-start.19 = (bf16[256,512]{1,0:T(8,128)(2,1)S(1)}, bf16[256,512]{1,0:T(8,128)(2,1)S(1)}, u32[]{:S(2)}, u32[]{:S(2)}) collective-permute-start(bf16[256,512]{1,0:T(8,128)(2,1)S(1)} %get-tuple-element.118), channel_id=1, source_target_pairs={{0,1},{1,0},{2,3},{3,2},{4,5},{5,4},{6,7},{7,6},{8,9},{9,8},{10,11... | collective-permute-start | bytes 786440 | tf_op jit(solution)/shard_map/ppermute | solution.py:532
  50.6 12.5 %collective-permute-start.17 = (bf16[256,512]{1,0:T(8,128)(2,1)S(1)}, bf16[256,512]{1,0:T(8,128)(2,1)S(1)}, u32[]{:S(2)}, u32[]{:S(2)}) collective-permute-start(bf16[256,512]{1,0:T(8,128)(2,1)S(1)} %get-tuple-element.114), channel_id=1, source_target_pairs={{0,1},{1,0},{2,3},{3,2},{4,5},{5,4},{6,7},{7,6},{8,9},{9,8},{10,11... | collective-permute-start | bytes 786440 | tf_op jit(solution)/shard_map/ppermute | solution.py:532
  51.9 16.8 %collective-permute-start.15 = (bf16[256,512]{1,0:T(8,128)(2,1)S(1)}, bf16[256,512]{1,0:T(8,128)(2,1)S(1)}, u32[]{:S(2)}, u32[]{:S(2)}) collective-permute-start(bf16[256,512]{1,0:T(8,128)(2,1)S(1)} %get-tuple-element.110), channel_id=1, source_target_pairs={{0,1},{1,0},{2,3},{3,2},{4,5},{5,4},{6,7},{7,6},{8,9},{9,8},{10,11... | collective-permute-start | bytes 786440 | tf_op jit(solution)/shard_map/ppermute | solution.py:532
  54.1 18.6 %collective-permute-start.13 = (bf16[192,512]{1,0:T(8,128)(2,1)S(1)}, bf16[192,512]{1,0:T(8,128)(2,1)S(1)}, u32[]{:S(2)}, u32[]{:S(2)}) collective-permute-start(bf16[192,512]{1,0:T(8,128)(2,1)S(1)} %get-tuple-element.106), channel_id=1, source_target_pairs={{0,1},{1,0},{2,3},{3,2},{4,5},{5,4},{6,7},{7,6},{8,9},{9,8},{10,11... | collective-permute-start | bytes 589832 | tf_op jit(solution)/shard_map/ppermute | solution.py:532
  54.8 1.3 %collective-permute-start.9 = (bf16[64,512]{1,0:T(8,128)(2,1)S(1)}, bf16[64,512]{1,0:T(8,128)(2,1)S(1)}, u32[]{:S(2)}, u32[]{:S(2)}) collective-permute-start(bf16[64,512]{1,0:T(8,128)(2,1)S(1)} %recall.5.own_ref), channel_id=1, source_target_pairs={{0,2},{2,0},{1,3},{3,1},{4,6},{6,4},{5,7},{7,5},{8,10},{10,8},{9,1... | collective-permute-start | bytes 196616 | tf_op jit(solution)/shard_map/ppermute | solution.py:527
  56.6 16.8 %collective-permute-start.11 = (bf16[64,512]{1,0:T(8,128)(2,1)S(1)}, bf16[64,512]{1,0:T(8,128)(2,1)S(1)}, u32[]{:S(2)}, u32[]{:S(2)}) collective-permute-start(bf16[64,512]{1,0:T(8,128)(2,1)S(1)} %get-tuple-element.102), channel_id=1, source_target_pairs={{0,1},{1,0},{2,3},{3,2},{4,5},{5,4},{6,7},{7,6},{8,9},{9,8},{10,11... | collective-permute-start | bytes 196616 | tf_op jit(solution)/shard_map/ppermute | solution.py:532
